TPU v7x, 32 devices: a whole 2x2x4 slice. The times are simulated.
32 devices in a mesh: expert: 8 (over z, x), dp: 4 (over y, core).
Axes of the slice: x: 2, y: 2, z: 4, core: 2. Of those that a mesh axis runs over, the one named last changes fastest.
Arguments:
- block_in: bfloat16 [32768, 1024], P(('expert', 'dp')), may hold values from -6 to 6
- seq_lengths: int32 [32, 16], P(('expert', 'dp')), may hold values from 0 to 1024, as said below
- slot_position: int32 [32, 1024], P(('expert', 'dp')), may hold values from 0 to 1023, as said below
- first_gain: float32 [1024], replicated, may hold values from 0.5 to 1.5
- first_bias: float32 [1024], replicated, may hold values from -1.2 to 1.2
- query_weight: bfloat16 [1024, 1024], replicated, may hold values from -0.1875 to 0.1875
- query_bias: float32 [1024], replicated, may hold values from -1.2 to 1.2
- key_weight: bfloat16 [1024, 1024], replicated, may hold values from -0.1875 to 0.1875
- value_weight: bfloat16 [1024, 1024], replicated, may hold values from -0.1875 to 0.1875
- value_bias: float32 [1024], replicated, may hold values from -1.2 to 1.2
- out_weight: bfloat16 [1024, 1024], replicated, may hold values from -1.5 to 1.5
- out_bias: float32 [1024], replicated, may hold values from -0.6 to 0.6
- second_gain: float32 [1024], replicated, may hold values from 0.5 to 1.5
- second_bias: float32 [1024], replicated, may hold values from -0.6 to 0.6
- expert_up: bfloat16 [8, 1024, 4096], P('expert', None, 'dp'), may hold values from -0.1875 to 0.1875
- expert_up_bias: float32 [8, 4096], P('expert'), may hold values from -0.6 to 0.6
- expert_down: bfloat16 [8, 4096, 1024], P('expert', 'dp'), may hold values from -0.09375 to 0.09375
- expert_down_bias: float32 [8, 1024], P('expert'), may hold values from -0.6 to 0.6
- block_cot: bfloat16 [32768, 1024], P(('expert', 'dp')), may hold values from -6 to 6
Outputs:
- block_out: bfloat16 [32768, 1024], P(('expert', 'dp'))
- input_grad: bfloat16 [32768, 1024], P(('expert', 'dp'))
- grad_first_gain: float32 [1024], replicated
- grad_first_bias: float32 [1024], replicated
- grad_query_weight: float32 [1024, 1024], replicated
- grad_query_bias: float32 [1024], replicated
- grad_key_weight: float32 [1024, 1024], replicated
- grad_value_weight: float32 [1024, 1024], replicated
- grad_value_bias: float32 [1024], replicated
- grad_out_weight: float32 [1024, 1024], replicated
- grad_out_bias: float32 [1024], replicated
- grad_second_gain: float32 [1024], replicated
- grad_second_bias: float32 [1024], replicated
- grad_expert_up: float32 [8, 1024, 4096], P('expert', None, 'dp')
- grad_expert_up_bias: float32 [8, 4096], P('expert', 'dp')
- grad_expert_down: float32 [8, 4096, 1024], P('expert', 'dp')
- grad_expert_down_bias: float32 [8, 1024], P('expert', 'dp')
Inputs may be any that keep to these rules, and one draw needn't show every extreme that they name: `seq_lengths`: each row lists the group's dialogue lengths, each 64 or more, first, then zeros; a row sums to at most 1024. `slot_position`: each row is a permutation of 0 to 1023.
All inputs are finite; a program needn't handle non-finite values.
Results may differ from a plain program's by a relative error of at most 0.012.
Values may be sent and summed in bfloat16 or wider, within the bound.
No kernel may reach another device: no remote copies, remote signals or barrier semaphores. Data moves between devices by JAX's collectives and lax.ppermute only.
A program may use at most 384 MiB of HBM per device.

v0:
```python
import math

import jax
import jax.numpy as jnp
from jax import lax
from jax.sharding import PartitionSpec as P

HEADS = 16
MAXLEN = 1024


epsilon = 1e-05
negative = -1e30


def inner_rows(left, right):
    return lax.dot_general(
        left, right, (((0,), (0,)), ((), ())), preferred_element_type=jnp.float32
    )


def outer_cols(left, right):
    return lax.dot_general(
        left, right, (((1,), (1,)), ((), ())), preferred_element_type=jnp.float32
    )


def layer_norm(values, gain_row, offset):
    center = values - jnp.mean(values, axis=-1, keepdims=True)
    variance = jnp.mean(center * center, axis=-1, keepdims=True)
    inverse_root = lax.rsqrt(variance + epsilon)
    normal = center * inverse_root
    return (normal * gain_row + offset, normal, inverse_root)


def norm_back(grad_norm, normal, inverse_root, gain_row):
    scaled = grad_norm * gain_row
    mean_plain = jnp.mean(scaled, axis=-1, keepdims=True)
    mean_normal = jnp.mean(scaled * normal, axis=-1, keepdims=True)
    grad_values = inverse_root * (scaled - mean_plain - normal * mean_normal)
    return (grad_values, jnp.sum(grad_norm * normal, axis=0), jnp.sum(grad_norm, axis=0))


def gelu_back(pre_act, grad_act):
    return jax.vjp(jax.nn.gelu, pre_act)[1](grad_act)[0]


def per_device(
    block_in,
    seq_lengths,
    slot_position,
    first_gain,
    first_bias,
    query_weight,
    query_bias,
    key_weight,
    value_weight,
    value_bias,
    out_weight,
    out_bias,
    second_gain,
    second_bias,
    expert_up,
    expert_up_bias,
    expert_down,
    expert_down_bias,
    block_cot,
):
    slot_count, model_width = block_in.shape
    head_count = HEADS
    head_dim = model_width // head_count
    scale_factor = 1.0 / math.sqrt(head_dim)
    query_rows = min(512, slot_count)
    key_rows = min(slot_count, MAXLEN + query_rows)
    block_count = slot_count // query_rows
    position = slot_position[0]
    indices = jnp.arange(slot_count, dtype=jnp.int32)
    inverse = jnp.zeros((slot_count,), jnp.int32).at[position].set(indices)
    end_points = jnp.cumsum(seq_lengths[0])
    segment = jnp.sum((indices[:, None] >= end_points[None, :]).astype(jnp.int32), axis=1)
    live_mask = (indices < end_points[-1]).astype(jnp.float32)
    arrived = lax.all_to_all(block_in, "expert", split_axis=0, concat_axis=0, tiled=True)
    tokens = arrived[inverse].astype(jnp.float32)
    normed_full, first_normal, first_root = layer_norm(tokens, first_gain, first_bias)
    normed = normed_full.astype(jnp.bfloat16)
    query = (jnp.dot(normed, query_weight, preferred_element_type=jnp.float32) + query_bias).astype(
        jnp.bfloat16
    )
    keys_all = jnp.dot(normed, key_weight, preferred_element_type=jnp.float32).astype(jnp.bfloat16)
    values_all = (
        jnp.dot(normed, value_weight, preferred_element_type=jnp.float32) + value_bias
    ).astype(jnp.bfloat16)

    def block_scores(block_id):
        query_start = block_id * query_rows
        key_start = jnp.clip(query_start + query_rows - key_rows, 0, slot_count - key_rows)
        query_block = lax.dynamic_slice_in_dim(query, query_start, query_rows, 0).reshape(
            query_rows, head_count, head_dim
        )
        key_block = keys_all.reshape(key_rows, head_count, head_dim)
        value_block = values_all.reshape(key_rows, head_count, head_dim)
        scores = (
            jnp.einsum("qhd,khd->hqk", query_block, key_block, preferred_element_type=jnp.float32)
            * scale_factor
        )
        query_pos = query_start + jnp.arange(query_rows, dtype=jnp.int32)
        key_pos = key_start + jnp.arange(key_rows, dtype=jnp.int32)
        query_seg = lax.dynamic_slice_in_dim(segment, query_start, query_rows, 0)
        query_live = lax.dynamic_slice_in_dim(live_mask, query_start, query_rows, 0) > 0.5
        allowed = (query_seg[:, None] == segment[None, :]) & (
            key_pos[None, :] <= query_pos[:, None]
        ) & query_live[:, None] | (key_pos[None, :] == query_pos[:, None])
        masked = jnp.where(allowed[None], scores, negative)
        return (masked, query_block, key_block, value_block, query_start, key_start)

    def forward_block(block_id):
        masked, query_block, key_block, value_block, query_start, key_start = block_scores(block_id)
        row_max = jnp.max(masked, axis=2, keepdims=True)
        exp_terms = jnp.exp(masked - row_max)
        row_total = jnp.sum(exp_terms, axis=2, keepdims=True)
        weights_low = (exp_terms / row_total).astype(jnp.bfloat16)
        mixed_block = jnp.einsum(
            "hqk,khd->qhd", weights_low, value_block, preferred_element_type=jnp.float32
        )
        return (
            mixed_block.reshape(query_rows, model_width).astype(jnp.bfloat16),
            (row_max + jnp.log(row_total))[:, :, 0],
        )

    mixed_blocks, log_totals = lax.map(forward_block, jnp.arange(block_count, dtype=jnp.int32))
    mixed_heads = mixed_blocks.reshape(slot_count, model_width)
    projected = jnp.dot(mixed_heads, out_weight, preferred_element_type=jnp.float32) + out_bias
    residual = tokens + live_mask[:, None] * projected
    residual_low = residual.astype(jnp.bfloat16)
    routed, route_live = (
        lax.all_to_all(residual_low[position], "expert", split_axis=0, concat_axis=0, tiled=True),
        lax.all_to_all(
            live_mask.astype(jnp.bfloat16)[position],
            "expert",
            split_axis=0,
            concat_axis=0,
            tiled=True,
        ),
    )
    routed_full = routed.astype(jnp.float32)
    expert_live = route_live.astype(jnp.float32)[:, None]
    ffn_full, second_normal, second_root = layer_norm(routed_full, second_gain, second_bias)
    ffn_in = ffn_full.astype(jnp.bfloat16)
    cot_full = block_cot.astype(jnp.float32)
    grad_branch = (expert_live * cot_full).astype(jnp.bfloat16)
    up_full, down_full = (
        lax.all_gather(expert_up, "dp", axis=2, tiled=True),
        lax.all_gather(expert_down, "dp", axis=1, tiled=True),
    )
    pre_act = jnp.dot(ffn_in, up_full[0], preferred_element_type=jnp.float32) + expert_up_bias[0]
    activation = jax.nn.gelu(pre_act).astype(jnp.bfloat16)
    branch_out = (
        jnp.dot(activation, down_full[0], preferred_element_type=jnp.float32) + expert_down_bias[0]
    )
    block_out = (routed_full + expert_live * branch_out).astype(jnp.bfloat16)
    up_full, down_full = (
        lax.all_gather(expert_up, "dp", axis=2, tiled=True),
        lax.all_gather(expert_down, "dp", axis=1, tiled=True),
    )
    grad_down = inner_rows(activation, grad_branch)
    grad_down_bias = jnp.sum(grad_branch.astype(jnp.float32), axis=0)
    grad_act = outer_cols(grad_branch, down_full[0])
    grad_pre = gelu_back(pre_act, grad_act).astype(jnp.bfloat16)
    grad_up = inner_rows(ffn_in, grad_pre)
    grad_up_bias = jnp.sum(grad_pre.astype(jnp.float32), axis=0)
    grad_ffn_in = outer_cols(grad_pre, up_full[0])
    grad_up_local, grad_down_local, grad_up_bias_local, grad_down_bias_local = (
        lax.psum_scatter(
            grad_up[None].astype(jnp.bfloat16), "dp", scatter_dimension=2, tiled=True
        ).astype(jnp.float32),
        lax.psum_scatter(
            grad_down[None].astype(jnp.bfloat16), "dp", scatter_dimension=1, tiled=True
        ).astype(jnp.float32),
        lax.psum_scatter(
            grad_up_bias[None].astype(jnp.bfloat16), "dp", scatter_dimension=1, tiled=True
        ).astype(jnp.float32),
        lax.psum_scatter(
            grad_down_bias[None].astype(jnp.bfloat16), "dp", scatter_dimension=1, tiled=True
        ).astype(jnp.float32),
    )
    grad_norm_in, grad_second_gain, grad_second_bias = norm_back(
        grad_ffn_in, second_normal, second_root, second_gain
    )
    grad_routed = (cot_full + grad_norm_in).astype(jnp.bfloat16)
    grad_arrived = lax.all_to_all(grad_routed, "expert", split_axis=0, concat_axis=0, tiled=True)
    grad_residual = grad_arrived[inverse].astype(jnp.float32)
    grad_proj = live_mask[:, None] * grad_residual
    grad_proj_low = grad_proj.astype(jnp.bfloat16)
    grad_out_weight = inner_rows(mixed_heads, grad_proj_low)
    grad_out_bias = jnp.sum(grad_proj, axis=0)
    grad_mixed = outer_cols(grad_proj_low, out_weight).astype(jnp.bfloat16)

    def backward_block(carried, block_id):
        grad_keys, grad_values = carried
        masked, query_block, key_block, value_block, query_start, key_start = block_scores(block_id)
        weights_full = jnp.exp(masked - log_totals[block_id][:, :, None])
        weights_low = weights_full.astype(jnp.bfloat16)
        grad_block = lax.dynamic_slice_in_dim(grad_mixed, query_start, query_rows, 0).reshape(
            query_rows, head_count, head_dim
        )
        value_part = jnp.einsum(
            "hqk,qhd->khd", weights_low, grad_block, preferred_element_type=jnp.float32
        )
        grad_weights = jnp.einsum(
            "qhd,khd->hqk", grad_block, value_block, preferred_element_type=jnp.float32
        )
        row_inner = jnp.sum(weights_full * grad_weights, axis=2, keepdims=True)
        grad_scores = (weights_full * (grad_weights - row_inner)).astype(jnp.bfloat16)
        query_part = (
            jnp.einsum("hqk,khd->qhd", grad_scores, key_block, preferred_element_type=jnp.float32)
            * scale_factor
        )
        key_part = (
            jnp.einsum("hqk,qhd->khd", grad_scores, query_block, preferred_element_type=jnp.float32)
            * scale_factor
        )
        old_keys = grad_keys
        grad_keys = old_keys + key_part.reshape(key_rows, model_width)
        old_values = grad_values
        grad_values = old_values + value_part.reshape(key_rows, model_width)
        return ((grad_keys, grad_values), query_part.reshape(query_rows, model_width))

    empty_grad = jnp.zeros((slot_count, model_width), jnp.float32)
    (grad_keys, grad_values), query_blocks = lax.scan(
        backward_block, (empty_grad, empty_grad), jnp.arange(block_count, dtype=jnp.int32)
    )
    grad_query = query_blocks.reshape(slot_count, model_width).astype(jnp.bfloat16)
    grad_key = grad_keys.astype(jnp.bfloat16)
    grad_value = grad_values.astype(jnp.bfloat16)
    grad_query_weight = inner_rows(normed, grad_query)
    grad_key_weight = inner_rows(normed, grad_key)
    grad_value_weight = inner_rows(normed, grad_value)
    grad_query_bias = jnp.sum(grad_query.astype(jnp.float32), axis=0)
    grad_value_bias = jnp.sum(grad_value.astype(jnp.float32), axis=0)
    grad_normed = (
        outer_cols(grad_query, query_weight)
        + outer_cols(grad_key, key_weight)
        + outer_cols(grad_value, value_weight)
    )
    grad_norm_tokens, grad_first_gain, grad_first_bias = norm_back(
        grad_normed, first_normal, first_root, first_gain
    )
    grad_tokens = (grad_residual + grad_norm_tokens).astype(jnp.bfloat16)
    input_grad = lax.all_to_all(
        grad_tokens[position], "expert", split_axis=0, concat_axis=0, tiled=True
    )
    shared = lax.psum(
        (
            grad_first_gain,
            grad_first_bias,
            grad_query_weight,
            grad_query_bias,
            grad_key_weight,
            grad_value_weight,
            grad_value_bias,
            grad_out_weight,
            grad_out_bias,
            grad_second_gain,
            grad_second_bias,
        ),
        ("expert", "dp"),
    )
    return (
        block_out,
        input_grad,
        shared[0],
        shared[1],
        shared[2],
        shared[3],
        shared[4],
        shared[5],
        shared[6],
        shared[7],
        shared[8],
        shared[9],
        shared[10],
        grad_up_local,
        grad_up_bias_local,
        grad_down_local,
        grad_down_bias_local,
    )


def solution(mesh):
    return jax.shard_map(
        per_device,
        mesh=mesh,
        in_specs=(
            P(("expert", "dp"), None),
            P(("expert", "dp"), None),
            P(("expert", "dp"), None),
            P(),
            P(),
            P(),
            P(),
            P(),
            P(),
            P(),
            P(),
            P(),
            P(),
            P(),
            P("expert", None, "dp"),
            P("expert", None),
            P("expert", "dp", None),
            P("expert", None),
            P(("expert", "dp"), None),
        ),
        out_specs=(
            P(("expert", "dp"), None),
            P(("expert", "dp"), None),
            P(),
            P(),
            P(),
            P(),
            P(),
            P(),
            P(),
            P(),
            P(),
            P(),
            P(),
            P("expert", None, "dp"),
            P("expert", "dp"),
            P("expert", "dp", None),
            P("expert", "dp"),
        ),
        check_vma=False,
    )
```

profile of v0, /device:TPU:9, one launch (start us, length us, event | category | flops | bytes accessed | tf_op | source)
XLA Modules:
  0.0 1054.7 jit_solution(4508909288248003772)
XLA Ops:
  8.0 5.7 all-to-all-start
  20.2 6.8 gather_fusion.2
  28.4 31.8 %all-to-all-done = bf16[8,128,1024]{2,1,0:T(8,128)(2,1)} async-done(((bf16[8,128,1024]{2,1,0:T(8,128)(2,1)}), bf16[8,128,1024]{2,1,0:T(8,128)(2,1)}, u32[]{:S(2)}, u32[]{:S(2)}) %all-to-all-start) | async-done | bytes 2097184 | tf_op jit(solution)/shard_map/all_to_all | solution.py:82
  60.2 5.6 all-to-all-start.2
  65.8 7.9 gather_fusion
  86.2 5.9 convolution_convert_fusion.1
  96.1 5.9 add_convert_fusion.1
  106.0 100.8 %while.35 = (s32[]{:T(128)}, bf16[2,512,1024]{2,1,0:T(8,128)(2,1)}, f32[2,16,512]{2,1,0:T(8,128)S(1)}, s32[2]{0:T(128)S(1)}, s32[1024]{0:T(1024)S(1)}, /*index=5...) while((s32[]{:T(128)}, bf16[2,512,1024]{2,1,0:T(8,128)(2,1)}, ...), condition=%wide.region_8.9_spmd, body=%wide.region_5.8_spmd.sunk | while | flops 2251810816 | bytes 132408632 | solution.py:130
  109.7 14.0 %fusion.147 = (f32[16,512]{1,0:T(8,128)S(1)}, f32[16,512,1024]{2,1,0:T(8,128)}) fusion(pred[512,1024]{1,0:T(8,128)(4,1)S(1)} %compare_or_fusion.4, bf16[512,16,64]{0,2,1:T(8,128)(2,1)S(1)} %bitcast.195, bf16[1024,16,64]{0,2,1:T(8,128)(2,1)S(1)} %bitcast.190), kind=kOutput, calls=%fused_computation.9.clone.1 | convolution fusion | flops 1098899456 | bytes 37257216 | tf_op jit(solution)/shard_map/while/body/eval_jaxpr/qhd,khd->hqk/dot_general | solution.py:103
  123.7 15.1 %fusion.148 = f32[16,512]{1,0:T(8,128)S(1)} fusion(f32[16,512,1024]{2,1,0:T(8,128)} %get-tuple-element.765, f32[16,512]{1,0:T(8,128)S(1)} %get-tuple-element.766, pred[512,1024]{1,0:T(8,128)(4,1)S(1)} %compare_or_fusion.4), kind=kLoop, calls=%fused_computation.10.clone.1 | loop fusion | flops 33546240 | bytes 34144256 | tf_op jit(solution)/shard_map/while/body/eval_jaxpr/reduce_sum | solution.py:120
  138.8 15.2 %fusion.149 = bf16[16,512,64]{1,2,0:T(8,128)(2,1)} fusion(bf16[1024,16,64]{0,2,1:T(8,128)(2,1)S(1)} %bitcast.198, f32[16,512,1024]{2,1,0:T(8,128)} %get-tuple-element.765, f32[16,512]{1,0:T(8,128)S(1)} %fusion.148, f32[16,512]{1,0:T(8,128)S(1)} %get-tuple-element.766, pred[512,1024]{1,0:T(8,128)(4,1)S(1)} %compare_or_fusion.4), kind=kOutput, calls=%fused_computation.13.clone.1 | convolution fusion | flops 1116209152 | bytes 37289984 | tf_op jit(solution)/shard_map/while/body/eval_jaxpr/hqk,khd->qhd/dot_general | solution.py:122
  160.1 13.8 %fusion.147 = (f32[16,512]{1,0:T(8,128)S(1)}, f32[16,512,1024]{2,1,0:T(8,128)}) fusion(pred[512,1024]{1,0:T(8,128)(4,1)S(1)} %compare_or_fusion.4, bf16[512,16,64]{0,2,1:T(8,128)(2,1)S(1)} %bitcast.195, bf16[1024,16,64]{0,2,1:T(8,128)(2,1)S(1)} %bitcast.190), kind=kOutput, calls=%fused_computation.9.clone.1 | convolution fusion | flops 1098899456 | bytes 37257216 | tf_op jit(solution)/shard_map/while/body/eval_jaxpr/qhd,khd->hqk/dot_general | solution.py:103
  173.9 15.0 %fusion.148 = f32[16,512]{1,0:T(8,128)S(1)} fusion(f32[16,512,1024]{2,1,0:T(8,128)} %get-tuple-element.765, f32[16,512]{1,0:T(8,128)S(1)} %get-tuple-element.766, pred[512,1024]{1,0:T(8,128)(4,1)S(1)} %compare_or_fusion.4), kind=kLoop, calls=%fused_computation.10.clone.1 | loop fusion | flops 33546240 | bytes 34144256 | tf_op jit(solution)/shard_map/while/body/eval_jaxpr/reduce_sum | solution.py:120
  189.0 15.2 %fusion.149 = bf16[16,512,64]{1,2,0:T(8,128)(2,1)} fusion(bf16[1024,16,64]{0,2,1:T(8,128)(2,1)S(1)} %bitcast.198, f32[16,512,1024]{2,1,0:T(8,128)} %get-tuple-element.765, f32[16,512]{1,0:T(8,128)S(1)} %fusion.148, f32[16,512]{1,0:T(8,128)S(1)} %get-tuple-element.766, pred[512,1024]{1,0:T(8,128)(4,1)S(1)} %compare_or_fusion.4), kind=kOutput, calls=%fused_computation.13.clone.1 | convolution fusion | flops 1116209152 | bytes 37289984 | tf_op jit(solution)/shard_map/while/body/eval_jaxpr/hqk,khd->qhd/dot_general | solution.py:122
  206.8 6.6 fusion.47
  213.4 7.9 gather_fusion.1
  221.3 5.4 all-to-all-start.1
  230.9 41.9 %all-to-all-done.1 = bf16[8,128,1024]{2,1,0:T(8,128)(2,1)} async-done(((bf16[8,128,1024]{2,1,0:T(8,128)(2,1)}), bf16[8,128,1024]{2,1,0:T(8,128)(2,1)}, u32[]{:S(2)}, u32[]{:S(2)}) %all-to-all-start.1) | async-done | bytes 2097184 | tf_op jit(solution)/shard_map/all_to_all | solution.py:136
  280.8 16.1 %fusion.25 = f32[1024,4096]{1,0:T(8,128)} fusion(bf16[1024,1024]{1,0:T(8,128)(2,1)} %bitcast.208, bf16[1,1024,4096]{2,1,0:T(8,128)(2,1)} %all-gather.3.cloned.1.call-done), kind=kOutput, calls=%fused_computation.58 | convolution fusion | flops 8589934592 | bytes 27262976 | tf_op jit(solution)/shard_map/dot_general | solution.py:155
  296.9 26.1 %fusion.95 = (bf16[4096]{0:T(1024)(128)(2,1)S(1)}, bf16[1024,4096]{1,0:T(8,128)(2,1)}) fusion(f32[1024,4096]{1,0:T(8,128)} %fusion.25, f32[4096]{0:T(1024)S(1)} %bitcast.217, bf16[1,4096,1024]{2,1,0:T(8,128)(2,1)} %all-gather.5.cloned.1.call-done, bf16[1024,1024]{1,0:T(8,128)(2,1)} %param.41, f32[1024]{0:T(1024)S(1)} %bitcast_convert_fusion), kind=kOutput, calls=%fused_computation.153 | convolution fusion | flops 8685350912 | bytes 35680256 | tf_op jit(solution)/shard_map/dot_general | solution.py:23
  324.9 19.6 %convert_bitcast_fusion = bf16[1,4096,1024]{2,1,0:T(8,128)(2,1)} fusion(bf16[1024,1024]{1,0:T(8,128)(2,1)} %param.41, f32[1024]{0:T(1024)S(1)} %bitcast_convert_fusion, f32[1024,4096]{1,0:T(8,128)} %fusion.25, f32[4096]{0:T(1024)S(1)} %bitcast.218), kind=kOutput, calls=%fused_computation.60 | convolution fusion | flops 8639217664 | bytes 27283456 | tf_op jit(solution)/shard_map/dot_general | solution.py:17
  344.5 16.8 %fusion.63 = (f32[1024]{0:T(1024)}, f32[1024]{0:T(1024)S(1)}, f32[1024]{0:T(1024)S(1)}, f32[1024]{0:T(1024)}, bf16[1024,1024]{1,0:T(8,128)(2,1)}, /*index=5*/f32[1024,1024]{1,0:T(8,128)S(1)}) fusion(bf16[8,128,1024]{2,1,0:T(8,128)(2,1)} %all-to-all-done.1, f32[1024]{0:T(1024)S(1)} %get-tuple-element.635, f32[1024]{0:T(1024)S(1)} %get-tuple-element.633, ...), kind=kOutput, calls=%fused_computation.107 | convolution fusion | flops 8603561984 | bytes 25198592 | tf_op jit(solution)/shard_map/dot_general | solution.py:23
  365.6 6.0 all-to-all-start.3
  372.1 14.9 %convert_bitcast_fusion.1 = bf16[1,1024,4096]{2,1,0:T(8,128)(2,1)} fusion(bf16[1024,1024]{1,0:T(8,128)(2,1)} %get-tuple-element.630, bf16[1024,4096]{1,0:T(8,128)(2,1)} %get-tuple-element.640), kind=kOutput, calls=%fused_computation.61 | convolution fusion | flops 8594128896 | bytes 18874368 | tf_op jit(solution)/shard_map/dot_general | solution.py:17
  387.1 31.0 %all-to-all-done.3 = bf16[8,128,1024]{2,1,0:T(8,128)(2,1)} async-done(((bf16[8,128,1024]{2,1,0:T(8,128)(2,1)}), bf16[8,128,1024]{2,1,0:T(8,128)(2,1)}, u32[]{:S(2)}, u32[]{:S(2)}) %all-to-all-start.3) | async-done | bytes 2097184 | tf_op jit(solution)/shard_map/all_to_all | solution.py:190
  418.1 7.9 gather_fusion.3
  426.1 6.9 fusion.72
  436.7 252.5 %while.36 = (s32[]{:T(128)}, f32[1024,1024]{0,1:T(8,128)}, f32[1024,1024]{0,1:T(8,128)}, bf16[2,512,1024]{2,1,0:T(8,128)(2,1)}, s32[2]{0:T(128)S(1)}, /*index=5*...) while((s32[]{:T(128)}, f32[1024,1024]{0,1:T(8,128)}, ...), condition=%wide.region_15.16_spmd.clone, body=%wide.region_13.15_spmd.clone.sunk | while | flops 5503969280 | bytes 330556864 | solution.py:229
  448.3 13.9 %fusion.160 = f32[16,512,1024]{2,1,0:T(8,128)} fusion(bf16[512,16,64]{0,2,1:T(8,128)(2,1)S(1)} %bitcast.193, bf16[1024,16,64]{0,2,1:T(8,128)(2,1)S(1)} %bitcast.192), kind=kOutput, calls=%fused_computation.154.clone.1 | convolution fusion | flops 1073741824 | bytes 36700160 | tf_op jit(solution)/shard_map/while/body/eval_jaxpr/qhd,khd->hqk/dot_general | solution.py:103
  462.2 16.7 %fusion.161 = f32[16,64,1024]{2,1,0:T(8,128)} fusion(bf16[512,16,64]{0,2,1:T(8,128)(2,1)S(1)} %bitcast.196, f32[16,512,1024]{2,1,0:T(8,128)} %fusion.160, f32[16,512]{1,0:T(8,128)S(1)} %dynamic-slice_bitcast_fusion.2, pred[512,1024]{1,0:T(8,128)(4,1)S(1)} %compare_or_fusion.5), kind=kOutput, calls=%fused_computation.26.clone.1 | convolution fusion | flops 1107296256 | bytes 39354368 | tf_op jit(solution)/shard_map/while/body/eval_jaxpr/hqk,qhd->khd/dot_general | solution.py:206
  478.9 25.8 %multiply_reduce_fusion.4 = (f32[16,512]{1,0:T(8,128)S(1)}, f32[16,512,1024]{2,1,0:T(8,128)}) fusion(f32[16,512,1024]{2,1,0:T(8,128)} %fusion.160, f32[16,512]{1,0:T(8,128)S(1)} %dynamic-slice_bitcast_fusion.2, pred[512,1024]{1,0:T(8,128)(4,1)S(1)} %compare_or_fusion.5, bf16[512,16,64]{0,2,1:T(8,128)(2,1)S(1)} %bitcast.197, ...), kind=kOutput, calls=%fused_computation.23.clone.1 | convolution fusion | flops 1115676672 | bytes 70844416 | tf_op jit(solution)/shard_map/while/body/eval_jaxpr/qhd,khd->hqk/dot_general | solution.py:209
  504.7 27.8 %multiply_convert_fusion.5 = bf16[16,512,1024]{2,1,0:T(8,128)(2,1)} fusion(f32[16,512,1024]{2,1,0:T(8,128)} %get-tuple-element.779, f32[16,512,1024]{2,1,0:T(8,128)} %fusion.160, f32[16,512]{1,0:T(8,128)S(1)} %get-tuple-element.780, f32[16,512]{1,0:T(8,128)S(1)} %dynamic-slice_bitcast_fusion.2, pred[512,1024]{1,0:T(8,128)(4,1)S(1)} %compare_or_fusion.5), kind=kLoop, calls=%fused_computation.22.clone.1 | loop fusion | flops 50331648 | bytes 84475904 | tf_op jit(solution)/shard_map/while/body/eval_jaxpr/convert_element_type | solution.py:213
  532.5 10.2 convolution_multiply_fusion.5
  542.7 8.9 convolution_multiply_fusion.4
  551.6 8.2 bitcast_add_fusion.4
  573.4 13.1 %fusion.160 = f32[16,512,1024]{2,1,0:T(8,128)} fusion(bf16[512,16,64]{0,2,1:T(8,128)(2,1)S(1)} %bitcast.193, bf16[1024,16,64]{0,2,1:T(8,128)(2,1)S(1)} %bitcast.192), kind=kOutput, calls=%fused_computation.154.clone.1 | convolution fusion | flops 1073741824 | bytes 36700160 | tf_op jit(solution)/shard_map/while/body/eval_jaxpr/qhd,khd->hqk/dot_general | solution.py:103
  586.5 16.3 %fusion.161 = f32[16,64,1024]{2,1,0:T(8,128)} fusion(bf16[512,16,64]{0,2,1:T(8,128)(2,1)S(1)} %bitcast.196, f32[16,512,1024]{2,1,0:T(8,128)} %fusion.160, f32[16,512]{1,0:T(8,128)S(1)} %dynamic-slice_bitcast_fusion.2, pred[512,1024]{1,0:T(8,128)(4,1)S(1)} %compare_or_fusion.5), kind=kOutput, calls=%fused_computation.26.clone.1 | convolution fusion | flops 1107296256 | bytes 39354368 | tf_op jit(solution)/shard_map/while/body/eval_jaxpr/hqk,qhd->khd/dot_general | solution.py:206
  602.9 25.7 %multiply_reduce_fusion.4 = (f32[16,512]{1,0:T(8,128)S(1)}, f32[16,512,1024]{2,1,0:T(8,128)}) fusion(f32[16,512,1024]{2,1,0:T(8,128)} %fusion.160, f32[16,512]{1,0:T(8,128)S(1)} %dynamic-slice_bitcast_fusion.2, pred[512,1024]{1,0:T(8,128)(4,1)S(1)} %compare_or_fusion.5, bf16[512,16,64]{0,2,1:T(8,128)(2,1)S(1)} %bitcast.197, ...), kind=kOutput, calls=%fused_computation.23.clone.1 | convolution fusion | flops 1115676672 | bytes 70844416 | tf_op jit(solution)/shard_map/while/body/eval_jaxpr/qhd,khd->hqk/dot_general | solution.py:209
  628.5 27.8 %multiply_convert_fusion.5 = bf16[16,512,1024]{2,1,0:T(8,128)(2,1)} fusion(f32[16,512,1024]{2,1,0:T(8,128)} %get-tuple-element.779, f32[16,512,1024]{2,1,0:T(8,128)} %fusion.160, f32[16,512]{1,0:T(8,128)S(1)} %get-tuple-element.780, f32[16,512]{1,0:T(8,128)S(1)} %dynamic-slice_bitcast_fusion.2, pred[512,1024]{1,0:T(8,128)(4,1)S(1)} %compare_or_fusion.5), kind=kLoop, calls=%fused_computation.22.clone.1 | loop fusion | flops 50331648 | bytes 84475904 | tf_op jit(solution)/shard_map/while/body/eval_jaxpr/convert_element_type | solution.py:213
  656.3 10.2 convolution_multiply_fusion.5
  666.6 8.9 convolution_multiply_fusion.4
  675.5 10.7 %bitcast_add_fusion.4 = (f32[1024,1024]{0,1:T(8,128)}, f32[1024,1024]{0,1:T(8,128)}) fusion(f32[16,64,1024]{2,1,0:T(8,128)} %fusion.161, f32[1024,1024]{0,1:T(8,128)} %get-tuple-element.845, pred[]{:T(512)S(6)} %compare.3, f32[16,64,1024]{2,1,0:T(8,128)S(1)} %convolution_multiply_fusion.4, f32[1024,1024]{0,1:T(8,128)} %get-tuple-element.844), kind=kLoop, calls=%fused_computation.28.clone.1 | loop fusion | flops 4194304 | bytes 25165824 | tf_op jit(solution)/shard_map/while/body/eval_jaxpr/add | solution.py:225
  689.2 7.0 fusion.90
  721.0 7.9 gather_fusion.4
  728.9 6.1 all-to-all-start.4
  736.6 18.2 %fusion.54 = bf16[1024,1024]{1,0:T(8,128)(2,1)} fusion(bf16[8,128,1024]{2,1,0:T(8,128)(2,1)} %all-to-all-done.1, bf16[1,4096,1024]{2,1,0:T(8,128)(2,1)} %all-gather.5.cloned.1.call-done, f32[1024]{0:T(1024)S(1)} %bitcast.220, f32[1024]{0:T(1024)S(1)} %copy-done.39, f32[1024,4096]{1,0:T(8,128)} %fusion.25, f32[4096]{0:T(1024)S(1)} %bitcast.219), kind=kOutput, calls=%fused_computation.98 | convolution fusion | flops 8637120512 | bytes 29384704 | tf_op jit(solution)/shard_map/dot_general | solution.py:158
  761.1 65.6 %all-reduce = (f32[1024]{0:T(1024)}, f32[1024]{0:T(1024)}, f32[1024]{0:T(1024)}, f32[1024]{0:T(1024)}, f32[1024]{0:T(1024)}, /*index=5*/f32[1024]{0:T(1024)}, f32[1024]{0:T(1024)}) all-reduce(f32[1024]{0:T(1024)S(1)} %get-tuple-element.565, f32[1024]{0:T(1024)S(1)} %get-tuple-element.570, ...), channel_id=1, replica_groups=mesh['expert'=8,'dp'=4] {'expert','dp'}, use_global_device_ids=true, to_apply=%region_19.20 | all-reduce | flops 7168 | bytes 57344 | tf_op jit(solution)/shard_map/psum | solution.py:252
  835.0 196.3 %all-reduce.4.cloned.1.call-done = (f32[1024,1024]{1,0:T(8,128)}, f32[1024,1024]{1,0:T(8,128)}, f32[1024,1024]{1,0:T(8,128)}, f32[1024,1024]{1,0:T(8,128)}) async-done(((f32[1024,1024]{1,0:T(8,128)}, f32[1024,1024]{1,0:T(8,128)}, f32[1024,1024]{1,0:T(8,128)}, f32[1024,1024]{1,0:T(8,128)}), (f32[1024,1024]{1,0:T(8,128)}, f32[1024,1024]{1,0:T(8,128)}, f32[1024,1024]{1,0:T(8,128)}, ...) | async-done | bytes 16777232 | tf_op jit(solution)/shard_map/psum | solution.py:252
  (251 shorter events, 141.5 us)
Async XLA Ops:
  7.2 71.0 %copy-start = (bf16[1024,1024]{1,0:T(8,128)(2,1)S(1)}, bf16[1024,1024]{1,0:T(8,128)(2,1)}, u32[]{:S(2)}) copy-start(bf16[1024,1024]{1,0:T(8,128)(2,1)} %param.31) | copy-start | bytes 6291460
  7.2 7.2 copy-start.45
  7.2 8.0 copy-start.43
  7.2 273.6 %all-gather.3.cloned.1.call-start = ((), (), s32[]{:S(2)}) async-start(), calls=%async_computation.9 | async-start | bytes 10485760 | tf_op jit(solution)/shard_map/all_gather | solution.py:152
  8.0 52.2 %all-to-all-start = ((bf16[8,128,1024]{2,1,0:T(8,128)(2,1)}), bf16[8,128,1024]{2,1,0:T(8,128)(2,1)}, u32[]{:S(2)}, u32[]{:S(2)}) async-start(bf16[8,128,1024]{2,1,0:T(8,128)(2,1)} %bitcast.205), calls=%async_computation | async-start | bytes 4194304 | tf_op jit(solution)/shard_map/all_to_all | solution.py:82
  13.7 283.2 %all-gather.5.cloned.1.call-start = ((), (), s32[]{:S(2)}) async-start(), calls=%async_computation.10 | async-start | bytes 10485760 | tf_op jit(solution)/shard_map/all_gather | solution.py:153
  20.2 53.5 %copy-start.27 = (s32[1024]{0:T(1024)}, s32[1024]{0:T(1024)S(1)}, u32[]{:S(2)}) copy-start(s32[1024]{0:T(1024)S(1)} %broadcast_clamp_fusion) | copy-start | bytes 12292
  28.4 45.3 %copy-start.34 = (s32[1024]{0:T(1024)}, s32[1024]{0:T(1024)S(1)}, u32[]{:S(2)}) copy-start(s32[1024]{0:T(1024)S(1)} %fusion.75) | copy-start | bytes 12292
  60.2 161.1 %all-to-all-start.2 = ((bf16[8,128,1]{1,2,0:T(2,128)(2,1)}), bf16[8,128,1]{1,2,0:T(2,128)(2,1)}, u32[]{:S(2)}, u32[]{:S(2)}) async-start(bf16[8,128,1]{1,2,0:T(2,128)(2,1)} %copy.71), calls=%async_computation.2 | async-start | bytes 8192 | tf_op jit(solution)/shard_map/all_to_all | solution.py:137
  75.8 20.2 %copy-start.30 = (f32[1024]{0:T(1024)}, f32[1024]{0:T(1024)S(1)}, u32[]{:S(2)}) copy-start(f32[1024]{0:T(1024)S(1)} %broadcast_multiply_fusion.5) | copy-start | bytes 12292
  78.3 17.8 %copy-start.32 = (f32[1024]{0:T(1024)}, f32[1024]{0:T(1024)S(1)}, u32[]{:S(2)}) copy-start(f32[1024]{0:T(1024)S(1)} %add_rsqrt_fusion.1) | copy-start | bytes 12292
  106.0 100.8 %copy-start.52 = (f32[1024]{0:T(1024)S(1)}, f32[1024]{0:T(1024)}, u32[]{:S(2)}) copy-start(f32[1024]{0:T(1024)} %param.34) | copy-start | bytes 12292
  123.7 15.1 %copy-start.8 = (bf16[1024,1024]{0,1:T(8,128)(2,1)S(1)}, bf16[1024,1024]{0,1:T(8,128)(2,1)}, u32[]{:S(2)}) copy-start(bf16[1024,1024]{0,1:T(8,128)(2,1)} %get-tuple-element.819) | copy-start | bytes 6291460 | tf_op jit(solution)/shard_map/while
  173.9 15.1 %copy-start.8 = (bf16[1024,1024]{0,1:T(8,128)(2,1)S(1)}, bf16[1024,1024]{0,1:T(8,128)(2,1)}, u32[]{:S(2)}) copy-start(bf16[1024,1024]{0,1:T(8,128)(2,1)} %get-tuple-element.819) | copy-start | bytes 6291460 | tf_op jit(solution)/shard_map/while
  206.8 6.6 copy-start.21
  206.8 6.6 copy-start.23
  206.8 6.6 copy-start.25
  206.8 6.6 copy-start.28
  221.3 51.5 %all-to-all-start.1 = ((bf16[8,128,1024]{2,1,0:T(8,128)(2,1)}), bf16[8,128,1024]{2,1,0:T(8,128)(2,1)}, u32[]{:S(2)}, u32[]{:S(2)}) async-start(bf16[8,128,1024]{2,1,0:T(8,128)(2,1)} %bitcast.204), calls=%async_computation.1 | async-start | bytes 4194304 | tf_op jit(solution)/shard_map/all_to_all | solution.py:136
  226.7 50.4 %copy-start.40 = (f32[1024]{0:T(1024)S(1)}, f32[1024]{0:T(1024)}, u32[]{:S(2)}) copy-start(f32[1024]{0:T(1024)} %param.35) | copy-start | bytes 12292
  226.7 50.4 %copy-start.44 = (f32[1024]{0:T(1024)S(1)}, f32[1024]{0:T(1024)}, u32[]{:S(2)}) copy-start(f32[1024]{0:T(1024)} %param.36) | copy-start | bytes 12292
  226.7 508.4 %reduce-scatter.15.cloned.1.call-start = ((), (), s32[]{:S(2)}) async-start(), calls=%async_computation.14 | async-start | bytes 327680
  227.5 97.4 %copy-start.38 = (f32[1024]{0:T(1024)}, f32[1024]{0:T(1024)S(1)}, u32[]{:S(2)}) copy-start(f32[1024]{0:T(1024)S(1)} %bitcast_convert_fusion) | copy-start | bytes 12292
  230.5 524.3 %reduce-scatter.13.cloned.1.call-start = ((), (), s32[]{:S(2)}) async-start(), calls=%async_computation.13 | async-start | bytes 1310720
  280.8 16.1 %copy-start.48 = (f32[1,4096]{1,0:T(1,128)S(1)}, f32[1,4096]{1,0:T(1,128)}, u32[]{:S(2)}) copy-start(f32[1,4096]{1,0:T(1,128)} %param.38) | copy-start | bytes 49156
  324.6 502.1 %reduce-scatter.11.cloned.1.call-start = ((), (), s32[]{:S(2)}) async-start(), calls=%async_computation.12 | async-start | bytes 10485760 | tf_op jit(solution)/shard_map/reduce_scatter | solution.py:176
  344.5 16.9 %copy-start.14 = (bf16[1024,1024]{1,0:T(8,128)(2,1)S(1)}, bf16[1024,1024]{1,0:T(8,128)(2,1)}, u32[]{:S(2)}) copy-start(bf16[1024,1024]{1,0:T(8,128)(2,1)} %param.41) | copy-start | bytes 6291460
  365.6 52.5 %all-to-all-start.3 = ((bf16[8,128,1024]{2,1,0:T(8,128)(2,1)}), bf16[8,128,1024]{2,1,0:T(8,128)(2,1)}, u32[]{:S(2)}, u32[]{:S(2)}) async-start(bf16[8,128,1024]{2,1,0:T(8,128)(2,1)} %bitcast.203), calls=%async_computation.3 | async-start | bytes 4194304 | tf_op jit(solution)/shard_map/all_to_all | solution.py:190
  371.6 459.2 %reduce-scatter.9.cloned.1.call-start = ((), (), s32[]{:S(2)}) async-start(), calls=%async_computation.11 | async-start | bytes 10485760 | tf_op jit(solution)/shard_map/reduce_scatter | solution.py:173
  387.0 31.1 %copy-start.35 = (s32[1024]{0:T(1024)S(1)}, s32[1024]{0:T(1024)}, u32[]{:S(2)}) copy-start(s32[1024]{0:T(1024)} %copy-done.34) | copy-start | bytes 12292
  387.0 644.2 %all-reduce.4.cloned.1.call-start = ((), (), s32[]{:S(2)}) async-start(), calls=%async_computation.15 | async-start | bytes 33554432 | tf_op jit(solution)/shard_map/psum | solution.py:252
  418.1 7.9 copy-start.26
  426.0 6.9 copy-start.15
  426.1 6.9 copy-start.46
  436.6 252.5 %copy-start.31 = (f32[1024]{0:T(1024)S(1)}, f32[1024]{0:T(1024)}, u32[]{:S(2)}) copy-start(f32[1024]{0:T(1024)} %copy-done.30) | copy-start | bytes 12292
  436.6 252.5 %copy-start.33 = (f32[1024]{0:T(1024)S(1)}, f32[1024]{0:T(1024)}, u32[]{:S(2)}) copy-start(f32[1024]{0:T(1024)} %copy-done.32) | copy-start | bytes 12292
  436.7 252.5 %copy-start.37 = (f32[1024]{0:T(1024)S(1)}, f32[1024]{0:T(1024)}, u32[]{:S(2)}) copy-start(f32[1024]{0:T(1024)} %param.26) | copy-start | bytes 12292
  436.7 252.5 %copy-start.54 = (f32[1024]{0:T(1024)S(1)}, f32[1024]{0:T(1024)}, u32[]{:S(2)}) copy-start(f32[1024]{0:T(1024)} %param.27) | copy-start | bytes 12292
  448.3 13.9 %copy-start.7 = (bf16[512,1024]{0,1:T(8,128)(2,1)S(1)}, bf16[512,1024]{0,1:T(8,128)(2,1)}, u32[]{:S(2)}) copy-start(bf16[512,1024]{0,1:T(8,128)(2,1)} %copy.109) | copy-start | bytes 3145732 | tf_op jit(solution)/shard_map/while
  532.5 10.3 copy-start.4
  573.4 13.1 %copy-start.7 = (bf16[512,1024]{0,1:T(8,128)(2,1)S(1)}, bf16[512,1024]{0,1:T(8,128)(2,1)}, u32[]{:S(2)}) copy-start(bf16[512,1024]{0,1:T(8,128)(2,1)} %copy.109) | copy-start | bytes 3145732 | tf_op jit(solution)/shard_map/while
  656.3 10.3 copy-start.4
  689.2 7.0 copy-start.5
  689.2 7.0 copy-start.12
  728.9 7.7 copy-start.39
  728.9 7.7 copy-start.49
  728.9 7.7 copy-start.55
  728.9 97.8 %all-to-all-start.4 = ((bf16[8,128,1024]{2,1,0:T(8,128)(2,1)}), bf16[8,128,1024]{2,1,0:T(8,128)(2,1)}, u32[]{:S(2)}, u32[]{:S(2)}) async-start(bf16[8,128,1024]{2,1,0:T(8,128)(2,1)} %bitcast.202), calls=%async_computation.4 | async-start | bytes 4194304 | tf_op jit(solution)/shard_map/all_to_all | solution.py:249
  (26 other events, 95.2 us)
Sparse Core Ops, SparseCore 0:
  9.6 59.8 all-gather.2
  71.1 58.2 all-gather.4
  230.6 22.0 reduce-scatter.14
  324.8 26.1 reduce-scatter.12
  353.4 71.7 reduce-scatter.10
  427.7 71.7 reduce-scatter.8
  705.8 325.4 all-reduce.3
where the time goes:
time: 1070 us; the launch traced here: 1050 us
  matrix products  380 us (36%)
  waiting for transfers between devices  303 us (28%)
  other arithmetic  146 us (14%)
  local copies, waits for them, and re-layouts  107 us (10%)
  blocking collectives  65.6 us (6%)
  starting transfers between devices  30.1 us (3%)
  between operations  14.9 us (1%)
    psum x1, waiting for transfers between devices, per_device(): lax.psum((grad_first_gain, grad_first_bias, grad_query_weight, grad_query...  196 us
    psum x1, blocking collectives, per_device(): lax.psum((grad_first_gain, grad_first_bias, grad_query_weight, grad_query...  65.6 us
    dot_general x6, matrix products, outer_cols(): lax.dot_general(left, right, (((1,), (1,)), ((), ())), preferred_element_...  57.9 us
    dot_general x6, matrix products, inner_rows(): lax.dot_general(left, right, (((0,), (0,)), ((), ())), preferred_element_...  57.8 us
    convert_element_type x2, other arithmetic, backward_block(): (weights_full * (grad_weights - row_inner)).astype(jnp.bfloat16)  55.5 us
    dot_general x4, matrix products, block_scores(): jnp.einsum('qhd,khd->hqk', query_block, key_block, preferred_element_type...  54.9 us
    dot_general x2, matrix products, backward_block(): jnp.einsum('qhd,khd->hqk', grad_block, value_block, preferred_element_typ...  51.4 us
    all_to_all x1, waiting for transfers between devices, per_device(): lax.all_to_all(residual_low[position], 'expert', split_axis=0, concat_axi...  41.9 us
  transfers between devices with their start and end apart: 12, of which 4 were waited for; matrix products, arithmetic and copies ran while one was open for 58% of the time, Pallas kernels for 0%

commit v1 on v0

v1 whole, which is shorter than its diff:
```python
import functools
import math

import jax
import jax.numpy as jnp
from jax import lax
from jax.experimental import pallas as pl
from jax.experimental.pallas import tpu as pltpu
from jax.sharding import PartitionSpec as P

HEADS = 16
EPS = 1e-05
NEG = -1e30
LOG2E = math.log2(math.e)
F32 = jnp.float32
BF16 = jnp.bfloat16
VMEM_LIMIT = 60 * 1024 * 1024
ROWS = 256


def nn(a, b):
    return lax.dot_general(a, b, (((1,), (0,)), ((), ())), preferred_element_type=F32)


def nt(a, b):
    return lax.dot_general(a, b, (((1,), (1,)), ((), ())), preferred_element_type=F32)


def tn(a, b):
    return lax.dot_general(a, b, (((0,), (0,)), ((), ())), preferred_element_type=F32)


def params(**more):
    return pltpu.CompilerParams(vmem_limit_bytes=VMEM_LIMIT, **more)


def cost(flops, bytes_accessed, transcendentals=0):
    return pl.CostEstimate(
        flops=int(flops), bytes_accessed=int(bytes_accessed), transcendentals=int(transcendentals)
    )


def whole(shape):
    return pl.BlockSpec(shape, lambda *_: (0,) * len(shape))


def rows_of(block, width):
    return pl.BlockSpec((block, width), lambda i, *_: (i, 0))


def norm_parts(values):
    mean = jnp.mean(values, axis=-1, keepdims=True)
    center = values - mean
    variance = jnp.mean(center * center, axis=-1, keepdims=True)
    root = lax.rsqrt(variance + EPS)
    return center * root, root


def norm_grad(grad, normal, root, gain):
    scaled = grad * gain
    mean_plain = jnp.mean(scaled, axis=-1, keepdims=True)
    mean_normal = jnp.mean(scaled * normal, axis=-1, keepdims=True)
    return root * (scaled - mean_plain - normal * mean_normal)


def pick_rows(first_row, pos_row, rows, count):
    ids = lax.broadcasted_iota(jnp.int32, (rows, count), 0) + first_row
    return jnp.where(ids == pos_row, 1.0, 0.0).astype(BF16)


def pick_slots(pos_col, count):
    ids = lax.broadcasted_iota(jnp.int32, (pos_col.shape[0], count), 1)
    return jnp.where(ids == pos_col, 1.0, 0.0).astype(BF16)


def entry_kernel(parts, *refs):
    slots = refs[:parts]
    pos_row, gain, offset, wq, bq, wk, wv, bv, tokens, normed, q, k, v = refs[parts:]
    i = pl.program_id(0)
    arrived = jnp.concatenate([r[...] for r in slots], axis=0)
    count = arrived.shape[0]
    rows = tokens.shape[0]
    picked = nn(pick_rows(i * rows, pos_row[...], rows, count), arrived)
    tokens[...] = picked.astype(BF16)
    normal, _ = norm_parts(picked)
    low = (normal * gain[...] + offset[...]).astype(BF16)
    normed[...] = low
    q[...] = ((nn(low, wq[...]) + bq[...]).astype(BF16).astype(F32) * 0.125).astype(BF16)
    k[...] = nn(low, wk[...]).astype(BF16)
    v[...] = (nn(low, wv[...]) + bv[...]).astype(BF16)


def entry(slots, pos_row, gain, offset, wq, bq, wk, wv, bv):
    parts = len(slots)
    piece, width = slots[0].shape
    count = piece * parts
    out = jax.ShapeDtypeStruct((count, width), BF16)
    return pl.pallas_call(
        functools.partial(entry_kernel, parts),
        grid=(count // ROWS,),
        in_specs=[whole((piece, width))] * parts
        + [whole((1, count))]
        + [whole((1, width))] * 2
        + [whole((width, width)), whole((1, width)), whole((width, width)), whole((width, width)), whole((1, width))],
        out_specs=[rows_of(ROWS, width)] * 5,
        out_shape=[out] * 5,
        compiler_params=params(),
        cost_estimate=cost(8 * count * width * width, 18 * count * width),
        name="entry",
    )(*slots, pos_row, gain, offset, wq, bq, wk, wv, bv)


def half_masks(width):
    lane = lax.broadcasted_iota(jnp.int32, (1, width), 1)
    return lane < width // 2


def split_heads(values):
    first = half_masks(values.shape[1])
    zero = jnp.zeros_like(values)
    return jnp.where(first, values, zero), jnp.where(first, zero, values)


def attend_kernel(start_col, q_ref, k_ref, v_ref, mixed_ref, lse_ref, bias):
    count = q_ref.shape[0]

    @pl.when(pl.program_id(0) == 0)
    def _():
        for i in range(count // ROWS):
            ext = (i + 1) * ROWS
            rows = pl.ds(i * ROWS, ROWS)
            kpos = lax.broadcasted_iota(jnp.int32, (ROWS, ext), 1)
            qpos = lax.broadcasted_iota(jnp.int32, (ROWS, ext), 0) + i * ROWS
            keep = (kpos >= start_col[rows, :]) & (kpos <= qpos)
            bias[rows, :ext] = jnp.where(keep, 0.0, NEG)

    values = split_heads(v_ref[...])
    keys = k_ref[...]
    first = half_masks(q_ref.shape[1])
    for i in range(count // ROWS):
        ext = (i + 1) * ROWS
        rows = pl.ds(i * ROWS, ROWS)
        total = None
        stats = []
        for query, value in zip(split_heads(q_ref[rows, :]), values):
            score = nt(query, keys[:ext]) * LOG2E + bias[rows, :ext]
            top = jnp.max(score, axis=1, keepdims=True)
            terms = jnp.exp2(score - top)
            sums = jnp.sum(terms, axis=1, keepdims=True)
            part = nn(terms.astype(BF16), value[:ext])
            total = part if total is None else total + part
            stats.append((top + jnp.log2(sums), 1.0 / sums))
        scale = jnp.where(first, stats[0][1], stats[1][1])
        mixed_ref[rows, :] = (total * scale).astype(BF16)
        both = jnp.where(first, stats[0][0], stats[1][0])
        turned = both.T
        lse_ref[0, 0:1, rows] = turned[0:1, :]
        lse_ref[0, 1:2, rows] = turned[64:65, :]


def attend(start_col, q, k, v):
    count, width = q.shape
    pairs = HEADS // 2
    lanes = width // pairs
    col = pl.BlockSpec((count, lanes), lambda p: (0, p))
    return pl.pallas_call(
        attend_kernel,
        grid=(pairs,),
        in_specs=[whole((count, 1)), col, col, col],
        out_specs=[col, pl.BlockSpec((1, 8, count), lambda p: (p, 0, 0))],
        out_shape=[
            jax.ShapeDtypeStruct((count, width), BF16),
            jax.ShapeDtypeStruct((pairs, 8, count), F32),
        ],
        scratch_shapes=[pltpu.VMEM((count, count), F32)],
        compiler_params=params(),
        cost_estimate=cost(8 * count * count * width, 8 * count * width, HEADS * count * count // 2),
        name="attend",
    )(start_col, q, k, v)


def leave_kernel(parts, mixed, wo, bo, tokens, live_col, pos_col, *refs):
    outs, kept = refs[:parts], refs[parts]
    i = pl.program_id(0)
    rows = mixed.shape[0]
    branch = nn(mixed[...], wo[...]) + bo[...]
    kept[pl.ds(pl.multiple_of(i * rows, rows), rows), :] = (
        tokens[...].astype(F32) + live_col[...] * branch
    ).astype(BF16)

    @pl.when(i == pl.num_programs(0) - 1)
    def _():
        count = kept.shape[0]
        piece = count // parts
        for r in range(parts):
            chosen = pick_slots(pos_col[pl.ds(r * piece, piece), :], count)
            outs[r][...] = nn(chosen, kept[...]).astype(BF16)


def leave(parts, mixed, wo, bo, tokens, live_col, pos_col):
    count, width = mixed.shape
    piece = count // parts
    return pl.pallas_call(
        functools.partial(leave_kernel, parts),
        grid=(count // ROWS,),
        in_specs=[
            rows_of(ROWS, width),
            whole((width, width)),
            whole((1, width)),
            rows_of(ROWS, width),
            rows_of(ROWS, 1),
            whole((count, 1)),
        ],
        out_specs=[whole((piece, width))] * parts,
        out_shape=[jax.ShapeDtypeStruct((piece, width), BF16)] * parts,
        scratch_shapes=[pltpu.VMEM((count, width), BF16)],
        compiler_params=params(),
        cost_estimate=cost(4 * count * width * width, 8 * count * width),
        name="leave",
    )(mixed, wo, bo, tokens, live_col, pos_col)


def reenter_kernel(parts, *refs):
    slots = refs[:parts]
    pos_row, live_col, wo, grad_residual, grad_proj, grad_mixed, bias_sum = refs[parts:]
    i = pl.program_id(0)
    arrived = jnp.concatenate([r[...] for r in slots], axis=0)
    rows = grad_residual.shape[0]
    picked = nn(pick_rows(i * rows, pos_row[...], rows, arrived.shape[0]), arrived)
    grad_residual[...] = picked.astype(BF16)
    masked = live_col[...] * picked
    low = masked.astype(BF16)
    grad_proj[...] = low
    grad_mixed[...] = nt(low, wo[...]).astype(BF16)

    @pl.when(i == 0)
    def _():
        bias_sum[...] = jnp.zeros_like(bias_sum)

    bias_sum[...] += jnp.sum(masked, axis=0, keepdims=True)


def reenter(slots, pos_row, live_col, wo):
    parts = len(slots)
    piece, width = slots[0].shape
    count = piece * parts
    out = jax.ShapeDtypeStruct((count, width), BF16)
    return pl.pallas_call(
        functools.partial(reenter_kernel, parts),
        grid=(count // ROWS,),
        in_specs=[whole((piece, width))] * parts
        + [whole((1, count)), rows_of(ROWS, 1), whole((width, width))],
        out_specs=[rows_of(ROWS, width)] * 3 + [whole((1, width))],
        out_shape=[out] * 3 + [jax.ShapeDtypeStruct((1, width), F32)],
        compiler_params=params(),
        cost_estimate=cost(4 * count * width * width, 10 * count * width),
        name="reenter",
    )(*slots, pos_row, live_col, wo)


def attend_back_kernel(
    start_row, q_ref, k_ref, v_ref, o_ref, g_ref, lse_ref, dq_ref, dk_ref, dv_ref, bias, dq_sum
):
    count, lanes = q_ref.shape

    @pl.when(pl.program_id(0) == 0)
    def _():
        for j in range(count // ROWS):
            cols = pl.ds(j * ROWS, count - j * ROWS)
            shape = (ROWS, count - j * ROWS)
            kpos = lax.broadcasted_iota(jnp.int32, shape, 0) + j * ROWS
            qpos = lax.broadcasted_iota(jnp.int32, shape, 1) + j * ROWS
            keep = (kpos >= start_row[:, cols]) & (kpos <= qpos)
            bias[pl.ds(j * ROWS, ROWS), cols] = jnp.where(keep, 0.0, NEG)

    products = o_ref[...].astype(F32) * g_ref[...].astype(F32)
    high = products.astype(BF16)
    low = (products - high.astype(F32)).astype(BF16)
    sel_row = lax.broadcasted_iota(jnp.int32, (8, lanes), 0)
    sel_lane = lax.broadcasted_iota(jnp.int32, (8, lanes), 1)
    select = jnp.where(sel_row == sel_lane // (lanes // 2), 1.0, 0.0).astype(BF16)
    deltas = nt(select, high) + nt(select, low)

    queries = split_heads(q_ref[...])
    grads = split_heads(g_ref[...])
    for j in range(count // ROWS):
        rows = pl.ds(j * ROWS, ROWS)
        ext = slice(j * ROWS, count)
        keys, vals = k_ref[rows, :], v_ref[rows, :]
        dk = dv = dq = None
        for h, key in enumerate(split_heads(keys)):
            query, grad = queries[h][ext], grads[h][ext]
            score = nt(keys, query) * LOG2E + bias[rows, ext]
            weights = jnp.exp2(score - lse_ref[0, h : h + 1, ext])
            weights_low = weights.astype(BF16)
            grad_weights = nt(vals, grad)
            grad_score = (weights * (grad_weights - deltas[h : h + 1, ext])).astype(BF16)
            dv_part = nn(weights_low, grad)
            dk_part = nn(grad_score, query)
            dq_part = tn(grad_score, key)
            dv = dv_part if dv is None else dv + dv_part
            dk = dk_part if dk is None else dk + dk_part
            dq = dq_part if dq is None else dq + dq_part
        dk_ref[rows, :] = dk.astype(BF16)
        dv_ref[rows, :] = dv.astype(BF16)
        if j == 0:
            dq_sum[...] = dq
        else:
            dq_sum[ext, :] += dq
    dq_ref[...] = (dq_sum[...] * 0.125).astype(BF16)


def attend_back(start_row, q, k, v, mixed, grad_mixed, lse):
    count, width = q.shape
    pairs = HEADS // 2
    lanes = width // pairs
    col = pl.BlockSpec((count, lanes), lambda p: (0, p))
    out = jax.ShapeDtypeStruct((count, width), BF16)
    return pl.pallas_call(
        attend_back_kernel,
        grid=(pairs,),
        in_specs=[whole((1, count))]
        + [col] * 5
        + [pl.BlockSpec((1, 8, count), lambda p: (p, 0, 0))],
        out_specs=[col] * 3,
        out_shape=[out] * 3,
        scratch_shapes=[pltpu.VMEM((count, count), F32), pltpu.VMEM((count, lanes), F32)],
        compiler_params=params(),
        cost_estimate=cost(20 * count * count * width, 16 * count * width, HEADS * count * count // 2),
        name="attend_back",
    )(start_row, q, k, v, mixed, grad_mixed, lse)


def finish_kernel(
    parts, dq, dk, dv, wq, wk, wv, tokens, grad_residual, gain, pos_col, *refs
):
    outs = refs[:parts]
    sums, kept = refs[parts:]
    i = pl.program_id(0)
    rows = dq.shape[0]
    grad = nt(dq[...], wq[...]) + nt(dk[...], wk[...]) + nt(dv[...], wv[...])
    normal, root = norm_parts(tokens[...].astype(F32))
    kept[pl.ds(pl.multiple_of(i * rows, rows), rows), :] = (
        grad_residual[...].astype(F32) + norm_grad(grad, normal, root, gain[...])
    ).astype(BF16)

    @pl.when(i == 0)
    def _():
        sums[...] = jnp.zeros_like(sums)

    sums[0:1, :] += jnp.sum(grad * normal, axis=0, keepdims=True)
    sums[1:2, :] += jnp.sum(grad, axis=0, keepdims=True)
    sums[2:3, :] += jnp.sum(dq[...].astype(F32), axis=0, keepdims=True)
    sums[3:4, :] += jnp.sum(dv[...].astype(F32), axis=0, keepdims=True)

    @pl.when(i == pl.num_programs(0) - 1)
    def _():
        count = kept.shape[0]
        piece = count // parts
        for r in range(parts):
            chosen = pick_slots(pos_col[pl.ds(r * piece, piece), :], count)
            outs[r][...] = nn(chosen, kept[...]).astype(BF16)


def finish(parts, dq, dk, dv, wq, wk, wv, tokens, grad_residual, gain, pos_col):
    count, width = dq.shape
    piece = count // parts
    return pl.pallas_call(
        functools.partial(finish_kernel, parts),
        grid=(count // ROWS,),
        in_specs=[rows_of(ROWS, width)] * 3
        + [whole((width, width))] * 3
        + [rows_of(ROWS, width)] * 2
        + [whole((1, width)), whole((count, 1))],
        out_specs=[whole((piece, width))] * parts + [whole((8, width))],
        out_shape=[jax.ShapeDtypeStruct((piece, width), BF16)] * parts
        + [jax.ShapeDtypeStruct((8, width), F32)],
        scratch_shapes=[pltpu.VMEM((count, width), BF16)],
        compiler_params=params(),
        cost_estimate=cost(8 * count * width * width, 20 * count * width),
        name="finish",
    )(dq, dk, dv, wq, wk, wv, tokens, grad_residual, gain, pos_col)


GELU_ROOT = math.sqrt(2.0 / math.pi)
GELU_CUBE = 0.044715
STEP = 512


def expert_kernel(parts, shards, first_chunk, source, *refs):
    it = iter(refs)
    take = lambda n: [next(it) for _ in range(n)]
    slots, cots, lives = take(parts), take(parts), take(parts)
    ups, downs = take(shards), take(shards)
    up_bias, down_bias, gain, offset = take(4)
    if not first_chunk:
        take(5)
    grads = take(parts)
    act_out, pre_out, ffn_out, branch_out, block_out, sums, up_sums = take(7)
    up, down, out_sum, grad_sum, out_low, up_sem, down_sem, out_sem = take(8)

    up_copies = [pltpu.make_async_copy(ups[k], up.at[k], up_sem.at[k]) for k in range(shards)]
    down_copies = [pltpu.make_async_copy(downs[k], down.at[k], down_sem.at[k]) for k in range(shards)]
    for k in range(shards):
        up_copies[k].start()
        down_copies[k].start()

    routed = jnp.concatenate([r[...] for r in slots], axis=0).astype(F32)
    cot = jnp.concatenate([r[...] for r in cots], axis=0).astype(F32)
    live = jnp.concatenate([r[...] for r in lives], axis=0)
    normal, root = norm_parts(routed)
    ffn_in = (normal * gain[...] + offset[...]).astype(BF16)
    branch = (live * cot).astype(BF16)
    ffn_out[...] = ffn_in
    branch_out[...] = branch
    out_sum[...] = jnp.broadcast_to(down_bias[...], out_sum.shape)
    grad_sum[...] = jnp.zeros_like(grad_sum)
    width = up.shape[2]
    for k in range(shards):
        up_copies[k].wait()
        down_copies[k].wait()

        for c in range(0, width, STEP):
            cols = pl.ds(c, STEP)
            pre = nn(ffn_out[...], up[k, :, cols]) + up_bias[k, :, cols]
            square = pre * pre
            tanh = jnp.tanh(pre * (GELU_ROOT + (GELU_ROOT * GELU_CUBE) * square))
            half = 0.5 * (1.0 + tanh)
            act = (pre * half).astype(BF16)
            slope = half + (0.5 * pre) * (1.0 - tanh * tanh) * (
                GELU_ROOT + (3.0 * GELU_ROOT * GELU_CUBE) * square
            )
            act_out[k, :, cols] = act
            grad_pre = (nt(branch_out[...], down[k, cols, :]) * slope).astype(BF16)
            pre_out[k, :, cols] = grad_pre
            up_sums[k, :, cols] = jnp.sum(grad_pre.astype(F32), axis=0, keepdims=True)
            grad_sum[...] += nt(grad_pre, up[k, :, cols])
            out_sum[...] += nn(act, down[k, cols, :])
    grad = grad_sum[...]
    grad_routed = (cot + norm_grad(grad, normal, root, gain[...])).astype(BF16)
    out_low[...] = (routed + live * out_sum[...]).astype(BF16)
    piece = slots[0].shape[0]
    out_copies = []
    for j in range(parts):
        grads[j][...] = grad_routed[j * piece : (j + 1) * piece]
        place = pl.multiple_of(source[j] * piece, piece)
        copy = pltpu.make_async_copy(
            out_low.at[pl.ds(j * piece, piece)], block_out.at[pl.ds(place, piece)], out_sem.at[j]
        )
        copy.start()
        out_copies.append(copy)
    sums[...] = jnp.zeros_like(sums)
    sums[0:1, :] = jnp.sum(grad * normal, axis=0, keepdims=True)
    sums[1:2, :] = jnp.sum(grad, axis=0, keepdims=True)
    sums[2:3, :] = jnp.sum(branch.astype(F32), axis=0, keepdims=True)
    for copy in out_copies:
        copy.wait()


def expert_chunk(chunk, source, slots, cot, live, ups, downs, up_bias, down_bias, gain, offset, carried):
    parts, shards = len(slots), len(ups)
    piece, width = slots[0].shape
    rows = parts * piece
    count = cot.shape[0]
    part = ups[0].shape[1]
    picked = lambda j, w: pl.BlockSpec((piece, w), lambda i, source, j=j: (source[j], 0))
    anywhere = pl.BlockSpec(memory_space=pl.ANY)
    big = pl.BlockSpec((shards, rows, part), lambda *_: (0, chunk, 0))
    flat = pl.BlockSpec((rows, width), lambda *_: (chunk, 0))
    first = carried is None
    previous = [] if first else list(carried)
    before = 1 + 3 * parts + 2 * shards + 4
    full = jax.ShapeDtypeStruct((count, width), BF16)
    wide = jax.ShapeDtypeStruct((shards, count, part), BF16)
    outs = pl.pallas_call(
        functools.partial(expert_kernel, parts, shards, first),
        grid_spec=pltpu.PrefetchScalarGridSpec(
            num_scalar_prefetch=1,
            grid=(1,),
            in_specs=[whole((piece, width))] * parts
            + [picked(j, width) for j in range(parts)]
            + [picked(j, 1) for j in range(parts)]
            + [anywhere] * (2 * shards)
            + [whole((shards, 1, part)), whole((1, width)), whole((1, width)), whole((1, width))]
            + [anywhere] * len(previous),
            out_specs=[whole((piece, width))] * parts
            + [big, big, flat, flat, anywhere, whole((8, width)), whole((shards, 1, part))],
            scratch_shapes=[
                pltpu.VMEM((shards, width, part), BF16),
                pltpu.VMEM((shards, part, width), BF16),
                pltpu.VMEM((rows, width), F32),
                pltpu.VMEM((rows, width), F32),
                pltpu.VMEM((rows, width), BF16),
                pltpu.SemaphoreType.DMA((shards,)),
                pltpu.SemaphoreType.DMA((shards,)),
                pltpu.SemaphoreType.DMA((parts,)),
            ],
        ),
        out_shape=[jax.ShapeDtypeStruct((piece, width), BF16)] * parts
        + [wide, wide, full, full, full]
        + [jax.ShapeDtypeStruct((8, width), F32), jax.ShapeDtypeStruct((shards, 1, part), F32)],
        input_output_aliases={before + n: parts + n for n in range(len(previous))},
        compiler_params=params(),
        cost_estimate=cost(
            8 * rows * width * part * shards, 4 * shards * width * part, rows * part * shards
        ),
        name="expert_chunk",
    )(
        source,
        *slots,
        *([cot] * parts),
        *([live] * parts),
        *ups,
        *downs,
        up_bias,
        down_bias,
        gain,
        offset,
        *previous,
    )
    grads = outs[:parts]
    return grads, outs[parts : parts + 5], outs[parts + 5], outs[parts + 6]


def expert_grads_kernel(act, pre, ffn_in, branch, down_out, up_out):
    down_out[0] = tn(act[0], branch[...]).astype(BF16)
    up_out[0] = tn(ffn_in[...], pre[0]).astype(BF16)


def expert_grads(first, step, act, pre, ffn_in, branch):
    shards, count, part = act.shape
    width = ffn_in.shape[1]
    number = shards // step
    pick = pl.BlockSpec((1, count, part), lambda i: (first + step * i, 0, 0))
    return pl.pallas_call(
        expert_grads_kernel,
        grid=(number,),
        in_specs=[pick, pick, whole((count, width)), whole((count, width))],
        out_specs=[
            pl.BlockSpec((1, part, width), lambda i: (i, 0, 0)),
            pl.BlockSpec((1, width, part), lambda i: (i, 0, 0)),
        ],
        out_shape=[
            jax.ShapeDtypeStruct((number, part, width), BF16),
            jax.ShapeDtypeStruct((number, width, part), BF16),
        ],
        compiler_params=params(),
        cost_estimate=cost(4 * number * count * width * part, 10 * number * width * part),
        name="expert_grads",
    )(act, pre, ffn_in, branch)


def shared_grads_kernel(blocks, code, left, right, keep, send, total):
    total[...] = tn(left[...], right[...])
    size = total.shape[0] // blocks
    half = blocks // 2
    for j in range(blocks):
        place = pl.multiple_of((code[0] ^ j) * size, size)
        target = keep if j < half else send
        target[0, pl.ds((j % half) * size, size), :] = total[pl.ds(place, size), :].astype(BF16)


def shared_grads(blocks, code, left, rights):
    count, width = left.shape
    number = len(rights)
    if number > 1:
        raise NotImplementedError
    half = pl.BlockSpec((1, width // 2, width), lambda i, *_: (0, 0, 0))
    return pl.pallas_call(
        functools.partial(shared_grads_kernel, blocks),
        grid_spec=pltpu.PrefetchScalarGridSpec(
            num_scalar_prefetch=1,
            grid=(1,),
            in_specs=[whole((count, width))] * 2,
            out_specs=[half, half],
            scratch_shapes=[pltpu.VMEM((width, width), F32)],
        ),
        out_shape=[jax.ShapeDtypeStruct((1, width // 2, width), BF16)] * 2,
        compiler_params=params(),
        cost_estimate=cost(2 * count * width * width, 6 * width * width),
        name="shared_grads",
    )(code, left, rights[0])


def unmix_kernel(blocks, code, low, high, out):
    half = blocks // 2
    size = out.shape[0] // blocks
    for j in range(blocks):
        place = pl.multiple_of((code[0] ^ j) * size, size)
        source = low if j < half else high
        out[pl.ds(place, size), :] = source[0, pl.ds((j % half) * size, size), :].astype(F32)


def unmix(blocks, code, low, high):
    _, rows, width = low.shape
    half = pl.BlockSpec((1, rows, width), lambda i, *_: (0, 0, 0))
    return pl.pallas_call(
        functools.partial(unmix_kernel, blocks),
        grid_spec=pltpu.PrefetchScalarGridSpec(
            num_scalar_prefetch=1,
            grid=(1,),
            in_specs=[half, half],
            out_specs=whole((2 * rows, width)),
        ),
        out_shape=jax.ShapeDtypeStruct((2 * rows, width), F32),
        compiler_params=params(),
        cost_estimate=cost(2 * rows * width, 12 * rows * width),
        name="unmix",
    )(code, low, high)


def assemble_kernel(parts, source, *refs):
    pieces, out, sem = refs[:parts], refs[parts], refs[parts + 1]
    size = pieces[0].shape[0]
    copies = []
    for r in range(parts):
        place = pl.multiple_of(source[r] * size, size)
        copies.append(pltpu.make_async_copy(pieces[r], out.at[pl.ds(place, size)], sem.at[r]))
    for copy in copies:
        copy.start()
    for copy in copies:
        copy.wait()


def assemble(source, pieces):
    parts = len(pieces)
    size, width = pieces[0].shape
    anywhere = pl.BlockSpec(memory_space=pl.ANY)
    return pl.pallas_call(
        functools.partial(assemble_kernel, parts),
        grid_spec=pltpu.PrefetchScalarGridSpec(
            num_scalar_prefetch=1,
            grid=(1,),
            in_specs=[anywhere] * parts,
            out_specs=anywhere,
            scratch_shapes=[pltpu.SemaphoreType.DMA((parts,))],
        ),
        out_shape=jax.ShapeDtypeStruct((parts * size, width), BF16),
        compiler_params=params(),
        cost_estimate=cost(0, 4 * parts * size * width),
        name="assemble",
    )(source, *pieces)


def turn(values, axis, size, by):
    return lax.ppermute(values, axis, [(i, (i + by) % size) for i in range(size)])


def swap(values, axis, size, bit):
    return lax.ppermute(values, axis, [(i, i ^ bit) for i in range(size)])


def swap_steps(n_expert, n_dp):
    bits_dp = [1 << b for b in range(n_dp.bit_length() - 1)]
    bits_expert = [1 << b for b in range(n_expert.bit_length() - 1)]
    steps = []
    for n in range(max(len(bits_dp), len(bits_expert))):
        if n < len(bits_dp):
            steps.append(("dp", n_dp, bits_dp[n]))
        if n < len(bits_expert):
            steps.append(("expert", n_expert, bits_expert[n]))
    return steps


def add_low(left, right):
    return (left.astype(F32) + right.astype(F32)).astype(BF16)


class SharedSum:
    def __init__(self, n_expert, n_dp, rows):
        steps = swap_steps(n_expert, n_dp)
        cut = 0
        while cut < len(steps) and rows >> (cut + 1) >= 32:
            cut += 1
        self.halving, self.whole_steps = steps[:cut], steps[cut:]
        self.blocks = 1 << cut
        code = jnp.int32(0)
        for axis, _, bit in self.halving:
            code = code * 2 + (lax.axis_index(axis) // bit) % 2
        self.code = code.astype(jnp.int32).reshape(1)

    def __call__(self, keep, send):
        for n, (axis, size, bit) in enumerate(self.halving):
            total = add_low(keep, swap(send, axis, size, bit))
            if n + 1 < len(self.halving):
                middle = total.shape[1] // 2
                keep, send = total[:, :middle], total[:, middle:]
        for axis, size, bit in self.whole_steps:
            total = add_low(total, swap(total, axis, size, bit))
        for n, (axis, size, bit) in reversed(list(enumerate(self.halving))):
            other = swap(total, axis, size, bit)
            if n > 0:
                total = jnp.concatenate([total, other], axis=1)
        return unmix(self.blocks, self.code, total, other)


def small_sum(values, n_expert, n_dp):
    for axis, size, bit in swap_steps(n_expert, n_dp):
        values = values + swap(values, axis, size, bit)
    return values


def per_device(
    n_expert,
    n_dp,
    block_in,
    seq_lengths,
    slot_position,
    first_gain,
    first_bias,
    query_weight,
    query_bias,
    key_weight,
    value_weight,
    value_bias,
    out_weight,
    out_bias,
    second_gain,
    second_bias,
    expert_up,
    expert_up_bias,
    expert_down,
    expert_down_bias,
    block_cot,
):
    count, width = block_in.shape
    piece = count // n_expert
    row = lambda v: v.reshape(1, -1)
    e = lax.axis_index("expert")
    d = lax.axis_index("dp")
    part = expert_up.shape[2]

    def gathered(own):
        found = [own]
        bit = 1
        own_list = [own]
        far = [own]
        bits = [1 << b for b in range(n_dp.bit_length() - 1)]
        shards = {0: own}
        for bit in reversed(bits):
            for k in list(shards):
                shards[k | bit] = swap(shards[k], "dp", n_dp, bit)
        return [shards[k] for k in range(n_dp)]

    blocks = block_in.reshape(n_expert, piece, width)
    arrived = []
    for r in range(n_expert):
        block = lax.dynamic_index_in_dim(blocks, (e - r) % n_expert, 0, keepdims=False)
        arrived.append(block if r == 0 else turn(block, "expert", n_expert, -r))
    ups, downs = gathered(expert_up[0]), gathered(expert_down[0])

    position = slot_position[0]
    ends = jnp.cumsum(seq_lengths[0])
    total_live = ends[-1]
    ids = jnp.arange(count, dtype=jnp.int32)
    live = ids < total_live
    begin = jnp.max(jnp.where(ends[None, :] <= ids[:, None], ends[None, :], 0), axis=1)
    begin = jnp.where(live, begin, ids).astype(jnp.int32)
    live_col = live.astype(F32).reshape(count, 1)
    turned = jnp.roll(position.reshape(n_expert, piece), -e, axis=0).reshape(count)
    pos_row, pos_col = turned.reshape(1, count), turned.reshape(count, 1)
    slot_live = (position < total_live).astype(F32).reshape(n_expert, piece)
    route_live = lax.all_to_all(slot_live, "expert", split_axis=0, concat_axis=0, tiled=True)
    route_live = route_live.reshape(count, 1)

    tokens, normed, query, key, value = entry(
        arrived, pos_row, row(first_gain), row(first_bias), query_weight, row(query_bias),
        key_weight, value_weight, row(value_bias),
    )
    mixed, lse = attend(begin.reshape(count, 1), query, key, value)
    sent = leave(n_expert, mixed, out_weight, row(out_bias), tokens, live_col, pos_col)

    routed = [v if r == 0 else turn(v, "expert", n_expert, r) for r, v in enumerate(sent)]
    order = [0]
    for n in range(1, n_expert):
        order.append((n + 1) // 2 if n % 2 else n_expert - n // 2)
    chunks = min(CHUNKS, n_expert)
    per = n_expert // chunks
    shard_order = jnp.arange(n_dp, dtype=jnp.int32) ^ d
    up_bias = jnp.take(expert_up_bias[0].reshape(n_dp, 1, part), shard_order, axis=0)
    carried = None
    returned = [None] * n_expert
    sums, up_sums = 0.0, 0.0
    for c in range(chunks):
        turns = order[c * per : (c + 1) * per]
        source = jnp.stack([(e - r) % n_expert for r in turns]).astype(jnp.int32)
        grads, carried, chunk_sums, chunk_up = expert_chunk(
            c, source, [routed[r] for r in turns], block_cot, route_live, ups, downs, up_bias,
            row(expert_down_bias[0]), row(second_gain), row(second_bias), carried,
        )
        sums, up_sums = sums + chunk_sums, up_sums + chunk_up
        for r, grad in zip(turns, grads):
            returned[r] = grad if r == 0 else turn(grad, "expert", n_expert, -r)
    act, grad_pre, ffn_in, branch, block_out = carried

    down_send, up_send = expert_grads(1, 2, act, grad_pre, ffn_in, branch)
    down_got, up_got = swap(down_send, "dp", n_dp, 1), swap(up_send, "dp", n_dp, 1)
    down_keep, up_keep = expert_grads(0, 2, act, grad_pre, ffn_in, branch)

    def reduced(keep, got):
        bits = [1 << b for b in range(1, n_dp.bit_length() - 1)]
        for bit in reversed(bits):
            middle = keep.shape[0] // 2
            other = swap(add_low(keep[middle:], got[middle:]), "dp", n_dp, bit)
            keep, got = keep[:middle].astype(F32) + got[:middle].astype(F32), other
        return keep + got.astype(F32)

    grad_down, grad_up = reduced(down_keep, down_got), reduced(up_keep, up_got)
    bias_sums = up_sums.reshape(n_dp, part)
    down_bias_sums = sums[2:3]
    for bit in [1 << b for b in range(n_dp.bit_length() - 1)]:
        packed = jnp.concatenate([bias_sums, down_bias_sums.reshape(-1, part)], axis=0)
        other = swap(packed, "dp", n_dp, bit)
        bias_sums = bias_sums + other[jnp.array([k ^ bit for k in range(n_dp)])]
        down_bias_sums = down_bias_sums + other[n_dp:].reshape(1, width)
    grad_up_bias = bias_sums[0:1]
    share = width // n_dp
    grad_down_bias = lax.dynamic_slice_in_dim(down_bias_sums, d * share, share, 1)

    grad_residual, grad_proj, grad_mixed, out_bias_sum = reenter(
        returned, pos_row, live_col, out_weight
    )
    shared = SharedSum(n_expert, n_dp, width)
    grad_out_weight = shared(*shared_grads(shared.blocks, shared.code, mixed, [grad_proj]))
    grad_query, grad_key, grad_value = attend_back(
        begin.reshape(1, count), query, key, value, mixed, grad_mixed, lse
    )
    *leaving, token_sums = finish(
        n_expert, grad_query, grad_key, grad_value, query_weight, key_weight, value_weight,
        tokens, grad_residual, row(first_gain), pos_col,
    )
    received = [v if r == 0 else turn(v, "expert", n_expert, r) for r, v in enumerate(leaving)]
    sources = jnp.stack([(e - r) % n_expert for r in range(n_expert)]).astype(jnp.int32)
    input_grad = assemble(sources, received)
    grad_query_weight, grad_key_weight, grad_value_weight = (
        shared(*shared_grads(shared.blocks, shared.code, normed, [g]))
        for g in (grad_query, grad_key, grad_value)
    )
    small = jnp.concatenate(
        [token_sums[0:4], out_bias_sum, sums[0:2], jnp.zeros((1, width), F32)], axis=0
    )
    small = small_sum(small, n_expert, n_dp)
    return (
        block_out,
        input_grad,
        small[0],
        small[1],
        grad_query_weight,
        small[2],
        grad_key_weight,
        grad_value_weight,
        small[3],
        grad_out_weight,
        small[4],
        small[5],
        small[6],
        grad_up,
        grad_up_bias,
        grad_down,
        grad_down_bias,
    )


CHUNKS = 4


def solution(mesh):
    both = P(("expert", "dp"), None)
    return jax.shard_map(
        functools.partial(per_device, mesh.shape["expert"], mesh.shape["dp"]),
        mesh=mesh,
        in_specs=(both,) * 3
        + (P(),) * 11
        + (P("expert", None, "dp"), P("expert", None), P("expert", "dp", None), P("expert", None), both),
        out_specs=(both,) * 2
        + (P(),) * 11
        + (P("expert", None, "dp"), P("expert", "dp"), P("expert", "dp", None), P("expert", "dp")),
        check_vma=False,
    )
```

time: 1070 us -> 707 us (0.66)
  matrix products: 380 us -> 0 us
  Pallas kernels: 0 us -> 326 us
  waiting for transfers between devices: 303 us -> 142 us
  starting transfers between devices: 30.1 us -> 168 us
  other arithmetic: 146 us -> 33.3 us
  local copies, waits for them, and re-layouts: 107 us -> 24.7 us
  blocking collectives: 65.6 us -> 0 us
  between operations: 14.9 us -> 2.26 us
    dot_general x32 -> x0, matrix products: 380 us -> none  [the longest x6 57.9 us: outer_cols(): lax.dot_general(left, right, (((1,), (1,)), ((), ())), preferred_element_...]
    pallas_call x0 -> x21, Pallas kernels: none -> 326 us  [the longest x4 80.2 us: expert_chunk(): pl.pallas_call(functools.partial(expert_kernel, parts, shards, first), gr...]
    psum x1 -> x0, waiting for transfers between devices: 196 us -> none  [per_device(): lax.psum((grad_first_gain, grad_first_bias, grad_query_weight, grad_query...]
    ppermute x0 -> x85, starting transfers between devices: none -> 163 us  [the longest x57 105 us: swap(): return lax.ppermute(values, axis, [(i, i ^ bit) for i in range(size)])]
    ppermute x0 -> x85, waiting for transfers between devices: none -> 142 us  [the longest x57 105 us: swap(): return lax.ppermute(values, axis, [(i, i ^ bit) for i in range(size)])]
    all_to_all x5 -> x1, waiting for transfers between devices: 105 us -> 0.01 us  [per_device(): lax.all_to_all(slot_live, 'expert', split_axis=0, concat_axis=0, tiled=True)]
    psum x1 -> x0, blocking collectives: 65.6 us -> none  [per_device(): lax.psum((grad_first_gain, grad_first_bias, grad_query_weight, grad_query...]
    convert_element_type x11 -> x20, other arithmetic: 74.9 us -> 11.4 us  [the longest x18 8.64 us: add_low(): return (left.astype(F32) + right.astype(F32)).astype(BF16)]
  transfers between devices with their start and end apart: 12 -> 86, of which waited for: 4 -> 26; matrix products, arithmetic and copies ran while one was open for 58% -> 7% of each run, Pallas kernels for 0% -> 44%
where the time goes in v1:
time: 707 us; the launch traced here: 695 us
  Pallas kernels  326 us (46%)
  starting transfers between devices  168 us (24%)
  waiting for transfers between devices  142 us (20%)
  other arithmetic  33.3 us (5%)
  local copies, waits for them, and re-layouts  24.7 us (3%)
    ppermute x57, waiting for transfers between devices, swap(): return lax.ppermute(values, axis, [(i, i ^ bit) for i in range(size)])  105 us
    ppermute x57, starting transfers between devices, swap(): return lax.ppermute(values, axis, [(i, i ^ bit) for i in range(size)])  105 us
    pallas_call x4, Pallas kernels, expert_chunk(): pl.pallas_call(functools.partial(expert_kernel, parts, shards, first), gr...  80.2 us
    pallas_call x1, Pallas kernels, assemble(): pl.pallas_call(functools.partial(assemble_kernel, parts), grid_spec=pltpu...  65.4 us
    ppermute x28, starting transfers between devices, turn(): lax.ppermute(values, axis, [(i, (i + by) % size) for i in range(size)])  58 us
    ppermute x28, waiting for transfers between devices, turn(): lax.ppermute(values, axis, [(i, (i + by) % size) for i in range(size)])  36.6 us
    pallas_call x1, Pallas kernels, attend_back(): pl.pallas_call(attend_back_kernel, grid=(pairs,), in_specs=[whole((1, cou...  35.8 us
    pallas_call x2, Pallas kernels, expert_grads(): pl.pallas_call(expert_grads_kernel, grid=(number,), in_specs=[pick, pick,...  27.9 us
  transfers between devices with their start and end apart: 86, of which 26 were waited for; matrix products, arithmetic and copies ran while one was open for 7% of the time, Pallas kernels for 44%

profile of v1, /device:TPU:9, one launch (start us, length us, event | category | flops | bytes accessed | tf_op | source)
XLA Modules:
  0.0 695.3 jit_solution(13299600466355456047)
XLA Ops:
  11.2 4.8 all-to-all-start
  24.5 13.4 %collective-permute-done.2.refs_3_ = bf16[128,1024]{1,0:T(8,128)(2,1)} collective-permute-done((bf16[128,1024]{1,0:T(8,128)(2,1)}, bf16[128,1024]{1,0:T(8,128)(2,1)}, u32[]{:S(2)}, u32[]{:S(2)}) %collective-permute-start.2) | collective-permute-done | bytes 262176 | tf_op jit(solution)/shard_map/ppermute | solution.py:646
  37.9 7.8 %collective-permute-start.5 = (bf16[128,1024]{1,0:T(8,128)(2,1)S(1)}, bf16[128,1024]{1,0:T(8,128)(2,1)}, u32[]{:S(2)}, u32[]{:S(2)}) collective-permute-start(bf16[128,1024]{1,0:T(8,128)(2,1)S(1)} %get-tuple-element.184), channel_id=1, source_target_pairs={{0,8},{4,12},{8,16},{12,20},{16,24},{20,28},{24,0},{28,4},{1,9},{5... | collective-permute-start | bytes 786440 | tf_op jit(solution)/shard_map/ppermute | solution.py:646
  49.1 4.5 collective-permute-start.12
  55.2 37.2 %collective-permute-done.13.refs_12_ = bf16[1024,1024]{1,0:T(8,128)(2,1)} collective-permute-done((bf16[1024,1024]{1,0:T(8,128)(2,1)}, bf16[1024,1024]{1,0:T(8,128)(2,1)}, u32[]{:S(2)}, u32[]{:S(2)}) %collective-permute-start.13) | collective-permute-done | bytes 2097184 | tf_op jit(solution)/shard_map/ppermute | solution.py:650
  94.0 15.4 %entry.1 = (bf16[1024,1024]{1,0:T(8,128)(2,1)}, bf16[1024,1024]{1,0:T(8,128)(2,1)}, bf16[1024,1024]{1,0:T(8,128)(2,1)}, bf16[1024,1024]{1,0:T(8,128)(2,1)}, bf16[1024,1024]{1,0:T(8,128)(2,1)}) custom-call(bf16[128,1024]{1,0:T(8,128)(2,1)} %get-tuple-element.190.refs_0_, bf16[128,1024]{1,0:T(8,128)(2,1)} %collective-permute-done.refs_1_, ...), custom_call_target="tpu_custom_call" | custom-call | flops 8589934592 | bytes 18874368 | tf_op jit(solution)/shard_map/entry/pallas_call | solution.py:98
  109.4 24.3 %attend.1 = (bf16[1024,1024]{1,0:T(8,128)(2,1)}, f32[8,8,1024]{2,1,0:T(8,128)}) custom-call(s32[1024,1]{1,0:T(8,128)} %iota_select_fusion.start_col, bf16[1024,1024]{1,0:T(8,128)(2,1)} %get-tuple-element.96.q_ref, bf16[1024,1024]{1,0:T(8,128)(2,1)} %get-tuple-element.97.k_ref, bf16[1024,1024]{1,0:T(8,128)(2,1)} %get-tuple-element.98.v_ref), custom_call_target="tpu_custom_call" | custom-call | flops 8589934592 | bytes 8388608 | tf_op jit(solution)/shard_map/attend/pallas_call | solution.py:166
  133.8 9.6 %leave.1 = (bf16[128,1024]{1,0:T(8,128)(2,1)}, bf16[128,1024]{1,0:T(8,128)(2,1)}, bf16[128,1024]{1,0:T(8,128)(2,1)}, bf16[128,1024]{1,0:T(8,128)(2,1)}, bf16[128...) custom-call(bf16[1024,1024]{1,0:T(8,128)(2,1)} %get-tuple-element.99.mixed, ...), custom_call_target="tpu_custom_call" | custom-call | flops 4294967296 | bytes 8388608 | tf_op jit(solution)/shard_map/leave/pallas_call | solution.py:203
  146.9 5.5 collective-permute-done.19.refs_1_
  159.4 20.0 %expert_chunk.4 = (bf16[128,1024]{1,0:T(8,128)(2,1)}, bf16[128,1024]{1,0:T(8,128)(2,1)}, bf16[4,1024,1024]{2,1,0:T(8,128)(2,1)}, bf16[4,1024,1024]{2,1,0:T(8,128...) custom-call(s32[2]{0:T(128)} %pad_add_fusion.3.source, ...), custom_call_target="tpu_custom_call" | custom-call | flops 8589934592 | bytes 16777216 | tf_op jit(solution)/shard_map/expert_chunk/pallas_call | solution.py:475
  182.3 20.2 %expert_chunk.5 = (bf16[128,1024]{1,0:T(8,128)(2,1)}, bf16[128,1024]{1,0:T(8,128)(2,1)}, bf16[4,1024,1024]{2,1,0:T(8,128)(2,1)}, bf16[4,1024,1024]{2,1,0:T(8,128...) custom-call(s32[2]{0:T(128)} %pad_add_fusion.2.source, ...), custom_call_target="tpu_custom_call", output_to_operand_aliasing={{2}: (19, {}), {3}: (20, {}), {4}: (21, {}), {5}: (22, {}),... | custom-call | flops 8589934592 | bytes 16777216 | tf_op jit(solution)/shard_map/expert_chunk/pallas_call | solution.py:475
  203.3 20.0 %expert_chunk.6 = (bf16[128,1024]{1,0:T(8,128)(2,1)}, bf16[128,1024]{1,0:T(8,128)(2,1)}, bf16[4,1024,1024]{2,1,0:T(8,128)(2,1)}, bf16[4,1024,1024]{2,1,0:T(8,128...) custom-call(s32[2]{0:T(128)} %pad_add_fusion.1.source, ...), custom_call_target="tpu_custom_call", output_to_operand_aliasing={{2}: (19, {}), {3}: (20, {}), {4}: (21, {}), {5}: (22, {}),... | custom-call | flops 8589934592 | bytes 16777216 | tf_op jit(solution)/shard_map/expert_chunk/pallas_call | solution.py:475
  224.1 20.0 %expert_chunk.7 = (bf16[128,1024]{1,0:T(8,128)(2,1)}, bf16[128,1024]{1,0:T(8,128)(2,1)}, bf16[4,1024,1024]{2,1,0:T(8,128)(2,1)}, bf16[4,1024,1024]{2,1,0:T(8,128...) custom-call(s32[2]{0:T(128)} %pad_add_fusion.source, ...), custom_call_target="tpu_custom_call", output_to_operand_aliasing={{2}: (19, {}), {3}: (20, {}), {4}: (21, {}), {5}: (22, {}),... | custom-call | flops 8589934592 | bytes 16777216 | tf_op jit(solution)/shard_map/expert_chunk/pallas_call | solution.py:475
  247.8 13.9 %expert_grads.2 = (bf16[2,1024,1024]{2,1,0:T(8,128)(2,1)}, bf16[2,1024,1024]{2,1,0:T(8,128)(2,1)}) custom-call(bf16[4,1024,1024]{2,1,0:T(8,128)(2,1)} %get-tuple-element.163.act, bf16[4,1024,1024]{2,1,0:T(8,128)(2,1)} %get-tuple-element.164.pre, bf16[1024,1024]{1,0:T(8,128)(2,1)} %get-tuple-element.165.ffn_in, bf16[1024,1024]{1,0:T(8,128)(2,1)} %get-tuple-element.166.branch), custom_call_target="tpu_custom_call" | custom-call | flops 8589934592 | bytes 20971520 | tf_op jit(solution)/shard_map/expert_grads/pallas_call | solution.py:535
  261.8 14.0 %expert_grads.3 = (bf16[2,1024,1024]{2,1,0:T(8,128)(2,1)}, bf16[2,1024,1024]{2,1,0:T(8,128)(2,1)}) custom-call(bf16[4,1024,1024]{2,1,0:T(8,128)(2,1)} %get-tuple-element.163.act, bf16[4,1024,1024]{2,1,0:T(8,128)(2,1)} %get-tuple-element.164.pre, bf16[1024,1024]{1,0:T(8,128)(2,1)} %get-tuple-element.165.ffn_in, bf16[1024,1024]{1,0:T(8,128)(2,1)} %get-tuple-element.166.branch), custom_call_target="tpu_custom_call" | custom-call | flops 8589934592 | bytes 20971520 | tf_op jit(solution)/shard_map/expert_grads/pallas_call | solution.py:535
  284.9 10.5 %collective-permute-start.81 = (f32[5,1024]{1,0:T(8,128)S(1)}, f32[5,1024]{1,0:T(8,128)S(1)}, u32[]{:S(2)}, u32[]{:S(2)}) collective-permute-start(f32[5,1024]{1,0:T(8,128)S(1)} %pad_maximum_fusion.12), channel_id=1, source_target_pairs={{0,1},{1,0},{2,3},{3,2},{4,5},{5,4},{6,7},{7,6},{8,9},{9,8},{10,11... | collective-permute-start | bytes 61448 | tf_op jit(solution)/shard_map/ppermute | solution.py:650
  295.4 5.9 collective-permute-done.21.refs_2_
  302.2 9.1 %reenter.1 = (bf16[1024,1024]{1,0:T(8,128)(2,1)}, bf16[1024,1024]{1,0:T(8,128)(2,1)}, bf16[1024,1024]{1,0:T(8,128)(2,1)}, f32[1,1024]{1,0:T(1,128)}) custom-call(bf16[128,1024]{1,0:T(8,128)(2,1)} %get-tuple-element.125.refs_0_, bf16[128,1024]{1,0:T(8,128)(2,1)} %copy-done.62, bf16[128,1024]{1,0:T(8,128)(2,1)} %copy-done.60, bf16[128,1024]{1,0:T(8,128)(2,1)} %copy-done.58, ...), custom_call_target="tpu_custom_call" | custom-call | flops 4294967296 | bytes 10485760 | tf_op jit(solution)/shard_map/reenter/pallas_call | solution.py:248
  311.3 6.0 shared_grads.7
  317.3 4.1 collective-permute-start.69
  321.3 35.8 %attend_back.1 = (bf16[1024,1024]{1,0:T(8,128)(2,1)}, bf16[1024,1024]{1,0:T(8,128)(2,1)}, bf16[1024,1024]{1,0:T(8,128)(2,1)}) custom-call(s32[1,1024]{1,0:T(1,128)} %compare_select_fusion.start_row, bf16[1024,1024]{1,0:T(8,128)(2,1)} %get-tuple-element.96.q_ref, bf16[1024,1024]{1,0:T(8,128)(2,1)} %get-tuple-element.97.k_ref, ...), custom_call_target="tpu_custom_call" | custom-call | flops 21474836480 | bytes 16777216 | tf_op jit(solution)/shard_map/attend_back/pallas_call | solution.py:319
  357.2 18.7 %finish.1 = (bf16[128,1024]{1,0:T(8,128)(2,1)}, bf16[128,1024]{1,0:T(8,128)(2,1)}, bf16[128,1024]{1,0:T(8,128)(2,1)}, bf16[128,1024]{1,0:T(8,128)(2,1)}, bf16[12...) custom-call(bf16[1024,1024]{1,0:T(8,128)(2,1)} %get-tuple-element.13, ...), custom_call_target="tpu_custom_call" | custom-call | flops 8589934592 | bytes 20971520 | tf_op jit(solution)/shard_map/finish/pallas_call | solution.py:368
  376.7 6.0 shared_grads.6
  382.7 6.0 shared_grads.5
  389.3 3.8 collective-permute-start.35
  393.1 6.0 shared_grads.4
  414.7 6.8 collective-permute-done.70
  421.9 10.8 %collective-permute-done.60 = bf16[1,256,1024]{2,1,0:T(8,128)(2,1)S(1)} collective-permute-done((bf16[1,256,1024]{2,1,0:T(8,128)(2,1)S(1)}, bf16[1,256,1024]{2,1,0:T(8,128)(2,1)S(1)}, u32[]{:S(2)}, u32[]{:S(2)}) %collective-permute-start.60) | collective-permute-done | bytes 524320 | tf_op jit(solution)/shard_map/ppermute | solution.py:650
  434.2 9.7 %collective-permute-done.50 = bf16[1,256,1024]{2,1,0:T(8,128)(2,1)S(1)} collective-permute-done((bf16[1,256,1024]{2,1,0:T(8,128)(2,1)S(1)}, bf16[1,256,1024]{2,1,0:T(8,128)(2,1)S(1)}, u32[]{:S(2)}, u32[]{:S(2)}) %collective-permute-start.50) | collective-permute-done | bytes 524320 | tf_op jit(solution)/shard_map/ppermute | solution.py:650
  445.4 9.7 %collective-permute-done.40 = bf16[1,256,1024]{2,1,0:T(8,128)(2,1)S(1)} collective-permute-done((bf16[1,256,1024]{2,1,0:T(8,128)(2,1)S(1)}, bf16[1,256,1024]{2,1,0:T(8,128)(2,1)S(1)}, u32[]{:S(2)}, u32[]{:S(2)}) %collective-permute-start.40) | collective-permute-done | bytes 524320 | tf_op jit(solution)/shard_map/ppermute | solution.py:650
  457.2 4.4 collective-permute-done.51
  461.7 5.5 collective-permute-done.41
  507.9 3.4 collective-permute-done.56
  511.2 5.4 collective-permute-start.38
  526.5 4.2 collective-permute-start.31
  530.7 6.9 collective-permute-start.32
  537.6 3.8 collective-permute-start.67
  542.4 15.7 %collective-permute-start.57 = (bf16[1,256,1024]{2,1,0:T(8,128)(2,1)S(1)}, bf16[1,256,1024]{2,1,0:T(8,128)(2,1)S(1)}, u32[]{:S(2)}, u32[]{:S(2)}) collective-permute-start(bf16[1,256,1024]{2,1,0:T(8,128)(2,1)S(1)} %pad_maximum_fusion.1), channel_id=1, source_target_pairs={{0,4},{4,0},{8,12},{12,8},{16,20},{20,16},{24,28},{28,24},{1,5},{5... | collective-permute-start | bytes 1572872 | tf_op jit(solution)/shard_map/ppermute | solution.py:650
  558.2 8.7 %collective-permute-start.78 = (bf16[1,512,1024]{2,1,0:T(8,128)(2,1)S(1)}, bf16[1,512,1024]{2,1,0:T(8,128)(2,1)S(1)}, u32[]{:S(2)}, u32[]{:S(2)}) collective-permute-start(bf16[1,512,1024]{2,1,0:T(8,128)(2,1)S(1)} %constant_dynamic-update-slice_fusion.15.low), channel_id=1, source_target_pairs={{0,1},{1,0},{2,3},{3,2},{4,5},{5,4},{6,7},{7,6},{8,9},{9,8},{10,11... | collective-permute-start | bytes 3145736 | tf_op jit(solution)/shard_map/ppermute | solution.py:650
  579.4 9.3 %collective-permute-done.33.refs_7_ = bf16[128,1024]{1,0:T(8,128)(2,1)S(1)} collective-permute-done((bf16[128,1024]{1,0:T(8,128)(2,1)S(1)}, bf16[128,1024]{1,0:T(8,128)(2,1)S(1)}, u32[]{:S(2)}, u32[]{:S(2)}) %collective-permute-start.33) | collective-permute-done | bytes 262176 | tf_op jit(solution)/shard_map/ppermute | solution.py:646
  588.6 7.7 %collective-permute-start.68 = (bf16[1,512,1024]{2,1,0:T(8,128)(2,1)}, bf16[1,512,1024]{2,1,0:T(8,128)(2,1)}, u32[]{:S(2)}, u32[]{:S(2)}) collective-permute-start(bf16[1,512,1024]{2,1,0:T(8,128)(2,1)} %constant_dynamic-update-slice_fusion.10.low), channel_id=1, source_target_pairs={{0,1},{1,0},{2,3},{3,2},{4,5},{5,4},{6,7},{7,6},{8,9},{9,8},{10,11... | collective-permute-start | bytes 3145736 | tf_op jit(solution)/shard_map/ppermute | solution.py:650
  601.7 65.4 %assemble.1 = bf16[1024,1024]{1,0:T(8,128)(2,1)} custom-call(s32[8]{0:T(128)} %stack.59.source, bf16[128,1024]{1,0:T(8,128)(2,1)} %get-tuple-element.139.refs_0_, bf16[128,1024]{1,0:T(8,128)(2,1)} %copy-done.20, bf16[128,1024]{1,0:T(8,128)(2,1)} %copy-done.21, bf16[128,1024]{1,0:T(8,128)(2,1)} %copy-done.22, bf16[128,1024]{1,0:T(8,128)(2,1)} %copy-done.23, ...), custom_call_target="tpu_custom_call" | custom-call | bytes 4194304 | tf_op jit(solution)/shard_map/assemble/pallas_call | solution.py:629
  667.1 3.8 unmix.7
  670.9 3.8 unmix.6
  674.7 3.8 unmix.5
  679.5 3.8 unmix.4
  683.4 6.5 convert_add_fusion
  689.9 5.0 convert_add_fusion.1
  (390 shorter events, 146.2 us)
Async XLA Ops:
  0.7 54.5 %collective-permute-start.10 = (bf16[1024,1024]{1,0:T(8,128)(2,1)}, bf16[1024,1024]{1,0:T(8,128)(2,1)}, u32[]{:S(2)}, u32[]{:S(2)}) collective-permute-start(bf16[1024,1024]{1,0:T(8,128)(2,1)} %bitcast.59), channel_id=1, source_target_pairs={{0,2},{1,3},{2,0},{3,1},{4,6},{5,7},{6,4},{7,5},{8,10},{9,11},{10,... | collective-permute-start | bytes 6291464 | tf_op jit(solution)/shard_map/ppermute | solution.py:650
  2.0 90.5 %collective-permute-start.13 = (bf16[1024,1024]{1,0:T(8,128)(2,1)}, bf16[1024,1024]{1,0:T(8,128)(2,1)}, u32[]{:S(2)}, u32[]{:S(2)}) collective-permute-start(bf16[1024,1024]{1,0:T(8,128)(2,1)} %bitcast.65), channel_id=1, source_target_pairs={{0,2},{1,3},{2,0},{3,1},{4,6},{5,7},{6,4},{7,5},{8,10},{9,11},{10,... | collective-permute-start | bytes 6291464 | tf_op jit(solution)/shard_map/ppermute | solution.py:650
  6.0 18.2 %collective-permute-start.1 = (bf16[128,1024]{1,0:T(8,128)(2,1)}, bf16[128,1024]{1,0:T(8,128)(2,1)}, u32[]{:S(2)}, u32[]{:S(2)}) collective-permute-start(bf16[128,1024]{1,0:T(8,128)(2,1)} %get-tuple-element.188), channel_id=1, source_target_pairs={{0,24},{4,28},{8,0},{12,4},{16,8},{20,12},{24,16},{28,20},{1,25},{... | collective-permute-start | bytes 786440 | tf_op jit(solution)/shard_map/ppermute | solution.py:646
  9.3 28.6 %collective-permute-start.2 = (bf16[128,1024]{1,0:T(8,128)(2,1)}, bf16[128,1024]{1,0:T(8,128)(2,1)}, u32[]{:S(2)}, u32[]{:S(2)}) collective-permute-start(bf16[128,1024]{1,0:T(8,128)(2,1)} %get-tuple-element.187), channel_id=1, source_target_pairs={{0,20},{4,24},{8,28},{12,0},{16,4},{20,8},{24,12},{28,16},{1,21},{... | collective-permute-start | bytes 786440 | tf_op jit(solution)/shard_map/ppermute | solution.py:646
  11.2 134.6 %all-to-all-start = ((f32[8,1,128]{2,1,0:T(1,128)}), f32[8,1,128]{2,1,0:T(1,128)S(1)}, u32[]{:S(2)}, u32[]{:S(2)}) async-start(f32[8,1,128]{2,1,0:T(1,128)} %fusion.3), calls=%async_computation | async-start | bytes 8192 | tf_op jit(solution)/shard_map/all_to_all | solution.py:763
  19.0 26.7 %collective-permute-start.3 = (bf16[128,1024]{1,0:T(8,128)(2,1)S(1)}, bf16[128,1024]{1,0:T(8,128)(2,1)}, u32[]{:S(2)}, u32[]{:S(2)}) collective-permute-start(bf16[128,1024]{1,0:T(8,128)(2,1)S(1)} %get-tuple-element.186), channel_id=1, source_target_pairs={{0,16},{4,20},{8,24},{12,28},{16,0},{20,4},{24,8},{28,12},{1,17},{... | collective-permute-start | bytes 786440 | tf_op jit(solution)/shard_map/ppermute | solution.py:646
  24.2 24.9 %collective-permute-start.4 = (bf16[128,1024]{1,0:T(8,128)(2,1)S(1)}, bf16[128,1024]{1,0:T(8,128)(2,1)}, u32[]{:S(2)}, u32[]{:S(2)}) collective-permute-start(bf16[128,1024]{1,0:T(8,128)(2,1)S(1)} %get-tuple-element.185), channel_id=1, source_target_pairs={{0,12},{4,16},{8,20},{12,24},{16,28},{20,0},{24,4},{28,8},{1,13},{... | collective-permute-start | bytes 786440 | tf_op jit(solution)/shard_map/ppermute | solution.py:646
  37.9 15.7 %collective-permute-start.5 = (bf16[128,1024]{1,0:T(8,128)(2,1)S(1)}, bf16[128,1024]{1,0:T(8,128)(2,1)}, u32[]{:S(2)}, u32[]{:S(2)}) collective-permute-start(bf16[128,1024]{1,0:T(8,128)(2,1)S(1)} %get-tuple-element.184), channel_id=1, source_target_pairs={{0,8},{4,12},{8,16},{12,20},{16,24},{20,28},{24,0},{28,4},{1,9},{5... | collective-permute-start | bytes 786440 | tf_op jit(solution)/shard_map/ppermute | solution.py:646
  45.7 48.3 %collective-permute-start.6 = (bf16[128,1024]{1,0:T(8,128)(2,1)S(1)}, bf16[128,1024]{1,0:T(8,128)(2,1)}, u32[]{:S(2)}, u32[]{:S(2)}) collective-permute-start(bf16[128,1024]{1,0:T(8,128)(2,1)S(1)} %get-tuple-element.183), channel_id=1, source_target_pairs={{0,4},{4,8},{8,12},{12,16},{16,20},{20,24},{24,28},{28,0},{1,5},{5... | collective-permute-start | bytes 786440 | tf_op jit(solution)/shard_map/ppermute | solution.py:646
  49.1 103.5 %collective-permute-start.12 = (bf16[1024,1024]{1,0:T(8,128)(2,1)}, bf16[1024,1024]{1,0:T(8,128)(2,1)}, u32[]{:S(2)}, u32[]{:S(2)}) collective-permute-start(bf16[1024,1024]{1,0:T(8,128)(2,1)} %bitcast.66), channel_id=1, source_target_pairs={{0,1},{1,0},{2,3},{3,2},{4,5},{5,4},{6,7},{7,6},{8,9},{9,8},{10,11... | collective-permute-start | bytes 6291464 | tf_op jit(solution)/shard_map/ppermute | solution.py:650
  53.6 100.2 %collective-permute-start.9 = (bf16[1024,1024]{1,0:T(8,128)(2,1)S(1)}, bf16[1024,1024]{1,0:T(8,128)(2,1)}, u32[]{:S(2)}, u32[]{:S(2)}) collective-permute-start(bf16[1024,1024]{1,0:T(8,128)(2,1)S(1)} %bitcast.64), channel_id=1, source_target_pairs={{0,1},{1,0},{2,3},{3,2},{4,5},{5,4},{6,7},{7,6},{8,9},{9,8},{10,11... | collective-permute-start | bytes 6291464 | tf_op jit(solution)/shard_map/ppermute | solution.py:650
  55.2 100.8 %collective-permute-start.11 = (bf16[1024,1024]{1,0:T(8,128)(2,1)}, bf16[1024,1024]{1,0:T(8,128)(2,1)}, u32[]{:S(2)}, u32[]{:S(2)}) collective-permute-start(bf16[1024,1024]{1,0:T(8,128)(2,1)} %collective-permute-done.10.refs_8_), channel_id=1, source_target_pairs={{0,1},{1,0},{2,3},{3,2},{4,5},{5,4},{6,7},{7,6},{8,9},{9,8},{10,11... | collective-permute-start | bytes 6291464 | tf_op jit(solution)/shard_map/ppermute | solution.py:650
  92.5 63.8 %collective-permute-start.14 = (bf16[1024,1024]{1,0:T(8,128)(2,1)}, bf16[1024,1024]{1,0:T(8,128)(2,1)}, u32[]{:S(2)}, u32[]{:S(2)}) collective-permute-start(bf16[1024,1024]{1,0:T(8,128)(2,1)} %collective-permute-done.13.refs_12_), channel_id=1, source_target_pairs={{0,1},{1,0},{2,3},{3,2},{4,5},{5,4},{6,7},{7,6},{8,9},{9,8},{10,11... | collective-permute-start | bytes 6291464 | tf_op jit(solution)/shard_map/ppermute | solution.py:650
  152.3 27.1 %collective-permute-start.17 = (bf16[128,1024]{1,0:T(8,128)(2,1)}, bf16[128,1024]{1,0:T(8,128)(2,1)S(1)}, u32[]{:S(2)}, u32[]{:S(2)}) collective-permute-start(bf16[128,1024]{1,0:T(8,128)(2,1)} %get-tuple-element.105), channel_id=1, source_target_pairs={{0,28},{4,0},{8,4},{12,8},{16,12},{20,16},{24,20},{28,24},{1,29},{... | collective-permute-start | bytes 786440 | tf_op jit(solution)/shard_map/ppermute | solution.py:646
  152.6 29.1 %collective-permute-start.18 = (bf16[128,1024]{1,0:T(8,128)(2,1)}, bf16[128,1024]{1,0:T(8,128)(2,1)S(1)}, u32[]{:S(2)}, u32[]{:S(2)}) collective-permute-start(bf16[128,1024]{1,0:T(8,128)(2,1)} %get-tuple-element.106), channel_id=1, source_target_pairs={{0,8},{4,12},{8,16},{12,20},{16,24},{20,28},{24,0},{28,4},{1,9},{5... | collective-permute-start | bytes 786440 | tf_op jit(solution)/shard_map/ppermute | solution.py:646
  153.9 48.7 %collective-permute-start.15 = (bf16[128,1024]{1,0:T(8,128)(2,1)}, bf16[128,1024]{1,0:T(8,128)(2,1)S(1)}, u32[]{:S(2)}, u32[]{:S(2)}) collective-permute-start(bf16[128,1024]{1,0:T(8,128)(2,1)} %get-tuple-element.103), channel_id=1, source_target_pairs={{0,24},{4,28},{8,0},{12,4},{16,8},{20,12},{24,16},{28,20},{1,25},{... | collective-permute-start | bytes 786440 | tf_op jit(solution)/shard_map/ppermute | solution.py:646
  155.9 46.6 %collective-permute-start.16 = (bf16[128,1024]{1,0:T(8,128)(2,1)}, bf16[128,1024]{1,0:T(8,128)(2,1)S(1)}, u32[]{:S(2)}, u32[]{:S(2)}) collective-permute-start(bf16[128,1024]{1,0:T(8,128)(2,1)} %get-tuple-element.104), channel_id=1, source_target_pairs={{0,12},{4,16},{8,20},{12,24},{16,28},{20,0},{24,4},{28,8},{1,13},{... | collective-permute-start | bytes 786440 | tf_op jit(solution)/shard_map/ppermute | solution.py:646
  156.3 67.1 %collective-permute-start.7 = (bf16[128,1024]{1,0:T(8,128)(2,1)}, bf16[128,1024]{1,0:T(8,128)(2,1)S(1)}, u32[]{:S(2)}, u32[]{:S(2)}) collective-permute-start(bf16[128,1024]{1,0:T(8,128)(2,1)} %get-tuple-element.101), channel_id=1, source_target_pairs={{0,20},{4,24},{8,28},{12,0},{16,4},{20,8},{24,12},{28,16},{1,21},{... | collective-permute-start | bytes 786440 | tf_op jit(solution)/shard_map/ppermute | solution.py:646
  179.5 43.9 %collective-permute-start.8 = (bf16[128,1024]{1,0:T(8,128)(2,1)S(1)}, bf16[128,1024]{1,0:T(8,128)(2,1)S(1)}, u32[]{:S(2)}, u32[]{:S(2)}) collective-permute-start(bf16[128,1024]{1,0:T(8,128)(2,1)S(1)} %copy-done.49), channel_id=1, source_target_pairs={{0,16},{4,20},{8,24},{12,28},{16,0},{20,4},{24,8},{28,12},{1,17},{... | collective-permute-start | bytes 786440 | tf_op jit(solution)/shard_map/ppermute | solution.py:646
  244.1 35.5 %collective-permute-start.23 = (bf16[128,1024]{1,0:T(8,128)(2,1)}, bf16[128,1024]{1,0:T(8,128)(2,1)S(1)}, u32[]{:S(2)}, u32[]{:S(2)}) collective-permute-start(bf16[128,1024]{1,0:T(8,128)(2,1)} %get-tuple-element.129), channel_id=1, source_target_pairs={{0,16},{4,20},{8,24},{12,28},{16,0},{20,4},{24,8},{28,12},{1,17},{... | collective-permute-start | bytes 786440 | tf_op jit(solution)/shard_map/ppermute | solution.py:646
  244.5 37.2 %collective-permute-start.24 = (bf16[128,1024]{1,0:T(8,128)(2,1)}, bf16[128,1024]{1,0:T(8,128)(2,1)S(1)}, u32[]{:S(2)}, u32[]{:S(2)}) collective-permute-start(bf16[128,1024]{1,0:T(8,128)(2,1)} %get-tuple-element.130), channel_id=1, source_target_pairs={{0,12},{4,16},{8,20},{12,24},{16,28},{20,0},{24,4},{28,8},{1,13},{... | collective-permute-start | bytes 786440 | tf_op jit(solution)/shard_map/ppermute | solution.py:646
  276.3 19.1 %collective-permute-start.25 = (bf16[128,1024]{1,0:T(8,128)(2,1)S(1)}, bf16[128,1024]{1,0:T(8,128)(2,1)S(1)}, u32[]{:S(2)}, u32[]{:S(2)}) collective-permute-start(bf16[128,1024]{1,0:T(8,128)(2,1)S(1)} %copy-done.54), channel_id=1, source_target_pairs={{0,8},{4,12},{8,16},{12,20},{16,24},{20,28},{24,0},{28,4},{1,9},{5... | collective-permute-start | bytes 786440 | tf_op jit(solution)/shard_map/ppermute | solution.py:646
  278.4 22.8 %collective-permute-start.21 = (bf16[128,1024]{1,0:T(8,128)(2,1)S(1)}, bf16[128,1024]{1,0:T(8,128)(2,1)S(1)}, u32[]{:S(2)}, u32[]{:S(2)}) collective-permute-start(bf16[128,1024]{1,0:T(8,128)(2,1)S(1)} %copy-done.53), channel_id=1, source_target_pairs={{0,24},{4,28},{8,0},{12,4},{16,8},{20,12},{24,16},{28,20},{1,25},{... | collective-permute-start | bytes 786440 | tf_op jit(solution)/shard_map/ppermute | solution.py:646
  279.6 21.8 %collective-permute-start.26 = (bf16[128,1024]{1,0:T(8,128)(2,1)S(1)}, bf16[128,1024]{1,0:T(8,128)(2,1)S(1)}, u32[]{:S(2)}, u32[]{:S(2)}) collective-permute-start(bf16[128,1024]{1,0:T(8,128)(2,1)S(1)} %copy-done.52), channel_id=1, source_target_pairs={{0,4},{4,8},{8,12},{12,16},{16,20},{20,24},{24,28},{28,0},{1,5},{5... | collective-permute-start | bytes 786440 | tf_op jit(solution)/shard_map/ppermute | solution.py:646
  281.6 19.8 %collective-permute-start.20 = (bf16[128,1024]{1,0:T(8,128)(2,1)S(1)}, bf16[128,1024]{1,0:T(8,128)(2,1)S(1)}, u32[]{:S(2)}, u32[]{:S(2)}) collective-permute-start(bf16[128,1024]{1,0:T(8,128)(2,1)S(1)} %copy-done.51), channel_id=1, source_target_pairs={{0,28},{4,0},{8,4},{12,8},{16,12},{20,16},{24,20},{28,24},{1,29},{... | collective-permute-start | bytes 786440 | tf_op jit(solution)/shard_map/ppermute | solution.py:646
  284.9 115.0 %collective-permute-start.81 = (f32[5,1024]{1,0:T(8,128)S(1)}, f32[5,1024]{1,0:T(8,128)S(1)}, u32[]{:S(2)}, u32[]{:S(2)}) collective-permute-start(f32[5,1024]{1,0:T(8,128)S(1)} %pad_maximum_fusion.12), channel_id=1, source_target_pairs={{0,1},{1,0},{2,3},{3,2},{4,5},{5,4},{6,7},{7,6},{8,9},{9,8},{10,11... | collective-permute-start | bytes 61448 | tf_op jit(solution)/shard_map/ppermute | solution.py:650
  317.3 90.6 %collective-permute-start.69 = (bf16[1,512,1024]{2,1,0:T(8,128)(2,1)}, bf16[1,512,1024]{2,1,0:T(8,128)(2,1)S(1)}, u32[]{:S(2)}, u32[]{:S(2)}) collective-permute-start(bf16[1,512,1024]{2,1,0:T(8,128)(2,1)} %get-tuple-element.162), channel_id=1, source_target_pairs={{0,1},{1,0},{2,3},{3,2},{4,5},{5,4},{6,7},{7,6},{8,9},{9,8},{10,11... | collective-permute-start | bytes 3145736 | tf_op jit(solution)/shard_map/ppermute | solution.py:650
  388.7 19.7 %collective-permute-start.59 = (bf16[1,512,1024]{2,1,0:T(8,128)(2,1)}, bf16[1,512,1024]{2,1,0:T(8,128)(2,1)}, u32[]{:S(2)}, u32[]{:S(2)}) collective-permute-start(bf16[1,512,1024]{2,1,0:T(8,128)(2,1)} %get-tuple-element.159), channel_id=1, source_target_pairs={{0,1},{1,0},{2,3},{3,2},{4,5},{5,4},{6,7},{7,6},{8,9},{9,8},{10,11... | collective-permute-start | bytes 3145736 | tf_op jit(solution)/shard_map/ppermute | solution.py:650
  389.2 21.7 %collective-permute-start.49 = (bf16[1,512,1024]{2,1,0:T(8,128)(2,1)}, bf16[1,512,1024]{2,1,0:T(8,128)(2,1)S(1)}, u32[]{:S(2)}, u32[]{:S(2)}) collective-permute-start(bf16[1,512,1024]{2,1,0:T(8,128)(2,1)} %get-tuple-element.157), channel_id=1, source_target_pairs={{0,1},{1,0},{2,3},{3,2},{4,5},{5,4},{6,7},{7,6},{8,9},{9,8},{10,11... | collective-permute-start | bytes 3145736 | tf_op jit(solution)/shard_map/ppermute | solution.py:650
  405.5 132.1 %collective-permute-start.83 = (bf16[2,1024,1024]{2,1,0:T(8,128)(2,1)}, bf16[2,1024,1024]{2,1,0:T(8,128)(2,1)S(1)}, u32[]{:S(2)}, u32[]{:S(2)}) collective-permute-start(bf16[2,1024,1024]{2,1,0:T(8,128)(2,1)} %get-tuple-element.174), channel_id=1, source_target_pairs={{0,1},{1,0},{2,3},{3,2},{4,5},{5,4},{6,7},{7,6},{8,9},{9,8},{10,11... | collective-permute-start | bytes 12582920 | tf_op jit(solution)/shard_map/ppermute | solution.py:650
  407.8 161.1 %collective-permute-start.79 = (bf16[2,1024,1024]{2,1,0:T(8,128)(2,1)}, bf16[2,1024,1024]{2,1,0:T(8,128)(2,1)S(1)}, u32[]{:S(2)}, u32[]{:S(2)}) collective-permute-start(bf16[2,1024,1024]{2,1,0:T(8,128)(2,1)} %get-tuple-element.168), channel_id=1, source_target_pairs={{0,1},{1,0},{2,3},{3,2},{4,5},{5,4},{6,7},{7,6},{8,9},{9,8},{10,11... | collective-permute-start | bytes 12582920 | tf_op jit(solution)/shard_map/ppermute | solution.py:650
  410.9 21.8 %collective-permute-start.60 = (bf16[1,256,1024]{2,1,0:T(8,128)(2,1)S(1)}, bf16[1,256,1024]{2,1,0:T(8,128)(2,1)S(1)}, u32[]{:S(2)}, u32[]{:S(2)}) collective-permute-start(bf16[1,256,1024]{2,1,0:T(8,128)(2,1)S(1)} %slice.245), channel_id=1, source_target_pairs={{0,4},{4,0},{8,12},{12,8},{16,20},{20,16},{24,28},{28,24},{1,5},{5... | collective-permute-start | bytes 1572872 | tf_op jit(solution)/shard_map/ppermute | solution.py:650
  412.2 31.7 %collective-permute-start.50 = (bf16[1,256,1024]{2,1,0:T(8,128)(2,1)S(1)}, bf16[1,256,1024]{2,1,0:T(8,128)(2,1)S(1)}, u32[]{:S(2)}, u32[]{:S(2)}) collective-permute-start(bf16[1,256,1024]{2,1,0:T(8,128)(2,1)S(1)} %slice.237), channel_id=1, source_target_pairs={{0,4},{4,0},{8,12},{12,8},{16,20},{20,16},{24,28},{28,24},{1,5},{5... | collective-permute-start | bytes 1572872 | tf_op jit(solution)/shard_map/ppermute | solution.py:650
  421.5 33.7 %collective-permute-start.40 = (bf16[1,256,1024]{2,1,0:T(8,128)(2,1)S(1)}, bf16[1,256,1024]{2,1,0:T(8,128)(2,1)S(1)}, u32[]{:S(2)}, u32[]{:S(2)}) collective-permute-start(bf16[1,256,1024]{2,1,0:T(8,128)(2,1)S(1)} %slice.228), channel_id=1, source_target_pairs={{0,4},{4,0},{8,12},{12,8},{16,20},{20,16},{24,28},{28,24},{1,5},{5... | collective-permute-start | bytes 1572872 | tf_op jit(solution)/shard_map/ppermute | solution.py:650
  432.7 24.0 %collective-permute-start.71 = (bf16[1,128,1024]{2,1,0:T(8,128)(2,1)S(1)}, bf16[1,128,1024]{2,1,0:T(8,128)(2,1)S(1)}, u32[]{:S(2)}, u32[]{:S(2)}) collective-permute-start(bf16[1,128,1024]{2,1,0:T(8,128)(2,1)S(1)} %slice.256), channel_id=1, source_target_pairs={{0,2},{1,3},{2,0},{3,1},{4,6},{5,7},{6,4},{7,5},{8,10},{9,11},{10,... | collective-permute-start | bytes 786440 | tf_op jit(solution)/shard_map/ppermute | solution.py:650
  501.4 18.3 %collective-permute-start.77 = (bf16[1,256,1024]{2,1,0:T(8,128)(2,1)S(1)}, bf16[1,256,1024]{2,1,0:T(8,128)(2,1)S(1)}, u32[]{:S(2)}, u32[]{:S(2)}) collective-permute-start(bf16[1,256,1024]{2,1,0:T(8,128)(2,1)S(1)} %pad_maximum_fusion.3), channel_id=1, source_target_pairs={{0,4},{4,0},{8,12},{12,8},{16,20},{20,16},{24,28},{28,24},{1,5},{5... | collective-permute-start | bytes 1572872 | tf_op jit(solution)/shard_map/ppermute | solution.py:650
  524.1 18.3 %collective-permute-start.30 = (bf16[128,1024]{1,0:T(8,128)(2,1)S(1)}, bf16[128,1024]{1,0:T(8,128)(2,1)S(1)}, u32[]{:S(2)}, u32[]{:S(2)}) collective-permute-start(bf16[128,1024]{1,0:T(8,128)(2,1)S(1)} %copy-done.45), channel_id=1, source_target_pairs={{0,16},{4,20},{8,24},{12,28},{16,0},{20,4},{24,8},{28,12},{1,17},{... | collective-permute-start | bytes 786440 | tf_op jit(solution)/shard_map/ppermute | solution.py:646
  526.5 31.7 %collective-permute-start.31 = (bf16[128,1024]{1,0:T(8,128)(2,1)S(1)}, bf16[128,1024]{1,0:T(8,128)(2,1)S(1)}, u32[]{:S(2)}, u32[]{:S(2)}) collective-permute-start(bf16[128,1024]{1,0:T(8,128)(2,1)S(1)} %copy-done.44), channel_id=1, source_target_pairs={{0,20},{4,24},{8,28},{12,0},{16,4},{20,8},{24,12},{28,16},{1,21},{... | collective-permute-start | bytes 786440 | tf_op jit(solution)/shard_map/ppermute | solution.py:646
  530.7 36.2 %collective-permute-start.32 = (bf16[128,1024]{1,0:T(8,128)(2,1)S(1)}, bf16[128,1024]{1,0:T(8,128)(2,1)S(1)}, u32[]{:S(2)}, u32[]{:S(2)}) collective-permute-start(bf16[128,1024]{1,0:T(8,128)(2,1)S(1)} %copy-done.43), channel_id=1, source_target_pairs={{0,24},{4,28},{8,0},{12,4},{16,8},{20,12},{24,16},{28,20},{1,25},{... | collective-permute-start | bytes 786440 | tf_op jit(solution)/shard_map/ppermute | solution.py:646
  537.6 35.0 %collective-permute-start.67 = (bf16[1,256,1024]{2,1,0:T(8,128)(2,1)S(1)}, bf16[1,256,1024]{2,1,0:T(8,128)(2,1)S(1)}, u32[]{:S(2)}, u32[]{:S(2)}) collective-permute-start(bf16[1,256,1024]{2,1,0:T(8,128)(2,1)S(1)} %pad_maximum_fusion.2), channel_id=1, source_target_pairs={{0,4},{4,0},{8,12},{12,8},{16,20},{20,16},{24,28},{28,24},{1,5},{5... | collective-permute-start | bytes 1572872 | tf_op jit(solution)/shard_map/ppermute | solution.py:650
  542.4 31.2 %collective-permute-start.57 = (bf16[1,256,1024]{2,1,0:T(8,128)(2,1)S(1)}, bf16[1,256,1024]{2,1,0:T(8,128)(2,1)S(1)}, u32[]{:S(2)}, u32[]{:S(2)}) collective-permute-start(bf16[1,256,1024]{2,1,0:T(8,128)(2,1)S(1)} %pad_maximum_fusion.1), channel_id=1, source_target_pairs={{0,4},{4,0},{8,12},{12,8},{16,20},{20,16},{24,28},{28,24},{1,5},{5... | collective-permute-start | bytes 1572872 | tf_op jit(solution)/shard_map/ppermute | solution.py:650
  558.2 39.1 %collective-permute-start.78 = (bf16[1,512,1024]{2,1,0:T(8,128)(2,1)S(1)}, bf16[1,512,1024]{2,1,0:T(8,128)(2,1)S(1)}, u32[]{:S(2)}, u32[]{:S(2)}) collective-permute-start(bf16[1,512,1024]{2,1,0:T(8,128)(2,1)S(1)} %constant_dynamic-update-slice_fusion.15.low), channel_id=1, source_target_pairs={{0,1},{1,0},{2,3},{3,2},{4,5},{5,4},{6,7},{7,6},{8,9},{9,8},{10,11... | collective-permute-start | bytes 3145736 | tf_op jit(solution)/shard_map/ppermute | solution.py:650
  566.9 116.4 %collective-permute-start.84 = (bf16[1,1024,1024]{2,1,0:T(8,128)(2,1)S(1)}, bf16[1,1024,1024]{2,1,0:T(8,128)(2,1)}, u32[]{:S(2)}, u32[]{:S(2)}) collective-permute-start(bf16[1,1024,1024]{2,1,0:T(8,128)(2,1)S(1)} %add_convert_fusion), channel_id=1, source_target_pairs={{0,2},{1,3},{2,0},{3,1},{4,6},{5,7},{6,4},{7,5},{8,10},{9,11},{10,... | collective-permute-start | bytes 6291464 | tf_op jit(solution)/shard_map/ppermute | solution.py:650
  568.9 27.4 %collective-permute-start.47 = (bf16[1,256,1024]{2,1,0:T(8,128)(2,1)S(1)}, bf16[1,256,1024]{2,1,0:T(8,128)(2,1)S(1)}, u32[]{:S(2)}, u32[]{:S(2)}) collective-permute-start(bf16[1,256,1024]{2,1,0:T(8,128)(2,1)S(1)} %pad_maximum_fusion), channel_id=1, source_target_pairs={{0,4},{4,0},{8,12},{12,8},{16,20},{20,16},{24,28},{28,24},{1,5},{5... | collective-permute-start | bytes 1572872 | tf_op jit(solution)/shard_map/ppermute | solution.py:650
  572.6 117.2 %collective-permute-start.80 = (bf16[1,1024,1024]{2,1,0:T(8,128)(2,1)}, bf16[1,1024,1024]{2,1,0:T(8,128)(2,1)}, u32[]{:S(2)}, u32[]{:S(2)}) collective-permute-start(bf16[1,1024,1024]{2,1,0:T(8,128)(2,1)} %add_convert_fusion.1), channel_id=1, source_target_pairs={{0,2},{1,3},{2,0},{3,1},{4,6},{5,7},{6,4},{7,5},{8,10},{9,11},{10,... | collective-permute-start | bytes 6291464 | tf_op jit(solution)/shard_map/ppermute | solution.py:650
  588.6 82.3 %collective-permute-start.68 = (bf16[1,512,1024]{2,1,0:T(8,128)(2,1)}, bf16[1,512,1024]{2,1,0:T(8,128)(2,1)}, u32[]{:S(2)}, u32[]{:S(2)}) collective-permute-start(bf16[1,512,1024]{2,1,0:T(8,128)(2,1)} %constant_dynamic-update-slice_fusion.10.low), channel_id=1, source_target_pairs={{0,1},{1,0},{2,3},{3,2},{4,5},{5,4},{6,7},{7,6},{8,9},{9,8},{10,11... | collective-permute-start | bytes 3145736 | tf_op jit(solution)/shard_map/ppermute | solution.py:650
  596.3 78.4 %collective-permute-start.58 = (bf16[1,512,1024]{2,1,0:T(8,128)(2,1)}, bf16[1,512,1024]{2,1,0:T(8,128)(2,1)}, u32[]{:S(2)}, u32[]{:S(2)}) collective-permute-start(bf16[1,512,1024]{2,1,0:T(8,128)(2,1)} %constant_dynamic-update-slice_fusion.5.low), channel_id=1, source_target_pairs={{0,1},{1,0},{2,3},{3,2},{4,5},{5,4},{6,7},{7,6},{8,9},{9,8},{10,11... | collective-permute-start | bytes 3145736 | tf_op jit(solution)/shard_map/ppermute | solution.py:650
  598.2 80.4 %collective-permute-start.48 = (bf16[1,512,1024]{2,1,0:T(8,128)(2,1)}, bf16[1,512,1024]{2,1,0:T(8,128)(2,1)S(1)}, u32[]{:S(2)}, u32[]{:S(2)}) collective-permute-start(bf16[1,512,1024]{2,1,0:T(8,128)(2,1)} %constant_dynamic-update-slice_fusion.low), channel_id=1, source_target_pairs={{0,1},{1,0},{2,3},{3,2},{4,5},{5,4},{6,7},{7,6},{8,9},{9,8},{10,11... | collective-permute-start | bytes 3145736 | tf_op jit(solution)/shard_map/ppermute | solution.py:650
  (101 other events, 1219.1 us)

commit v2 on v1

--- a/solution.py
+++ b/solution.py
@@ -92,13 +92,13 @@
 
 def entry(slots, pos_row, gain, offset, wq, bq, wk, wv, bv):
     parts = len(slots)
-    piece, width = slots[0].shape
-    count = piece * parts
+    width = slots[0].shape[1]
+    count = sum(v.shape[0] for v in slots)
     out = jax.ShapeDtypeStruct((count, width), BF16)
     return pl.pallas_call(
         functools.partial(entry_kernel, parts),
         grid=(count // ROWS,),
-        in_specs=[whole((piece, width))] * parts
+        in_specs=[whole(v.shape) for v in slots]
         + [whole((1, count))]
         + [whole((1, width))] * 2
         + [whole((width, width)), whole((1, width)), whole((width, width)), whole((width, width)), whole((1, width))],
@@ -242,13 +242,13 @@
 
 def reenter(slots, pos_row, live_col, wo):
     parts = len(slots)
-    piece, width = slots[0].shape
-    count = piece * parts
+    width = slots[0].shape[1]
+    count = sum(v.shape[0] for v in slots)
     out = jax.ShapeDtypeStruct((count, width), BF16)
     return pl.pallas_call(
         functools.partial(reenter_kernel, parts),
         grid=(count // ROWS,),
-        in_specs=[whole((piece, width))] * parts
+        in_specs=[whole(v.shape) for v in slots]
         + [whole((1, count)), rows_of(ROWS, 1), whole((width, width))],
         out_specs=[rows_of(ROWS, width)] * 3 + [whole((1, width))],
         out_shape=[out] * 3 + [jax.ShapeDtypeStruct((1, width), F32)],
@@ -387,34 +387,33 @@
 STEP = 512
 
 
-def expert_kernel(parts, shards, first_chunk, source, *refs):
+def expert_kernel(first_chunk, parts, *refs):
     it = iter(refs)
     take = lambda n: [next(it) for _ in range(n)]
-    slots, cots, lives = take(parts), take(parts), take(parts)
-    ups, downs = take(shards), take(shards)
-    up_bias, down_bias, gain, offset = take(4)
+    (source,) = take(1)
+    slots, cots, lives, ups, downs, up_bias, down_bias, gain, offset = take(9)
     if not first_chunk:
         take(5)
     grads = take(parts)
     act_out, pre_out, ffn_out, branch_out, block_out, sums, up_sums = take(7)
-    up, down, out_sum, grad_sum, out_low, up_sem, down_sem, out_sem = take(8)
-
-    up_copies = [pltpu.make_async_copy(ups[k], up.at[k], up_sem.at[k]) for k in range(shards)]
-    down_copies = [pltpu.make_async_copy(downs[k], down.at[k], down_sem.at[k]) for k in range(shards)]
+    up, down, out_sum, grad_sum, grad_low, up_sem, down_sem = take(7)
+    shards = up.shape[0]
+    rows, model = slots.shape
+
+    up_copies = [pltpu.make_async_copy(ups.at[k], up.at[k], up_sem.at[k]) for k in range(shards)]
+    down_copies = [
+        pltpu.make_async_copy(downs.at[k], down.at[k], down_sem.at[k]) for k in range(shards)
+    ]
     for k in range(shards):
         up_copies[k].start()
         down_copies[k].start()
 
-    routed = jnp.concatenate([r[...] for r in slots], axis=0).astype(F32)
-    cot = jnp.concatenate([r[...] for r in cots], axis=0).astype(F32)
-    live = jnp.concatenate([r[...] for r in lives], axis=0)
-    normal, root = norm_parts(routed)
-    ffn_in = (normal * gain[...] + offset[...]).astype(BF16)
-    branch = (live * cot).astype(BF16)
-    ffn_out[...] = ffn_in
-    branch_out[...] = branch
-    out_sum[...] = jnp.broadcast_to(down_bias[...], out_sum.shape)
-    grad_sum[...] = jnp.zeros_like(grad_sum)
+    routed = slots[...].astype(F32)
+    cot = cots[...].reshape(rows, model).astype(F32)
+    live = lives[...].reshape(rows, 1)
+    normal, _ = norm_parts(routed)
+    ffn_out[...] = (normal * gain[...] + offset[...]).astype(BF16)
+    branch_out[...] = (live * cot).astype(BF16)
     width = up.shape[2]
     for k in range(shards):
         up_copies[k].wait()
@@ -434,57 +433,69 @@
             grad_pre = (nt(branch_out[...], down[k, cols, :]) * slope).astype(BF16)
             pre_out[k, :, cols] = grad_pre
             up_sums[k, :, cols] = jnp.sum(grad_pre.astype(F32), axis=0, keepdims=True)
-            grad_sum[...] += nt(grad_pre, up[k, :, cols])
-            out_sum[...] += nn(act, down[k, cols, :])
+            grad_part = nt(grad_pre, up[k, :, cols])
+            out_part = nn(act, down[k, cols, :])
+            if k == 0 and c == 0:
+                grad_sum[...] = grad_part
+                out_sum[...] = out_part
+            else:
+                grad_sum[...] += grad_part
+                out_sum[...] += out_part
+    routed = slots[...].astype(F32)
+    normal, root = norm_parts(routed)
     grad = grad_sum[...]
+    cot = cots[...].reshape(rows, model).astype(F32)
     grad_routed = (cot + norm_grad(grad, normal, root, gain[...])).astype(BF16)
-    out_low[...] = (routed + live * out_sum[...]).astype(BF16)
-    piece = slots[0].shape[0]
-    out_copies = []
-    for j in range(parts):
-        grads[j][...] = grad_routed[j * piece : (j + 1) * piece]
-        place = pl.multiple_of(source[j] * piece, piece)
-        copy = pltpu.make_async_copy(
-            out_low.at[pl.ds(j * piece, piece)], block_out.at[pl.ds(place, piece)], out_sem.at[j]
-        )
-        copy.start()
-        out_copies.append(copy)
+    if parts == 1:
+        grads[0][...] = grad_routed
+    else:
+        grad_low[...] = grad_routed
+        short = rows // parts
+        for r in range(parts):
+            grads[r][...] = grad_low[pl.ds(pl.multiple_of(source[r] * short, short), short), :]
+    out = routed + lives[...].reshape(rows, 1) * (out_sum[...] + down_bias[...])
+    block_out[...] = out.astype(BF16).reshape(block_out.shape)
     sums[...] = jnp.zeros_like(sums)
     sums[0:1, :] = jnp.sum(grad * normal, axis=0, keepdims=True)
     sums[1:2, :] = jnp.sum(grad, axis=0, keepdims=True)
-    sums[2:3, :] = jnp.sum(branch.astype(F32), axis=0, keepdims=True)
-    for copy in out_copies:
-        copy.wait()
-
-
-def expert_chunk(chunk, source, slots, cot, live, ups, downs, up_bias, down_bias, gain, offset, carried):
-    parts, shards = len(slots), len(ups)
-    piece, width = slots[0].shape
-    rows = parts * piece
-    count = cot.shape[0]
-    part = ups[0].shape[1]
-    picked = lambda j, w: pl.BlockSpec((piece, w), lambda i, source, j=j: (source[j], 0))
+    sums[2:3, :] = jnp.sum(branch_out[...].astype(F32), axis=0, keepdims=True)
+
+
+def expert_chunk(
+    chunk, parts, source, slots, cot, live, ups, downs, up_bias, down_bias, gain, offset, carried
+):
+    rows, width = slots.shape
+    groups, piece, _ = cot.shape
+    short = rows // groups
+    count = groups * piece
+    shards, _, part = ups.shape
     anywhere = pl.BlockSpec(memory_space=pl.ANY)
-    big = pl.BlockSpec((shards, rows, part), lambda *_: (0, chunk, 0))
-    flat = pl.BlockSpec((rows, width), lambda *_: (chunk, 0))
+    big = pl.BlockSpec((shards, rows, part), lambda i, *_: (0, chunk, 0))
+    flat = pl.BlockSpec((rows, width), lambda i, *_: (chunk, 0))
+    block = pl.BlockSpec((groups, short, width), lambda i, *_: (0, chunk, 0))
     first = carried is None
     previous = [] if first else list(carried)
-    before = 1 + 3 * parts + 2 * shards + 4
     full = jax.ShapeDtypeStruct((count, width), BF16)
     wide = jax.ShapeDtypeStruct((shards, count, part), BF16)
     outs = pl.pallas_call(
-        functools.partial(expert_kernel, parts, shards, first),
+        functools.partial(expert_kernel, first, parts),
         grid_spec=pltpu.PrefetchScalarGridSpec(
             num_scalar_prefetch=1,
             grid=(1,),
-            in_specs=[whole((piece, width))] * parts
-            + [picked(j, width) for j in range(parts)]
-            + [picked(j, 1) for j in range(parts)]
-            + [anywhere] * (2 * shards)
-            + [whole((shards, 1, part)), whole((1, width)), whole((1, width)), whole((1, width))]
+            in_specs=[
+                whole((rows, width)),
+                block,
+                pl.BlockSpec((groups, short, 1), lambda i, *_: (0, chunk, 0)),
+                anywhere,
+                anywhere,
+                whole((shards, 1, part)),
+                whole((1, width)),
+                whole((1, width)),
+                whole((1, width)),
+            ]
             + [anywhere] * len(previous),
-            out_specs=[whole((piece, width))] * parts
-            + [big, big, flat, flat, anywhere, whole((8, width)), whole((shards, 1, part))],
+            out_specs=[whole((rows // parts, width))] * parts
+            + [big, big, flat, flat, block, whole((8, width)), whole((shards, 1, part))],
             scratch_shapes=[
                 pltpu.VMEM((shards, width, part), BF16),
                 pltpu.VMEM((shards, part, width), BF16),
@@ -493,147 +504,151 @@
                 pltpu.VMEM((rows, width), BF16),
                 pltpu.SemaphoreType.DMA((shards,)),
                 pltpu.SemaphoreType.DMA((shards,)),
-                pltpu.SemaphoreType.DMA((parts,)),
             ],
         ),
-        out_shape=[jax.ShapeDtypeStruct((piece, width), BF16)] * parts
-        + [wide, wide, full, full, full]
-        + [jax.ShapeDtypeStruct((8, width), F32), jax.ShapeDtypeStruct((shards, 1, part), F32)],
-        input_output_aliases={before + n: parts + n for n in range(len(previous))},
+        out_shape=[jax.ShapeDtypeStruct((rows // parts, width), BF16)] * parts
+        + [
+            wide,
+            wide,
+            full,
+            full,
+            jax.ShapeDtypeStruct((groups, piece, width), BF16),
+            jax.ShapeDtypeStruct((8, width), F32),
+            jax.ShapeDtypeStruct((shards, 1, part), F32),
+        ],
+        input_output_aliases={10 + n: parts + n for n in range(len(previous))},
         compiler_params=params(),
         cost_estimate=cost(
             8 * rows * width * part * shards, 4 * shards * width * part, rows * part * shards
         ),
         name="expert_chunk",
-    )(
-        source,
-        *slots,
-        *([cot] * parts),
-        *([live] * parts),
-        *ups,
-        *downs,
-        up_bias,
-        down_bias,
-        gain,
-        offset,
-        *previous,
-    )
-    grads = outs[:parts]
-    return grads, outs[parts : parts + 5], outs[parts + 5], outs[parts + 6]
-
-
-def expert_grads_kernel(act, pre, ffn_in, branch, down_out, up_out):
-    down_out[0] = tn(act[0], branch[...]).astype(BF16)
-    up_out[0] = tn(ffn_in[...], pre[0]).astype(BF16)
-
-
-def expert_grads(first, step, act, pre, ffn_in, branch):
-    shards, count, part = act.shape
-    width = ffn_in.shape[1]
-    number = shards // step
-    pick = pl.BlockSpec((1, count, part), lambda i: (first + step * i, 0, 0))
+    )(source, slots, cot, live, ups, downs, up_bias, down_bias, gain, offset, *previous)
+    return outs[:parts], outs[parts : parts + 5], outs[parts + 5], outs[parts + 6]
+
+
+def shard_grads_kernel(left, right, out):
+    first = left[0] if len(left.shape) == 3 else left[...]
+    second = right[0] if len(right.shape) == 3 else right[...]
+    out[0] = tn(first, second).astype(BF16)
+
+
+def shard_grads(left, right):
+    def spec(v):
+        if v.ndim == 2:
+            return whole(v.shape)
+        return pl.BlockSpec((1,) + v.shape[1:], lambda i: (i, 0, 0))
+
+    shards = left.shape[0] if left.ndim == 3 else right.shape[0]
+    count = left.shape[-2]
+    tall, wide = left.shape[-1], right.shape[-1]
     return pl.pallas_call(
-        expert_grads_kernel,
-        grid=(number,),
-        in_specs=[pick, pick, whole((count, width)), whole((count, width))],
-        out_specs=[
-            pl.BlockSpec((1, part, width), lambda i: (i, 0, 0)),
-            pl.BlockSpec((1, width, part), lambda i: (i, 0, 0)),
-        ],
-        out_shape=[
-            jax.ShapeDtypeStruct((number, part, width), BF16),
-            jax.ShapeDtypeStruct((number, width, part), BF16),
-        ],
-        compiler_params=params(),
-        cost_estimate=cost(4 * number * count * width * part, 10 * number * width * part),
-        name="expert_grads",
-    )(act, pre, ffn_in, branch)
-
-
-def shared_grads_kernel(blocks, code, left, right, keep, send, total):
+        shard_grads_kernel,
+        grid=(shards,),
+        in_specs=[spec(left), spec(right)],
+        out_specs=pl.BlockSpec((1, tall, wide), lambda i: (i, 0, 0)),
+        out_shape=jax.ShapeDtypeStruct((shards, tall, wide), BF16),
+        compiler_params=params(),
+        cost_estimate=cost(2 * shards * count * tall * wide, 6 * shards * tall * wide),
+        name="shard_grads",
+    )(left, right)
+
+
+def block_place(codes, streams, blocks, j, size):
+    stream = (j // (blocks // (2 * streams))) % streams
+    return pl.multiple_of((codes[stream] ^ j) * size, size)
+
+
+def shared_grads_kernel(streams, blocks, codes, left, right, keep, send, total):
     total[...] = tn(left[...], right[...])
     size = total.shape[0] // blocks
     half = blocks // 2
     for j in range(blocks):
-        place = pl.multiple_of((code[0] ^ j) * size, size)
+        place = block_place(codes, streams, blocks, j, size)
         target = keep if j < half else send
         target[0, pl.ds((j % half) * size, size), :] = total[pl.ds(place, size), :].astype(BF16)
 
 
-def shared_grads(blocks, code, left, rights):
-    count, width = left.shape
+def shared_grads_many_kernel(streams, blocks, owners, lefts, codes, *refs):
+    number = len(owners)
+    left_refs, rights, (keep, send, total) = refs[:lefts], refs[lefts : lefts + number], refs[lefts + number :]
+    for m in range(number):
+
+        @pl.when(pl.program_id(0) == m)
+        def _():
+            shared_grads_kernel(streams, blocks, codes, left_refs[owners[m]], rights[m], keep, send, total)
+
+
+def shared_grads(layout, lefts, owners, rights):
+    count, width = lefts[0].shape
     number = len(rights)
-    if number > 1:
-        raise NotImplementedError
-    half = pl.BlockSpec((1, width // 2, width), lambda i, *_: (0, 0, 0))
+    half = pl.BlockSpec((1, width // 2, width), lambda i, *_: (i, 0, 0))
     return pl.pallas_call(
-        functools.partial(shared_grads_kernel, blocks),
+        functools.partial(
+            shared_grads_many_kernel, layout.streams, layout.blocks, owners, len(lefts)
+        ),
         grid_spec=pltpu.PrefetchScalarGridSpec(
             num_scalar_prefetch=1,
-            grid=(1,),
-            in_specs=[whole((count, width))] * 2,
+            grid=(number,),
+            in_specs=[whole((count, width))] * (len(lefts) + number),
             out_specs=[half, half],
             scratch_shapes=[pltpu.VMEM((width, width), F32)],
         ),
-        out_shape=[jax.ShapeDtypeStruct((1, width // 2, width), BF16)] * 2,
-        compiler_params=params(),
-        cost_estimate=cost(2 * count * width * width, 6 * width * width),
+        out_shape=[jax.ShapeDtypeStruct((number, width // 2, width), BF16)] * 2,
+        compiler_params=params(),
+        cost_estimate=cost(2 * number * count * width * width, 6 * number * width * width),
         name="shared_grads",
-    )(code, left, rights[0])
-
-
-def unmix_kernel(blocks, code, low, high, out):
+    )(layout.codes, *lefts, *rights)
+
+
+def unmix_kernel(streams, blocks, number, codes, half_place, *refs):
+    pieces, outs = refs[0], refs[-number:]
     half = blocks // 2
-    size = out.shape[0] // blocks
-    for j in range(blocks):
-        place = pl.multiple_of((code[0] ^ j) * size, size)
-        source = low if j < half else high
-        out[pl.ds(place, size), :] = source[0, pl.ds((j % half) * size, size), :].astype(F32)
-
-
-def unmix(blocks, code, low, high):
-    _, rows, width = low.shape
-    half = pl.BlockSpec((1, rows, width), lambda i, *_: (0, 0, 0))
+    size = outs[0].shape[0] // half
+    for m in range(number):
+        for j in range(half):
+            place = block_place(codes, streams, blocks, j, size)
+            place = pl.multiple_of(place % (half * size), size)
+            outs[m][pl.ds(place, size), :] = pieces[m, pl.ds(j * size, size), :].astype(F32)
+
+
+def unmix(layout, half_place, pieces, before=None):
+    number, rows, width = pieces.shape
+    earlier = [] if before is None else list(before)
+    out = pl.BlockSpec((rows, width), lambda i, codes, half_place: (half_place[0], 0))
     return pl.pallas_call(
-        functools.partial(unmix_kernel, blocks),
+        functools.partial(unmix_kernel, layout.streams, layout.blocks, number),
         grid_spec=pltpu.PrefetchScalarGridSpec(
-            num_scalar_prefetch=1,
+            num_scalar_prefetch=2,
             grid=(1,),
-            in_specs=[half, half],
-            out_specs=whole((2 * rows, width)),
+            in_specs=[whole((number, rows, width))]
+            + [pl.BlockSpec(memory_space=pl.ANY)] * len(earlier),
+            out_specs=[out] * number,
         ),
-        out_shape=jax.ShapeDtypeStruct((2 * rows, width), F32),
-        compiler_params=params(),
-        cost_estimate=cost(2 * rows * width, 12 * rows * width),
+        out_shape=[jax.ShapeDtypeStruct((2 * rows, width), F32)] * number,
+        input_output_aliases={3 + m: m for m in range(len(earlier))},
+        compiler_params=params(),
+        cost_estimate=cost(number * rows * width, 6 * number * rows * width),
         name="unmix",
-    )(code, low, high)
+    )(layout.codes, half_place, pieces, *earlier)
 
 
 def assemble_kernel(parts, source, *refs):
-    pieces, out, sem = refs[:parts], refs[parts], refs[parts + 1]
+    pieces, out = refs[:parts], refs[parts]
     size = pieces[0].shape[0]
-    copies = []
     for r in range(parts):
-        place = pl.multiple_of(source[r] * size, size)
-        copies.append(pltpu.make_async_copy(pieces[r], out.at[pl.ds(place, size)], sem.at[r]))
-    for copy in copies:
-        copy.start()
-    for copy in copies:
-        copy.wait()
+        out[pl.ds(pl.multiple_of(source[r] * size, size), size), :] = pieces[r][...]
 
 
 def assemble(source, pieces):
     parts = len(pieces)
     size, width = pieces[0].shape
-    anywhere = pl.BlockSpec(memory_space=pl.ANY)
     return pl.pallas_call(
         functools.partial(assemble_kernel, parts),
         grid_spec=pltpu.PrefetchScalarGridSpec(
             num_scalar_prefetch=1,
             grid=(1,),
-            in_specs=[anywhere] * parts,
-            out_specs=anywhere,
-            scratch_shapes=[pltpu.SemaphoreType.DMA((parts,))],
+            in_specs=[whole((size, width))] * parts,
+            out_specs=whole((parts * size, width)),
         ),
         out_shape=jax.ShapeDtypeStruct((parts * size, width), BF16),
         compiler_params=params(),
@@ -642,62 +657,111 @@
     )(source, *pieces)
 
 
-def turn(values, axis, size, by):
-    return lax.ppermute(values, axis, [(i, (i + by) % size) for i in range(size)])
-
-
-def swap(values, axis, size, bit):
+def swap(values, step):
+    axis, size, bit = step
     return lax.ppermute(values, axis, [(i, i ^ bit) for i in range(size)])
 
 
-def swap_steps(n_expert, n_dp):
-    bits_dp = [1 << b for b in range(n_dp.bit_length() - 1)]
-    bits_expert = [1 << b for b in range(n_expert.bit_length() - 1)]
-    steps = []
-    for n in range(max(len(bits_dp), len(bits_expert))):
-        if n < len(bits_dp):
-            steps.append(("dp", n_dp, bits_dp[n]))
-        if n < len(bits_expert):
-            steps.append(("expert", n_expert, bits_expert[n]))
-    return steps
+def exchange(values):
+    return lax.all_to_all(values, "expert", split_axis=0, concat_axis=0, tiled=True)
+
+
+def turn(values, size, by):
+    return lax.ppermute(values, "expert", [(i, (i + by) % size) for i in range(size)])
+
+
+def bits_of(size):
+    return [1 << b for b in range(size.bit_length() - 1)]
 
 
 def add_low(left, right):
     return (left.astype(F32) + right.astype(F32)).astype(BF16)
 
 
+def tie(*values):
+    return lax.optimization_barrier(values)
+
+
 class SharedSum:
+    streams = 2
+    least = 16
+
     def __init__(self, n_expert, n_dp, rows):
-        steps = swap_steps(n_expert, n_dp)
-        cut = 0
-        while cut < len(steps) and rows >> (cut + 1) >= 32:
-            cut += 1
-        self.halving, self.whole_steps = steps[:cut], steps[cut:]
-        self.blocks = 1 << cut
-        code = jnp.int32(0)
-        for axis, _, bit in self.halving:
-            code = code * 2 + (lax.axis_index(axis) // bit) % 2
-        self.code = code.astype(jnp.int32).reshape(1)
-
-    def __call__(self, keep, send):
-        for n, (axis, size, bit) in enumerate(self.halving):
-            total = add_low(keep, swap(send, axis, size, bit))
-            if n + 1 < len(self.halving):
-                middle = total.shape[1] // 2
-                keep, send = total[:, :middle], total[:, middle:]
-        for axis, size, bit in self.whole_steps:
-            total = add_low(total, swap(total, axis, size, bit))
-        for n, (axis, size, bit) in reversed(list(enumerate(self.halving))):
-            other = swap(total, axis, size, bit)
-            if n > 0:
-                total = jnp.concatenate([total, other], axis=1)
-        return unmix(self.blocks, self.code, total, other)
-
-
-def small_sum(values, n_expert, n_dp):
-    for axis, size, bit in swap_steps(n_expert, n_dp):
-        values = values + swap(values, axis, size, bit)
+        steps = [("dp", n_dp, b) for b in bits_of(n_dp)] + [
+            ("expert", n_expert, b) for b in bits_of(n_expert)
+        ]
+        steps.sort(key=lambda s: (s[2], s[0]))
+        self.steps = steps
+        self.first, one, two, *rest = steps
+        self.pair = ((two, one), (one, two))
+        cut = rows // (2 * self.streams * 4)
+        self.rest = []
+        while rest and cut // 2 >= self.least:
+            self.rest.append(rest.pop(0))
+            cut //= 2
+        self.left = rest
+        self.blocks = rows // cut
+        self.codes = jnp.stack([self.code([self.first, None, *pair, *self.rest]) for pair in self.pair])
+
+    def code(self, steps):
+        total = jnp.int32(0)
+        for step in steps:
+            mine = 0 if step is None else (lax.axis_index(step[0]) // step[2]) % 2
+            total = total * 2 + mine
+        return total.astype(jnp.int32)
+
+    @staticmethod
+    def halve(values, step, axis):
+        middle = values.shape[axis] // 2
+        keep = lax.slice_in_dim(values, 0, middle, axis=axis)
+        send = lax.slice_in_dim(values, middle, 2 * middle, axis=axis)
+        return add_low(keep, swap(send, step))
+
+    @staticmethod
+    def double(values, step, axis):
+        return jnp.concatenate([values, swap(values, step)], axis=axis)
+
+    def reduce_first(self, keep, send):
+        total = add_low(keep, swap(send, self.first))
+        middle = total.shape[1] // 2
+        return [total[:, :middle], total[:, middle:]]
+
+    def reduce_pair(self, parts, n):
+        return [self.halve(part, pair[n], 1) for part, pair in zip(parts, self.pair)]
+
+    def reduce_rest(self, total, n):
+        if n < len(self.rest):
+            return self.halve(total, self.rest[n], 2)
+        return total
+
+    def reduce_left(self, total):
+        for step in self.left:
+            total = add_low(total, swap(total, step))
+        return total
+
+    def gather(self, total):
+        for step in reversed(self.rest):
+            total = self.double(total, step, 2)
+        parts = []
+        for stream, pair in enumerate(self.pair):
+            part = total[:, stream]
+            for step in reversed(pair):
+                part = self.double(part, step, 1)
+            parts.append(part)
+        total = jnp.concatenate(parts, axis=1)
+        other = swap(total, self.first)
+        mine = ((lax.axis_index(self.first[0]) // self.first[2]) % 2).astype(jnp.int32).reshape(1)
+        done = unmix(self, mine, total)
+        return unmix(self, 1 - mine, other, done)
+
+
+def small_sum(values, steps):
+    for step in steps:
+        values = values + swap(values, step)
     return values
+
+
+CHUNKS = 2
 
 
 def per_device(
@@ -726,28 +790,14 @@
     count, width = block_in.shape
     piece = count // n_expert
     row = lambda v: v.reshape(1, -1)
-    e = lax.axis_index("expert")
-    d = lax.axis_index("dp")
+    device = lax.axis_index("dp")
     part = expert_up.shape[2]
-
-    def gathered(own):
-        found = [own]
-        bit = 1
-        own_list = [own]
-        far = [own]
-        bits = [1 << b for b in range(n_dp.bit_length() - 1)]
-        shards = {0: own}
-        for bit in reversed(bits):
-            for k in list(shards):
-                shards[k | bit] = swap(shards[k], "dp", n_dp, bit)
-        return [shards[k] for k in range(n_dp)]
-
-    blocks = block_in.reshape(n_expert, piece, width)
-    arrived = []
-    for r in range(n_expert):
-        block = lax.dynamic_index_in_dim(blocks, (e - r) % n_expert, 0, keepdims=False)
-        arrived.append(block if r == 0 else turn(block, "expert", n_expert, -r))
-    ups, downs = gathered(expert_up[0]), gathered(expert_down[0])
+    dp_steps = [("dp", n_dp, b) for b in bits_of(n_dp)]
+    all_steps = dp_steps + [("expert", n_expert, b) for b in bits_of(n_expert)]
+
+    arrived = exchange(block_in)
+    ups = lax.all_gather(expert_up[0], "dp", axis=0)
+    downs = lax.all_gather(expert_down[0], "dp", axis=0)
 
     position = slot_position[0]
     ends = jnp.cumsum(seq_lengths[0])
@@ -757,91 +807,85 @@
     begin = jnp.max(jnp.where(ends[None, :] <= ids[:, None], ends[None, :], 0), axis=1)
     begin = jnp.where(live, begin, ids).astype(jnp.int32)
     live_col = live.astype(F32).reshape(count, 1)
-    turned = jnp.roll(position.reshape(n_expert, piece), -e, axis=0).reshape(count)
-    pos_row, pos_col = turned.reshape(1, count), turned.reshape(count, 1)
+    in_chunks = position.reshape(n_expert, CHUNKS, -1).transpose(1, 0, 2).reshape(count)
     slot_live = (position < total_live).astype(F32).reshape(n_expert, piece)
-    route_live = lax.all_to_all(slot_live, "expert", split_axis=0, concat_axis=0, tiled=True)
-    route_live = route_live.reshape(count, 1)
+    route_live = exchange(slot_live).reshape(n_expert, piece, 1)
 
     tokens, normed, query, key, value = entry(
-        arrived, pos_row, row(first_gain), row(first_bias), query_weight, row(query_bias),
-        key_weight, value_weight, row(value_bias),
+        [arrived], position.reshape(1, count), row(first_gain), row(first_bias), query_weight,
+        row(query_bias), key_weight, value_weight, row(value_bias),
     )
     mixed, lse = attend(begin.reshape(count, 1), query, key, value)
-    sent = leave(n_expert, mixed, out_weight, row(out_bias), tokens, live_col, pos_col)
-
-    routed = [v if r == 0 else turn(v, "expert", n_expert, r) for r, v in enumerate(sent)]
-    order = [0]
-    for n in range(1, n_expert):
-        order.append((n + 1) // 2 if n % 2 else n_expert - n // 2)
-    chunks = min(CHUNKS, n_expert)
-    per = n_expert // chunks
-    shard_order = jnp.arange(n_dp, dtype=jnp.int32) ^ d
-    up_bias = jnp.take(expert_up_bias[0].reshape(n_dp, 1, part), shard_order, axis=0)
+    sent = leave(
+        CHUNKS, mixed, out_weight, row(out_bias), tokens, live_col, in_chunks.reshape(count, 1)
+    )
+
+    blocks = lambda v: v.reshape(n_expert, piece, width)
+    group = lax.axis_index("expert")
+    ranks = jnp.arange(n_expert, dtype=jnp.int32)
     carried = None
-    returned = [None] * n_expert
+    returned = []
     sums, up_sums = 0.0, 0.0
-    for c in range(chunks):
-        turns = order[c * per : (c + 1) * per]
-        source = jnp.stack([(e - r) % n_expert for r in turns]).astype(jnp.int32)
-        grads, carried, chunk_sums, chunk_up = expert_chunk(
-            c, source, [routed[r] for r in turns], block_cot, route_live, ups, downs, up_bias,
-            row(expert_down_bias[0]), row(second_gain), row(second_bias), carried,
+    for c in range(CHUNKS):
+        (grads,), carried, chunk_sums, chunk_up = expert_chunk(
+            c, 1, ((group + ranks) % n_expert).astype(jnp.int32),
+            exchange(sent[c]), blocks(block_cot), route_live, ups, downs,
+            expert_up_bias[0].reshape(n_dp, 1, part), row(expert_down_bias[0]), row(second_gain),
+            row(second_bias), carried,
         )
         sums, up_sums = sums + chunk_sums, up_sums + chunk_up
-        for r, grad in zip(turns, grads):
-            returned[r] = grad if r == 0 else turn(grad, "expert", n_expert, -r)
+        if returned:
+            returned[-1], carried = tie(returned[-1], carried)
+        returned.append(exchange(grads))
     act, grad_pre, ffn_in, branch, block_out = carried
 
-    down_send, up_send = expert_grads(1, 2, act, grad_pre, ffn_in, branch)
-    down_got, up_got = swap(down_send, "dp", n_dp, 1), swap(up_send, "dp", n_dp, 1)
-    down_keep, up_keep = expert_grads(0, 2, act, grad_pre, ffn_in, branch)
-
-    def reduced(keep, got):
-        bits = [1 << b for b in range(1, n_dp.bit_length() - 1)]
-        for bit in reversed(bits):
-            middle = keep.shape[0] // 2
-            other = swap(add_low(keep[middle:], got[middle:]), "dp", n_dp, bit)
-            keep, got = keep[:middle].astype(F32) + got[:middle].astype(F32), other
-        return keep + got.astype(F32)
-
-    grad_down, grad_up = reduced(down_keep, down_got), reduced(up_keep, up_got)
-    bias_sums = up_sums.reshape(n_dp, part)
-    down_bias_sums = sums[2:3]
-    for bit in [1 << b for b in range(n_dp.bit_length() - 1)]:
-        packed = jnp.concatenate([bias_sums, down_bias_sums.reshape(-1, part)], axis=0)
-        other = swap(packed, "dp", n_dp, bit)
-        bias_sums = bias_sums + other[jnp.array([k ^ bit for k in range(n_dp)])]
-        down_bias_sums = down_bias_sums + other[n_dp:].reshape(1, width)
-    grad_up_bias = bias_sums[0:1]
-    share = width // n_dp
-    grad_down_bias = lax.dynamic_slice_in_dim(down_bias_sums, d * share, share, 1)
-
+    down_terms = shard_grads(act, branch)
+    up_terms = shard_grads(ffn_in, grad_pre)
+    bias_sums = jnp.concatenate([up_sums.reshape(1, -1), sums[2:3]], axis=1)
+    bias_sums = small_sum(bias_sums, dp_steps)
+
+    returned, down_terms, up_terms = tie(returned, down_terms, up_terms)
+    down_sum = lax.psum_scatter(down_terms, "dp", scatter_dimension=0, tiled=True)
+    up_sum = lax.psum_scatter(up_terms, "dp", scatter_dimension=0, tiled=True)
     grad_residual, grad_proj, grad_mixed, out_bias_sum = reenter(
-        returned, pos_row, live_col, out_weight
+        returned, in_chunks.reshape(1, count), live_col, out_weight
     )
     shared = SharedSum(n_expert, n_dp, width)
-    grad_out_weight = shared(*shared_grads(shared.blocks, shared.code, mixed, [grad_proj]))
-    grad_query, grad_key, grad_value = attend_back(
-        begin.reshape(1, count), query, key, value, mixed, grad_mixed, lse
+    token_grads = attend_back(begin.reshape(1, count), query, key, value, mixed, grad_mixed, lse)
+    leaving, token_sums = finish(
+        1, *token_grads, query_weight, key_weight, value_weight,
+        tokens, grad_residual, row(first_gain), position.reshape(count, 1),
     )
-    *leaving, token_sums = finish(
-        n_expert, grad_query, grad_key, grad_value, query_weight, key_weight, value_weight,
-        tokens, grad_residual, row(first_gain), pos_col,
-    )
-    received = [v if r == 0 else turn(v, "expert", n_expert, r) for r, v in enumerate(leaving)]
-    sources = jnp.stack([(e - r) % n_expert for r in range(n_expert)]).astype(jnp.int32)
-    input_grad = assemble(sources, received)
-    grad_query_weight, grad_key_weight, grad_value_weight = (
-        shared(*shared_grads(shared.blocks, shared.code, normed, [g]))
-        for g in (grad_query, grad_key, grad_value)
-    )
+    token_grads, leaving = tie(token_grads, leaving)
+    halves = shared_grads(shared, [normed, mixed], (0, 0, 0, 1), [*token_grads, grad_proj])
     small = jnp.concatenate(
         [token_sums[0:4], out_bias_sum, sums[0:2], jnp.zeros((1, width), F32)], axis=0
     )
-    small = small_sum(small, n_expert, n_dp)
+    small_steps = list(shared.steps)
+
+    def small_step(small):
+        return small_sum(small, [small_steps.pop(0)])
+
+    total = shared.reduce_first(*halves)
+    small = small_step(small)
+    leaving, total, small = tie(leaving, total, small)
+    input_grad = exchange(leaving)
+    total = shared.reduce_pair(total, 0)
+    total = jnp.stack(shared.reduce_pair(total, 1), axis=1)
+    small = small_step(small)
+    total, small, down_sum, input_grad, bias_sums = tie(total, small, down_sum, input_grad, bias_sums)
+    for n in range(len(shared.rest)):
+        total, small = tie(shared.reduce_rest(total, n), small_step(small))
+    total = shared.reduce_left(total)
+    small = small_sum(small, small_steps)
+    total, up_sum, small = tie(total, up_sum, small)
+    share = width // n_dp
+    grad_up_bias = lax.dynamic_slice_in_dim(bias_sums, device * part, part, 1)
+    grad_down_bias = lax.dynamic_slice_in_dim(bias_sums, n_dp * part + device * share, share, 1)
+    grad_down, grad_up = down_sum.astype(F32), up_sum.astype(F32)
+    grad_query_weight, grad_key_weight, grad_value_weight, grad_out_weight = shared.gather(total)
     return (
-        block_out,
+        block_out.reshape(count, width),
         input_grad,
         small[0],
         small[1],
@@ -861,9 +905,6 @@
     )
 
 
-CHUNKS = 4
-
-
 def solution(mesh):
     both = P(("expert", "dp"), None)
     return jax.shard_map(

time: 707 us -> 573 us (0.81)
  starting transfers between devices: 168 us -> 61.1 us
  Pallas kernels: 326 us -> 236 us
  waiting for transfers between devices: 142 us -> 183 us
  blocking collectives: 0 us -> 29.4 us
  other arithmetic: 33.3 us -> 20.7 us
  between operations: 2.26 us -> 14.5 us
    pallas_call x15 -> x7, Pallas kernels: 213 us -> 122 us  [the longest x2 64.6 us: expert_chunk(): pl.pallas_call(functools.partial(expert_kernel, first, parts), grid_spec=...]
    ppermute x57 -> x21, starting transfers between devices: 105 us -> 27.4 us  [swap(): return lax.ppermute(values, axis, [(i, i ^ bit) for i in range(size)])]
    ppermute x28 -> x0, starting transfers between devices: 58 us -> none  [turn(): lax.ppermute(values, axis, [(i, (i + by) % size) for i in range(size)])]
    all_to_all x1 -> x6, waiting for transfers between devices: 0.01 us -> 38.7 us  [exchange(): lax.all_to_all(values, 'expert', split_axis=0, concat_axis=0, tiled=True)]
    ppermute x57 -> x21, waiting for transfers between devices: 105 us -> 142 us  [swap(): return lax.ppermute(values, axis, [(i, i ^ bit) for i in range(size)])]
    ppermute x28 -> x0, waiting for transfers between devices: 36.6 us -> none  [turn(): lax.ppermute(values, axis, [(i, (i + by) % size) for i in range(size)])]
    all_to_all x0 -> x1, blocking collectives: none -> 29.4 us  [exchange(): lax.all_to_all(values, 'expert', split_axis=0, concat_axis=0, tiled=True)]
    all_to_all x1 -> x6, starting transfers between devices: 4.82 us -> 33.6 us  [exchange(): lax.all_to_all(values, 'expert', split_axis=0, concat_axis=0, tiled=True)]
  transfers between devices with their start and end apart: 86 -> 31, of which waited for: 26 -> 14; matrix products, arithmetic and copies ran while one was open for 7% -> 7% of each run, Pallas kernels for 44% -> 41%
where the time goes in v2:
time: 573 us; the launch traced here: 564 us
  Pallas kernels  236 us (41%)
  waiting for transfers between devices  183 us (32%)
  starting transfers between devices  61.1 us (11%)
  blocking collectives  29.4 us (5%)
  other arithmetic  20.7 us (4%)
  local copies, waits for them, and re-layouts  19.5 us (3%)
  between operations  14.5 us (3%)
    ppermute x21, waiting for transfers between devices, swap(): return lax.ppermute(values, axis, [(i, i ^ bit) for i in range(size)])  142 us
    pallas_call x2, Pallas kernels, expert_chunk(): pl.pallas_call(functools.partial(expert_kernel, first, parts), grid_spec=...  64.6 us
    all_to_all x6, waiting for transfers between devices, exchange(): lax.all_to_all(values, 'expert', split_axis=0, concat_axis=0, tiled=True)  38.7 us
    pallas_call x1, Pallas kernels, attend_back(): pl.pallas_call(attend_back_kernel, grid=(pairs,), in_specs=[whole((1, cou...  36.4 us
    all_to_all x6, starting transfers between devices, exchange(): lax.all_to_all(values, 'expert', split_axis=0, concat_axis=0, tiled=True)  33.6 us
    all_to_all x1, blocking collectives, exchange(): lax.all_to_all(values, 'expert', split_axis=0, concat_axis=0, tiled=True)  29.4 us
    ppermute x21, starting transfers between devices, swap(): return lax.ppermute(values, axis, [(i, i ^ bit) for i in range(size)])  27.4 us
    pallas_call x2, Pallas kernels, shard_grads(): pl.pallas_call(shard_grads_kernel, grid=(shards,), in_specs=[spec(left),...  26.2 us
  transfers between devices with their start and end apart: 31, of which 14 were waited for; matrix products, arithmetic and copies ran while one was open for 7% of the time, Pallas kernels for 41%

profile of v2, /device:TPU:9, one launch (start us, length us, event | category | flops | bytes accessed | tf_op | source)
XLA Modules:
  0.0 563.6 jit_solution(18200005748045137751)
XLA Ops:
  8.7 5.7 %all-to-all-start = ((bf16[8,128,1024]{2,1,0:T(8,128)(2,1)}), bf16[8,128,1024]{2,1,0:T(8,128)(2,1)S(1)}, u32[]{:S(2)}, u32[]{:S(2)}) async-start(bf16[8,128,1024]{2,1,0:T(8,128)(2,1)} %bitcast.3), calls=%async_computation | async-start | bytes 4194304 | tf_op jit(solution)/shard_map/all_to_all | solution.py:666
  18.0 1.5 fusion.2.live_col.refs_3_
  20.8 1.5 iota_select_fusion.start_col
  22.3 38.6 %all-to-all-done = bf16[8,128,1024]{2,1,0:T(8,128)(2,1)S(1)} async-done(((bf16[8,128,1024]{2,1,0:T(8,128)(2,1)}), bf16[8,128,1024]{2,1,0:T(8,128)(2,1)S(1)}, u32[]{:S(2)}, u32[]{:S(2)}) %all-to-all-start) | async-done | bytes 2097184 | tf_op jit(solution)/shard_map/all_to_all | solution.py:666
  60.9 5.5 all-to-all-start.2
  66.5 15.4 %entry.1 = (bf16[1024,1024]{1,0:T(8,128)(2,1)}, bf16[1024,1024]{1,0:T(8,128)(2,1)}, bf16[1024,1024]{1,0:T(8,128)(2,1)}, bf16[1024,1024]{1,0:T(8,128)(2,1)}, bf16[1024,1024]{1,0:T(8,128)(2,1)}) custom-call(bf16[1024,1024]{1,0:T(8,128)(2,1)} %bitcast.61, s32[1,1024]{1,0:T(1,128)} %refs_1_.1, f32[1,1024]{1,0:T(1,128)} %bitcast.97, f32[1,1024]{1,0:T(1,128)} %bitcast.89, ...), custom_call_target="tpu_custom_call" | custom-call | flops 8589934592 | bytes 18874368 | tf_op jit(solution)/shard_map/entry/pallas_call | solution.py:98
  81.9 24.7 %attend.1 = (bf16[1024,1024]{1,0:T(8,128)(2,1)}, f32[8,8,1024]{2,1,0:T(8,128)}) custom-call(s32[1024,1]{1,0:T(8,128)} %iota_select_fusion.start_col, bf16[1024,1024]{1,0:T(8,128)(2,1)} %get-tuple-element.91.q_ref, bf16[1024,1024]{1,0:T(8,128)(2,1)} %get-tuple-element.92.k_ref, bf16[1024,1024]{1,0:T(8,128)(2,1)} %get-tuple-element.93.v_ref), custom_call_target="tpu_custom_call" | custom-call | flops 8589934592 | bytes 8388608 | tf_op jit(solution)/shard_map/attend/pallas_call | solution.py:166
  106.6 9.5 %leave.1 = (bf16[512,1024]{1,0:T(8,128)(2,1)}, bf16[512,1024]{1,0:T(8,128)(2,1)}) custom-call(bf16[1024,1024]{1,0:T(8,128)(2,1)} %get-tuple-element.94.mixed.o_ref.refs_1_, bf16[1024,1024]{1,0:T(8,128)(2,1)} %refs_4_.3, f32[1,1024]{1,0:T(1,128)} %bitcast.92, bf16[1024,1024]{1,0:T(8,128)(2,1)} %get-tuple-element.95.tokens, f32[1024,1]{1,0:T(8,128)} %fusion.2.live_col.refs_3_, ...), custom_call_target="tpu_custom_call" | custom-call | flops 4294967296 | bytes 8388608 | tf_op jit(solution)/shard_map/leave/pallas_call | solution.py:203
  116.1 29.4 %all_to_all.75 = bf16[8,64,1024]{2,1,0:T(8,128)(2,1)} all-to-all(bf16[8,64,1024]{2,1,0:T(8,128)(2,1)} %bitcast.68), channel_id=1, replica_groups=mesh['expert'=8,'dp'=4] {'expert'}, dimensions={0} | all-to-all | bytes 2097152 | tf_op jit(solution)/shard_map/all_to_all | solution.py:666
  145.6 5.5 all-to-all-start.4
  152.6 32.4 %expert_chunk.2 = (bf16[512,1024]{1,0:T(8,128)(2,1)}, bf16[4,1024,1024]{2,1,0:T(8,128)(2,1)}, bf16[4,1024,1024]{2,1,0:T(8,128)(2,1)}, bf16[1024,1024]{1,0:T(8,12...) custom-call(s32[8]{0:T(128)} %and_select_fusion.refs_0_, ...), custom_call_target="tpu_custom_call" | custom-call | flops 17179869184 | bytes 16777216 | tf_op jit(solution)/shard_map/expert_chunk/pallas_call | solution.py:480
  185.1 5.6 all-to-all-start.3
  190.7 32.1 %expert_chunk.3 = (bf16[512,1024]{1,0:T(8,128)(2,1)}, bf16[4,1024,1024]{2,1,0:T(8,128)(2,1)}, bf16[4,1024,1024]{2,1,0:T(8,128)(2,1)}, bf16[1024,1024]{1,0:T(8,12...) custom-call(s32[8]{0:T(128)} %and_select_fusion.refs_0_, ...), custom_call_target="tpu_custom_call", output_to_operand_aliasing={{1}: (10, {}), {2}: (11, {}), {3}: (12, {}), {4}: (13, {}),... | custom-call | flops 17179869184 | bytes 16777216 | tf_op jit(solution)/shard_map/expert_chunk/pallas_call | solution.py:480
  222.8 5.5 all-to-all-start.5
  228.3 13.1 %shard_grads.3 = bf16[4,1024,1024]{2,1,0:T(8,128)(2,1)} custom-call(bf16[1024,1024]{1,0:T(8,128)(2,1)} %get-tuple-element.114.left, bf16[4,1024,1024]{2,1,0:T(8,128)(2,1)} %get-tuple-element.115.right), custom_call_target="tpu_custom_call" | custom-call | flops 8589934592 | bytes 25165824 | tf_op jit(solution)/shard_map/shard_grads/pallas_call | solution.py:544
  241.4 13.0 %shard_grads.2 = bf16[4,1024,1024]{2,1,0:T(8,128)(2,1)} custom-call(bf16[4,1024,1024]{2,1,0:T(8,128)(2,1)} %get-tuple-element.112.left, bf16[1024,1024]{1,0:T(8,128)(2,1)} %get-tuple-element.113.right), custom_call_target="tpu_custom_call" | custom-call | flops 8589934592 | bytes 25165824 | tf_op jit(solution)/shard_map/shard_grads/pallas_call | solution.py:544
  259.6 9.4 %reenter.1 = (bf16[1024,1024]{1,0:T(8,128)(2,1)}, bf16[1024,1024]{1,0:T(8,128)(2,1)}, bf16[1024,1024]{1,0:T(8,128)(2,1)}, f32[1,1024]{1,0:T(1,128)}) custom-call(bf16[512,1024]{1,0:T(8,128)(2,1)} %bitcast.62, bf16[512,1024]{1,0:T(8,128)(2,1)} %bitcast.63, s32[1,1024]{1,0:T(1,128)} %reshape_reshape.7.refs_2_, f32[1024,1]{1,0:T(8,128)} %fusion.2.live_col.refs_3_, ...), custom_call_target="tpu_custom_call" | custom-call | flops 4294967296 | bytes 10485760 | tf_op jit(solution)/shard_map/reenter/pallas_call | solution.py:248
  268.9 36.4 %attend_back.1 = (bf16[1024,1024]{1,0:T(8,128)(2,1)}, bf16[1024,1024]{1,0:T(8,128)(2,1)}, bf16[1024,1024]{1,0:T(8,128)(2,1)}) custom-call(s32[1,1024]{1,0:T(1,128)} %compare_select_fusion.start_row, bf16[1024,1024]{1,0:T(8,128)(2,1)} %get-tuple-element.91.q_ref, bf16[1024,1024]{1,0:T(8,128)(2,1)} %get-tuple-element.92.k_ref, ...), custom_call_target="tpu_custom_call" | custom-call | flops 21474836480 | bytes 16777216 | tf_op jit(solution)/shard_map/attend_back/pallas_call | solution.py:319
  305.4 18.6 %finish.1 = (bf16[1024,1024]{1,0:T(8,128)(2,1)}, f32[8,1024]{1,0:T(8,128)}) custom-call(bf16[1024,1024]{1,0:T(8,128)(2,1)} %get-tuple-element.127.dq.refs_2_, bf16[1024,1024]{1,0:T(8,128)(2,1)} %get-tuple-element.128.dk.refs_3_, bf16[1024,1024]{1,0:T(8,128)(2,1)} %get-tuple-element.129.dv.refs_4_, bf16[1024,1024]{1,0:T(8,128)(2,1)} %wq.1, ...), custom_call_target="tpu_custom_call" | custom-call | flops 8589934592 | bytes 20971520 | tf_op jit(solution)/shard_map/finish/pallas_call | solution.py:368
  324.1 17.6 %shared_grads.1 = (bf16[4,512,1024]{2,1,0:T(8,128)(2,1)}, bf16[4,512,1024]{2,1,0:T(8,128)(2,1)}) custom-call(s32[2]{0:T(128)} %pad_add_fusion.codes, bf16[1024,1024]{1,0:T(8,128)(2,1)} %get-tuple-element.126.refs_0_, bf16[1024,1024]{1,0:T(8,128)(2,1)} %get-tuple-element.94.mixed.o_ref.refs_1_, bf16[1024,1024]{1,0:T(8,128)(2,1)} %get-tuple-element.127.dq.refs_2_, ...), custom_call_target="tpu_custom_call" | custom-call | flops 8589934592 | bytes 25165824 | tf_op jit(solution)/shard_map/shared_grads/pallas_call | solution.py:585
  341.6 2.6 collective-permute-start
  344.5 4.2 collective-permute-done.1
  348.7 4.1 collective-permute-done
  352.8 4.4 add_convert_fusion
  357.2 2.6 fusion.7
  359.8 5.9 %all-to-all-start.6 = ((bf16[8,128,1024]{2,1,0:T(8,128)(2,1)}), bf16[8,128,1024]{2,1,0:T(8,128)(2,1)S(1)}, u32[]{:S(2)}, u32[]{:S(2)}) async-start(bf16[8,128,1024]{2,1,0:T(8,128)(2,1)} %bitcast.60), calls=%async_computation.7 | async-start | bytes 4194304 | tf_op jit(solution)/shard_map/all_to_all | solution.py:666
  365.7 1.5 slice.88
  369.8 1.5 collective-permute-start.7
  371.6 42.9 %collective-permute-done.2 = bf16[4,128,1024]{2,1,0:T(8,128)(2,1)S(1)} collective-permute-done((bf16[4,128,1024]{2,1,0:T(8,128)(2,1)S(1)}, bf16[4,128,1024]{2,1,0:T(8,128)(2,1)S(1)}, u32[]{:S(2)}, u32[]{:S(2)}) %collective-permute-start.2) | collective-permute-done | bytes 1048608 | tf_op jit(solution)/shard_map/ppermute | solution.py:662
  418.4 20.1 %collective-permute-done.8 = f32[1,5120]{1,0:T(1,128)S(1)} collective-permute-done((f32[1,5120]{1,0:T(1,128)S(1)}, f32[1,5120]{1,0:T(1,128)S(1)}, u32[]{:S(2)}, u32[]{:S(2)}) %collective-permute-start.8) | collective-permute-done | bytes 20512 | tf_op jit(solution)/shard_map/ppermute | solution.py:662
  439.6 2.7 collective-permute-done.10
  442.3 9.2 %collective-permute-done.9 = bf16[4,2,32,1024]{3,2,0,1:T(8,128)(2,1)S(1)} collective-permute-done((bf16[4,2,32,1024]{3,2,0,1:T(8,128)(2,1)S(1)}, bf16[4,2,32,1024]{3,2,0,1:T(8,128)(2,1)S(1)}, u32[]{:S(2)}, u32[]{:S(2)}) %collective-permute-start.9) | collective-permute-done | bytes 524320 | tf_op jit(solution)/shard_map/ppermute | solution.py:662
  451.7 2.2 collective-permute-start.11
  454.2 5.0 collective-permute-done.12
  459.2 6.3 %collective-permute-done.11 = bf16[4,2,16,1024]{3,2,0,1:T(8,128)(2,1)S(1)} collective-permute-done((bf16[4,2,16,1024]{3,2,0,1:T(8,128)(2,1)S(1)}, bf16[4,2,16,1024]{3,2,0,1:T(8,128)(2,1)S(1)}, u32[]{:S(2)}, u32[]{:S(2)}) %collective-permute-start.11) | collective-permute-done | bytes 262176 | tf_op jit(solution)/shard_map/ppermute | solution.py:662
  465.6 3.2 collective-permute-start.13
  470.1 2.4 collective-permute-start.14
  472.5 7.1 %collective-permute-done.14 = bf16[4,2,16,1024]{3,2,0,1:T(8,128)(2,1)S(1)} collective-permute-done((bf16[4,2,16,1024]{3,2,0,1:T(8,128)(2,1)S(1)}, bf16[4,2,16,1024]{3,2,0,1:T(8,128)(2,1)S(1)}, u32[]{:S(2)}, u32[]{:S(2)}) %collective-permute-start.14) | collective-permute-done | bytes 262176 | tf_op jit(solution)/shard_map/ppermute | solution.py:662
  479.7 3.1 collective-permute-start.15
  482.8 10.0 %collective-permute-done.15 = bf16[4,2,32,1024]{3,2,0,1:T(8,128)(2,1)S(1)} collective-permute-done((bf16[4,2,32,1024]{3,2,0,1:T(8,128)(2,1)S(1)}, bf16[4,2,32,1024]{3,2,0,1:T(8,128)(2,1)S(1)}, u32[]{:S(2)}, u32[]{:S(2)}) %collective-permute-start.15) | collective-permute-done | bytes 524320 | tf_op jit(solution)/shard_map/ppermute | solution.py:662
  493.7 9.8 %collective-permute-done.16 = bf16[4,64,1024]{2,1,0:T(8,128)(2,1)S(1)} collective-permute-done((bf16[4,64,1024]{2,1,0:T(8,128)(2,1)S(1)}, bf16[4,64,1024]{2,1,0:T(8,128)(2,1)S(1)}, u32[]{:S(2)}, u32[]{:S(2)}) %collective-permute-start.16) | collective-permute-done | bytes 524320 | tf_op jit(solution)/shard_map/ppermute | solution.py:662
  506.5 19.3 %collective-permute-done.17 = bf16[4,128,1024]{2,1,0:T(8,128)(2,1)S(1)} collective-permute-done((bf16[4,128,1024]{2,1,0:T(8,128)(2,1)S(1)}, bf16[4,128,1024]{2,1,0:T(8,128)(2,1)S(1)}, u32[]{:S(2)}, u32[]{:S(2)}) %collective-permute-start.17) | collective-permute-done | bytes 1048608 | tf_op jit(solution)/shard_map/ppermute | solution.py:662
  529.6 4.1 collective-permute-start.20
  533.7 4.2 convert_element_type.118
  539.0 2.5 convert_element_type.117
  542.1 6.7 %unmix.2 = (f32[1024,1024]{1,0:T(8,128)}, f32[1024,1024]{1,0:T(8,128)}, f32[1024,1024]{1,0:T(8,128)}, f32[1024,1024]{1,0:T(8,128)}) custom-call(s32[2]{0:T(128)} %pad_add_fusion.codes, s32[1]{0:T(128)} %bitcast.38.half_place, bf16[4,512,1024]{2,1,0:T(8,128)(2,1)} %constant_dynamic-update-slice_fusion.3.refs_0_), custom_call_target="tpu_custom_call" | custom-call | flops 2097152 | bytes 12582912 | tf_op jit(solution)/shard_map/unmix/pallas_call | solution.py:618
  548.9 6.7 %unmix.3 = (f32[1024,1024]{1,0:T(8,128)}, f32[1024,1024]{1,0:T(8,128)}, f32[1024,1024]{1,0:T(8,128)}, f32[1024,1024]{1,0:T(8,128)}) custom-call(s32[2]{0:T(128)} %pad_add_fusion.codes, s32[1]{0:T(128)S(6)} %sub.24.half_place, ...), custom_call_target="tpu_custom_call", output_to_operand_aliasing={{0}: (3, {}), {1}: (4, {}), {2}: (5, {}), {3}: (6, {})} | custom-call | flops 2097152 | bytes 12582912 | tf_op jit(solution)/shard_map/unmix/pallas_call | solution.py:618
  555.6 1.3 copy.89
  (133 shorter events, 32.3 us)
Async XLA Ops:
  7.2 145.4 %all-gather.3.cloned.1.call-start = ((), (), s32[]{:S(2)}) async-start(), calls=%async_computation.9 | async-start | bytes 10485760 | tf_op jit(solution)/shard_map/all_gather | solution.py:799
  7.9 144.7 %all-gather.5.cloned.1.call-start = ((), (), s32[]{:S(2)}) async-start(), calls=%async_computation.10 | async-start | bytes 10485760 | tf_op jit(solution)/shard_map/all_gather | solution.py:800
  8.7 5.7 %copy-start.15 = (s32[1,16]{1,0:T(1,128)S(1)}, s32[1,16]{1,0:T(1,128)}, u32[]{:S(2)}) copy-start(s32[1,16]{1,0:T(1,128)} %param.20) | copy-start | bytes 196
  8.7 7.3 %copy-start.7 = (s32[1,1024]{1,0:T(1,128)S(1)}, s32[1,1024]{1,0:T(1,128)}, u32[]{:S(2)}) copy-start(s32[1,1024]{1,0:T(1,128)} %refs_1_.1) | copy-start | bytes 12292
  8.7 52.2 %all-to-all-start = ((bf16[8,128,1024]{2,1,0:T(8,128)(2,1)}), bf16[8,128,1024]{2,1,0:T(8,128)(2,1)S(1)}, u32[]{:S(2)}, u32[]{:S(2)}) async-start(bf16[8,128,1024]{2,1,0:T(8,128)(2,1)} %bitcast.3), calls=%async_computation | async-start | bytes 4194304 | tf_op jit(solution)/shard_map/all_to_all | solution.py:666
  60.9 5.5 copy-start.3
  60.9 55.2 %all-to-all-start.2 = ((f32[8,1,128]{2,1,0:T(1,128)}), f32[8,1,128]{2,1,0:T(1,128)S(1)}, u32[]{:S(2)}, u32[]{:S(2)}) async-start(f32[8,1,128]{2,1,0:T(1,128)} %fusion.3), calls=%async_computation.2 | async-start | bytes 8192 | tf_op jit(solution)/shard_map/all_to_all | solution.py:666
  145.6 39.5 %all-to-all-start.4 = ((bf16[8,64,1024]{2,1,0:T(8,128)(2,1)}), bf16[8,64,1024]{2,1,0:T(8,128)(2,1)S(1)}, u32[]{:S(2)}, u32[]{:S(2)}) async-start(bf16[8,64,1024]{2,1,0:T(8,128)(2,1)} %bitcast.22), calls=%async_computation.4 | async-start | bytes 2097152 | tf_op jit(solution)/shard_map/all_to_all | solution.py:666
  185.0 5.6 copy-start.6
  185.1 37.8 %all-to-all-start.3 = ((bf16[8,64,1024]{2,1,0:T(8,128)(2,1)}), bf16[8,64,1024]{2,1,0:T(8,128)(2,1)S(1)}, u32[]{:S(2)}, u32[]{:S(2)}) async-start(bf16[8,64,1024]{2,1,0:T(8,128)(2,1)} %bitcast.67), calls=%async_computation.3 | async-start | bytes 2097152 | tf_op jit(solution)/shard_map/all_to_all | solution.py:666
  222.8 18.6 %copy-start.4 = (bf16[8,64,1024]{2,1,0:T(8,128)(2,1)}, bf16[8,64,1024]{2,1,0:T(8,128)(2,1)S(1)}, u32[]{:S(2)}) copy-start(bf16[8,64,1024]{2,1,0:T(8,128)(2,1)S(1)} %all-to-all-done.3) | copy-start | bytes 3145732
  222.8 31.6 %all-to-all-start.5 = ((bf16[8,64,1024]{2,1,0:T(8,128)(2,1)}), bf16[8,64,1024]{2,1,0:T(8,128)(2,1)S(1)}, u32[]{:S(2)}, u32[]{:S(2)}) async-start(bf16[8,64,1024]{2,1,0:T(8,128)(2,1)} %bitcast.65), calls=%async_computation.5 | async-start | bytes 2097152 | tf_op jit(solution)/shard_map/all_to_all | solution.py:666
  228.3 210.8 %reduce-scatter.3.cloned.1.call-start = ((), (), s32[]{:S(2)}) async-start(), calls=%async_computation.11 | async-start | bytes 10485760 | tf_op jit(solution)/shard_map/reduce_scatter | solution.py:848
  254.5 1.0 copy-start.5
  255.4 1.2 copy-start.8
  255.4 214.6 %reduce-scatter.5.cloned.1.call-start = ((), (), s32[]{:S(2)}) async-start(), calls=%async_computation.12 | async-start | bytes 10485760 | tf_op jit(solution)/shard_map/reduce_scatter | solution.py:849
  324.0 20.3 %copy-start.9 = (f32[8,1024]{1,0:T(8,128)S(1)}, f32[8,1024]{1,0:T(8,128)}, u32[]{:S(2)}) copy-start(f32[8,1024]{1,0:T(8,128)} %get-tuple-element.135) | copy-start | bytes 98308
  324.0 20.3 %copy-start.10 = (f32[8,1024]{1,0:T(8,128)S(1)}, f32[8,1024]{1,0:T(8,128)}, u32[]{:S(2)}) copy-start(f32[8,1024]{1,0:T(8,128)} %get-tuple-element.136) | copy-start | bytes 98308
  324.0 20.3 %copy-start.14 = (f32[8,1024]{1,0:T(8,128)S(1)}, f32[8,1024]{1,0:T(8,128)}, u32[]{:S(2)}) copy-start(f32[8,1024]{1,0:T(8,128)} %get-tuple-element.133) | copy-start | bytes 98308
  324.1 20.3 %copy-start.13 = (f32[1,1024]{1,0:T(1,128)S(1)}, f32[1,1024]{1,0:T(1,128)}, u32[]{:S(2)}) copy-start(f32[1,1024]{1,0:T(1,128)} %get-tuple-element.134) | copy-start | bytes 12292
  341.6 11.2 %collective-permute-start = (bf16[4,512,1024]{2,1,0:T(8,128)(2,1)}, bf16[4,512,1024]{2,1,0:T(8,128)(2,1)S(1)}, u32[]{:S(2)}, u32[]{:S(2)}) collective-permute-start(bf16[4,512,1024]{2,1,0:T(8,128)(2,1)} %get-tuple-element.132), channel_id=1, source_target_pairs={{0,1},{1,0},{2,3},{3,2},{4,5},{5,4},{6,7},{7,6},{8,9},{9,8},{10,11... | collective-permute-start | bytes 12582920 | tf_op jit(solution)/shard_map/ppermute | solution.py:662
  344.4 4.2 collective-permute-start.1
  359.8 10.0 %copy-start.11 = (f32[4,1,1024]{2,1,0:T(1,128)S(1)}, f32[4,1,1024]{2,1,0:T(1,128)}, u32[]{:S(2)}) copy-start(f32[4,1,1024]{2,1,0:T(1,128)} %get-tuple-element.142) | copy-start | bytes 49156
  359.8 10.0 %copy-start.12 = (f32[4,1,1024]{2,1,0:T(1,128)S(1)}, f32[4,1,1024]{2,1,0:T(1,128)}, u32[]{:S(2)}) copy-start(f32[4,1,1024]{2,1,0:T(1,128)} %get-tuple-element.143) | copy-start | bytes 49156
  359.8 79.3 %all-to-all-start.6 = ((bf16[8,128,1024]{2,1,0:T(8,128)(2,1)}), bf16[8,128,1024]{2,1,0:T(8,128)(2,1)S(1)}, u32[]{:S(2)}, u32[]{:S(2)}) async-start(bf16[8,128,1024]{2,1,0:T(8,128)(2,1)} %bitcast.60), calls=%async_computation.7 | async-start | bytes 4194304 | tf_op jit(solution)/shard_map/all_to_all | solution.py:666
  365.6 2.8 copy-start
  365.7 48.9 %copy-start.1 = (bf16[4,256,1024]{2,1,0:T(8,128)(2,1)S(1)}, bf16[4,256,1024]{2,1,0:T(8,128)(2,1)}, u32[]{:S(2)}) copy-start(bf16[4,256,1024]{2,1,0:T(8,128)(2,1)} %get-tuple-element.137) | copy-start | bytes 6291460
  367.2 47.4 %collective-permute-start.2 = (bf16[4,128,1024]{2,1,0:T(8,128)(2,1)S(1)}, bf16[4,128,1024]{2,1,0:T(8,128)(2,1)S(1)}, u32[]{:S(2)}, u32[]{:S(2)}) collective-permute-start(bf16[4,128,1024]{2,1,0:T(8,128)(2,1)S(1)} %slice.88), channel_id=1, source_target_pairs={{0,2},{1,3},{2,0},{3,1},{4,6},{5,7},{6,4},{7,5},{8,10},{9,11},{10,... | collective-permute-start | bytes 3145736 | tf_op jit(solution)/shard_map/ppermute | solution.py:662
  368.5 47.8 %collective-permute-start.4 = (bf16[4,128,1024]{2,1,0:T(8,128)(2,1)S(1)}, bf16[4,128,1024]{2,1,0:T(8,128)(2,1)S(1)}, u32[]{:S(2)}, u32[]{:S(2)}) collective-permute-start(bf16[4,128,1024]{2,1,0:T(8,128)(2,1)S(1)} %slice.92), channel_id=1, source_target_pairs={{0,4},{4,0},{8,12},{12,8},{16,20},{20,16},{24,28},{28,24},{1,5},{5... | collective-permute-start | bytes 3145736 | tf_op jit(solution)/shard_map/ppermute | solution.py:662
  369.8 48.1 %collective-permute-start.7 = (f32[1,5120]{1,0:T(1,128)S(1)}, f32[1,5120]{1,0:T(1,128)S(1)}, u32[]{:S(2)}, u32[]{:S(2)}) collective-permute-start(f32[1,5120]{1,0:T(1,128)S(1)} %pad_maximum_fusion.4), channel_id=1, source_target_pairs={{0,1},{1,0},{2,3},{3,2},{4,5},{5,4},{6,7},{7,6},{8,9},{9,8},{10,11... | collective-permute-start | bytes 61448 | tf_op jit(solution)/shard_map/ppermute | solution.py:662
  371.3 67.2 %collective-permute-start.6 = (f32[8,1024]{1,0:T(8,128)S(1)}, f32[8,1024]{1,0:T(8,128)S(1)}, u32[]{:S(2)}, u32[]{:S(2)}) collective-permute-start(f32[8,1024]{1,0:T(8,128)S(1)} %fusion.5), channel_id=1, source_target_pairs={{0,4},{4,0},{8,12},{12,8},{16,20},{20,16},{24,28},{28,24},{1,5},{5... | collective-permute-start | bytes 98312 | tf_op jit(solution)/shard_map/ppermute | solution.py:662
  415.0 23.5 %collective-permute-start.3 = (bf16[4,64,1024]{2,1,0:T(8,128)(2,1)S(1)}, bf16[4,64,1024]{2,1,0:T(8,128)(2,1)S(1)}, u32[]{:S(2)}, u32[]{:S(2)}) collective-permute-start(bf16[4,64,1024]{2,1,0:T(8,128)(2,1)S(1)} %slice.114), channel_id=1, source_target_pairs={{0,4},{4,0},{8,12},{12,8},{16,20},{20,16},{24,28},{28,24},{1,5},{5... | collective-permute-start | bytes 1572872 | tf_op jit(solution)/shard_map/ppermute | solution.py:662
  416.7 22.0 %collective-permute-start.5 = (bf16[4,64,1024]{2,1,0:T(8,128)(2,1)S(1)}, bf16[4,64,1024]{2,1,0:T(8,128)(2,1)S(1)}, u32[]{:S(2)}, u32[]{:S(2)}) collective-permute-start(bf16[4,64,1024]{2,1,0:T(8,128)(2,1)S(1)} %slice.116), channel_id=1, source_target_pairs={{0,2},{1,3},{2,0},{3,1},{4,6},{5,7},{6,4},{7,5},{8,10},{9,11},{10,... | collective-permute-start | bytes 1572872 | tf_op jit(solution)/shard_map/ppermute | solution.py:662
  418.0 20.5 %collective-permute-start.8 = (f32[1,5120]{1,0:T(1,128)S(1)}, f32[1,5120]{1,0:T(1,128)S(1)}, u32[]{:S(2)}, u32[]{:S(2)}) collective-permute-start(f32[1,5120]{1,0:T(1,128)S(1)} %fusion.6), channel_id=1, source_target_pairs={{0,2},{1,3},{2,0},{3,1},{4,6},{5,7},{6,4},{7,5},{8,10},{9,11},{10,... | collective-permute-start | bytes 61448 | tf_op jit(solution)/shard_map/ppermute | solution.py:662
  439.2 12.3 %collective-permute-start.9 = (bf16[4,2,32,1024]{3,2,0,1:T(8,128)(2,1)S(1)}, bf16[4,2,32,1024]{3,2,0,1:T(8,128)(2,1)S(1)}, u32[]{:S(2)}, u32[]{:S(2)}) collective-permute-start(bf16[4,2,32,1024]{3,2,0,1:T(8,128)(2,1)S(1)} %slice.97), channel_id=1, source_target_pairs={{0,8},{4,12},{8,0},{12,4},{16,24},{20,28},{24,16},{28,20},{1,9},{5... | collective-permute-start | bytes 1572872 | tf_op jit(solution)/shard_map/ppermute | solution.py:662
  439.5 2.8 collective-permute-start.10
  451.7 13.8 %collective-permute-start.11 = (bf16[4,2,16,1024]{3,2,0,1:T(8,128)(2,1)S(1)}, bf16[4,2,16,1024]{3,2,0,1:T(8,128)(2,1)S(1)}, u32[]{:S(2)}, u32[]{:S(2)}) collective-permute-start(bf16[4,2,16,1024]{3,2,0,1:T(8,128)(2,1)S(1)} %slice.99), channel_id=1, source_target_pairs={{0,16},{4,20},{8,24},{12,28},{16,0},{20,4},{24,8},{28,12},{1,17},{... | collective-permute-start | bytes 786440 | tf_op jit(solution)/shard_map/ppermute | solution.py:662
  453.9 5.3 collective-permute-start.12
  465.6 4.5 collective-permute-start.13
  470.1 9.6 %collective-permute-start.14 = (bf16[4,2,16,1024]{3,2,0,1:T(8,128)(2,1)S(1)}, bf16[4,2,16,1024]{3,2,0,1:T(8,128)(2,1)S(1)}, u32[]{:S(2)}, u32[]{:S(2)}) collective-permute-start(bf16[4,2,16,1024]{3,2,0,1:T(8,128)(2,1)S(1)} %add_convert_fusion.6), channel_id=1, source_target_pairs={{0,16},{4,20},{8,24},{12,28},{16,0},{20,4},{24,8},{28,12},{1,17},{... | collective-permute-start | bytes 786440 | tf_op jit(solution)/shard_map/ppermute | solution.py:662
  479.7 13.1 %collective-permute-start.15 = (bf16[4,2,32,1024]{3,2,0,1:T(8,128)(2,1)S(1)}, bf16[4,2,32,1024]{3,2,0,1:T(8,128)(2,1)S(1)}, u32[]{:S(2)}, u32[]{:S(2)}) collective-permute-start(bf16[4,2,32,1024]{3,2,0,1:T(8,128)(2,1)S(1)} %pad_maximum_fusion.3), channel_id=1, source_target_pairs={{0,8},{4,12},{8,0},{12,4},{16,24},{20,28},{24,16},{28,20},{1,9},{5... | collective-permute-start | bytes 1572872 | tf_op jit(solution)/shard_map/ppermute | solution.py:662
  492.9 10.6 %collective-permute-start.16 = (bf16[4,64,1024]{2,1,0:T(8,128)(2,1)S(1)}, bf16[4,64,1024]{2,1,0:T(8,128)(2,1)S(1)}, u32[]{:S(2)}, u32[]{:S(2)}) collective-permute-start(bf16[4,64,1024]{2,1,0:T(8,128)(2,1)S(1)} %get-tuple-element.168), channel_id=1, source_target_pairs={{0,4},{4,0},{8,12},{12,8},{16,20},{20,16},{24,28},{28,24},{1,5},{5... | collective-permute-start | bytes 1572872 | tf_op jit(solution)/shard_map/ppermute | solution.py:662
  493.0 11.1 %collective-permute-start.18 = (bf16[4,64,1024]{2,1,0:T(8,128)(2,1)S(1)}, bf16[4,64,1024]{2,1,0:T(8,128)(2,1)S(1)}, u32[]{:S(2)}, u32[]{:S(2)}) collective-permute-start(bf16[4,64,1024]{2,1,0:T(8,128)(2,1)S(1)} %get-tuple-element.167), channel_id=1, source_target_pairs={{0,2},{1,3},{2,0},{3,1},{4,6},{5,7},{6,4},{7,5},{8,10},{9,11},{10,... | collective-permute-start | bytes 1572872 | tf_op jit(solution)/shard_map/ppermute | solution.py:662
  503.6 22.2 %collective-permute-start.17 = (bf16[4,128,1024]{2,1,0:T(8,128)(2,1)S(1)}, bf16[4,128,1024]{2,1,0:T(8,128)(2,1)S(1)}, u32[]{:S(2)}, u32[]{:S(2)}) collective-permute-start(bf16[4,128,1024]{2,1,0:T(8,128)(2,1)S(1)} %pad_maximum_fusion.1), channel_id=1, source_target_pairs={{0,2},{1,3},{2,0},{3,1},{4,6},{5,7},{6,4},{7,5},{8,10},{9,11},{10,... | collective-permute-start | bytes 3145736 | tf_op jit(solution)/shard_map/ppermute | solution.py:662
  504.2 24.3 %collective-permute-start.19 = (bf16[4,128,1024]{2,1,0:T(8,128)(2,1)S(1)}, bf16[4,128,1024]{2,1,0:T(8,128)(2,1)S(1)}, u32[]{:S(2)}, u32[]{:S(2)}) collective-permute-start(bf16[4,128,1024]{2,1,0:T(8,128)(2,1)S(1)} %pad_maximum_fusion.2), channel_id=1, source_target_pairs={{0,4},{4,0},{8,12},{12,8},{16,20},{20,16},{24,28},{28,24},{1,5},{5... | collective-permute-start | bytes 3145736 | tf_op jit(solution)/shard_map/ppermute | solution.py:662
  529.6 19.3 %collective-permute-start.20 = (bf16[4,512,1024]{2,1,0:T(8,128)(2,1)}, bf16[4,512,1024]{2,1,0:T(8,128)(2,1)}, u32[]{:S(2)}, u32[]{:S(2)}) collective-permute-start(bf16[4,512,1024]{2,1,0:T(8,128)(2,1)} %constant_dynamic-update-slice_fusion.3.refs_0_), channel_id=1, source_target_pairs={{0,1},{1,0},{2,3},{3,2},{4,5},{5,4},{6,7},{7,6},{8,9},{9,8},{10,11... | collective-permute-start | bytes 12582920 | tf_op jit(solution)/shard_map/ppermute | solution.py:662
  533.7 5.4 copy-start.2
Sparse Core Ops, SparseCore 0:
  9.6 59.8 all-gather.2
  71.0 58.3 all-gather.4
  254.6 74.5 reduce-scatter.2
  331.8 103.9 reduce-scatter.4

commit v3 on v2

v3 whole, which is shorter than its diff:
```python
import functools
import math

import jax
import jax.numpy as jnp
from jax import lax
from jax.experimental import pallas as pl
from jax.experimental.pallas import tpu as pltpu
from jax.sharding import PartitionSpec as P

HEADS = 16
EPS = 1e-05
NEG = -1e30
LOG2E = math.log2(math.e)
F32 = jnp.float32
BF16 = jnp.bfloat16
VMEM_LIMIT = 60 * 1024 * 1024
ROWS = 256


def nn(a, b):
    return lax.dot_general(a, b, (((1,), (0,)), ((), ())), preferred_element_type=F32)


def nt(a, b):
    return lax.dot_general(a, b, (((1,), (1,)), ((), ())), preferred_element_type=F32)


def tn(a, b):
    return lax.dot_general(a, b, (((0,), (0,)), ((), ())), preferred_element_type=F32)


def params(**more):
    return pltpu.CompilerParams(vmem_limit_bytes=VMEM_LIMIT, **more)


def cost(flops, bytes_accessed, transcendentals=0):
    return pl.CostEstimate(
        flops=int(flops), bytes_accessed=int(bytes_accessed), transcendentals=int(transcendentals)
    )


def whole(shape):
    return pl.BlockSpec(shape, lambda *_: (0,) * len(shape))


def rows_of(block, width):
    return pl.BlockSpec((block, width), lambda i, *_: (i, 0))


def norm_parts(values):
    mean = jnp.mean(values, axis=-1, keepdims=True)
    center = values - mean
    variance = jnp.mean(center * center, axis=-1, keepdims=True)
    root = lax.rsqrt(variance + EPS)
    return center * root, root


def norm_grad(grad, normal, root, gain):
    scaled = grad * gain
    mean_plain = jnp.mean(scaled, axis=-1, keepdims=True)
    mean_normal = jnp.mean(scaled * normal, axis=-1, keepdims=True)
    return root * (scaled - mean_plain - normal * mean_normal)


def pick_rows(first_row, pos_row, rows, count):
    ids = lax.broadcasted_iota(jnp.int32, (rows, count), 0) + first_row
    return jnp.where(ids == pos_row, 1.0, 0.0).astype(BF16)


def pick_slots(pos_col, count):
    ids = lax.broadcasted_iota(jnp.int32, (pos_col.shape[0], count), 1)
    return jnp.where(ids == pos_col, 1.0, 0.0).astype(BF16)


ANYWHERE = pl.BlockSpec(memory_space=pl.ANY)


class Copies:
    def __init__(self, sems):
        self.sems, self.used = sems, 0

    def start(self, source, target):
        copy = pltpu.make_async_copy(source, target, self.sems.at[self.used])
        self.used += 1
        copy.start()
        return copy


def entry_kernel(
    slots, pos_row, gain, offset, wq, bq, wk, wv, bv, tokens, normed, q, k, v,
    slots_in, weights, low_tokens, low_normed, low_out, sems
):
    copies = Copies(sems)
    count = slots.shape[0]
    half = count // 2
    came = copies.start(slots, slots_in)
    weights_came = [copies.start(w, weights.at[n]) for n, w in enumerate((wq, wk, wv))]
    came.wait()
    left = []
    for r in range(0, count, ROWS):
        rows = pl.ds(r, ROWS)
        picked = nn(pick_rows(r, pos_row[...], ROWS, count), slots_in[...])
        low_tokens[rows, :] = picked.astype(BF16)
        normal, _ = norm_parts(picked)
        low_normed[rows, :] = (normal * gain[...] + offset[...]).astype(BF16)
    left += [copies.start(low_tokens, tokens), copies.start(low_normed, normed)]
    for n, out in enumerate((q, k, v)):
        weights_came[n].wait()
        for r in range(0, count, half):
            rows = pl.ds(r, half)
            value = nn(low_normed[rows, :], weights[n])
            if n == 0:
                value = (value + bq[...]).astype(BF16).astype(F32) * 0.125
            elif n == 2:
                value = value + bv[...]
            low_out[n, rows, :] = value.astype(BF16)
            left.append(copies.start(low_out.at[n, rows], out.at[rows]))
    for copy in left:
        copy.wait()


def entry(slots, pos_row, gain, offset, wq, bq, wk, wv, bv):
    count, width = slots.shape
    out = jax.ShapeDtypeStruct((count, width), BF16)
    return pl.pallas_call(
        entry_kernel,
        grid=(1,),
        in_specs=[
            ANYWHERE,
            whole((1, count)),
            whole((1, width)),
            whole((1, width)),
            ANYWHERE,
            whole((1, width)),
            ANYWHERE,
            ANYWHERE,
            whole((1, width)),
        ],
        out_specs=[ANYWHERE] * 5,
        out_shape=[out] * 5,
        scratch_shapes=[
            pltpu.VMEM((count, width), BF16),
            pltpu.VMEM((3, width, width), BF16),
            pltpu.VMEM((count, width), BF16),
            pltpu.VMEM((count, width), BF16),
            pltpu.VMEM((3, count, width), BF16),
            pltpu.SemaphoreType.DMA((12,)),
        ],
        compiler_params=params(),
        cost_estimate=cost(8 * count * width * width, 18 * count * width),
        name="entry",
    )(slots, pos_row, gain, offset, wq, bq, wk, wv, bv)


def half_masks(width):
    lane = lax.broadcasted_iota(jnp.int32, (1, width), 1)
    return lane < width // 2


def split_heads(values):
    first = half_masks(values.shape[1])
    zero = jnp.zeros_like(values)
    return jnp.where(first, values, zero), jnp.where(first, zero, values)


def fill_bias(bias, start_col):
    count = bias.shape[0]
    for i in range(count // ROWS):
        ext = (i + 1) * ROWS
        rows = pl.ds(i * ROWS, ROWS)
        kpos = lax.broadcasted_iota(jnp.int32, (ROWS, ext), 1)
        qpos = lax.broadcasted_iota(jnp.int32, (ROWS, ext), 0) + i * ROWS
        keep = (kpos >= start_col[rows, :]) & (kpos <= qpos)
        bias[rows, :ext] = jnp.where(keep, 0.0, NEG)


def largest_square(values):
    lanes = values.shape[1]
    row = lax.broadcasted_iota(jnp.int32, (8, lanes), 0)
    lane = lax.broadcasted_iota(jnp.int32, (8, lanes), 1)
    select = jnp.where(row == lane // (lanes // 2), 1.0, 0.0).astype(BF16)
    wide = values.astype(F32)
    return jnp.max(nt(select, (wide * wide).astype(BF16)), axis=1, keepdims=True)


SAFE = 50.0


def attend_kernel(start_col, q_ref, k_ref, v_ref, mixed_ref, lse_ref, bias, total, sums):
    count, lanes = q_ref.shape

    @pl.when(pl.program_id(0) == 0)
    def _():
        fill_bias(bias, start_col)

    first = half_masks(lanes)
    bound = jnp.max(largest_square(q_ref[...]) * largest_square(k_ref[...]))
    safe = bound * (LOG2E * LOG2E) < SAFE * SAFE

    @pl.when(safe)
    def _():
        queries = split_heads(q_ref[...])
        work = [(j, h) for j in range(count // ROWS) for h in range(2)]

        def scores(j, h):
            return nt(queries[h][j * ROWS :], k_ref[j * ROWS : (j + 1) * ROWS, :])

        ahead = scores(*work[0])
        for n, (j, h) in enumerate(work):
            score = ahead
            if n + 1 < len(work):
                ahead = scores(*work[n + 1])
            ext = pl.ds(j * ROWS, count - j * ROWS)
            cols = pl.ds(j * ROWS, ROWS)
            terms = jnp.exp2(score * LOG2E + bias[ext, cols])
            part_sum = terms[:, :lanes]
            for c in range(lanes, ROWS, lanes):
                part_sum = part_sum + terms[:, c : c + lanes]
            value = split_heads(v_ref[cols, :])[h]
            part = nn(terms.astype(BF16), value)
            if j == 0:
                sums[h] = part_sum
                total[h] = part
            else:
                sums[h, ext, :] += part_sum
                total[h, ext, :] += part
        norms = [jnp.sum(sums[h], axis=1, keepdims=True) for h in range(2)]
        norm = jnp.where(first, norms[0], norms[1])
        mixed_ref[...] = ((total[0] + total[1]) / norm).astype(BF16)
        turned = jnp.log2(norm).T
        lse_ref[0, 0:1, :] = turned[0:1, :]
        lse_ref[0, 1:2, :] = turned[lanes // 2 : lanes // 2 + 1, :]

    @pl.when(jnp.logical_not(safe))
    def _():
        for i in range(count // ROWS):
            ext = (i + 1) * ROWS
            rows = pl.ds(i * ROWS, ROWS)
            out, stats = None, []
            for query, value in zip(split_heads(q_ref[rows, :]), split_heads(v_ref[:ext, :])):
                score = nt(query, k_ref[:ext, :]) * LOG2E + bias[rows, :ext]
                top = jnp.max(score, axis=1, keepdims=True)
                terms = jnp.exp2(score - top)
                norm = jnp.sum(terms, axis=1, keepdims=True)
                part = nn(terms.astype(BF16), value)
                out = part if out is None else out + part
                stats.append((top + jnp.log2(norm), norm))
            norm = jnp.where(first, stats[0][1], stats[1][1])
            mixed_ref[rows, :] = (out / norm).astype(BF16)
            turned = jnp.where(first, stats[0][0], stats[1][0]).T
            lse_ref[0, 0:1, rows] = turned[0:1, :]
            lse_ref[0, 1:2, rows] = turned[lanes // 2 : lanes // 2 + 1, :]


def attend(start_col, q, k, v):
    count, width = q.shape
    pairs = HEADS // 2
    lanes = width // pairs
    col = pl.BlockSpec((count, lanes), lambda p: (0, p))
    return pl.pallas_call(
        attend_kernel,
        grid=(pairs,),
        in_specs=[whole((count, 1)), col, col, col],
        out_specs=[col, pl.BlockSpec((1, 8, count), lambda p: (p, 0, 0))],
        out_shape=[
            jax.ShapeDtypeStruct((count, width), BF16),
            jax.ShapeDtypeStruct((pairs, 8, count), F32),
        ],
        scratch_shapes=[
            pltpu.VMEM((count, count), F32),
            pltpu.VMEM((2, count, lanes), F32),
            pltpu.VMEM((2, count, lanes), F32),
        ],
        compiler_params=params(),
        cost_estimate=cost(8 * count * count * width, 8 * count * width, HEADS * count * count // 2),
        name="attend",
    )(start_col, q, k, v)


def leave_kernel(mixed, wo, bo, tokens, live_col, pos_col, *refs):
    mixed_in, wo_in, tokens_in, kept, low, sems = refs[-6:]
    outs = refs[:-6]
    copies = Copies(sems)
    came = [copies.start(mixed, mixed_in), copies.start(wo, wo_in), copies.start(tokens, tokens_in)]
    for copy in came:
        copy.wait()
    count = kept.shape[0]
    half = count // 2
    for r in range(0, count, half):
        rows = pl.ds(r, half)
        branch = nn(mixed_in[rows, :], wo_in[...]) + bo[...]
        kept[rows, :] = (tokens_in[rows, :].astype(F32) + live_col[rows, :] * branch).astype(BF16)
    piece = count // len(outs)
    left = []
    for n, out in enumerate(outs):
        rows = pl.ds(n * piece, piece)
        low[rows, :] = nn(pick_slots(pos_col[rows, :], count), kept[...]).astype(BF16)
        left.append(copies.start(low.at[rows], out))
    for copy in left:
        copy.wait()


def leave(parts, mixed, wo, bo, tokens, live_col, pos_col):
    count, width = mixed.shape
    return pl.pallas_call(
        leave_kernel,
        grid=(1,),
        in_specs=[
            ANYWHERE,
            ANYWHERE,
            whole((1, width)),
            ANYWHERE,
            whole((count, 1)),
            whole((count, 1)),
        ],
        out_specs=[ANYWHERE] * parts,
        out_shape=[jax.ShapeDtypeStruct((count // parts, width), BF16)] * parts,
        scratch_shapes=[
            pltpu.VMEM((count, width), BF16),
            pltpu.VMEM((width, width), BF16),
            pltpu.VMEM((count, width), BF16),
            pltpu.VMEM((count, width), BF16),
            pltpu.VMEM((count, width), BF16),
            pltpu.SemaphoreType.DMA((3 + parts,)),
        ],
        compiler_params=params(),
        cost_estimate=cost(4 * count * width * width, 8 * count * width),
        name="leave",
    )(mixed, wo, bo, tokens, live_col, pos_col)


def reenter_kernel(parts, *refs):
    slots = refs[:parts]
    pos_row, live_col, wo, grad_residual, grad_proj, grad_mixed, bias_sum = refs[parts : parts + 7]
    slots_in, wo_in, low, sems = refs[parts + 7 :]
    copies = Copies(sems)
    came, start = [], 0
    for part in slots:
        size = part.shape[0]
        came.append(copies.start(part, slots_in.at[pl.ds(start, size)]))
        start += size
    wo_came = copies.start(wo, wo_in)
    for copy in came:
        copy.wait()
    count = slots_in.shape[0]
    half = count // 2
    total, left = None, []
    for r in range(0, count, half):
        rows = pl.ds(r, half)
        picked = nn(pick_rows(r, pos_row[...], half, count), slots_in[...])
        masked = live_col[rows, :] * picked
        low[0, rows, :] = picked.astype(BF16)
        low[1, rows, :] = masked.astype(BF16)
        part = jnp.sum(masked, axis=0, keepdims=True)
        total = part if total is None else total + part
        left.append(copies.start(low.at[0, rows], grad_residual.at[rows]))
        left.append(copies.start(low.at[1, rows], grad_proj.at[rows]))
    bias_sum[...] = total
    wo_came.wait()
    for r in range(0, count, half):
        rows = pl.ds(r, half)
        low[2, rows, :] = nt(low[1, rows, :], wo_in[...]).astype(BF16)
        left.append(copies.start(low.at[2, rows], grad_mixed.at[rows]))
    for copy in left:
        copy.wait()


def reenter(slots, pos_row, live_col, wo):
    parts = len(slots)
    width = slots[0].shape[1]
    count = sum(v.shape[0] for v in slots)
    out = jax.ShapeDtypeStruct((count, width), BF16)
    return pl.pallas_call(
        functools.partial(reenter_kernel, parts),
        grid=(1,),
        in_specs=[ANYWHERE] * parts + [whole((1, count)), whole((count, 1)), ANYWHERE],
        out_specs=[ANYWHERE] * 3 + [whole((1, width))],
        out_shape=[out] * 3 + [jax.ShapeDtypeStruct((1, width), F32)],
        scratch_shapes=[
            pltpu.VMEM((count, width), BF16),
            pltpu.VMEM((width, width), BF16),
            pltpu.VMEM((3, count, width), BF16),
            pltpu.SemaphoreType.DMA((parts + 7,)),
        ],
        compiler_params=params(),
        cost_estimate=cost(4 * count * width * width, 10 * count * width),
        name="reenter",
    )(*slots, pos_row, live_col, wo)


def attend_back_kernel(
    start_row, q_ref, k_ref, v_ref, o_ref, g_ref, lse_ref, out_ref, bias, dq_sum
):
    count, lanes = q_ref.shape

    @pl.when(pl.program_id(0) == 0)
    def _():
        for j in range(count // ROWS):
            cols = pl.ds(j * ROWS, count - j * ROWS)
            shape = (ROWS, count - j * ROWS)
            kpos = lax.broadcasted_iota(jnp.int32, shape, 0) + j * ROWS
            qpos = lax.broadcasted_iota(jnp.int32, shape, 1) + j * ROWS
            keep = (kpos >= start_row[:, cols]) & (kpos <= qpos)
            bias[pl.ds(j * ROWS, ROWS), cols] = jnp.where(keep, 0.0, NEG)

    products = o_ref[...].astype(F32) * g_ref[...].astype(F32)
    high = products.astype(BF16)
    low = (products - high.astype(F32)).astype(BF16)
    sel_row = lax.broadcasted_iota(jnp.int32, (8, lanes), 0)
    sel_lane = lax.broadcasted_iota(jnp.int32, (8, lanes), 1)
    select = jnp.where(sel_row == sel_lane // (lanes // 2), 1.0, 0.0).astype(BF16)
    deltas = nt(select, high) + nt(select, low)

    queries = split_heads(q_ref[...])
    grads = split_heads(g_ref[...])
    for j in range(count // ROWS):
        rows = pl.ds(j * ROWS, ROWS)
        ext = slice(j * ROWS, count)
        keys, vals = k_ref[rows, :], v_ref[rows, :]
        dk = dv = dq = None
        for h, key in enumerate(split_heads(keys)):
            query, grad = queries[h][ext], grads[h][ext]
            score = nt(keys, query) * LOG2E + bias[rows, ext]
            weights = jnp.exp2(score - lse_ref[0, h : h + 1, ext])
            weights_low = weights.astype(BF16)
            grad_weights = nt(vals, grad)
            grad_score = (weights * (grad_weights - deltas[h : h + 1, ext])).astype(BF16)
            dv_part = nn(weights_low, grad)
            dk_part = nn(grad_score, query)
            dq_part = tn(grad_score, key)
            dv = dv_part if dv is None else dv + dv_part
            dk = dk_part if dk is None else dk + dk_part
            dq = dq_part if dq is None else dq + dq_part
        out_ref[1, rows, :] = dk.astype(BF16)
        out_ref[2, rows, :] = dv.astype(BF16)
        if j == 0:
            dq_sum[...] = dq
        else:
            dq_sum[ext, :] += dq
    out_ref[0] = (dq_sum[...] * 0.125).astype(BF16)


def attend_back(start_row, q, k, v, mixed, grad_mixed, lse):
    count, width = q.shape
    pairs = HEADS // 2
    lanes = width // pairs
    col = pl.BlockSpec((count, lanes), lambda p: (0, p))
    return pl.pallas_call(
        attend_back_kernel,
        grid=(pairs,),
        in_specs=[whole((1, count))]
        + [col] * 5
        + [pl.BlockSpec((1, 8, count), lambda p: (p, 0, 0))],
        out_specs=pl.BlockSpec((3, count, lanes), lambda p: (0, 0, p)),
        out_shape=jax.ShapeDtypeStruct((3, count, width), BF16),
        scratch_shapes=[pltpu.VMEM((count, count), F32), pltpu.VMEM((count, lanes), F32)],
        compiler_params=params(),
        cost_estimate=cost(20 * count * count * width, 16 * count * width, HEADS * count * count // 2),
        name="attend_back",
    )(start_row, q, k, v, mixed, grad_mixed, lse)


def finish_kernel(
    grads, wq, wk, wv, tokens, grad_residual, gain, pos_col, others, out, sums,
    grads_in, weights, tokens_in, residual_in, total, kept, sems
):
    copies = Copies(sems)
    came = []
    for n, w in enumerate((wq, wk, wv)):
        came.append((copies.start(grads.at[n], grads_in.at[n]), copies.start(w, weights.at[n])))
    rest = [copies.start(tokens, tokens_in), copies.start(grad_residual, residual_in)]
    count = kept.shape[0]
    half = count // 2
    for n in range(3):
        for copy in came[n]:
            copy.wait()
        for r in range(0, count, half):
            rows = pl.ds(r, half)
            part = nt(grads_in[n, rows, :], weights[n])
            if n == 0:
                total[rows, :] = part
            else:
                total[rows, :] += part
    for copy in rest:
        copy.wait()
    sums[...] = others[...]
    for r in range(0, count, ROWS):
        rows = pl.ds(r, ROWS)
        grad = total[rows, :]
        normal, root = norm_parts(tokens_in[rows, :].astype(F32))
        kept[rows, :] = (
            residual_in[rows, :].astype(F32) + norm_grad(grad, normal, root, gain[...])
        ).astype(BF16)
        sums[0:1, :] += jnp.sum(grad * normal, axis=0, keepdims=True)
        sums[1:2, :] += jnp.sum(grad, axis=0, keepdims=True)
        sums[2:3, :] += jnp.sum(grads_in[0, rows, :].astype(F32), axis=0, keepdims=True)
        sums[3:4, :] += jnp.sum(grads_in[2, rows, :].astype(F32), axis=0, keepdims=True)
    left = []
    for r in range(0, count, half):
        rows = pl.ds(r, half)
        chosen = pick_slots(pos_col[rows, :], count)
        residual_in[rows, :] = nn(chosen, kept[...]).astype(BF16)
        left.append(copies.start(residual_in.at[rows], out.at[rows]))
    for copy in left:
        copy.wait()


def finish(grads, weights, tokens, grad_residual, gain, pos_col, others):
    count, width = tokens.shape
    return pl.pallas_call(
        finish_kernel,
        grid=(1,),
        in_specs=[ANYWHERE] * 6 + [whole((1, width)), whole((count, 1)), whole((8, width))],
        out_specs=[ANYWHERE, whole((8, width))],
        out_shape=[
            jax.ShapeDtypeStruct((count, width), BF16),
            jax.ShapeDtypeStruct((8, width), F32),
        ],
        scratch_shapes=[
            pltpu.VMEM((3, count, width), BF16),
            pltpu.VMEM((3, width, width), BF16),
            pltpu.VMEM((count, width), BF16),
            pltpu.VMEM((count, width), BF16),
            pltpu.VMEM((count, width), F32),
            pltpu.VMEM((count, width), BF16),
            pltpu.SemaphoreType.DMA((10,)),
        ],
        compiler_params=params(),
        cost_estimate=cost(8 * count * width * width, 20 * count * width),
        name="finish",
    )(grads, *weights, tokens, grad_residual, gain, pos_col, others)


GELU_ROOT = math.sqrt(2.0 / math.pi)
GELU_CUBE = 0.044715
STEP = 1024


def shard_of(step):
    return (step % 2) * 2 + step // 2


def expert_kernel(device, *refs):
    it = iter(refs)
    take = lambda n: [next(it) for _ in range(n)]
    slots, cots, lives = take(3)
    up, down, up_bias, gain, offset = take(5)
    grads, mine, theirs, sums, up_sums = take(5)
    ffn_in, branch, grad_sum = take(3)
    rows, model = slots.shape
    t = pl.program_id(0)

    @pl.when(t == 0)
    def _():
        normal, _ = norm_parts(slots[...].astype(F32))
        ffn_in[...] = (normal * gain[...] + offset[...]).astype(BF16)
        cot = cots[...].reshape(rows, model).astype(F32)
        branch[...] = (lives[...].reshape(rows, 1) * cot).astype(BF16)
        theirs[0] = ffn_in[...]
        theirs[1] = branch[...]
        grad_sum[...] = jnp.zeros_like(grad_sum)

    @pl.when(t == 2)
    def _():
        mine[0] = ffn_in[...]
        mine[1] = branch[...]

    width = up.shape[2]

    def compute(out):
        for c in range(0, width, STEP):
            cols = pl.ds(c, STEP)
            pre = nn(ffn_in[...], up[0, :, cols]) + up_bias[0, :, cols]
            square = pre * pre
            tanh = jnp.tanh(pre * (GELU_ROOT + (GELU_ROOT * GELU_CUBE) * square))
            half = 0.5 * (1.0 + tanh)
            slope = half + (0.5 * pre) * (1.0 - tanh * tanh) * (
                GELU_ROOT + (3.0 * GELU_ROOT * GELU_CUBE) * square
            )
            out[0, :, cols] = (pre * half).astype(BF16)
            grad_pre = (nt(branch[...], down[0, cols, :]) * slope).astype(BF16)
            out[1, :, cols] = grad_pre
            up_sums[0, :, cols] = jnp.sum(grad_pre.astype(F32), axis=0, keepdims=True)
            grad_sum[...] += nt(grad_pre, up[0, :, cols])

    @pl.when(t < 2)
    def _():
        compute(mine)

    @pl.when(t >= 2)
    def _():
        compute(theirs)

    @pl.when(t == 3)
    def _():
        routed = slots[...].astype(F32)
        normal, root = norm_parts(routed)
        grad = grad_sum[...]
        cot = cots[...].reshape(rows, model).astype(F32)
        grads[...] = (cot + norm_grad(grad, normal, root, gain[...])).astype(BF16)
        sums[...] = jnp.zeros_like(sums)
        sums[0:1, :] = jnp.sum(grad * normal, axis=0, keepdims=True)
        sums[1:2, :] = jnp.sum(grad, axis=0, keepdims=True)
        sums[2:3, :] = jnp.sum(branch[...].astype(F32), axis=0, keepdims=True)


def expert_chunk(chunk, device, slots, cot, live, ups, downs, up_bias, gain, offset):
    rows, width = slots.shape
    groups, piece, _ = cot.shape
    short = rows // groups
    part = ups.shape[2]
    assert part == width and ups.shape[0] == 4
    block = pl.BlockSpec((groups, short, width), lambda t, *_: (0, chunk, 0))
    packet = jax.ShapeDtypeStruct((6, rows, width), BF16)
    weights = pl.BlockSpec((1, width, part), lambda t, device: (shard_of(t) ^ device[0], 0, 0))
    bias = pl.BlockSpec((1, 1, part), lambda t, device: (shard_of(t) ^ device[0], 0, 0))
    return pl.pallas_call(
        expert_kernel,
        grid_spec=pltpu.PrefetchScalarGridSpec(
            num_scalar_prefetch=1,
            grid=(4,),
            in_specs=[
                whole((rows, width)),
                block,
                pl.BlockSpec((groups, short, 1), lambda t, *_: (0, chunk, 0)),
            ]
            + [weights, weights, bias, whole((1, width)), whole((1, width))],
            out_specs=[
                whole((rows, width)),
                pl.BlockSpec((2, rows, width), lambda t, *_: (jnp.minimum(t, 2), 0, 0)),
                pl.BlockSpec((2, rows, width), lambda t, *_: (jnp.where(t < 2, 2, t - 2), 0, 0)),
                whole((8, width)),
                bias,
            ],
            scratch_shapes=[
                pltpu.VMEM((rows, width), BF16),
                pltpu.VMEM((rows, width), BF16),
                pltpu.VMEM((rows, width), F32),
            ],
        ),
        out_shape=[
            jax.ShapeDtypeStruct((rows, width), BF16),
            packet,
            packet,
            jax.ShapeDtypeStruct((8, width), F32),
            jax.ShapeDtypeStruct((4, 1, part), F32),
        ],
        compiler_params=params(),
        cost_estimate=cost(24 * rows * width * part, 16 * width * part, 4 * rows * part),
        name="expert_chunk",
    )(device, slots, cot, live, ups, downs, up_bias, gain, offset)


def expert_out_kernel(chunks, device, *refs):
    mine, theirs, slots = refs[:chunks], refs[chunks : 2 * chunks], refs[2 * chunks : 3 * chunks]
    down, bias, live, out, total = refs[3 * chunks :]
    t = pl.program_id(0)
    rows = slots[0].shape[0]
    for n in range(4):

        @pl.when(t == n)
        def _(n=n):
            for c in range(chunks):
                part = nn((mine if n < 2 else theirs)[c][0], down[0])
                if n == 0:
                    total[c * rows : (c + 1) * rows, :] = part
                else:
                    total[c * rows : (c + 1) * rows, :] += part

    @pl.when(t == 3)
    def _():
        groups, piece, width = out.shape
        short = piece // chunks
        for c in range(chunks):
            branch = total[c * rows : (c + 1) * rows, :] + bias[...]
            keep = live[:, c * short : (c + 1) * short, :].reshape(rows, 1)
            value = (slots[c][...].astype(F32) + keep * branch).astype(BF16)
            out[:, c * short : (c + 1) * short, :] = value.reshape(groups, short, width)


def expert_out(device, mine, theirs, slots, downs, bias, live):
    chunks = len(slots)
    rows, width = slots[0].shape
    part = downs.shape[1]
    groups, piece, _ = live.shape
    act = lambda index: pl.BlockSpec((1, rows, part), index)
    return pl.pallas_call(
        functools.partial(expert_out_kernel, chunks),
        grid_spec=pltpu.PrefetchScalarGridSpec(
            num_scalar_prefetch=1,
            grid=(4,),
            in_specs=[act(lambda t, *_: (2 * jnp.minimum(t, 1), 0, 0))] * chunks
            + [act(lambda t, *_: (2 * jnp.maximum(t - 2, 0), 0, 0))] * chunks
            + [whole((rows, width))] * chunks
            + [pl.BlockSpec((1, part, width), lambda t, device: (shard_of(t) ^ device[0], 0, 0))]
            + [whole((1, width)), whole((groups, piece, 1))],
            out_specs=whole((groups, piece, width)),
            scratch_shapes=[pltpu.VMEM((chunks * rows, width), F32)],
        ),
        out_shape=jax.ShapeDtypeStruct((groups, piece, width), BF16),
        compiler_params=params(),
        cost_estimate=cost(8 * chunks * rows * part * width, 32 * rows * width),
        name="expert_out",
    )(device, *mine, *theirs, *slots, downs, bias, live)


CUTS = ((768, 256), (448, 576))


def expert_grads_kernel(count, *refs):
    packets, near, fars = refs[:count], refs[count : count + 2], refs[count + 2 : count + 6]
    far_act, branch, ffn_in, far_pre, near_act, near_pre, far_low, near_full, sems = refs[count + 6 :]
    copies = Copies(sems)
    rows = packets[0].shape[1]

    def fetch(slot, target):
        return [copies.start(p.at[slot], target.at[pl.ds(n * rows, rows)]) for n, p in enumerate(packets)]

    first = fetch(2, far_act) + fetch(5, branch)
    second = fetch(4, ffn_in) + fetch(3, far_pre)
    third = fetch(0, near_act)
    fourth = fetch(1, near_pre)
    left = []

    def far(m, came, one, two):
        for copy in came:
            copy.wait()
        far_low[m] = tn(one[...], two[...]).astype(BF16)
        start = 0
        for n, cut in enumerate(CUTS[m]):
            left.append(copies.start(far_low.at[m, pl.ds(start, cut)], fars[2 * m + n]))
            start += cut

    def close(m, came, one, two):
        for copy in came:
            copy.wait()
        near_full[m] = tn(one[...], two[...])
        left.append(copies.start(near_full.at[m], near[m].at[0]))

    far(0, first, far_act, branch)
    far(1, second, ffn_in, far_pre)
    close(0, third, near_act, branch)
    close(1, fourth, ffn_in, near_pre)
    for copy in left:
        copy.wait()


def expert_grads(packets):
    _, rows, width = packets[0].shape
    count = len(packets)
    assert sum(CUTS[0]) == sum(CUTS[1]) == width
    cuts = [c for cuts in CUTS for c in cuts]
    return pl.pallas_call(
        functools.partial(expert_grads_kernel, count),
        grid=(1,),
        in_specs=[ANYWHERE] * count,
        out_specs=[ANYWHERE] * 6,
        out_shape=[jax.ShapeDtypeStruct((1, width, width), F32)] * 2
        + [jax.ShapeDtypeStruct((c, width), BF16) for c in cuts],
        scratch_shapes=[pltpu.VMEM((count * rows, width), BF16)] * 6
        + [
            pltpu.VMEM((2, width, width), BF16),
            pltpu.VMEM((2, width, width), F32),
            pltpu.SemaphoreType.DMA((6 * count + 6,)),
        ],
        compiler_params=params(),
        cost_estimate=cost(8 * count * rows * width * width, 30 * width * width),
        name="expert_grads",
    )(*packets)


def shared_grads_kernel(
    streams, blocks, codes, normed, mixed, token_grads, grad_proj, keep, send,
    left_in, right_in, total, low, sems
):
    copies = Copies(sems)
    number = right_in.shape[0]
    came = [[copies.start(normed, left_in.at[0]), copies.start(token_grads.at[0], right_in.at[0])]]
    came += [[copies.start(token_grads.at[m], right_in.at[m])] for m in range(1, number - 1)]
    came.append([copies.start(mixed, left_in.at[1]), copies.start(grad_proj, right_in.at[number - 1])])
    half = blocks // 2
    rows = total.shape[1]
    size = rows // half
    first = codes[0] // half
    left = []
    for m in range(number):
        for copy in came[m]:
            copy.wait()
        for h, target in enumerate((keep, send)):
            n = (2 * m + h) % 2
            side = pl.ds(pl.multiple_of((first ^ h) * rows, rows), rows)
            total[n] = tn(left_in[0 if m < number - 1 else 1, :, side], right_in[m])
            for j in range(half):
                code = codes[(j // (half // streams)) % streams] % half
                place = pl.multiple_of((code ^ j) * size, size)
                low[m, h, pl.ds(j * size, size), :] = total[n, pl.ds(place, size), :].astype(BF16)
            left.append(copies.start(low.at[m, h], target.at[m]))
    for copy in left:
        copy.wait()


def shared_grads(layout, normed, mixed, token_grads, grad_proj):
    count, width = normed.shape
    number = token_grads.shape[0] + 1
    half = width // 2
    return pl.pallas_call(
        functools.partial(shared_grads_kernel, layout.streams, layout.blocks),
        grid_spec=pltpu.PrefetchScalarGridSpec(
            num_scalar_prefetch=1,
            grid=(1,),
            in_specs=[ANYWHERE] * 4,
            out_specs=[ANYWHERE] * 2,
            scratch_shapes=[
                pltpu.VMEM((2, count, width), BF16),
                pltpu.VMEM((number, count, width), BF16),
                pltpu.VMEM((2, half, width), F32),
                pltpu.VMEM((number, 2, half, width), BF16),
                pltpu.SemaphoreType.DMA((3 * number + 2,)),
            ],
        ),
        out_shape=[jax.ShapeDtypeStruct((number, half, width), BF16)] * 2,
        compiler_params=params(),
        cost_estimate=cost(2 * number * count * width * width, 6 * number * width * width),
        name="shared_grads",
    )(layout.codes, normed, mixed, token_grads, grad_proj)


def unmix_kernel(group, number, codes, half_place, *refs):
    pieces, outs = refs[:number], refs[-number:]
    size = outs[0].shape[0] // group
    code = codes[pl.program_id(0) // 2] % group
    for piece, out in zip(pieces, outs):
        for j in range(group):
            place = pl.multiple_of((code ^ j) * size, size)
            out[pl.ds(place, size), :] = piece[0, pl.ds(j * size, size), :].astype(F32)


def unmix(layout, half_place, pieces, before=None):
    number = len(pieces)
    _, rows, width = pieces[0].shape
    earlier = [] if before is None else list(before)
    group = layout.blocks // 8
    part = rows // 4

    def place(i, codes, half_place):
        return (0, i ^ ((codes[i // 2] // group) % 2), 0)

    return pl.pallas_call(
        functools.partial(unmix_kernel, group, number),
        grid_spec=pltpu.PrefetchScalarGridSpec(
            num_scalar_prefetch=2,
            grid=(4,),
            in_specs=[pl.BlockSpec((1, part, width), place)] * number
            + [pl.BlockSpec(memory_space=pl.ANY)] * len(earlier),
            out_specs=[
                pl.BlockSpec((part, width), lambda i, codes, half_place: (half_place[0] * 4 + i, 0))
            ]
            * number,
        ),
        out_shape=[jax.ShapeDtypeStruct((2 * rows, width), F32)] * number,
        input_output_aliases={2 + number + m: m for m in range(len(earlier))},
        compiler_params=params(),
        cost_estimate=cost(number * rows * width, 6 * number * rows * width),
        name="unmix",
    )(layout.codes, half_place, *pieces, *earlier)


def swap(values, step):
    axis, size, bit = step
    return lax.ppermute(values, axis, [(i, i ^ bit) for i in range(size)])


def exchange(values):
    return lax.all_to_all(values, "expert", split_axis=0, concat_axis=0, tiled=True)


def turn(values, size, by):
    return lax.ppermute(values, "expert", [(i, (i + by) % size) for i in range(size)])


def bits_of(size):
    return [1 << b for b in range(size.bit_length() - 1)]


def add_low(left, right):
    return (left.astype(F32) + right.astype(F32)).astype(BF16)


def tie(*values):
    return lax.optimization_barrier(values)


class SharedSum:
    streams = 2
    least = 16

    def __init__(self, n_expert, n_dp, rows):
        steps = [("dp", n_dp, b) for b in bits_of(n_dp)] + [
            ("expert", n_expert, b) for b in bits_of(n_expert)
        ]
        steps.sort(key=lambda s: (s[2], s[0]))
        self.steps = steps
        self.first, one, two, *rest = steps
        self.pair = ((two, one), (one, two))
        self.rest, self.left = rest[:2], rest[2:]
        self.blocks = 2 * self.streams * 4 * 4
        assert rows // self.blocks >= self.least and self.rest[0][0] == self.rest[1][0]
        self.codes = jnp.stack([self.code([self.first, None, *pair, *self.rest]) for pair in self.pair])

    def code(self, steps):
        total = jnp.int32(0)
        for step in steps:
            mine = 0 if step is None else (lax.axis_index(step[0]) // step[2]) % 2
            total = total * 2 + mine
        return total.astype(jnp.int32)

    @staticmethod
    def halve(values, step, axis):
        middle = values.shape[axis] // 2
        keep = lax.slice_in_dim(values, 0, middle, axis=axis)
        send = lax.slice_in_dim(values, middle, 2 * middle, axis=axis)
        return add_low(keep, swap(send, step))

    @staticmethod
    def double(values, step, axis):
        return jnp.concatenate([values, swap(values, step)], axis=axis)

    def reduce_first(self, keep, send):
        total = add_low(keep, swap(send, self.first))
        middle = total.shape[1] // 2
        return [total[:, :middle], total[:, middle:]]

    def reduce_pair(self, parts, n):
        return [self.halve(part, pair[n], 1) for part, pair in zip(parts, self.pair)]

    def partners(self, total, j):
        (axis, size, high), (_, _, low) = self.rest
        return swap(total, (axis, size, (j // 2) * high + (j % 2) * low))

    def reduce_rest(self, total):
        size = total.shape[2] // 4
        piece = lambda j: total[:, :, j * size : (j + 1) * size]
        sum_all = piece(0).astype(F32)
        for j in range(1, 4):
            sum_all = sum_all + self.partners(piece(j), j).astype(F32)
        total = sum_all.astype(BF16)
        for step in self.left:
            total = add_low(total, swap(total, step))
        return total

    def gather_rest(self, total):
        return jnp.concatenate([total] + [self.partners(total, j) for j in range(1, 4)], axis=2)

    def gather_pair(self, parts, n):
        return [self.double(part, pair[n], 1) for part, pair in zip(parts, self.pair)]

    def gather_first(self, parts):
        total = jnp.concatenate(parts, axis=1)
        pieces = [total[m : m + 1] for m in range(total.shape[0])]
        mine = ((lax.axis_index(self.first[0]) // self.first[2]) % 2).astype(jnp.int32).reshape(1)
        return (mine, pieces), (1 - mine, [swap(v, self.first) for v in pieces])


def small_sum(values, steps):
    for step in steps:
        if step[0] == "dp":
            values = values + swap(values, step)
        else:
            part = values[:8]
            values = jnp.concatenate([part + swap(part, step), values[8:]], axis=0)
    return values


CHUNKS = 2


def per_device(
    n_expert,
    n_dp,
    block_in,
    seq_lengths,
    slot_position,
    first_gain,
    first_bias,
    query_weight,
    query_bias,
    key_weight,
    value_weight,
    value_bias,
    out_weight,
    out_bias,
    second_gain,
    second_bias,
    expert_up,
    expert_up_bias,
    expert_down,
    expert_down_bias,
    block_cot,
):
    count, width = block_in.shape
    piece = count // n_expert
    row = lambda v: v.reshape(1, -1)
    device = lax.axis_index("dp")
    part = expert_up.shape[2]
    dp_steps = [("dp", n_dp, b) for b in bits_of(n_dp)]
    all_steps = dp_steps + [("expert", n_expert, b) for b in bits_of(n_expert)]

    core, far = dp_steps
    ups = lax.all_gather(expert_up[0], "dp", axis=0)
    downs = lax.all_gather(expert_down[0], "dp", axis=0)
    arrived = exchange(block_in)

    position = slot_position[0]
    ends = jnp.cumsum(seq_lengths[0])
    total_live = ends[-1]
    ids = jnp.arange(count, dtype=jnp.int32)
    live = ids < total_live
    begin = jnp.max(jnp.where(ends[None, :] <= ids[:, None], ends[None, :], 0), axis=1)
    begin = jnp.where(live, begin, ids).astype(jnp.int32)
    live_col = live.astype(F32).reshape(count, 1)
    in_chunks = position.reshape(n_expert, CHUNKS, -1).transpose(1, 0, 2).reshape(count)
    slot_live = (position < total_live).astype(F32).reshape(n_expert, piece)
    route_live = exchange(slot_live).reshape(n_expert, piece, 1)

    tokens, normed, query, key, value = entry(
        arrived, position.reshape(1, count), row(first_gain), row(first_bias), query_weight,
        row(query_bias), key_weight, value_weight, row(value_bias),
    )
    mixed, lse = attend(begin.reshape(count, 1), query, key, value)
    sent = leave(
        CHUNKS, mixed, out_weight, row(out_bias), tokens, live_col, in_chunks.reshape(count, 1)
    )
    routed = [exchange(sent[0])]

    blocks = lambda v: v.reshape(n_expert, piece, width)
    place = device.astype(jnp.int32).reshape(1)
    up_bias = expert_up_bias[0].reshape(n_dp, 1, part)
    grads, mine, theirs, got, sums, up_sums = ([None] * CHUNKS for _ in range(6))
    returned = []
    for c in range(CHUNKS):
        grads[c], mine[c], theirs[c], sums[c], up_sums[c] = expert_chunk(
            c, place, routed[c], blocks(block_cot), route_live, ups, downs, up_bias,
            row(second_gain), row(second_bias),
        )
        if c > 0:
            returned.append(exchange(grads[c - 1]))
            got[c - 1] = swap(theirs[c - 1], core)
            returned[-1], got[c - 1], grads[c], mine[c], theirs[c] = tie(
                returned[-1], got[c - 1], grads[c], mine[c], theirs[c]
            )
        if c + 1 < CHUNKS:
            routed.append(exchange(sent[c + 1]))
            routed[c + 1], grads[c], mine[c], theirs[c] = tie(
                routed[c + 1], grads[c], mine[c], theirs[c]
            )
    returned.append(exchange(grads[-1]))
    got[-1] = swap(theirs[-1], core)

    *near, down_a, down_b, up_a, up_b = expert_grads([*mine, *got])
    sums, up_sums = sum(sums), sum(up_sums)
    empty = jnp.zeros((8, width), F32)
    biases = jnp.concatenate([up_sums.reshape(-1, width), sums[2:3], empty[: 7 - n_dp]], axis=0)

    fars = [down_a, down_b, up_a, up_b]

    def over_y(n):
        fars[n] = swap(fars[n], far)

    returned, near, fars, biases = tie(returned, near, fars, biases)
    grad_residual, grad_proj, grad_mixed, out_bias_sum = reenter(
        returned, in_chunks.reshape(1, count), live_col, out_weight
    )
    others = jnp.concatenate([empty[:4], out_bias_sum, sums[0:2], empty[:1]], axis=0)
    grad_mixed, fars, others = tie(grad_mixed, fars, others)
    shared = SharedSum(n_expert, n_dp, width)
    unstack = lambda v: [v[:, n] for n in range(shared.streams)]

    over_y(0)
    token_grads = attend_back(
        begin.reshape(1, count), query, key, value, mixed, grad_mixed, lse
    )
    token_grads, fars = tie(token_grads, fars)

    over_y(1)
    halves = shared_grads(shared, normed, mixed, token_grads, grad_proj)
    token_grads, halves, fars = tie(token_grads, halves, fars)

    over_y(2)
    leaving, token_sums = finish(
        token_grads, [query_weight, key_weight, value_weight], tokens, grad_residual,
        row(first_gain), position.reshape(count, 1), others,
    )
    total = shared.reduce_first(*halves)
    small = jnp.concatenate([token_sums, biases], axis=0)
    leaving, total, small, fars = tie(leaving, total, small, fars)

    small_steps = list(shared.steps)
    small_step = lambda v: small_sum(v, [small_steps.pop(0)])
    total = shared.reduce_pair(total, 0)
    small = small_step(small)
    total, small = tie(total, small)

    total = jnp.stack(shared.reduce_pair(total, 1), axis=1)
    small = small_step(small)
    total, small, fars, mine = tie(total, small, fars, mine)

    over_y(3)
    block_out = expert_out(place, mine, theirs, routed, downs, row(expert_down_bias[0]), route_live)
    total = shared.reduce_rest(total)
    small = small_step(small)
    total, small, block_out, near, fars = tie(total, small, block_out, near, fars)

    total = unstack(shared.gather_rest(total))
    grad_down = near[0] + jnp.concatenate(fars[:2], axis=0).astype(F32)[None]
    grad_up = near[1] + jnp.concatenate(fars[2:], axis=0).astype(F32)[None]
    small = small_step(small)
    total, small, grad_down, grad_up, leaving = tie(total, small, grad_down, grad_up, leaving)

    input_grad = exchange(leaving)
    total = shared.gather_pair(total, 1)
    total, small = tie(total, small)

    total = shared.gather_pair(total, 0)
    small = small_sum(small, small_steps)
    total, small = tie(total, small)

    nearest, farthest = shared.gather_first(total)
    grads = unmix(shared, *nearest)
    grads, farthest, input_grad = tie(grads, farthest, input_grad)
    grad_query_weight, grad_key_weight, grad_value_weight, grad_out_weight = unmix(
        shared, *farthest, grads
    )
    share = width // n_dp
    grad_up_bias = lax.dynamic_slice_in_dim(small, 8 + device, 1, 0)
    grad_down_bias = lax.dynamic_slice_in_dim(small[8 + n_dp : 9 + n_dp], device * share, share, 1)
    return (
        block_out.reshape(count, width),
        input_grad,
        small[0],
        small[1],
        grad_query_weight,
        small[2],
        grad_key_weight,
        grad_value_weight,
        small[3],
        grad_out_weight,
        small[4],
        small[5],
        small[6],
        grad_up,
        grad_up_bias,
        grad_down,
        grad_down_bias,
    )


def solution(mesh):
    both = P(("expert", "dp"), None)
    return jax.shard_map(
        functools.partial(per_device, mesh.shape["expert"], mesh.shape["dp"]),
        mesh=mesh,
        in_specs=(both,) * 3
        + (P(),) * 11
        + (P("expert", None, "dp"), P("expert", None), P("expert", "dp", None), P("expert", None), both),
        out_specs=(both,) * 2
        + (P(),) * 11
        + (P("expert", None, "dp"), P("expert", "dp"), P("expert", "dp", None), P("expert", "dp")),
        check_vma=False,
    )
```

time: 573 us -> 515 us (0.90)
  waiting for transfers between devices: 183 us -> 142 us
  Pallas kernels: 236 us -> 219 us
  other arithmetic: 20.7 us -> 28.6 us
  local copies, waits for them, and re-layouts: 19.5 us -> 13.2 us
    ppermute x21 -> x30, waiting for transfers between devices: 142 us -> 102 us  [swap(): return lax.ppermute(values, axis, [(i, i ^ bit) for i in range(size)])]
    pallas_call x11, Pallas kernels: 175 us -> 164 us  [the longest x2 46.7 us: expert_chunk(): pl.pallas_call(expert_kernel, grid_spec=pltpu.PrefetchScalarGridSpec(num_...]
    add x2 -> x5, other arithmetic: 0.03 us -> 7.1 us  [the longest x1 6.32 us: per_device(): grad_up = near[1] + jnp.concatenate(fars[2:], axis=0).astype(F32)[None]]
    pallas_call x1, Pallas kernels: 24.7 us -> 18.8 us  [attend(): pl.pallas_call(attend_kernel, grid=(pairs,), in_specs=[whole((count, 1)),...]
    ppermute x21 -> x30, starting transfers between devices: 27.4 us -> 26.9 us  [swap(): return lax.ppermute(values, axis, [(i, i ^ bit) for i in range(size)])]
  transfers between devices with their start and end apart: 31 -> 38, of which waited for: 14 -> 14; matrix products, arithmetic and copies ran while one was open for 7% -> 7% of each run, Pallas kernels for 41% -> 40%
where the time goes in v3:
time: 515 us; the launch traced here: 507 us
  Pallas kernels  219 us (43%)
  waiting for transfers between devices  142 us (28%)
  starting transfers between devices  58.6 us (11%)
  blocking collectives  29.5 us (6%)
  other arithmetic  28.6 us (6%)
  between operations  15.1 us (3%)
  local copies, waits for them, and re-layouts  13.2 us (3%)
    ppermute x30, waiting for transfers between devices, swap(): return lax.ppermute(values, axis, [(i, i ^ bit) for i in range(size)])  102 us
    pallas_call x2, Pallas kernels, expert_chunk(): pl.pallas_call(expert_kernel, grid_spec=pltpu.PrefetchScalarGridSpec(num_...  46.7 us
    all_to_all x6, waiting for transfers between devices, exchange(): lax.all_to_all(values, 'expert', split_axis=0, concat_axis=0, tiled=True)  39.2 us
    pallas_call x1, Pallas kernels, attend_back(): pl.pallas_call(attend_back_kernel, grid=(pairs,), in_specs=[whole((1, cou...  36.1 us
    all_to_all x6, starting transfers between devices, exchange(): lax.all_to_all(values, 'expert', split_axis=0, concat_axis=0, tiled=True)  31.7 us
    all_to_all x1, blocking collectives, exchange(): lax.all_to_all(values, 'expert', split_axis=0, concat_axis=0, tiled=True)  29.5 us
    ppermute x30, starting transfers between devices, swap(): return lax.ppermute(values, axis, [(i, i ^ bit) for i in range(size)])  26.9 us
    pallas_call x1, Pallas kernels, expert_grads(): pl.pallas_call(functools.partial(expert_grads_kernel, count), grid=(1,),...  23.8 us
  transfers between devices with their start and end apart: 38, of which 14 were waited for; matrix products, arithmetic and copies ran while one was open for 7% of the time, Pallas kernels for 40%

profile of v3, /device:TPU:9, one launch (start us, length us, event | category | flops | bytes accessed | tf_op | source)
XLA Modules:
  0.0 506.8 jit_solution(7275139412035959357)
XLA Ops:
  8.7 5.7 %all-to-all-start = ((bf16[8,128,1024]{2,1,0:T(8,128)(2,1)}), bf16[8,128,1024]{2,1,0:T(8,128)(2,1)S(1)}, u32[]{:S(2)}, u32[]{:S(2)}) async-start(bf16[8,128,1024]{2,1,0:T(8,128)(2,1)} %bitcast.3), calls=%async_computation | async-start | bytes 4194304 | tf_op jit(solution)/shard_map/all_to_all | solution.py:875
  16.7 1.3 reshape_reshape.8.pos_col
  18.0 1.5 fusion.2.live_col.refs_3_
  19.5 1.2 fusion.4
  20.8 1.5 iota_select_fusion.start_col
  22.3 38.6 %all-to-all-done = bf16[8,128,1024]{2,1,0:T(8,128)(2,1)S(1)} async-done(((bf16[8,128,1024]{2,1,0:T(8,128)(2,1)}), bf16[8,128,1024]{2,1,0:T(8,128)(2,1)S(1)}, u32[]{:S(2)}, u32[]{:S(2)}) %all-to-all-start) | async-done | bytes 2097184 | tf_op jit(solution)/shard_map/all_to_all | solution.py:875
  60.9 5.5 %all-to-all-start.3 = ((f32[8,1,128]{2,1,0:T(1,128)}), f32[8,1,128]{2,1,0:T(1,128)S(1)}, u32[]{:S(2)}, u32[]{:S(2)}) async-start(f32[8,1,128]{2,1,0:T(1,128)} %fusion.4), calls=%async_computation.3 | async-start | bytes 8192 | tf_op jit(solution)/shard_map/all_to_all | solution.py:875
  66.5 13.7 %entry.1 = (bf16[1024,1024]{1,0:T(8,128)(2,1)}, bf16[1024,1024]{1,0:T(8,128)(2,1)}, bf16[1024,1024]{1,0:T(8,128)(2,1)}, bf16[1024,1024]{1,0:T(8,128)(2,1)}, bf16[1024,1024]{1,0:T(8,128)(2,1)}) custom-call(bf16[1024,1024]{1,0:T(8,128)(2,1)} %bitcast.67, s32[1,1024]{1,0:T(1,128)} %pos_row.1, f32[1,1024]{1,0:T(1,128)} %bitcast.103, f32[1,1024]{1,0:T(1,128)} %bitcast.95, ...), custom_call_target="tpu_custom_call" | custom-call | flops 8589934592 | bytes 18874368 | tf_op jit(solution)/shard_map/entry/pallas_call | solution.py:126
  80.2 18.8 %attend.1 = (bf16[1024,1024]{1,0:T(8,128)(2,1)}, f32[8,8,1024]{2,1,0:T(8,128)}) custom-call(s32[1024,1]{1,0:T(8,128)} %iota_select_fusion.start_col, bf16[1024,1024]{1,0:T(8,128)(2,1)} %get-tuple-element.144.q_ref, bf16[1024,1024]{1,0:T(8,128)(2,1)} %get-tuple-element.145.k_ref, bf16[1024,1024]{1,0:T(8,128)(2,1)} %get-tuple-element.146.v_ref), custom_call_target="tpu_custom_call" | custom-call | flops 8589934592 | bytes 8388608 | tf_op jit(solution)/shard_map/attend/pallas_call | solution.py:261
  99.0 9.7 %leave.1 = (bf16[512,1024]{1,0:T(8,128)(2,1)}, bf16[512,1024]{1,0:T(8,128)(2,1)}) custom-call(bf16[1024,1024]{1,0:T(8,128)(2,1)} %get-tuple-element.147.mixed.o_ref, bf16[1024,1024]{1,0:T(8,128)(2,1)} %refs_4_.1, f32[1,1024]{1,0:T(1,128)} %bitcast.98, bf16[1024,1024]{1,0:T(8,128)(2,1)} %get-tuple-element.148.tokens, f32[1024,1]{1,0:T(8,128)} %fusion.2.live_col.refs_3_, ...), custom_call_target="tpu_custom_call" | custom-call | flops 4294967296 | bytes 8388608 | tf_op jit(solution)/shard_map/leave/pallas_call | solution.py:306
  108.7 29.5 %all_to_all.76 = bf16[8,64,1024]{2,1,0:T(8,128)(2,1)} all-to-all(bf16[8,64,1024]{2,1,0:T(8,128)(2,1)} %bitcast.75), channel_id=1, replica_groups=mesh['expert'=8,'dp'=4] {'expert'}, dimensions={0} | all-to-all | bytes 2097152 | tf_op jit(solution)/shard_map/all_to_all | solution.py:875
  138.2 5.4 %all-to-all-start.1 = ((bf16[8,64,1024]{2,1,0:T(8,128)(2,1)}), bf16[8,64,1024]{2,1,0:T(8,128)(2,1)S(1)}, u32[]{:S(2)}, u32[]{:S(2)}) async-start(bf16[8,64,1024]{2,1,0:T(8,128)(2,1)} %bitcast.12), calls=%async_computation.1 | async-start | bytes 2097152 | tf_op jit(solution)/shard_map/all_to_all | solution.py:875
  144.6 23.4 %expert_chunk.2 = (bf16[512,1024]{1,0:T(8,128)(2,1)}, bf16[6,512,1024]{2,1,0:T(8,128)(2,1)}, bf16[6,512,1024]{2,1,0:T(8,128)(2,1)}, f32[8,1024]{1,0:T(8,128)}, f32[4,1,1024]{2,1,0:T(1,128)}) custom-call(s32[1]{0:T(128)} %bitcast.14.device, bf16[512,1024]{1,0:T(8,128)(2,1)} %bitcast.62, bf16[8,128,1024]{2,1,0:T(8,128)(2,1)} %bitcast.91, ...), custom_call_target="tpu_custom_call" | custom-call | flops 12884901888 | bytes 16777216 | tf_op jit(solution)/shard_map/expert_chunk/pallas_call | solution.py:618
  168.0 1.8 collective-permute-start
  169.8 5.6 %all-to-all-start.4 = ((bf16[8,64,1024]{2,1,0:T(8,128)(2,1)}), bf16[8,64,1024]{2,1,0:T(8,128)(2,1)S(1)}, u32[]{:S(2)}, u32[]{:S(2)}) async-start(bf16[8,64,1024]{2,1,0:T(8,128)(2,1)} %bitcast.74), calls=%async_computation.4 | async-start | bytes 2097152 | tf_op jit(solution)/shard_map/all_to_all | solution.py:875
  175.4 23.4 %expert_chunk.3 = (bf16[512,1024]{1,0:T(8,128)(2,1)}, bf16[6,512,1024]{2,1,0:T(8,128)(2,1)}, bf16[6,512,1024]{2,1,0:T(8,128)(2,1)}, f32[8,1024]{1,0:T(8,128)}, f32[4,1,1024]{2,1,0:T(1,128)}) custom-call(s32[1]{0:T(128)} %bitcast.14.device, bf16[512,1024]{1,0:T(8,128)(2,1)} %bitcast.64, bf16[8,128,1024]{2,1,0:T(8,128)(2,1)} %bitcast.92, ...), custom_call_target="tpu_custom_call" | custom-call | flops 12884901888 | bytes 16777216 | tf_op jit(solution)/shard_map/expert_chunk/pallas_call | solution.py:618
  201.3 1.2 compare_select_fusion.start_row
  204.0 5.9 %all-to-all-start.5 = ((bf16[8,64,1024]{2,1,0:T(8,128)(2,1)}), bf16[8,64,1024]{2,1,0:T(8,128)(2,1)S(1)}, u32[]{:S(2)}, u32[]{:S(2)}) async-start(bf16[8,64,1024]{2,1,0:T(8,128)(2,1)} %bitcast.72), calls=%async_computation.5 | async-start | bytes 2097152 | tf_op jit(solution)/shard_map/all_to_all | solution.py:875
  210.0 23.8 %expert_grads.1 = (f32[1,1024,1024]{2,1,0:T(8,128)}, f32[1,1024,1024]{2,1,0:T(8,128)}, bf16[768,1024]{1,0:T(8,128)(2,1)}, bf16[256,1024]{1,0:T(8,128)(2,1)}, bf1...) custom-call(bf16[6,512,1024]{2,1,0:T(8,128)(2,1)} %get-tuple-element.223.refs_0_, ...), custom_call_target="tpu_custom_call" | custom-call | flops 17179869184 | bytes 31457280 | tf_op jit(solution)/shard_map/expert_grads/pallas_call | solution.py:754
  234.9 9.4 %reenter.1 = (bf16[1024,1024]{1,0:T(8,128)(2,1)}, bf16[1024,1024]{1,0:T(8,128)(2,1)}, bf16[1024,1024]{1,0:T(8,128)(2,1)}, f32[1,1024]{1,0:T(1,128)}) custom-call(bf16[512,1024]{1,0:T(8,128)(2,1)} %bitcast.71, bf16[512,1024]{1,0:T(8,128)(2,1)} %bitcast.73, s32[1,1024]{1,0:T(1,128)} %reshape_reshape.7.refs_2_, f32[1024,1]{1,0:T(8,128)} %fusion.2.live_col.refs_3_, ...), custom_call_target="tpu_custom_call" | custom-call | flops 4294967296 | bytes 10485760 | tf_op jit(solution)/shard_map/reenter/pallas_call | solution.py:374
  244.3 1.4 maximum_maximum_fusion.1.others
  246.9 36.1 %attend_back.1.token_grads.grads = bf16[3,1024,1024]{2,1,0:T(8,128)(2,1)} custom-call(s32[1,1024]{1,0:T(1,128)} %compare_select_fusion.start_row, bf16[1024,1024]{1,0:T(8,128)(2,1)} %get-tuple-element.144.q_ref, bf16[1024,1024]{1,0:T(8,128)(2,1)} %get-tuple-element.145.k_ref, bf16[1024,1024]{1,0:T(8,128)(2,1)} %get-tuple-element.146.v_ref, ...), custom_call_target="tpu_custom_call" | custom-call | flops 21474836480 | bytes 16777216 | tf_op jit(solution)/shard_map/attend_back/pallas_call | solution.py:449
  283.3 14.2 %shared_grads.1 = (bf16[4,512,1024]{2,1,0:T(8,128)(2,1)}, bf16[4,512,1024]{2,1,0:T(8,128)(2,1)}) custom-call(s32[2]{0:T(128)} %pad_add_fusion.codes, bf16[1024,1024]{1,0:T(8,128)(2,1)} %get-tuple-element.191.normed, bf16[1024,1024]{1,0:T(8,128)(2,1)} %get-tuple-element.147.mixed.o_ref, bf16[3,1024,1024]{2,1,0:T(8,128)(2,1)} %attend_back.1.token_grads.grads, ...), custom_call_target="tpu_custom_call" | custom-call | flops 8589934592 | bytes 25165824 | tf_op jit(solution)/shard_map/shared_grads/pallas_call | solution.py:807
  297.6 1.4 collective-permute-start.4
  301.2 18.1 %finish.1 = (bf16[1024,1024]{1,0:T(8,128)(2,1)}, f32[8,1024]{1,0:T(8,128)}) custom-call(bf16[3,1024,1024]{2,1,0:T(8,128)(2,1)} %attend_back.1.token_grads.grads, bf16[1024,1024]{1,0:T(8,128)(2,1)} %wq.3, bf16[1024,1024]{1,0:T(8,128)(2,1)} %wk.3, bf16[1024,1024]{1,0:T(8,128)(2,1)} %wv.3, bf16[1024,1024]{1,0:T(8,128)(2,1)} %get-tuple-element.148.tokens, ...), custom_call_target="tpu_custom_call" | custom-call | flops 8589934592 | bytes 20971520 | tf_op jit(solution)/shard_map/finish/pallas_call | solution.py:511
  320.1 5.6 %add_convert_fusion = bf16[4,512,1024]{2,1,0:T(8,128)(2,1)S(1)} fusion(bf16[4,512,1024]{2,1,0:T(8,128)(2,1)} %collective-permute-done.4, bf16[4,512,1024]{2,1,0:T(8,128)(2,1)} %get-tuple-element.203), kind=kLoop, calls=%fused_computation | loop fusion | flops 8388608 | bytes 12582912 | tf_op jit(solution)/shard_map/convert_element_type | solution.py:887
  326.5 1.2 collective-permute-start.7
  329.9 21.1 %collective-permute-done.7 = bf16[4,128,1024]{2,1,0:T(8,128)(2,1)S(1)} collective-permute-done((bf16[4,128,1024]{2,1,0:T(8,128)(2,1)S(1)}, bf16[4,128,1024]{2,1,0:T(8,128)(2,1)S(1)}, u32[]{:S(2)}, u32[]{:S(2)}) %collective-permute-start.7) | collective-permute-done | bytes 1048608 | tf_op jit(solution)/shard_map/ppermute | solution.py:871
  354.4 10.8 %collective-permute-done.11 = f32[8,1024]{1,0:T(8,128)S(1)} collective-permute-done((f32[8,1024]{1,0:T(8,128)S(1)}, f32[8,1024]{1,0:T(8,128)S(1)}, u32[]{:S(2)}, u32[]{:S(2)}) %collective-permute-start.11) | collective-permute-done | bytes 32800 | tf_op jit(solution)/shard_map/ppermute | solution.py:871
  368.2 2.2 collective-permute-start.12
  371.4 15.4 %expert_out.1 = bf16[8,128,1024]{2,1,0:T(8,128)(2,1)} custom-call(s32[1]{0:T(128)} %bitcast.14.device, bf16[6,512,1024]{2,1,0:T(8,128)(2,1)} %get-tuple-element.223.refs_0_, bf16[6,512,1024]{2,1,0:T(8,128)(2,1)} %get-tuple-element.224.refs_1_, bf16[6,512,1024]{2,1,0:T(8,128)(2,1)} %get-tuple-element.155.refs_2_, ...), custom_call_target="tpu_custom_call" | custom-call | flops 8589934592 | bytes 16777216 | tf_op jit(solution)/shard_map/expert_out/pallas_call | solution.py:688
  387.7 5.4 %collective-permute-done.14 = bf16[4,2,16,1024]{3,2,0,1:T(8,128)(2,1)} collective-permute-done((bf16[4,2,16,1024]{3,2,0,1:T(8,128)(2,1)}, bf16[4,2,16,1024]{3,2,0,1:T(8,128)(2,1)}, u32[]{:S(2)}, u32[]{:S(2)}) %collective-permute-start.14) | collective-permute-done | bytes 262176 | tf_op jit(solution)/shard_map/ppermute | solution.py:871
  394.4 2.6 collective-permute-start.18
  398.3 6.3 %convert_add_fusion = (f32[1,1024,1024]{2,1,0:T(8,128)}, f32[1,1024,1024]{2,1,0:T(8,128)}) fusion(f32[1,1024,1024]{2,1,0:T(8,128)} %get-tuple-element.237, bf16[1,576,1024]{2,1,0:T(8,128)(2,1)S(1)} %bitcast.70, bf16[1,448,1024]{2,1,0:T(8,128)(2,1)S(1)} %bitcast.76, f32[1,1024,1024]{2,1,0:T(8,128)} %get-tuple-element.234, bf16[1,256,1024]{2,1,0:T(8,128)(2,1)} %bitcast.39, ...), kind=kLoop, calls=%fused_computation.1 | loop fusion | flops 10485760 | bytes 20971520 | tf_op jit(solution)/shard_map/add | solution.py:1116
  404.6 9.1 %collective-permute-done.20 = f32[8,1024]{1,0:T(8,128)S(1)} collective-permute-done((f32[8,1024]{1,0:T(8,128)S(1)}, f32[8,1024]{1,0:T(8,128)S(1)}, u32[]{:S(2)}, u32[]{:S(2)}) %collective-permute-start.20) | collective-permute-done | bytes 32800 | tf_op jit(solution)/shard_map/ppermute | solution.py:871
  413.8 4.6 collective-permute-done.19
  419.4 1.7 collective-permute-start.21
  421.0 3.6 all-to-all-start.6
  424.6 6.1 %collective-permute-done.22 = bf16[4,64,1024]{2,1,0:T(8,128)(2,1)} collective-permute-done((bf16[4,64,1024]{2,1,0:T(8,128)(2,1)S(1)}, bf16[4,64,1024]{2,1,0:T(8,128)(2,1)}, u32[]{:S(2)}, u32[]{:S(2)}) %collective-permute-start.22) | collective-permute-done | bytes 524320 | tf_op jit(solution)/shard_map/ppermute | solution.py:871
  431.8 10.3 %collective-permute-done.21 = bf16[4,64,1024]{2,1,0:T(8,128)(2,1)} collective-permute-done((bf16[4,64,1024]{2,1,0:T(8,128)(2,1)S(1)}, bf16[4,64,1024]{2,1,0:T(8,128)(2,1)}, u32[]{:S(2)}, u32[]{:S(2)}) %collective-permute-start.21) | collective-permute-done | bytes 524320 | tf_op jit(solution)/shard_map/ppermute | solution.py:871
  443.1 2.4 collective-permute-start.24
  445.5 25.2 %collective-permute-done.25 = f32[8,1024]{1,0:T(8,128)S(1)} collective-permute-done((f32[8,1024]{1,0:T(8,128)S(1)}, f32[8,1024]{1,0:T(8,128)S(1)}, u32[]{:S(2)}, u32[]{:S(2)}) %collective-permute-start.25) | collective-permute-done | bytes 32800 | tf_op jit(solution)/shard_map/ppermute | solution.py:871
  470.8 7.7 %collective-permute-done.24 = bf16[4,128,1024]{2,1,0:T(8,128)(2,1)S(1)} collective-permute-done((bf16[4,128,1024]{2,1,0:T(8,128)(2,1)S(1)}, bf16[4,128,1024]{2,1,0:T(8,128)(2,1)S(1)}, u32[]{:S(2)}, u32[]{:S(2)}) %collective-permute-start.24) | collective-permute-done | bytes 1048608 | tf_op jit(solution)/shard_map/ppermute | solution.py:871
  479.2 1.7 fusion.5
  480.9 2.2 collective-permute-start.26
  483.6 6.6 %unmix.2 = (f32[1024,1024]{1,0:T(8,128)}, f32[1024,1024]{1,0:T(8,128)}, f32[1024,1024]{1,0:T(8,128)}, f32[1024,1024]{1,0:T(8,128)}) custom-call(s32[2]{0:T(128)} %pad_add_fusion.codes, s32[1]{0:T(128)} %bitcast.35.half_place, bf16[1,512,1024]{2,1,0:T(8,128)(2,1)} %get-tuple-element.274.refs_0_, bf16[1,512,1024]{2,1,0:T(8,128)(2,1)} %get-tuple-element.273.refs_1_, ...), custom_call_target="tpu_custom_call" | custom-call | flops 2097152 | bytes 12582912 | tf_op jit(solution)/shard_map/unmix/pallas_call | solution.py:849
  491.5 6.7 %unmix.3 = (f32[1024,1024]{1,0:T(8,128)}, f32[1024,1024]{1,0:T(8,128)}, f32[1024,1024]{1,0:T(8,128)}, f32[1024,1024]{1,0:T(8,128)}) custom-call(s32[2]{0:T(128)} %pad_add_fusion.codes, s32[1]{0:T(128)S(6)} %sub.24.half_place, ...), custom_call_target="tpu_custom_call", output_to_operand_aliasing={{0}: (6, {}), {1}: (7, {}), {2}: (8, {}), {3}: (9, {})} | custom-call | flops 2097152 | bytes 12582912 | tf_op jit(solution)/shard_map/unmix/pallas_call | solution.py:849
  498.2 1.3 copy.91
  (146 shorter events, 33.8 us)
Async XLA Ops:
  7.2 137.4 %all-gather.5.cloned.1.call-start = ((), (), s32[]{:S(2)}) async-start(), calls=%async_computation.8 | async-start | bytes 10485760 | tf_op jit(solution)/shard_map/all_gather | solution.py:1011
  7.9 136.7 %all-gather.3.cloned.1.call-start = ((), (), s32[]{:S(2)}) async-start(), calls=%async_computation.7 | async-start | bytes 10485760 | tf_op jit(solution)/shard_map/all_gather | solution.py:1010
  8.7 52.2 %all-to-all-start = ((bf16[8,128,1024]{2,1,0:T(8,128)(2,1)}), bf16[8,128,1024]{2,1,0:T(8,128)(2,1)S(1)}, u32[]{:S(2)}, u32[]{:S(2)}) async-start(bf16[8,128,1024]{2,1,0:T(8,128)(2,1)} %bitcast.3), calls=%async_computation | async-start | bytes 4194304 | tf_op jit(solution)/shard_map/all_to_all | solution.py:875
  60.9 47.8 %all-to-all-start.3 = ((f32[8,1,128]{2,1,0:T(1,128)}), f32[8,1,128]{2,1,0:T(1,128)S(1)}, u32[]{:S(2)}, u32[]{:S(2)}) async-start(f32[8,1,128]{2,1,0:T(1,128)} %fusion.4), calls=%async_computation.3 | async-start | bytes 8192 | tf_op jit(solution)/shard_map/all_to_all | solution.py:875
  138.2 29.8 %all-to-all-start.1 = ((bf16[8,64,1024]{2,1,0:T(8,128)(2,1)}), bf16[8,64,1024]{2,1,0:T(8,128)(2,1)S(1)}, u32[]{:S(2)}, u32[]{:S(2)}) async-start(bf16[8,64,1024]{2,1,0:T(8,128)(2,1)} %bitcast.12), calls=%async_computation.1 | async-start | bytes 2097152 | tf_op jit(solution)/shard_map/all_to_all | solution.py:875
  168.0 7.4 %copy-start = (bf16[8,64,1024]{2,1,0:T(8,128)(2,1)}, bf16[8,64,1024]{2,1,0:T(8,128)(2,1)S(1)}, u32[]{:S(2)}) copy-start(bf16[8,64,1024]{2,1,0:T(8,128)(2,1)S(1)} %all-to-all-done.1) | copy-start | bytes 3145732
  168.0 31.4 %collective-permute-start = (bf16[6,512,1024]{2,1,0:T(8,128)(2,1)}, bf16[6,512,1024]{2,1,0:T(8,128)(2,1)}, u32[]{:S(2)}, u32[]{:S(2)}) collective-permute-start(bf16[6,512,1024]{2,1,0:T(8,128)(2,1)} %get-tuple-element.155.refs_2_), channel_id=1, source_target_pairs={{0,1},{1,0},{2,3},{3,2},{4,5},{5,4},{6,7},{7,6},{8,9},{9,8},{10,11... | collective-permute-start | bytes 18874376 | tf_op jit(solution)/shard_map/ppermute | solution.py:871
  169.8 29.6 %all-to-all-start.4 = ((bf16[8,64,1024]{2,1,0:T(8,128)(2,1)}), bf16[8,64,1024]{2,1,0:T(8,128)(2,1)S(1)}, u32[]{:S(2)}, u32[]{:S(2)}) async-start(bf16[8,64,1024]{2,1,0:T(8,128)(2,1)} %bitcast.74), calls=%async_computation.4 | async-start | bytes 2097152 | tf_op jit(solution)/shard_map/all_to_all | solution.py:875
  175.4 27.1 %copy-start.10 = (f32[8,1024]{1,0:T(8,128)S(1)}, f32[8,1024]{1,0:T(8,128)}, u32[]{:S(2)}) copy-start(f32[8,1024]{1,0:T(8,128)} %get-tuple-element.174) | copy-start | bytes 98308
  175.4 27.9 %copy-start.11 = (f32[4,1,1024]{2,1,0:T(1,128)S(1)}, f32[4,1,1024]{2,1,0:T(1,128)}, u32[]{:S(2)}) copy-start(f32[4,1,1024]{2,1,0:T(1,128)} %get-tuple-element.172) | copy-start | bytes 49156
  199.4 34.5 %copy-start.3 = (bf16[8,64,1024]{2,1,0:T(8,128)(2,1)}, bf16[8,64,1024]{2,1,0:T(8,128)(2,1)S(1)}, u32[]{:S(2)}) copy-start(bf16[8,64,1024]{2,1,0:T(8,128)(2,1)S(1)} %all-to-all-done.4) | copy-start | bytes 3145732
  199.4 10.6 %collective-permute-start.1 = (bf16[6,512,1024]{2,1,0:T(8,128)(2,1)}, bf16[6,512,1024]{2,1,0:T(8,128)(2,1)}, u32[]{:S(2)}, u32[]{:S(2)}) collective-permute-start(bf16[6,512,1024]{2,1,0:T(8,128)(2,1)} %get-tuple-element.165.refs_3_), channel_id=1, source_target_pairs={{0,1},{1,0},{2,3},{3,2},{4,5},{5,4},{6,7},{7,6},{8,9},{9,8},{10,11... | collective-permute-start | bytes 18874376 | tf_op jit(solution)/shard_map/ppermute | solution.py:871
  203.3 30.6 %copy-start.7 = (f32[8,1024]{1,0:T(8,128)}, f32[8,1024]{1,0:T(8,128)S(1)}, u32[]{:S(2)}) copy-start(f32[8,1024]{1,0:T(8,128)S(1)} %add.111) | copy-start | bytes 98308
  204.0 29.8 %all-to-all-start.5 = ((bf16[8,64,1024]{2,1,0:T(8,128)(2,1)}), bf16[8,64,1024]{2,1,0:T(8,128)(2,1)S(1)}, u32[]{:S(2)}, u32[]{:S(2)}) async-start(bf16[8,64,1024]{2,1,0:T(8,128)(2,1)} %bitcast.72), calls=%async_computation.5 | async-start | bytes 2097152 | tf_op jit(solution)/shard_map/all_to_all | solution.py:875
  234.9 9.4 %slice-start = ((f32[8,1024]{1,0:T(8,128)}), f32[2,1024]{1,0:T(2,128)S(1)}, s32[]{:S(2)}) async-start(f32[8,1024]{1,0:T(8,128)} %copy-done.7), calls=%async_computation.9 | async-start | bytes 16384 | tf_op jit(solution)/shard_map/slice | solution.py:1074
  245.7 37.3 %collective-permute-start.2 = (bf16[768,1024]{1,0:T(8,128)(2,1)}, bf16[768,1024]{1,0:T(8,128)(2,1)S(1)}, u32[]{:S(2)}, u32[]{:S(2)}) collective-permute-start(bf16[768,1024]{1,0:T(8,128)(2,1)} %get-tuple-element.186), channel_id=1, source_target_pairs={{0,2},{1,3},{2,0},{3,1},{4,6},{5,7},{6,4},{7,5},{8,10},{9,11},{10,... | collective-permute-start | bytes 4718600 | tf_op jit(solution)/shard_map/ppermute | solution.py:871
  246.9 36.1 %copy-start.14 = (bf16[256,1024]{1,0:T(8,128)(2,1)S(1)}, bf16[256,1024]{1,0:T(8,128)(2,1)}, u32[]{:S(2)}) copy-start(bf16[256,1024]{1,0:T(8,128)(2,1)} %get-tuple-element.196) | copy-start | bytes 1572868
  283.0 14.6 %collective-permute-start.3 = (bf16[256,1024]{1,0:T(8,128)(2,1)S(1)}, bf16[256,1024]{1,0:T(8,128)(2,1)}, u32[]{:S(2)}, u32[]{:S(2)}) collective-permute-start(bf16[256,1024]{1,0:T(8,128)(2,1)S(1)} %copy-done.14), channel_id=1, source_target_pairs={{0,2},{1,3},{2,0},{3,1},{4,6},{5,7},{6,4},{7,5},{8,10},{9,11},{10,... | collective-permute-start | bytes 1572872 | tf_op jit(solution)/shard_map/ppermute | solution.py:871
  283.3 15.7 %copy-start.9 = (s32[1,1024]{1,0:T(1,128)S(1)}, s32[1,1024]{1,0:T(1,128)}, u32[]{:S(2)}) copy-start(s32[1,1024]{1,0:T(1,128)} %pos_row.1) | copy-start | bytes 12292
  283.3 16.7 %copy-start.13 = (bf16[448,1024]{1,0:T(8,128)(2,1)S(1)}, bf16[448,1024]{1,0:T(8,128)(2,1)}, u32[]{:S(2)}) copy-start(bf16[448,1024]{1,0:T(8,128)(2,1)} %get-tuple-element.209) | copy-start | bytes 2752516
  297.6 22.5 %collective-permute-start.4 = (bf16[4,512,1024]{2,1,0:T(8,128)(2,1)}, bf16[4,512,1024]{2,1,0:T(8,128)(2,1)}, u32[]{:S(2)}, u32[]{:S(2)}) collective-permute-start(bf16[4,512,1024]{2,1,0:T(8,128)(2,1)} %get-tuple-element.204), channel_id=1, source_target_pairs={{0,1},{1,0},{2,3},{3,2},{4,5},{5,4},{6,7},{7,6},{8,9},{9,8},{10,11... | collective-permute-start | bytes 12582920 | tf_op jit(solution)/shard_map/ppermute | solution.py:871
  300.0 26.4 %collective-permute-start.5 = (bf16[448,1024]{1,0:T(8,128)(2,1)S(1)}, bf16[448,1024]{1,0:T(8,128)(2,1)S(1)}, u32[]{:S(2)}, u32[]{:S(2)}) collective-permute-start(bf16[448,1024]{1,0:T(8,128)(2,1)S(1)} %copy-done.13), channel_id=1, source_target_pairs={{0,2},{1,3},{2,0},{3,1},{4,6},{5,7},{6,4},{7,5},{8,10},{9,11},{10,... | collective-permute-start | bytes 2752520 | tf_op jit(solution)/shard_map/ppermute | solution.py:871
  326.5 24.5 %collective-permute-start.7 = (bf16[4,128,1024]{2,1,0:T(8,128)(2,1)S(1)}, bf16[4,128,1024]{2,1,0:T(8,128)(2,1)S(1)}, u32[]{:S(2)}, u32[]{:S(2)}) collective-permute-start(bf16[4,128,1024]{2,1,0:T(8,128)(2,1)S(1)} %slice.132), channel_id=1, source_target_pairs={{0,4},{4,0},{8,12},{12,8},{16,20},{20,16},{24,28},{28,24},{1,5},{5... | collective-permute-start | bytes 3145736 | tf_op jit(solution)/shard_map/ppermute | solution.py:871
  327.8 24.2 %collective-permute-start.6 = (bf16[4,128,1024]{2,1,0:T(8,128)(2,1)S(1)}, bf16[4,128,1024]{2,1,0:T(8,128)(2,1)S(1)}, u32[]{:S(2)}, u32[]{:S(2)}) collective-permute-start(bf16[4,128,1024]{2,1,0:T(8,128)(2,1)S(1)} %slice.130), channel_id=1, source_target_pairs={{0,2},{1,3},{2,0},{3,1},{4,6},{5,7},{6,4},{7,5},{8,10},{9,11},{10,... | collective-permute-start | bytes 3145736 | tf_op jit(solution)/shard_map/ppermute | solution.py:871
  328.2 1.8 collective-permute-start.8
  352.5 12.8 %collective-permute-start.9 = (bf16[4,64,1024]{2,1,0:T(8,128)(2,1)S(1)}, bf16[4,64,1024]{2,1,0:T(8,128)(2,1)S(1)}, u32[]{:S(2)}, u32[]{:S(2)}) collective-permute-start(bf16[4,64,1024]{2,1,0:T(8,128)(2,1)S(1)} %slice.134), channel_id=1, source_target_pairs={{0,4},{4,0},{8,12},{12,8},{16,20},{20,16},{24,28},{28,24},{1,5},{5... | collective-permute-start | bytes 1572872 | tf_op jit(solution)/shard_map/ppermute | solution.py:871
  353.5 11.7 %collective-permute-start.11 = (f32[8,1024]{1,0:T(8,128)S(1)}, f32[8,1024]{1,0:T(8,128)S(1)}, u32[]{:S(2)}, u32[]{:S(2)}) collective-permute-start(f32[8,1024]{1,0:T(8,128)S(1)} %slice.137), channel_id=1, source_target_pairs={{0,4},{4,0},{8,12},{12,8},{16,20},{20,16},{24,28},{28,24},{1,5},{5... | collective-permute-start | bytes 98312 | tf_op jit(solution)/shard_map/ppermute | solution.py:871
  354.0 11.5 %collective-permute-start.10 = (bf16[4,64,1024]{2,1,0:T(8,128)(2,1)S(1)}, bf16[4,64,1024]{2,1,0:T(8,128)(2,1)S(1)}, u32[]{:S(2)}, u32[]{:S(2)}) collective-permute-start(bf16[4,64,1024]{2,1,0:T(8,128)(2,1)S(1)} %slice.136), channel_id=1, source_target_pairs={{0,2},{1,3},{2,0},{3,1},{4,6},{5,7},{6,4},{7,5},{8,10},{9,11},{10,... | collective-permute-start | bytes 1572872 | tf_op jit(solution)/shard_map/ppermute | solution.py:871
  365.8 21.0 %collective-permute-start.15 = (f32[16,1024]{1,0:T(8,128)S(1)}, f32[16,1024]{1,0:T(8,128)}, u32[]{:S(2)}, u32[]{:S(2)}) collective-permute-start(f32[16,1024]{1,0:T(8,128)S(1)} %pad_maximum_fusion.6), channel_id=1, source_target_pairs={{0,2},{1,3},{2,0},{3,1},{4,6},{5,7},{6,4},{7,5},{8,10},{9,11},{10,... | collective-permute-start | bytes 196616 | tf_op jit(solution)/shard_map/ppermute | solution.py:871
  366.2 28.2 %collective-permute-start.16 = (bf16[576,1024]{1,0:T(8,128)(2,1)}, bf16[576,1024]{1,0:T(8,128)(2,1)S(1)}, u32[]{:S(2)}, u32[]{:S(2)}) collective-permute-start(bf16[576,1024]{1,0:T(8,128)(2,1)} %get-tuple-element.230), channel_id=1, source_target_pairs={{0,2},{1,3},{2,0},{3,1},{4,6},{5,7},{6,4},{7,5},{8,10},{9,11},{10,... | collective-permute-start | bytes 3538952 | tf_op jit(solution)/shard_map/ppermute | solution.py:871
  368.2 19.5 %collective-permute-start.12 = (bf16[4,2,16,1024]{3,2,0,1:T(8,128)(2,1)}, bf16[4,2,16,1024]{3,2,0,1:T(8,128)(2,1)S(1)}, u32[]{:S(2)}, u32[]{:S(2)}) collective-permute-start(bf16[4,2,16,1024]{3,2,0,1:T(8,128)(2,1)} %get-tuple-element.279), channel_id=1, source_target_pairs={{0,16},{4,20},{8,24},{12,28},{16,0},{20,4},{24,8},{28,12},{1,17},{... | collective-permute-start | bytes 786440 | tf_op jit(solution)/shard_map/ppermute | solution.py:871
  370.5 17.3 %collective-permute-start.13 = (bf16[4,2,16,1024]{3,2,0,1:T(8,128)(2,1)}, bf16[4,2,16,1024]{3,2,0,1:T(8,128)(2,1)}, u32[]{:S(2)}, u32[]{:S(2)}) collective-permute-start(bf16[4,2,16,1024]{3,2,0,1:T(8,128)(2,1)} %get-tuple-element.281), channel_id=1, source_target_pairs={{0,8},{4,12},{8,0},{12,4},{16,24},{20,28},{24,16},{28,20},{1,9},{5... | collective-permute-start | bytes 786440 | tf_op jit(solution)/shard_map/ppermute | solution.py:871
  370.6 22.5 %collective-permute-start.14 = (bf16[4,2,16,1024]{3,2,0,1:T(8,128)(2,1)}, bf16[4,2,16,1024]{3,2,0,1:T(8,128)(2,1)}, u32[]{:S(2)}, u32[]{:S(2)}) collective-permute-start(bf16[4,2,16,1024]{3,2,0,1:T(8,128)(2,1)} %get-tuple-element.280), channel_id=1, source_target_pairs={{0,24},{4,28},{8,16},{12,20},{16,8},{20,12},{24,0},{28,4},{1,25},{... | collective-permute-start | bytes 786440 | tf_op jit(solution)/shard_map/ppermute | solution.py:871
  386.8 11.5 %copy-start.6 = (bf16[448,1024]{1,0:T(8,128)(2,1)S(1)}, bf16[448,1024]{1,0:T(8,128)(2,1)}, u32[]{:S(2)}) copy-start(bf16[448,1024]{1,0:T(8,128)(2,1)} %copy-done.5) | copy-start | bytes 2752516
  394.3 19.4 %collective-permute-start.17 = (bf16[4,2,16,1024]{3,2,0,1:T(8,128)(2,1)S(1)}, bf16[4,2,16,1024]{3,2,0,1:T(8,128)(2,1)S(1)}, u32[]{:S(2)}, u32[]{:S(2)}) collective-permute-start(bf16[4,2,16,1024]{3,2,0,1:T(8,128)(2,1)S(1)} %add_convert_fusion.5), channel_id=1, source_target_pairs={{0,16},{4,20},{8,24},{12,28},{16,0},{20,4},{24,8},{28,12},{1,17},{... | collective-permute-start | bytes 786440 | tf_op jit(solution)/shard_map/ppermute | solution.py:871
  394.4 19.4 %collective-permute-start.18 = (bf16[4,2,16,1024]{3,2,0,1:T(8,128)(2,1)S(1)}, bf16[4,2,16,1024]{3,2,0,1:T(8,128)(2,1)S(1)}, u32[]{:S(2)}, u32[]{:S(2)}) collective-permute-start(bf16[4,2,16,1024]{3,2,0,1:T(8,128)(2,1)S(1)} %add_convert_fusion.5), channel_id=1, source_target_pairs={{0,8},{4,12},{8,0},{12,4},{16,24},{20,28},{24,16},{28,20},{1,9},{5... | collective-permute-start | bytes 786440 | tf_op jit(solution)/shard_map/ppermute | solution.py:871
  397.0 21.5 %collective-permute-start.19 = (bf16[4,2,16,1024]{3,2,0,1:T(8,128)(2,1)S(1)}, bf16[4,2,16,1024]{3,2,0,1:T(8,128)(2,1)S(1)}, u32[]{:S(2)}, u32[]{:S(2)}) collective-permute-start(bf16[4,2,16,1024]{3,2,0,1:T(8,128)(2,1)S(1)} %add_convert_fusion.5), channel_id=1, source_target_pairs={{0,24},{4,28},{8,16},{12,20},{16,8},{20,12},{24,0},{28,4},{1,25},{... | collective-permute-start | bytes 786440 | tf_op jit(solution)/shard_map/ppermute | solution.py:871
  397.0 16.7 %collective-permute-start.20 = (f32[8,1024]{1,0:T(8,128)S(1)}, f32[8,1024]{1,0:T(8,128)S(1)}, u32[]{:S(2)}, u32[]{:S(2)}) collective-permute-start(f32[8,1024]{1,0:T(8,128)S(1)} %slice.145), channel_id=1, source_target_pairs={{0,8},{4,12},{8,0},{12,4},{16,24},{20,28},{24,16},{28,20},{1,9},{5... | collective-permute-start | bytes 98312 | tf_op jit(solution)/shard_map/ppermute | solution.py:871
  418.6 12.1 %collective-permute-start.22 = (bf16[4,64,1024]{2,1,0:T(8,128)(2,1)S(1)}, bf16[4,64,1024]{2,1,0:T(8,128)(2,1)}, u32[]{:S(2)}, u32[]{:S(2)}) collective-permute-start(bf16[4,64,1024]{2,1,0:T(8,128)(2,1)S(1)} %get-tuple-element.242), channel_id=1, source_target_pairs={{0,2},{1,3},{2,0},{3,1},{4,6},{5,7},{6,4},{7,5},{8,10},{9,11},{10,... | collective-permute-start | bytes 1572872 | tf_op jit(solution)/shard_map/ppermute | solution.py:871
  419.4 22.7 %collective-permute-start.21 = (bf16[4,64,1024]{2,1,0:T(8,128)(2,1)S(1)}, bf16[4,64,1024]{2,1,0:T(8,128)(2,1)}, u32[]{:S(2)}, u32[]{:S(2)}) collective-permute-start(bf16[4,64,1024]{2,1,0:T(8,128)(2,1)S(1)} %get-tuple-element.241), channel_id=1, source_target_pairs={{0,4},{4,0},{8,12},{12,8},{16,20},{20,16},{24,28},{28,24},{1,5},{5... | collective-permute-start | bytes 1572872 | tf_op jit(solution)/shard_map/ppermute | solution.py:871
  421.0 70.5 %all-to-all-start.6 = ((bf16[8,128,1024]{2,1,0:T(8,128)(2,1)}), bf16[8,128,1024]{2,1,0:T(8,128)(2,1)S(1)}, u32[]{:S(2)}, u32[]{:S(2)}) async-start(bf16[8,128,1024]{2,1,0:T(8,128)(2,1)} %bitcast.66), calls=%async_computation.6 | async-start | bytes 4194304 | tf_op jit(solution)/shard_map/all_to_all | solution.py:875
  443.1 35.3 %collective-permute-start.24 = (bf16[4,128,1024]{2,1,0:T(8,128)(2,1)S(1)}, bf16[4,128,1024]{2,1,0:T(8,128)(2,1)S(1)}, u32[]{:S(2)}, u32[]{:S(2)}) collective-permute-start(bf16[4,128,1024]{2,1,0:T(8,128)(2,1)S(1)} %pad_maximum_fusion.4), channel_id=1, source_target_pairs={{0,4},{4,0},{8,12},{12,8},{16,20},{20,16},{24,28},{28,24},{1,5},{5... | collective-permute-start | bytes 3145736 | tf_op jit(solution)/shard_map/ppermute | solution.py:871
  445.5 33.1 %collective-permute-start.23 = (bf16[4,128,1024]{2,1,0:T(8,128)(2,1)S(1)}, bf16[4,128,1024]{2,1,0:T(8,128)(2,1)S(1)}, u32[]{:S(2)}, u32[]{:S(2)}) collective-permute-start(bf16[4,128,1024]{2,1,0:T(8,128)(2,1)S(1)} %pad_maximum_fusion.3), channel_id=1, source_target_pairs={{0,2},{1,3},{2,0},{3,1},{4,6},{5,7},{6,4},{7,5},{8,10},{9,11},{10,... | collective-permute-start | bytes 3145736 | tf_op jit(solution)/shard_map/ppermute | solution.py:871
  445.5 25.2 %collective-permute-start.25 = (f32[8,1024]{1,0:T(8,128)S(1)}, f32[8,1024]{1,0:T(8,128)S(1)}, u32[]{:S(2)}, u32[]{:S(2)}) collective-permute-start(f32[8,1024]{1,0:T(8,128)S(1)} %slice.147), channel_id=1, source_target_pairs={{0,16},{4,20},{8,24},{12,28},{16,0},{20,4},{24,8},{28,12},{1,17},{... | collective-permute-start | bytes 98312 | tf_op jit(solution)/shard_map/ppermute | solution.py:871
  480.9 10.6 %collective-permute-start.26 = (bf16[1,512,1024]{2,1,0:T(8,128)(2,1)}, bf16[1,512,1024]{2,1,0:T(8,128)(2,1)}, u32[]{:S(2)}, u32[]{:S(2)}) collective-permute-start(bf16[1,512,1024]{2,1,0:T(8,128)(2,1)} %get-tuple-element.274.refs_0_), channel_id=1, source_target_pairs={{0,1},{1,0},{2,3},{3,2},{4,5},{5,4},{6,7},{7,6},{8,9},{9,8},{10,11... | collective-permute-start | bytes 3145736 | tf_op jit(solution)/shard_map/ppermute | solution.py:871
  483.1 8.4 %collective-permute-start.27 = (bf16[1,512,1024]{2,1,0:T(8,128)(2,1)}, bf16[1,512,1024]{2,1,0:T(8,128)(2,1)}, u32[]{:S(2)}, u32[]{:S(2)}) collective-permute-start(bf16[1,512,1024]{2,1,0:T(8,128)(2,1)} %get-tuple-element.273.refs_1_), channel_id=1, source_target_pairs={{0,1},{1,0},{2,3},{3,2},{4,5},{5,4},{6,7},{7,6},{8,9},{9,8},{10,11... | collective-permute-start | bytes 3145736 | tf_op jit(solution)/shard_map/ppermute | solution.py:871
  483.1 8.4 %collective-permute-start.28 = (bf16[1,512,1024]{2,1,0:T(8,128)(2,1)}, bf16[1,512,1024]{2,1,0:T(8,128)(2,1)}, u32[]{:S(2)}, u32[]{:S(2)}) collective-permute-start(bf16[1,512,1024]{2,1,0:T(8,128)(2,1)} %get-tuple-element.272.refs_2_), channel_id=1, source_target_pairs={{0,1},{1,0},{2,3},{3,2},{4,5},{5,4},{6,7},{7,6},{8,9},{9,8},{10,11... | collective-permute-start | bytes 3145736 | tf_op jit(solution)/shard_map/ppermute | solution.py:871
  483.6 7.9 %collective-permute-start.29 = (bf16[1,512,1024]{2,1,0:T(8,128)(2,1)S(1)}, bf16[1,512,1024]{2,1,0:T(8,128)(2,1)}, u32[]{:S(2)}, u32[]{:S(2)}) collective-permute-start(bf16[1,512,1024]{2,1,0:T(8,128)(2,1)S(1)} %get-tuple-element.271.refs_3_), channel_id=1, source_target_pairs={{0,1},{1,0},{2,3},{3,2},{4,5},{5,4},{6,7},{7,6},{8,9},{9,8},{10,11... | collective-permute-start | bytes 3145736 | tf_op jit(solution)/shard_map/ppermute | solution.py:871
  (6 other events, 23.7 us)
Sparse Core Ops, SparseCore 0:
  9.6 59.8 all-gather.4
  71.0 58.2 all-gather.2

commit v4 on v3

--- a/solution.py
+++ b/solution.py
@@ -278,31 +278,36 @@
     )(start_col, q, k, v)
 
 
-def leave_kernel(mixed, wo, bo, tokens, live_col, pos_col, *refs):
-    mixed_in, wo_in, tokens_in, kept, low, sems = refs[-6:]
-    outs = refs[:-6]
+def leave_kernel(
+    mixed, wo, bo, tokens, live_col, pos_col, out, residual, mixed_in, wo_in, tokens_in, kept, low, sems
+):
     copies = Copies(sems)
-    came = [copies.start(mixed, mixed_in), copies.start(wo, wo_in), copies.start(tokens, tokens_in)]
-    for copy in came:
-        copy.wait()
     count = kept.shape[0]
     half = count // 2
+    first = copies.start(wo, wo_in)
+    came = []
     for r in range(0, count, half):
         rows = pl.ds(r, half)
+        came.append(copies.start(mixed.at[rows], mixed_in.at[rows]))
+        came.append(copies.start(tokens.at[rows], tokens_in.at[rows]))
+    first.wait()
+    for r in range(0, count, half):
+        rows = pl.ds(r, half)
+        for copy in came[:2]:
+            copy.wait()
+        came = came[2:]
         branch = nn(mixed_in[rows, :], wo_in[...]) + bo[...]
         kept[rows, :] = (tokens_in[rows, :].astype(F32) + live_col[rows, :] * branch).astype(BF16)
-    piece = count // len(outs)
-    left = []
-    for n, out in enumerate(outs):
-        rows = pl.ds(n * piece, piece)
-        low[rows, :] = nn(pick_slots(pos_col[rows, :], count), kept[...]).astype(BF16)
-        left.append(copies.start(low.at[rows], out))
+    left = [copies.start(kept, residual)]
+    low[...] = nn(pick_slots(pos_col[...], count), kept[...]).astype(BF16)
+    left.append(copies.start(low, out))
     for copy in left:
         copy.wait()
 
 
-def leave(parts, mixed, wo, bo, tokens, live_col, pos_col):
+def leave(mixed, wo, bo, tokens, live_col, pos_col):
     count, width = mixed.shape
+    rows = pos_col.shape[0]
     return pl.pallas_call(
         leave_kernel,
         grid=(1,),
@@ -312,22 +317,44 @@
             whole((1, width)),
             ANYWHERE,
             whole((count, 1)),
-            whole((count, 1)),
+            whole((rows, 1)),
         ],
-        out_specs=[ANYWHERE] * parts,
-        out_shape=[jax.ShapeDtypeStruct((count // parts, width), BF16)] * parts,
+        out_specs=[ANYWHERE] * 2,
+        out_shape=[
+            jax.ShapeDtypeStruct((rows, width), BF16),
+            jax.ShapeDtypeStruct((count, width), BF16),
+        ],
         scratch_shapes=[
             pltpu.VMEM((count, width), BF16),
             pltpu.VMEM((width, width), BF16),
             pltpu.VMEM((count, width), BF16),
             pltpu.VMEM((count, width), BF16),
-            pltpu.VMEM((count, width), BF16),
-            pltpu.SemaphoreType.DMA((3 + parts,)),
+            pltpu.VMEM((rows, width), BF16),
+            pltpu.SemaphoreType.DMA((7,)),
         ],
         compiler_params=params(),
-        cost_estimate=cost(4 * count * width * width, 8 * count * width),
+        cost_estimate=cost(3 * count * width * width, 10 * count * width),
         name="leave",
     )(mixed, wo, bo, tokens, live_col, pos_col)
+
+
+def pick_kernel(residual, pos_col, out):
+    out[...] = nn(pick_slots(pos_col[...], residual.shape[0]), residual[...]).astype(BF16)
+
+
+def pick(residual, pos_col):
+    count, width = residual.shape
+    rows = pos_col.shape[0]
+    return pl.pallas_call(
+        pick_kernel,
+        grid=(1,),
+        in_specs=[whole((count, width)), whole((rows, 1))],
+        out_specs=whole((rows, width)),
+        out_shape=jax.ShapeDtypeStruct((rows, width), BF16),
+        compiler_params=params(),
+        cost_estimate=cost(2 * rows * count * width, 6 * count * width),
+        name="pick",
+    )(residual, pos_col)
 
 
 def reenter_kernel(parts, *refs):
@@ -461,10 +488,9 @@
     )(start_row, q, k, v, mixed, grad_mixed, lse)
 
 
-def finish_kernel(
-    grads, wq, wk, wv, tokens, grad_residual, gain, pos_col, others, out, sums,
-    grads_in, weights, tokens_in, residual_in, total, kept, sems
-):
+def finish_kernel(grads, wq, wk, wv, tokens, grad_residual, gain, pos_col, others, *refs):
+    outs, sums = refs[:-8], refs[-8]
+    grads_in, weights, tokens_in, residual_in, total, kept, sems = refs[-7:]
     copies = Copies(sems)
     came = []
     for n, w in enumerate((wq, wk, wv)):
@@ -501,22 +527,24 @@
         rows = pl.ds(r, half)
         chosen = pick_slots(pos_col[rows, :], count)
         residual_in[rows, :] = nn(chosen, kept[...]).astype(BF16)
-        left.append(copies.start(residual_in.at[rows], out.at[rows]))
+    start = 0
+    for out in outs:
+        rows = out.shape[0]
+        left.append(copies.start(residual_in.at[pl.ds(start, rows)], out))
+        start += rows
     for copy in left:
         copy.wait()
 
 
-def finish(grads, weights, tokens, grad_residual, gain, pos_col, others):
+def finish(sizes, grads, weights, tokens, grad_residual, gain, pos_col, others):
     count, width = tokens.shape
     return pl.pallas_call(
         finish_kernel,
         grid=(1,),
         in_specs=[ANYWHERE] * 6 + [whole((1, width)), whole((count, 1)), whole((8, width))],
-        out_specs=[ANYWHERE, whole((8, width))],
-        out_shape=[
-            jax.ShapeDtypeStruct((count, width), BF16),
-            jax.ShapeDtypeStruct((8, width), F32),
-        ],
+        out_specs=[ANYWHERE] * len(sizes) + [whole((8, width))],
+        out_shape=[jax.ShapeDtypeStruct((rows, width), BF16) for rows in sizes]
+        + [jax.ShapeDtypeStruct((8, width), F32)],
         scratch_shapes=[
             pltpu.VMEM((3, count, width), BF16),
             pltpu.VMEM((3, width, width), BF16),
@@ -524,7 +552,7 @@
             pltpu.VMEM((count, width), BF16),
             pltpu.VMEM((count, width), F32),
             pltpu.VMEM((count, width), BF16),
-            pltpu.SemaphoreType.DMA((10,)),
+            pltpu.SemaphoreType.DMA((8 + len(sizes),)),
         ],
         compiler_params=params(),
         cost_estimate=cost(8 * count * width * width, 20 * count * width),
@@ -705,12 +733,12 @@
     )(device, *mine, *theirs, *slots, downs, bias, live)
 
 
-CUTS = ((768, 256), (448, 576))
+CUTS = ((224, 800), (304, 400, 320))
 
 
 def expert_grads_kernel(count, *refs):
-    packets, near, fars = refs[:count], refs[count : count + 2], refs[count + 2 : count + 6]
-    far_act, branch, ffn_in, far_pre, near_act, near_pre, far_low, near_full, sems = refs[count + 6 :]
+    packets, near, fars = refs[:count], refs[count : count + 2], refs[count + 2 : -9]
+    far_act, branch, ffn_in, far_pre, near_act, near_pre, far_low, near_full, sems = refs[-9:]
     copies = Copies(sems)
     rows = packets[0].shape[1]
 
@@ -727,9 +755,9 @@
         for copy in came:
             copy.wait()
         far_low[m] = tn(one[...], two[...]).astype(BF16)
-        start = 0
+        start, skip = 0, sum(len(cuts) for cuts in CUTS[:m])
         for n, cut in enumerate(CUTS[m]):
-            left.append(copies.start(far_low.at[m, pl.ds(start, cut)], fars[2 * m + n]))
+            left.append(copies.start(far_low.at[m, pl.ds(start, cut)], fars[skip + n]))
             start += cut
 
     def close(m, came, one, two):
@@ -755,14 +783,14 @@
         functools.partial(expert_grads_kernel, count),
         grid=(1,),
         in_specs=[ANYWHERE] * count,
-        out_specs=[ANYWHERE] * 6,
+        out_specs=[ANYWHERE] * (2 + len(cuts)),
         out_shape=[jax.ShapeDtypeStruct((1, width, width), F32)] * 2
         + [jax.ShapeDtypeStruct((c, width), BF16) for c in cuts],
         scratch_shapes=[pltpu.VMEM((count * rows, width), BF16)] * 6
         + [
             pltpu.VMEM((2, width, width), BF16),
             pltpu.VMEM((2, width, width), F32),
-            pltpu.SemaphoreType.DMA((6 * count + 6,)),
+            pltpu.SemaphoreType.DMA((6 * count + 2 + len(cuts),)),
         ],
         compiler_params=params(),
         cost_estimate=cost(8 * count * rows * width * width, 30 * width * width),
@@ -826,44 +854,66 @@
     )(layout.codes, normed, mixed, token_grads, grad_proj)
 
 
-def unmix_kernel(group, number, codes, half_place, *refs):
-    pieces, outs = refs[:number], refs[-number:]
-    size = outs[0].shape[0] // group
-    code = codes[pl.program_id(0) // 2] % group
-    for piece, out in zip(pieces, outs):
-        for j in range(group):
-            place = pl.multiple_of((code ^ j) * size, size)
-            out[pl.ds(place, size), :] = piece[0, pl.ds(j * size, size), :].astype(F32)
-
-
-def unmix(layout, half_place, pieces, before=None):
-    number = len(pieces)
-    _, rows, width = pieces[0].shape
+def unmix_kernel(group, parts, codes, half_place, source, pieces, *refs):
+    rows_in, came_in, full, sems = refs[-4:]
+    number, half, _ = came_in.shape
+    outs = refs[-4 - number - min(parts, 1) : -4]
+    copies = Copies(sems)
+    came = [copies.start(pieces.at[m], came_in.at[m]) for m in range(number)]
+    joined, left = [], []
+    for r in range(parts):
+        size = refs[r].shape[0]
+        place = pl.multiple_of(source[r] * size, size)
+        joined.append(copies.start(refs[r], rows_in.at[pl.ds(place, size)]))
+    rows = half // 4
+    size = rows // group
+    for m in range(number):
+        came[m].wait()
+        for n in range(4):
+            code = codes[n // 2]
+            low = code % group
+            block = n ^ ((code // group) % 2)
+            for j in range(group):
+                place = pl.multiple_of(block * rows + (low ^ j) * size, size)
+                start = n * rows + j * size
+                full[m, pl.ds(place, size), :] = came_in[m, start : start + size, :].astype(F32)
+        target = outs[m].at[pl.ds(pl.multiple_of(half_place[0] * half, half), half)]
+        left.append(copies.start(full.at[m], target))
+        if m == 0 and parts:
+            for copy in joined:
+                copy.wait()
+            left.append(copies.start(rows_in, outs[number]))
+    for copy in left:
+        copy.wait()
+
+
+def unmix(layout, half_place, pieces, before=None, source=None, joined=()):
+    number, rows, width = pieces.shape
     earlier = [] if before is None else list(before)
-    group = layout.blocks // 8
-    part = rows // 4
-
-    def place(i, codes, half_place):
-        return (0, i ^ ((codes[i // 2] // group) % 2), 0)
-
+    parts = len(joined)
+    source = half_place if source is None else source
+    total = sum(v.shape[0] for v in joined)
     return pl.pallas_call(
-        functools.partial(unmix_kernel, group, number),
+        functools.partial(unmix_kernel, layout.blocks // 8, parts),
         grid_spec=pltpu.PrefetchScalarGridSpec(
-            num_scalar_prefetch=2,
-            grid=(4,),
-            in_specs=[pl.BlockSpec((1, part, width), place)] * number
-            + [pl.BlockSpec(memory_space=pl.ANY)] * len(earlier),
-            out_specs=[
-                pl.BlockSpec((part, width), lambda i, codes, half_place: (half_place[0] * 4 + i, 0))
-            ]
-            * number,
+            num_scalar_prefetch=3,
+            grid=(1,),
+            in_specs=[ANYWHERE] * (1 + parts + len(earlier)),
+            out_specs=[ANYWHERE] * (number + min(parts, 1)),
+            scratch_shapes=[
+                pltpu.VMEM((max(total, 16), width), BF16),
+                pltpu.VMEM((number, rows, width), BF16),
+                pltpu.VMEM((number, rows, width), F32),
+                pltpu.SemaphoreType.DMA((2 * number + parts + 1,)),
+            ],
         ),
-        out_shape=[jax.ShapeDtypeStruct((2 * rows, width), F32)] * number,
-        input_output_aliases={2 + number + m: m for m in range(len(earlier))},
+        out_shape=[jax.ShapeDtypeStruct((2 * rows, width), F32)] * number
+        + [jax.ShapeDtypeStruct((total, width), BF16)] * min(parts, 1),
+        input_output_aliases={4 + parts + m: m for m in range(len(earlier))},
         compiler_params=params(),
         cost_estimate=cost(number * rows * width, 6 * number * rows * width),
         name="unmix",
-    )(layout.codes, half_place, *pieces, *earlier)
+    )(layout.codes, half_place, source, pieces, *joined, *earlier)
 
 
 def swap(values, step):
@@ -927,9 +977,16 @@
         return jnp.concatenate([values, swap(values, step)], axis=axis)
 
     def reduce_first(self, keep, send):
-        total = add_low(keep, swap(send, self.first))
-        middle = total.shape[1] // 2
-        return [total[:, :middle], total[:, middle:]]
+        came = swap(send, self.first)
+        size = keep.shape[1] // 4
+        quarter = lambda v, n: lax.slice_in_dim(v, n * size, (n + 1) * size, axis=1)
+        return [add_low(quarter(keep, n), quarter(came, n)) for n in range(4)]
+
+    def reduce_pair_first(self, quarters):
+        return [
+            add_low(quarters[2 * n], swap(quarters[2 * n + 1], self.pair[n][0]))
+            for n in range(self.streams)
+        ]
 
     def reduce_pair(self, parts, n):
         return [self.halve(part, pair[n], 1) for part, pair in zip(parts, self.pair)]
@@ -957,9 +1014,8 @@
 
     def gather_first(self, parts):
         total = jnp.concatenate(parts, axis=1)
-        pieces = [total[m : m + 1] for m in range(total.shape[0])]
         mine = ((lax.axis_index(self.first[0]) // self.first[2]) % 2).astype(jnp.int32).reshape(1)
-        return (mine, pieces), (1 - mine, [swap(v, self.first) for v in pieces])
+        return (mine, total), (1 - mine, swap(total, self.first))
 
 
 def small_sum(values, steps):
@@ -1021,16 +1077,32 @@
     live_col = live.astype(F32).reshape(count, 1)
     in_chunks = position.reshape(n_expert, CHUNKS, -1).transpose(1, 0, 2).reshape(count)
     slot_live = (position < total_live).astype(F32).reshape(n_expert, piece)
+    start_row, start_col = begin.reshape(1, count), begin.reshape(count, 1)
+    pos_row, pos_col = position.reshape(1, count), position.reshape(count, 1)
+    chunk_row, chunk_col = in_chunks.reshape(1, count), in_chunks.reshape(count, 1)
+    shared = SharedSum(n_expert, n_dp, width)
+    expert = lax.axis_index("expert")
+    codes = jnp.concatenate([jnp.arange(xs, n_expert, 2, dtype=jnp.int32) for xs in range(2)])
+    partners = (expert ^ codes).astype(jnp.int32)
+    leave_col = jnp.take(position.reshape(n_expert, piece), partners, axis=0).reshape(count, 1)
+    leave_col, partners = tie(leave_col, partners)
+    arrived, start_row, start_col, pos_row, pos_col, chunk_row, chunk_col, live_col, shared.codes = tie(
+        arrived, start_row, start_col, pos_row, pos_col, chunk_row, chunk_col, live_col, shared.codes
+    )
     route_live = exchange(slot_live).reshape(n_expert, piece, 1)
 
     tokens, normed, query, key, value = entry(
-        arrived, position.reshape(1, count), row(first_gain), row(first_bias), query_weight,
+        arrived, pos_row, row(first_gain), row(first_bias), query_weight,
         row(query_bias), key_weight, value_weight, row(value_bias),
     )
-    mixed, lse = attend(begin.reshape(count, 1), query, key, value)
-    sent = leave(
-        CHUNKS, mixed, out_weight, row(out_bias), tokens, live_col, in_chunks.reshape(count, 1)
+    mixed, lse = attend(start_col, query, key, value)
+    some = count // CHUNKS
+    first, residual = leave(
+        mixed, out_weight, row(out_bias), tokens, live_col, chunk_col[:some]
     )
+    sent = [first] + [
+        pick(residual, chunk_col[c * some : (c + 1) * some]) for c in range(1, CHUNKS)
+    ]
     routed = [exchange(sent[0])]
 
     blocks = lambda v: v.reshape(n_expert, piece, width)
@@ -1057,79 +1129,97 @@
     returned.append(exchange(grads[-1]))
     got[-1] = swap(theirs[-1], core)
 
-    *near, down_a, down_b, up_a, up_b = expert_grads([*mine, *got])
+    *near, down_a, down_b, up_a, up_b, up_c = expert_grads([*mine, *got])
     sums, up_sums = sum(sums), sum(up_sums)
     empty = jnp.zeros((8, width), F32)
     biases = jnp.concatenate([up_sums.reshape(-1, width), sums[2:3], empty[: 7 - n_dp]], axis=0)
 
-    fars = [down_a, down_b, up_a, up_b]
+    fars = [down_a, down_b, up_a, up_b, up_c]
 
     def over_y(n):
         fars[n] = swap(fars[n], far)
 
     returned, near, fars, biases = tie(returned, near, fars, biases)
     grad_residual, grad_proj, grad_mixed, out_bias_sum = reenter(
-        returned, in_chunks.reshape(1, count), live_col, out_weight
+        returned, chunk_row, live_col, out_weight
     )
-    others = jnp.concatenate([empty[:4], out_bias_sum, sums[0:2], empty[:1]], axis=0)
-    grad_mixed, fars, others = tie(grad_mixed, fars, others)
-    shared = SharedSum(n_expert, n_dp, width)
+    over_y(0)
+    grad_mixed, fars = tie(grad_mixed, fars)
     unstack = lambda v: [v[:, n] for n in range(shared.streams)]
 
-    over_y(0)
+    over_y(1)
     token_grads = attend_back(
-        begin.reshape(1, count), query, key, value, mixed, grad_mixed, lse
+        start_row, query, key, value, mixed, grad_mixed, lse
     )
     token_grads, fars = tie(token_grads, fars)
 
-    over_y(1)
+    over_y(2)
     halves = shared_grads(shared, normed, mixed, token_grads, grad_proj)
-    token_grads, halves, fars = tie(token_grads, halves, fars)
-
-    over_y(2)
-    leaving, token_sums = finish(
-        token_grads, [query_weight, key_weight, value_weight], tokens, grad_residual,
-        row(first_gain), position.reshape(count, 1), others,
+    token_grads, halves, fars, out_bias_sum = tie(token_grads, halves, fars, out_bias_sum)
+
+    others = jnp.concatenate([empty[:4], out_bias_sum, sums[0:2], empty[:1]], axis=0)
+    total = shared.reduce_first(*halves)
+    token_grads, total, others = tie(token_grads, total, others)
+
+    side = n_expert // 2
+    *leaving, token_sums = finish(
+        [piece] * side + [piece * side // 2] * 2, token_grads, [query_weight, key_weight, value_weight],
+        tokens, grad_residual, row(first_gain), leave_col, others,
     )
-    total = shared.reduce_first(*halves)
-    small = jnp.concatenate([token_sums, biases], axis=0)
-    leaving, total, small, fars = tie(leaving, total, small, fars)
-
+    total = shared.reduce_pair_first(total)
+    leaving, token_sums, total = tie(leaving, token_sums, total)
+
+    *stay, cross, cross_rest = leaving
+    to_partner = lambda v, j: swap(v, ("expert", n_expert, 2 * j))
+    early = range(1, 1 + (2 * side - 2 + 2) // 3)
+    late = range(early.stop, side)
     small_steps = list(shared.steps)
     small_step = lambda v: small_sum(v, [small_steps.pop(0)])
-    total = shared.reduce_pair(total, 0)
+    small = jnp.concatenate([token_sums, biases], axis=0)
+    for j in early:
+        stay[j] = to_partner(stay[j], j)
     small = small_step(small)
-    total, small = tie(total, small)
-
     total = jnp.stack(shared.reduce_pair(total, 1), axis=1)
-    small = small_step(small)
-    total, small, fars, mine = tie(total, small, fars, mine)
+    total, small, fars, mine, stay, cross, cross_rest = tie(
+        total, small, fars, mine, stay, cross, cross_rest
+    )
 
     over_y(3)
+    cross = swap(cross, ("expert", n_expert, 1))
     block_out = expert_out(place, mine, theirs, routed, downs, row(expert_down_bias[0]), route_live)
     total = shared.reduce_rest(total)
-    small = small_step(small)
-    total, small, block_out, near, fars = tie(total, small, block_out, near, fars)
-
+    total, small, block_out, near, fars, cross, cross_rest = tie(
+        total, small, block_out, near, fars, cross, cross_rest
+    )
+
+    over_y(4)
     total = unstack(shared.gather_rest(total))
     grad_down = near[0] + jnp.concatenate(fars[:2], axis=0).astype(F32)[None]
+    cross_rest = swap(cross_rest, ("expert", n_expert, 1))
+    total, small, grad_down, fars, stay, cross, cross_rest = tie(
+        total, small, grad_down, fars, stay, cross, cross_rest
+    )
+    across = [v[j * piece : (j + 1) * piece] for v in (cross, cross_rest) for j in range(side // 2)]
+
+    for j in late:
+        stay[j] = to_partner(stay[j], j)
+    across[1] = to_partner(across[1], 1)
+    small = small_step(small_step(small))
+    total = shared.gather_pair(total, 1)
     grad_up = near[1] + jnp.concatenate(fars[2:], axis=0).astype(F32)[None]
-    small = small_step(small)
-    total, small, grad_down, grad_up, leaving = tie(total, small, grad_down, grad_up, leaving)
-
-    input_grad = exchange(leaving)
-    total = shared.gather_pair(total, 1)
-    total, small = tie(total, small)
-
+    total, small, stay, across, grad_up = tie(total, small, stay, across, grad_up)
+
+    for j in range(2, side):
+        across[j] = to_partner(across[j], j)
     total = shared.gather_pair(total, 0)
     small = small_sum(small, small_steps)
-    total, small = tie(total, small)
+    total, small, across = tie(total, small, across)
 
     nearest, farthest = shared.gather_first(total)
     grads = unmix(shared, *nearest)
-    grads, farthest, input_grad = tie(grads, farthest, input_grad)
-    grad_query_weight, grad_key_weight, grad_value_weight, grad_out_weight = unmix(
-        shared, *farthest, grads
+    grads, farthest = tie(grads, farthest)
+    grad_query_weight, grad_key_weight, grad_value_weight, grad_out_weight, input_grad = unmix(
+        shared, *farthest, grads, partners, [*stay, *across]
     )
     share = width // n_dp
     grad_up_bias = lax.dynamic_slice_in_dim(small, 8 + device, 1, 0)

time: 515 us -> 493 us (0.957)
  blocking collectives: 29.5 us -> 0 us
  starting transfers between devices: 58.6 us -> 71.8 us
  waiting for transfers between devices: 142 us -> 135 us
    all_to_all x1 -> x0, blocking collectives: 29.5 us -> none  [exchange(): lax.all_to_all(values, 'expert', split_axis=0, concat_axis=0, tiled=True)]
    ppermute x30 -> x36, waiting for transfers between devices: 102 us -> 76.9 us  [swap(): return lax.ppermute(values, axis, [(i, i ^ bit) for i in range(size)])]
    all_to_all x6, waiting for transfers between devices: 39.2 us -> 57 us  [exchange(): lax.all_to_all(values, 'expert', split_axis=0, concat_axis=0, tiled=True)]
    ppermute x30 -> x36, starting transfers between devices: 26.9 us -> 36.5 us  [swap(): return lax.ppermute(values, axis, [(i, i ^ bit) for i in range(size)])]
    add x0 -> x1, other arithmetic: none -> 5.36 us  [per_device(): grad_down = near[0] + jnp.concatenate(fars[:2], axis=0).astype(F32)[None]]
    pallas_call x2 -> x3, Pallas kernels: 13.3 us -> 17 us  [the longest x2 13.1 us: unmix(): pl.pallas_call(functools.partial(unmix_kernel, layout.blocks // 8, parts)...]
  transfers between devices with their start and end apart: 38 -> 44, of which waited for: 14 -> 22; matrix products, arithmetic and copies ran while one was open for 7% -> 6% of each run, Pallas kernels for 40% -> 44%
where the time goes in v4:
time: 493 us; the launch traced here: 486 us
  Pallas kernels  222 us (45%)
  waiting for transfers between devices  135 us (27%)
  starting transfers between devices  71.8 us (15%)
  other arithmetic  28.5 us (6%)
  between operations  15.3 us (3%)
  local copies, waits for them, and re-layouts  13.1 us (3%)
    ppermute x36, waiting for transfers between devices, swap(): return lax.ppermute(values, axis, [(i, i ^ bit) for i in range(size)])  76.9 us
    all_to_all x6, waiting for transfers between devices, exchange(): lax.all_to_all(values, 'expert', split_axis=0, concat_axis=0, tiled=True)  57 us
    pallas_call x2, Pallas kernels, expert_chunk(): pl.pallas_call(expert_kernel, grid_spec=pltpu.PrefetchScalarGridSpec(num_...  46.6 us
    ppermute x36, starting transfers between devices, swap(): return lax.ppermute(values, axis, [(i, i ^ bit) for i in range(size)])  36.5 us
    pallas_call x1, Pallas kernels, attend_back(): pl.pallas_call(attend_back_kernel, grid=(pairs,), in_specs=[whole((1, cou...  36.1 us
    all_to_all x6, starting transfers between devices, exchange(): lax.all_to_all(values, 'expert', split_axis=0, concat_axis=0, tiled=True)  35.3 us
    pallas_call x1, Pallas kernels, expert_grads(): pl.pallas_call(functools.partial(expert_grads_kernel, count), grid=(1,),...  23.8 us
    pallas_call x1, Pallas kernels, attend(): pl.pallas_call(attend_kernel, grid=(pairs,), in_specs=[whole((count, 1)),...  19.1 us
  transfers between devices with their start and end apart: 44, of which 22 were waited for; matrix products, arithmetic and copies ran while one was open for 6% of the time, Pallas kernels for 44%

profile of v4, /device:TPU:9, one launch (start us, length us, event | category | flops | bytes accessed | tf_op | source)
XLA Modules:
  0.0 485.5 jit_solution(15820916117044000894)
XLA Ops:
  8.7 5.7 %all-to-all-start = ((bf16[8,128,1024]{2,1,0:T(8,128)(2,1)}), bf16[8,128,1024]{2,1,0:T(8,128)(2,1)S(1)}, u32[]{:S(2)}, u32[]{:S(2)}) async-start(bf16[8,128,1024]{2,1,0:T(8,128)(2,1)} %bitcast), calls=%async_computation | async-start | bytes 4194304 | tf_op jit(solution)/shard_map/all_to_all | solution.py:925
  23.7 37.3 %all-to-all-done = bf16[8,128,1024]{2,1,0:T(8,128)(2,1)S(1)} async-done(((bf16[8,128,1024]{2,1,0:T(8,128)(2,1)}), bf16[8,128,1024]{2,1,0:T(8,128)(2,1)S(1)}, u32[]{:S(2)}, u32[]{:S(2)}) %all-to-all-start) | async-done | bytes 2097184 | tf_op jit(solution)/shard_map/all_to_all | solution.py:925
  60.9 5.5 %all-to-all-start.3 = ((f32[8,1,128]{2,1,0:T(1,128)}), f32[8,1,128]{2,1,0:T(1,128)S(1)}, u32[]{:S(2)}, u32[]{:S(2)}) async-start(f32[8,1,128]{2,1,0:T(1,128)} %fusion.4), calls=%async_computation.3 | async-start | bytes 8192 | tf_op jit(solution)/shard_map/all_to_all | solution.py:925
  67.5 13.7 %entry.1 = (bf16[1024,1024]{1,0:T(8,128)(2,1)}, bf16[1024,1024]{1,0:T(8,128)(2,1)}, bf16[1024,1024]{1,0:T(8,128)(2,1)}, bf16[1024,1024]{1,0:T(8,128)(2,1)}, bf16[1024,1024]{1,0:T(8,128)(2,1)}) custom-call(bf16[1024,1024]{1,0:T(8,128)(2,1)} %bitcast.71, s32[1,1024]{1,0:T(1,128)} %pos_row, f32[1,1024]{1,0:T(1,128)} %bitcast.111, f32[1,1024]{1,0:T(1,128)} %bitcast.103, ...), custom_call_target="tpu_custom_call" | custom-call | flops 8589934592 | bytes 18874368 | tf_op jit(solution)/shard_map/entry/pallas_call | solution.py:126
  81.2 19.1 %attend.1 = (bf16[1024,1024]{1,0:T(8,128)(2,1)}, f32[8,8,1024]{2,1,0:T(8,128)}) custom-call(s32[1024,1]{1,0:T(8,128)} %iota_select_fusion.start_col, bf16[1024,1024]{1,0:T(8,128)(2,1)} %get-tuple-element.198.q_ref, bf16[1024,1024]{1,0:T(8,128)(2,1)} %get-tuple-element.199.k_ref, bf16[1024,1024]{1,0:T(8,128)(2,1)} %get-tuple-element.200.v_ref), custom_call_target="tpu_custom_call" | custom-call | flops 8589934592 | bytes 8388608 | tf_op jit(solution)/shard_map/attend/pallas_call | solution.py:261
  100.3 8.0 %leave.1 = (bf16[512,1024]{1,0:T(8,128)(2,1)}, bf16[1024,1024]{1,0:T(8,128)(2,1)}) custom-call(bf16[1024,1024]{1,0:T(8,128)(2,1)} %get-tuple-element.202.mixed.o_ref, bf16[1024,1024]{1,0:T(8,128)(2,1)} %refs_4_.1, f32[1,1024]{1,0:T(1,128)} %bitcast.106, bf16[1024,1024]{1,0:T(8,128)(2,1)} %get-tuple-element.203.tokens, f32[1024,1]{1,0:T(8,128)} %fusion.2.live_col.refs_3_, ...), custom_call_target="tpu_custom_call" | custom-call | flops 3221225472 | bytes 10485760 | tf_op jit(solution)/shard_map/leave/pallas_call | solution.py:311
  108.3 5.5 %all-to-all-start.2 = ((bf16[8,64,1024]{2,1,0:T(8,128)(2,1)}), bf16[8,64,1024]{2,1,0:T(8,128)(2,1)S(1)}, u32[]{:S(2)}, u32[]{:S(2)}) async-start(bf16[8,64,1024]{2,1,0:T(8,128)(2,1)} %bitcast.79), calls=%async_computation.2 | async-start | bytes 2097152 | tf_op jit(solution)/shard_map/all_to_all | solution.py:925
  113.8 3.8 pick.1
  117.6 19.1 %all-to-all-done.2 = bf16[8,64,1024]{2,1,0:T(8,128)(2,1)S(1)} async-done(((bf16[8,64,1024]{2,1,0:T(8,128)(2,1)}), bf16[8,64,1024]{2,1,0:T(8,128)(2,1)S(1)}, u32[]{:S(2)}, u32[]{:S(2)}) %all-to-all-start.2) | async-done | bytes 1048608 | tf_op jit(solution)/shard_map/all_to_all | solution.py:925
  136.7 7.1 %all-to-all-start.1 = ((bf16[8,64,1024]{2,1,0:T(8,128)(2,1)}), bf16[8,64,1024]{2,1,0:T(8,128)(2,1)S(1)}, u32[]{:S(2)}, u32[]{:S(2)}) async-start(bf16[8,64,1024]{2,1,0:T(8,128)(2,1)} %bitcast.77), calls=%async_computation.1 | async-start | bytes 2097152 | tf_op jit(solution)/shard_map/all_to_all | solution.py:925
  144.8 23.3 %expert_chunk.2 = (bf16[512,1024]{1,0:T(8,128)(2,1)}, bf16[6,512,1024]{2,1,0:T(8,128)(2,1)}, bf16[6,512,1024]{2,1,0:T(8,128)(2,1)}, f32[8,1024]{1,0:T(8,128)}, f32[4,1,1024]{2,1,0:T(1,128)}) custom-call(s32[1]{0:T(128)} %bitcast.16.device, bf16[512,1024]{1,0:T(8,128)(2,1)} %bitcast.67, bf16[8,128,1024]{2,1,0:T(8,128)(2,1)} %bitcast.99, ...), custom_call_target="tpu_custom_call" | custom-call | flops 12884901888 | bytes 16777216 | tf_op jit(solution)/shard_map/expert_chunk/pallas_call | solution.py:646
  169.3 5.7 %all-to-all-start.4 = ((bf16[8,64,1024]{2,1,0:T(8,128)(2,1)}), bf16[8,64,1024]{2,1,0:T(8,128)(2,1)S(1)}, u32[]{:S(2)}, u32[]{:S(2)}) async-start(bf16[8,64,1024]{2,1,0:T(8,128)(2,1)} %bitcast.78), calls=%async_computation.4 | async-start | bytes 2097152 | tf_op jit(solution)/shard_map/all_to_all | solution.py:925
  175.0 23.3 %expert_chunk.3 = (bf16[512,1024]{1,0:T(8,128)(2,1)}, bf16[6,512,1024]{2,1,0:T(8,128)(2,1)}, bf16[6,512,1024]{2,1,0:T(8,128)(2,1)}, f32[8,1024]{1,0:T(8,128)}, f32[4,1,1024]{2,1,0:T(1,128)}) custom-call(s32[1]{0:T(128)} %bitcast.16.device, bf16[512,1024]{1,0:T(8,128)(2,1)} %bitcast.69, bf16[8,128,1024]{2,1,0:T(8,128)(2,1)} %bitcast.100, ...), custom_call_target="tpu_custom_call" | custom-call | flops 12884901888 | bytes 16777216 | tf_op jit(solution)/shard_map/expert_chunk/pallas_call | solution.py:646
  201.0 5.9 %all-to-all-start.5 = ((bf16[8,64,1024]{2,1,0:T(8,128)(2,1)}), bf16[8,64,1024]{2,1,0:T(8,128)(2,1)S(1)}, u32[]{:S(2)}, u32[]{:S(2)}) async-start(bf16[8,64,1024]{2,1,0:T(8,128)(2,1)} %bitcast.75), calls=%async_computation.5 | async-start | bytes 2097152 | tf_op jit(solution)/shard_map/all_to_all | solution.py:925
  206.9 2.6 collective-permute-done.1.refs_3_
  209.5 23.8 %expert_grads.1 = (f32[1,1024,1024]{2,1,0:T(8,128)}, f32[1,1024,1024]{2,1,0:T(8,128)}, bf16[224,1024]{1,0:T(8,128)(2,1)}, bf16[800,1024]{1,0:T(8,128)(2,1)}, bf1...) custom-call(bf16[6,512,1024]{2,1,0:T(8,128)(2,1)} %get-tuple-element.298.refs_0_, ...), custom_call_target="tpu_custom_call" | custom-call | flops 17179869184 | bytes 31457280 | tf_op jit(solution)/shard_map/expert_grads/pallas_call | solution.py:782
  234.7 9.4 %reenter.1 = (bf16[1024,1024]{1,0:T(8,128)(2,1)}, bf16[1024,1024]{1,0:T(8,128)(2,1)}, bf16[1024,1024]{1,0:T(8,128)(2,1)}, f32[1,1024]{1,0:T(1,128)}) custom-call(bf16[512,1024]{1,0:T(8,128)(2,1)} %bitcast.74, bf16[512,1024]{1,0:T(8,128)(2,1)} %bitcast.76, s32[1,1024]{1,0:T(1,128)} %reshape_reshape.6.refs_2_, f32[1024,1]{1,0:T(8,128)} %fusion.2.live_col.refs_3_, ...), custom_call_target="tpu_custom_call" | custom-call | flops 4294967296 | bytes 10485760 | tf_op jit(solution)/shard_map/reenter/pallas_call | solution.py:401
  247.4 36.1 %attend_back.1.token_grads.grads = bf16[3,1024,1024]{2,1,0:T(8,128)(2,1)} custom-call(s32[1,1024]{1,0:T(1,128)} %compare_select_fusion.start_row, bf16[1024,1024]{1,0:T(8,128)(2,1)} %get-tuple-element.198.q_ref, bf16[1024,1024]{1,0:T(8,128)(2,1)} %get-tuple-element.199.k_ref, bf16[1024,1024]{1,0:T(8,128)(2,1)} %get-tuple-element.200.v_ref, ...), custom_call_target="tpu_custom_call" | custom-call | flops 21474836480 | bytes 16777216 | tf_op jit(solution)/shard_map/attend_back/pallas_call | solution.py:476
  283.8 14.2 %shared_grads.1 = (bf16[4,512,1024]{2,1,0:T(8,128)(2,1)}, bf16[4,512,1024]{2,1,0:T(8,128)(2,1)}) custom-call(s32[2]{0:T(128)} %pad_add_fusion.codes, bf16[1024,1024]{1,0:T(8,128)(2,1)} %get-tuple-element.252.normed, bf16[1024,1024]{1,0:T(8,128)(2,1)} %get-tuple-element.202.mixed.o_ref, bf16[3,1024,1024]{2,1,0:T(8,128)(2,1)} %attend_back.1.token_grads.grads, ...), custom_call_target="tpu_custom_call" | custom-call | flops 8589934592 | bytes 25165824 | tf_op jit(solution)/shard_map/shared_grads/pallas_call | solution.py:835
  298.1 2.5 collective-permute-start.5
  301.4 6.1 %collective-permute-done.5 = bf16[4,512,1024]{2,1,0:T(8,128)(2,1)S(1)} collective-permute-done((bf16[4,512,1024]{2,1,0:T(8,128)(2,1)}, bf16[4,512,1024]{2,1,0:T(8,128)(2,1)S(1)}, u32[]{:S(2)}, u32[]{:S(2)}) %collective-permute-start.5) | collective-permute-done | bytes 4194336 | tf_op jit(solution)/shard_map/ppermute | solution.py:921
  307.5 4.5 add_convert_fusion.2
  315.8 18.2 %finish.1 = (bf16[128,1024]{1,0:T(8,128)(2,1)}, bf16[128,1024]{1,0:T(8,128)(2,1)}, bf16[128,1024]{1,0:T(8,128)(2,1)}, bf16[128,1024]{1,0:T(8,128)(2,1)}, bf16[25...) custom-call(bf16[3,1024,1024]{2,1,0:T(8,128)(2,1)} %attend_back.1.token_grads.grads, ...), custom_call_target="tpu_custom_call" | custom-call | flops 8589934592 | bytes 20971520 | tf_op jit(solution)/shard_map/finish/pallas_call | solution.py:541
  334.0 2.7 collective-permute-done.7
  336.8 1.6 add_convert_fusion
  339.2 1.9 add_convert_fusion.1
  342.8 2.1 collective-permute-start.10
  344.9 2.3 collective-permute-start.11
  348.0 5.1 %collective-permute-done.8 = bf16[4,64,1024]{2,1,0:T(8,128)(2,1)S(1)} collective-permute-done((bf16[4,64,1024]{2,1,0:T(8,128)(2,1)S(1)}, bf16[4,64,1024]{2,1,0:T(8,128)(2,1)S(1)}, u32[]{:S(2)}, u32[]{:S(2)}) %collective-permute-start.8) | collective-permute-done | bytes 524320 | tf_op jit(solution)/shard_map/ppermute | solution.py:921
  353.9 4.0 collective-permute-done.11.refs_1_
  358.0 2.2 collective-permute-done.12.refs_2_
  361.1 2.2 collective-permute-start.13
  365.7 15.5 %expert_out.1 = bf16[8,128,1024]{2,1,0:T(8,128)(2,1)} custom-call(s32[1]{0:T(128)} %bitcast.16.device, bf16[6,512,1024]{2,1,0:T(8,128)(2,1)} %get-tuple-element.298.refs_0_, bf16[6,512,1024]{2,1,0:T(8,128)(2,1)} %get-tuple-element.299.refs_1_, bf16[6,512,1024]{2,1,0:T(8,128)(2,1)} %get-tuple-element.212.refs_2_, ...), custom_call_target="tpu_custom_call" | custom-call | flops 8589934592 | bytes 16777216 | tf_op jit(solution)/shard_map/expert_out/pallas_call | solution.py:716
  381.2 4.5 collective-permute-done.15
  387.1 3.4 collective-permute-start.19
  392.7 5.4 %convert_add_fusion.1 = f32[1,1024,1024]{2,1,0:T(8,128)} fusion(f32[1,1024,1024]{2,1,0:T(8,128)} %get-tuple-element.312, bf16[1,800,1024]{2,1,0:T(8,128)(2,1)S(1)} %bitcast.73, bf16[1,224,1024]{2,1,0:T(8,128)(2,1)} %bitcast.83), kind=kLoop, calls=%fused_computation.2 | loop fusion | flops 5242880 | bytes 10485760 | tf_op jit(solution)/shard_map/add | solution.py:1197
  398.1 3.9 collective-permute-done.19
  402.0 10.7 %collective-permute-done.20 = bf16[4,2,16,1024]{3,2,0,1:T(8,128)(2,1)S(1)} collective-permute-done((bf16[4,2,16,1024]{3,2,0,1:T(8,128)(2,1)S(1)}, bf16[4,2,16,1024]{3,2,0,1:T(8,128)(2,1)S(1)}, u32[]{:S(2)}, u32[]{:S(2)}) %collective-permute-start.20) | collective-permute-done | bytes 262176 | tf_op jit(solution)/shard_map/ppermute | solution.py:921
  416.0 2.8 convert_add_fusion
  419.6 7.7 %collective-permute-done.26 = f32[16,1024]{1,0:T(8,128)S(1)} collective-permute-done((f32[16,1024]{1,0:T(8,128)S(1)}, f32[16,1024]{1,0:T(8,128)S(1)}, u32[]{:S(2)}, u32[]{:S(2)}) %collective-permute-start.26) | collective-permute-done | bytes 65568 | tf_op jit(solution)/shard_map/ppermute | solution.py:921
  429.4 1.5 collective-permute-start.31
  432.3 1.6 collective-permute-start.32
  436.4 13.2 %collective-permute-done.30 = bf16[4,128,1024]{2,1,0:T(8,128)(2,1)S(1)} collective-permute-done((bf16[4,128,1024]{2,1,0:T(8,128)(2,1)S(1)}, bf16[4,128,1024]{2,1,0:T(8,128)(2,1)S(1)}, u32[]{:S(2)}, u32[]{:S(2)}) %collective-permute-start.30) | collective-permute-done | bytes 1048608 | tf_op jit(solution)/shard_map/ppermute | solution.py:921
  451.4 7.3 %collective-permute-done.34.refs_7_ = bf16[128,1024]{1,0:T(8,128)(2,1)S(1)} collective-permute-done((bf16[128,1024]{1,0:T(8,128)(2,1)S(1)}, bf16[128,1024]{1,0:T(8,128)(2,1)S(1)}, u32[]{:S(2)}, u32[]{:S(2)}) %collective-permute-start.34) | collective-permute-done | bytes 262176 | tf_op jit(solution)/shard_map/ppermute | solution.py:921
  460.2 1.5 constant_dynamic-update-slice_fusion.6.pieces
  461.7 1.7 collective-permute-start.35
  463.4 5.5 %unmix.2 = (f32[1024,1024]{1,0:T(8,128)}, f32[1024,1024]{1,0:T(8,128)}, f32[1024,1024]{1,0:T(8,128)}, f32[1024,1024]{1,0:T(8,128)}) custom-call(s32[2]{0:T(128)} %pad_add_fusion.codes, s32[1]{0:T(128)} %bitcast.39.half_place.source, s32[1]{0:T(128)} %bitcast.39.half_place.source, bf16[4,512,1024]{2,1,0:T(8,128)(2,1)} %constant_dynamic-update-slice_fusion.6.pieces), custom_call_target="tpu_custom_call" | custom-call | flops 2097152 | bytes 12582912 | tf_op jit(solution)/shard_map/unmix/pallas_call | solution.py:896
  470.5 7.7 %unmix.3 = (f32[1024,1024]{1,0:T(8,128)}, f32[1024,1024]{1,0:T(8,128)}, f32[1024,1024]{1,0:T(8,128)}, f32[1024,1024]{1,0:T(8,128)}, bf16[1024,1024]{1,0:T(8,128)(2,1)}) custom-call(s32[2]{0:T(128)} %pad_add_fusion.codes, s32[1]{0:T(128)S(6)} %sub.24.half_place, ...), custom_call_target="tpu_custom_call", output_to_operand_aliasing={{0}: (12, {}), {1}: (13, {}), {2}: (14, {}), {3}: (15, {})} | custom-call | flops 2097152 | bytes 12582912 | tf_op jit(solution)/shard_map/unmix/pallas_call | solution.py:896
  (189 shorter events, 52.2 us)
Async XLA Ops:
  7.2 137.6 %all-gather.5.cloned.1.call-start = ((), (), s32[]{:S(2)}) async-start(), calls=%async_computation.7 | async-start | bytes 10485760 | tf_op jit(solution)/shard_map/all_gather | solution.py:1067
  7.9 136.9 %all-gather.3.cloned.1.call-start = ((), (), s32[]{:S(2)}) async-start(), calls=%async_computation.6 | async-start | bytes 10485760 | tf_op jit(solution)/shard_map/all_gather | solution.py:1066
  8.7 52.2 %all-to-all-start = ((bf16[8,128,1024]{2,1,0:T(8,128)(2,1)}), bf16[8,128,1024]{2,1,0:T(8,128)(2,1)S(1)}, u32[]{:S(2)}, u32[]{:S(2)}) async-start(bf16[8,128,1024]{2,1,0:T(8,128)(2,1)} %bitcast), calls=%async_computation | async-start | bytes 4194304 | tf_op jit(solution)/shard_map/all_to_all | solution.py:925
  60.9 47.4 %all-to-all-start.3 = ((f32[8,1,128]{2,1,0:T(1,128)}), f32[8,1,128]{2,1,0:T(1,128)S(1)}, u32[]{:S(2)}, u32[]{:S(2)}) async-start(f32[8,1,128]{2,1,0:T(1,128)} %fusion.4), calls=%async_computation.3 | async-start | bytes 8192 | tf_op jit(solution)/shard_map/all_to_all | solution.py:925
  108.3 28.4 %all-to-all-start.2 = ((bf16[8,64,1024]{2,1,0:T(8,128)(2,1)}), bf16[8,64,1024]{2,1,0:T(8,128)(2,1)S(1)}, u32[]{:S(2)}, u32[]{:S(2)}) async-start(bf16[8,64,1024]{2,1,0:T(8,128)(2,1)} %bitcast.79), calls=%async_computation.2 | async-start | bytes 2097152 | tf_op jit(solution)/shard_map/all_to_all | solution.py:925
  136.7 31.4 %all-to-all-start.1 = ((bf16[8,64,1024]{2,1,0:T(8,128)(2,1)}), bf16[8,64,1024]{2,1,0:T(8,128)(2,1)S(1)}, u32[]{:S(2)}, u32[]{:S(2)}) async-start(bf16[8,64,1024]{2,1,0:T(8,128)(2,1)} %bitcast.77), calls=%async_computation.1 | async-start | bytes 2097152 | tf_op jit(solution)/shard_map/all_to_all | solution.py:925
  168.2 30.8 %collective-permute-start = (bf16[6,512,1024]{2,1,0:T(8,128)(2,1)}, bf16[6,512,1024]{2,1,0:T(8,128)(2,1)}, u32[]{:S(2)}, u32[]{:S(2)}) collective-permute-start(bf16[6,512,1024]{2,1,0:T(8,128)(2,1)} %get-tuple-element.212.refs_2_), channel_id=1, source_target_pairs={{0,1},{1,0},{2,3},{3,2},{4,5},{5,4},{6,7},{7,6},{8,9},{9,8},{10,11... | collective-permute-start | bytes 18874376 | tf_op jit(solution)/shard_map/ppermute | solution.py:921
  169.3 29.6 %all-to-all-start.4 = ((bf16[8,64,1024]{2,1,0:T(8,128)(2,1)}), bf16[8,64,1024]{2,1,0:T(8,128)(2,1)S(1)}, u32[]{:S(2)}, u32[]{:S(2)}) async-start(bf16[8,64,1024]{2,1,0:T(8,128)(2,1)} %bitcast.78), calls=%async_computation.4 | async-start | bytes 2097152 | tf_op jit(solution)/shard_map/all_to_all | solution.py:925
  175.0 25.3 %copy-start.21 = (f32[4,1,1024]{2,1,0:T(1,128)S(1)}, f32[4,1,1024]{2,1,0:T(1,128)}, u32[]{:S(2)}) copy-start(f32[4,1,1024]{2,1,0:T(1,128)} %get-tuple-element.230) | copy-start | bytes 49156
  198.9 34.4 %copy-start.6 = (bf16[8,64,1024]{2,1,0:T(8,128)(2,1)}, bf16[8,64,1024]{2,1,0:T(8,128)(2,1)S(1)}, u32[]{:S(2)}) copy-start(bf16[8,64,1024]{2,1,0:T(8,128)(2,1)S(1)} %all-to-all-done.4) | copy-start | bytes 3145732
  198.9 10.6 %collective-permute-start.1 = (bf16[6,512,1024]{2,1,0:T(8,128)(2,1)}, bf16[6,512,1024]{2,1,0:T(8,128)(2,1)}, u32[]{:S(2)}, u32[]{:S(2)}) collective-permute-start(bf16[6,512,1024]{2,1,0:T(8,128)(2,1)} %get-tuple-element.222.refs_3_), channel_id=1, source_target_pairs={{0,1},{1,0},{2,3},{3,2},{4,5},{5,4},{6,7},{7,6},{8,9},{9,8},{10,11... | collective-permute-start | bytes 18874376 | tf_op jit(solution)/shard_map/ppermute | solution.py:921
  201.0 32.4 %all-to-all-start.5 = ((bf16[8,64,1024]{2,1,0:T(8,128)(2,1)}), bf16[8,64,1024]{2,1,0:T(8,128)(2,1)S(1)}, u32[]{:S(2)}, u32[]{:S(2)}) async-start(bf16[8,64,1024]{2,1,0:T(8,128)(2,1)} %bitcast.75), calls=%async_computation.5 | async-start | bytes 2097152 | tf_op jit(solution)/shard_map/all_to_all | solution.py:925
  233.3 12.0 %collective-permute-start.2 = (bf16[224,1024]{1,0:T(8,128)(2,1)}, bf16[224,1024]{1,0:T(8,128)(2,1)S(1)}, u32[]{:S(2)}, u32[]{:S(2)}) collective-permute-start(bf16[224,1024]{1,0:T(8,128)(2,1)} %get-tuple-element.238), channel_id=1, source_target_pairs={{0,2},{1,3},{2,0},{3,1},{4,6},{5,7},{6,4},{7,5},{8,10},{9,11},{10,... | collective-permute-start | bytes 1376264 | tf_op jit(solution)/shard_map/ppermute | solution.py:921
  246.1 37.3 %collective-permute-start.3 = (bf16[800,1024]{1,0:T(8,128)(2,1)}, bf16[800,1024]{1,0:T(8,128)(2,1)S(1)}, u32[]{:S(2)}, u32[]{:S(2)}) collective-permute-start(bf16[800,1024]{1,0:T(8,128)(2,1)} %get-tuple-element.246), channel_id=1, source_target_pairs={{0,2},{1,3},{2,0},{3,1},{4,6},{5,7},{6,4},{7,5},{8,10},{9,11},{10,... | collective-permute-start | bytes 4915208 | tf_op jit(solution)/shard_map/ppermute | solution.py:921
  247.4 36.1 %copy-start.24 = (bf16[304,1024]{1,0:T(8,128)(2,1)S(1)}, bf16[304,1024]{1,0:T(8,128)(2,1)}, u32[]{:S(2)}) copy-start(bf16[304,1024]{1,0:T(8,128)(2,1)} %get-tuple-element.258) | copy-start | bytes 1867780
  283.5 14.5 %collective-permute-start.4 = (bf16[304,1024]{1,0:T(8,128)(2,1)S(1)}, bf16[304,1024]{1,0:T(8,128)(2,1)S(1)}, u32[]{:S(2)}, u32[]{:S(2)}) collective-permute-start(bf16[304,1024]{1,0:T(8,128)(2,1)S(1)} %copy-done.24), channel_id=1, source_target_pairs={{0,2},{1,3},{2,0},{3,1},{4,6},{5,7},{6,4},{7,5},{8,10},{9,11},{10,... | collective-permute-start | bytes 1867784 | tf_op jit(solution)/shard_map/ppermute | solution.py:921
  298.1 9.5 %collective-permute-start.5 = (bf16[4,512,1024]{2,1,0:T(8,128)(2,1)}, bf16[4,512,1024]{2,1,0:T(8,128)(2,1)S(1)}, u32[]{:S(2)}, u32[]{:S(2)}) collective-permute-start(bf16[4,512,1024]{2,1,0:T(8,128)(2,1)} %get-tuple-element.264), channel_id=1, source_target_pairs={{0,1},{1,0},{2,3},{3,2},{4,5},{5,4},{6,7},{7,6},{8,9},{9,8},{10,11... | collective-permute-start | bytes 12582920 | tf_op jit(solution)/shard_map/ppermute | solution.py:921
  312.0 24.8 %collective-permute-start.7 = (bf16[4,128,1024]{2,1,0:T(8,128)(2,1)}, bf16[4,128,1024]{2,1,0:T(8,128)(2,1)}, u32[]{:S(2)}, u32[]{:S(2)}) collective-permute-start(bf16[4,128,1024]{2,1,0:T(8,128)(2,1)} %get-tuple-element.280), channel_id=1, source_target_pairs={{0,4},{4,0},{8,12},{12,8},{16,20},{20,16},{24,28},{28,24},{1,5},{5... | collective-permute-start | bytes 3145736 | tf_op jit(solution)/shard_map/ppermute | solution.py:921
  315.1 24.2 %collective-permute-start.6 = (bf16[4,128,1024]{2,1,0:T(8,128)(2,1)S(1)}, bf16[4,128,1024]{2,1,0:T(8,128)(2,1)}, u32[]{:S(2)}, u32[]{:S(2)}) collective-permute-start(bf16[4,128,1024]{2,1,0:T(8,128)(2,1)S(1)} %get-tuple-element.278), channel_id=1, source_target_pairs={{0,2},{1,3},{2,0},{3,1},{4,6},{5,7},{6,4},{7,5},{8,10},{9,11},{10,... | collective-permute-start | bytes 3145736 | tf_op jit(solution)/shard_map/ppermute | solution.py:921
  341.1 12.0 %collective-permute-start.8 = (bf16[4,64,1024]{2,1,0:T(8,128)(2,1)S(1)}, bf16[4,64,1024]{2,1,0:T(8,128)(2,1)S(1)}, u32[]{:S(2)}, u32[]{:S(2)}) collective-permute-start(bf16[4,64,1024]{2,1,0:T(8,128)(2,1)S(1)} %slice.144), channel_id=1, source_target_pairs={{0,4},{4,0},{8,12},{12,8},{16,20},{20,16},{24,28},{28,24},{1,5},{5... | collective-permute-start | bytes 1572872 | tf_op jit(solution)/shard_map/ppermute | solution.py:921
  342.0 11.7 %collective-permute-start.9 = (bf16[4,64,1024]{2,1,0:T(8,128)(2,1)S(1)}, bf16[4,64,1024]{2,1,0:T(8,128)(2,1)S(1)}, u32[]{:S(2)}, u32[]{:S(2)}) collective-permute-start(bf16[4,64,1024]{2,1,0:T(8,128)(2,1)S(1)} %slice.146), channel_id=1, source_target_pairs={{0,2},{1,3},{2,0},{3,1},{4,6},{5,7},{6,4},{7,5},{8,10},{9,11},{10,... | collective-permute-start | bytes 1572872 | tf_op jit(solution)/shard_map/ppermute | solution.py:921
  342.8 5.2 %collective-permute-start.10 = (f32[16,1024]{1,0:T(8,128)S(1)}, f32[16,1024]{1,0:T(8,128)S(1)}, u32[]{:S(2)}, u32[]{:S(2)}) collective-permute-start(f32[16,1024]{1,0:T(8,128)S(1)} %constant_dynamic-update-slice_fusion), channel_id=1, source_target_pairs={{0,1},{1,0},{2,3},{3,2},{4,5},{5,4},{6,7},{7,6},{8,9},{9,8},{10,11... | collective-permute-start | bytes 196616 | tf_op jit(solution)/shard_map/ppermute | solution.py:921
  344.9 13.1 %collective-permute-start.11 = (bf16[128,1024]{1,0:T(8,128)(2,1)S(1)}, bf16[128,1024]{1,0:T(8,128)(2,1)S(1)}, u32[]{:S(2)}, u32[]{:S(2)}) collective-permute-start(bf16[128,1024]{1,0:T(8,128)(2,1)S(1)} %copy-done.27), channel_id=1, source_target_pairs={{0,8},{4,12},{8,0},{12,4},{16,24},{20,28},{24,16},{28,20},{1,9},{5... | collective-permute-start | bytes 786440 | tf_op jit(solution)/shard_map/ppermute | solution.py:921
  347.2 13.0 %collective-permute-start.12 = (bf16[128,1024]{1,0:T(8,128)(2,1)S(1)}, bf16[128,1024]{1,0:T(8,128)(2,1)S(1)}, u32[]{:S(2)}, u32[]{:S(2)}) collective-permute-start(bf16[128,1024]{1,0:T(8,128)(2,1)S(1)} %copy-done.26), channel_id=1, source_target_pairs={{0,16},{4,20},{8,24},{12,28},{16,0},{20,4},{24,8},{28,12},{1,17},{... | collective-permute-start | bytes 786440 | tf_op jit(solution)/shard_map/ppermute | solution.py:921
  361.1 20.1 %collective-permute-start.13 = (bf16[4,2,16,1024]{3,2,0,1:T(8,128)(2,1)}, bf16[4,2,16,1024]{3,2,0,1:T(8,128)(2,1)}, u32[]{:S(2)}, u32[]{:S(2)}) collective-permute-start(bf16[4,2,16,1024]{3,2,0,1:T(8,128)(2,1)} %get-tuple-element.381), channel_id=1, source_target_pairs={{0,16},{4,20},{8,24},{12,28},{16,0},{20,4},{24,8},{28,12},{1,17},{... | collective-permute-start | bytes 786440 | tf_op jit(solution)/shard_map/ppermute | solution.py:921
  363.4 17.8 %collective-permute-start.14 = (bf16[4,2,16,1024]{3,2,0,1:T(8,128)(2,1)}, bf16[4,2,16,1024]{3,2,0,1:T(8,128)(2,1)}, u32[]{:S(2)}, u32[]{:S(2)}) collective-permute-start(bf16[4,2,16,1024]{3,2,0,1:T(8,128)(2,1)} %get-tuple-element.383), channel_id=1, source_target_pairs={{0,8},{4,12},{8,0},{12,4},{16,24},{20,28},{24,16},{28,20},{1,9},{5... | collective-permute-start | bytes 786440 | tf_op jit(solution)/shard_map/ppermute | solution.py:921
  363.4 22.3 %collective-permute-start.15 = (bf16[4,2,16,1024]{3,2,0,1:T(8,128)(2,1)}, bf16[4,2,16,1024]{3,2,0,1:T(8,128)(2,1)}, u32[]{:S(2)}, u32[]{:S(2)}) collective-permute-start(bf16[4,2,16,1024]{3,2,0,1:T(8,128)(2,1)} %get-tuple-element.382), channel_id=1, source_target_pairs={{0,24},{4,28},{8,16},{12,20},{16,8},{20,12},{24,0},{28,4},{1,25},{... | collective-permute-start | bytes 786440 | tf_op jit(solution)/shard_map/ppermute | solution.py:921
  363.8 23.2 %collective-permute-start.16 = (bf16[400,1024]{1,0:T(8,128)(2,1)}, bf16[400,1024]{1,0:T(8,128)(2,1)S(1)}, u32[]{:S(2)}, u32[]{:S(2)}) collective-permute-start(bf16[400,1024]{1,0:T(8,128)(2,1)} %get-tuple-element.305), channel_id=1, source_target_pairs={{0,2},{1,3},{2,0},{3,1},{4,6},{5,7},{6,4},{7,5},{8,10},{9,11},{10,... | collective-permute-start | bytes 2457608 | tf_op jit(solution)/shard_map/ppermute | solution.py:921
  364.5 22.5 %collective-permute-start.17 = (bf16[256,1024]{1,0:T(8,128)(2,1)}, bf16[256,1024]{1,0:T(8,128)(2,1)S(1)}, u32[]{:S(2)}, u32[]{:S(2)}) collective-permute-start(bf16[256,1024]{1,0:T(8,128)(2,1)} %get-tuple-element.307), channel_id=1, source_target_pairs={{0,4},{4,0},{8,12},{12,8},{16,20},{20,16},{24,28},{28,24},{1,5},{5... | collective-permute-start | bytes 1572872 | tf_op jit(solution)/shard_map/ppermute | solution.py:921
  365.7 27.0 %copy-start.5 = (bf16[800,1024]{1,0:T(8,128)(2,1)S(1)}, bf16[800,1024]{1,0:T(8,128)(2,1)}, u32[]{:S(2)}) copy-start(bf16[800,1024]{1,0:T(8,128)(2,1)} %copy-done.4) | copy-start | bytes 4915204
  387.0 11.0 %collective-permute-start.18 = (bf16[4,2,16,1024]{3,2,0,1:T(8,128)(2,1)S(1)}, bf16[4,2,16,1024]{3,2,0,1:T(8,128)(2,1)S(1)}, u32[]{:S(2)}, u32[]{:S(2)}) collective-permute-start(bf16[4,2,16,1024]{3,2,0,1:T(8,128)(2,1)S(1)} %add_convert_fusion.8), channel_id=1, source_target_pairs={{0,16},{4,20},{8,24},{12,28},{16,0},{20,4},{24,8},{28,12},{1,17},{... | collective-permute-start | bytes 786440 | tf_op jit(solution)/shard_map/ppermute | solution.py:921
  387.1 15.0 %collective-permute-start.19 = (bf16[4,2,16,1024]{3,2,0,1:T(8,128)(2,1)S(1)}, bf16[4,2,16,1024]{3,2,0,1:T(8,128)(2,1)S(1)}, u32[]{:S(2)}, u32[]{:S(2)}) collective-permute-start(bf16[4,2,16,1024]{3,2,0,1:T(8,128)(2,1)S(1)} %add_convert_fusion.8), channel_id=1, source_target_pairs={{0,8},{4,12},{8,0},{12,4},{16,24},{20,28},{24,16},{28,20},{1,9},{5... | collective-permute-start | bytes 786440 | tf_op jit(solution)/shard_map/ppermute | solution.py:921
  390.4 22.3 %collective-permute-start.20 = (bf16[4,2,16,1024]{3,2,0,1:T(8,128)(2,1)S(1)}, bf16[4,2,16,1024]{3,2,0,1:T(8,128)(2,1)S(1)}, u32[]{:S(2)}, u32[]{:S(2)}) collective-permute-start(bf16[4,2,16,1024]{3,2,0,1:T(8,128)(2,1)S(1)} %add_convert_fusion.8), channel_id=1, source_target_pairs={{0,24},{4,28},{8,16},{12,20},{16,8},{20,12},{24,0},{28,4},{1,25},{... | collective-permute-start | bytes 786440 | tf_op jit(solution)/shard_map/ppermute | solution.py:921
  390.4 22.4 %collective-permute-start.21 = (bf16[320,1024]{1,0:T(8,128)(2,1)}, bf16[320,1024]{1,0:T(8,128)(2,1)S(1)}, u32[]{:S(2)}, u32[]{:S(2)}) collective-permute-start(bf16[320,1024]{1,0:T(8,128)(2,1)} %get-tuple-element.317), channel_id=1, source_target_pairs={{0,2},{1,3},{2,0},{3,1},{4,6},{5,7},{6,4},{7,5},{8,10},{9,11},{10,... | collective-permute-start | bytes 1966088 | tf_op jit(solution)/shard_map/ppermute | solution.py:921
  391.2 21.7 %collective-permute-start.22 = (bf16[256,1024]{1,0:T(8,128)(2,1)}, bf16[256,1024]{1,0:T(8,128)(2,1)S(1)}, u32[]{:S(2)}, u32[]{:S(2)}) collective-permute-start(bf16[256,1024]{1,0:T(8,128)(2,1)} %get-tuple-element.323), channel_id=1, source_target_pairs={{0,4},{4,0},{8,12},{12,8},{16,20},{20,16},{24,28},{28,24},{1,5},{5... | collective-permute-start | bytes 1572872 | tf_op jit(solution)/shard_map/ppermute | solution.py:921
  412.9 5.9 %collective-permute-start.25 = (f32[8,1024]{1,0:T(8,128)S(1)}, f32[8,1024]{1,0:T(8,128)S(1)}, u32[]{:S(2)}, u32[]{:S(2)}) collective-permute-start(f32[8,1024]{1,0:T(8,128)S(1)} %slice.153), channel_id=1, source_target_pairs={{0,4},{4,0},{8,12},{12,8},{16,20},{20,16},{24,28},{28,24},{1,5},{5... | collective-permute-start | bytes 98312 | tf_op jit(solution)/shard_map/ppermute | solution.py:921
  413.0 14.3 %collective-permute-start.24 = (bf16[4,64,1024]{2,1,0:T(8,128)(2,1)S(1)}, bf16[4,64,1024]{2,1,0:T(8,128)(2,1)S(1)}, u32[]{:S(2)}, u32[]{:S(2)}) collective-permute-start(bf16[4,64,1024]{2,1,0:T(8,128)(2,1)S(1)} %get-tuple-element.325), channel_id=1, source_target_pairs={{0,2},{1,3},{2,0},{3,1},{4,6},{5,7},{6,4},{7,5},{8,10},{9,11},{10,... | collective-permute-start | bytes 1572872 | tf_op jit(solution)/shard_map/ppermute | solution.py:921
  413.8 13.6 %collective-permute-start.23 = (bf16[4,64,1024]{2,1,0:T(8,128)(2,1)S(1)}, bf16[4,64,1024]{2,1,0:T(8,128)(2,1)S(1)}, u32[]{:S(2)}, u32[]{:S(2)}) collective-permute-start(bf16[4,64,1024]{2,1,0:T(8,128)(2,1)S(1)} %get-tuple-element.324), channel_id=1, source_target_pairs={{0,4},{4,0},{8,12},{12,8},{16,20},{20,16},{24,28},{28,24},{1,5},{5... | collective-permute-start | bytes 1572872 | tf_op jit(solution)/shard_map/ppermute | solution.py:921
  415.9 11.6 %collective-permute-start.28 = (bf16[128,1024]{1,0:T(8,128)(2,1)S(1)}, bf16[128,1024]{1,0:T(8,128)(2,1)S(1)}, u32[]{:S(2)}, u32[]{:S(2)}) collective-permute-start(bf16[128,1024]{1,0:T(8,128)(2,1)S(1)} %get-tuple-element.386), channel_id=1, source_target_pairs={{0,8},{4,12},{8,0},{12,4},{16,24},{20,28},{24,16},{28,20},{1,9},{5... | collective-permute-start | bytes 786440 | tf_op jit(solution)/shard_map/ppermute | solution.py:921
  415.9 11.6 %collective-permute-start.27 = (bf16[128,1024]{1,0:T(8,128)(2,1)S(1)}, bf16[128,1024]{1,0:T(8,128)(2,1)S(1)}, u32[]{:S(2)}, u32[]{:S(2)}) collective-permute-start(bf16[128,1024]{1,0:T(8,128)(2,1)S(1)} %copy-done.25), channel_id=1, source_target_pairs={{0,24},{4,28},{8,16},{12,20},{16,8},{20,12},{24,0},{28,4},{1,25},{... | collective-permute-start | bytes 786440 | tf_op jit(solution)/shard_map/ppermute | solution.py:921
  418.8 8.5 %collective-permute-start.26 = (f32[16,1024]{1,0:T(8,128)S(1)}, f32[16,1024]{1,0:T(8,128)S(1)}, u32[]{:S(2)}, u32[]{:S(2)}) collective-permute-start(f32[16,1024]{1,0:T(8,128)S(1)} %pad_maximum_fusion.5), channel_id=1, source_target_pairs={{0,2},{1,3},{2,0},{3,1},{4,6},{5,7},{6,4},{7,5},{8,10},{9,11},{10,... | collective-permute-start | bytes 196616 | tf_op jit(solution)/shard_map/ppermute | solution.py:921
  427.6 22.1 %collective-permute-start.30 = (bf16[4,128,1024]{2,1,0:T(8,128)(2,1)S(1)}, bf16[4,128,1024]{2,1,0:T(8,128)(2,1)S(1)}, u32[]{:S(2)}, u32[]{:S(2)}) collective-permute-start(bf16[4,128,1024]{2,1,0:T(8,128)(2,1)S(1)} %pad_maximum_fusion.4), channel_id=1, source_target_pairs={{0,4},{4,0},{8,12},{12,8},{16,20},{20,16},{24,28},{28,24},{1,5},{5... | collective-permute-start | bytes 3145736 | tf_op jit(solution)/shard_map/ppermute | solution.py:921
  428.7 22.5 %collective-permute-start.29 = (bf16[4,128,1024]{2,1,0:T(8,128)(2,1)S(1)}, bf16[4,128,1024]{2,1,0:T(8,128)(2,1)S(1)}, u32[]{:S(2)}, u32[]{:S(2)}) collective-permute-start(bf16[4,128,1024]{2,1,0:T(8,128)(2,1)S(1)} %pad_maximum_fusion.3), channel_id=1, source_target_pairs={{0,2},{1,3},{2,0},{3,1},{4,6},{5,7},{6,4},{7,5},{8,10},{9,11},{10,... | collective-permute-start | bytes 3145736 | tf_op jit(solution)/shard_map/ppermute | solution.py:921
  429.4 2.8 collective-permute-start.31
  432.3 4.2 collective-permute-start.32
  433.9 17.5 %collective-permute-start.33 = (bf16[128,1024]{1,0:T(8,128)(2,1)S(1)}, bf16[128,1024]{1,0:T(8,128)(2,1)S(1)}, u32[]{:S(2)}, u32[]{:S(2)}) collective-permute-start(bf16[128,1024]{1,0:T(8,128)(2,1)S(1)} %get-tuple-element.342), channel_id=1, source_target_pairs={{0,16},{4,20},{8,24},{12,28},{16,0},{20,4},{24,8},{28,12},{1,17},{... | collective-permute-start | bytes 786440 | tf_op jit(solution)/shard_map/ppermute | solution.py:921
  434.7 24.0 %collective-permute-start.34 = (bf16[128,1024]{1,0:T(8,128)(2,1)S(1)}, bf16[128,1024]{1,0:T(8,128)(2,1)S(1)}, u32[]{:S(2)}, u32[]{:S(2)}) collective-permute-start(bf16[128,1024]{1,0:T(8,128)(2,1)S(1)} %get-tuple-element.343), channel_id=1, source_target_pairs={{0,24},{4,28},{8,16},{12,20},{16,8},{20,12},{24,0},{28,4},{1,25},{... | collective-permute-start | bytes 786440 | tf_op jit(solution)/shard_map/ppermute | solution.py:921
  461.7 8.8 %collective-permute-start.35 = (bf16[4,512,1024]{2,1,0:T(8,128)(2,1)}, bf16[4,512,1024]{2,1,0:T(8,128)(2,1)}, u32[]{:S(2)}, u32[]{:S(2)}) collective-permute-start(bf16[4,512,1024]{2,1,0:T(8,128)(2,1)} %constant_dynamic-update-slice_fusion.6.pieces), channel_id=1, source_target_pairs={{0,1},{1,0},{2,3},{3,2},{4,5},{5,4},{6,7},{7,6},{8,9},{9,8},{10,11... | collective-permute-start | bytes 12582920 | tf_op jit(solution)/shard_map/ppermute | solution.py:921
  (24 other events, 246.8 us)
Sparse Core Ops, SparseCore 0:
  9.6 59.8 all-gather.4
  71.0 58.2 all-gather.2

commit v5 on v4

--- a/solution.py
+++ b/solution.py
@@ -417,7 +417,7 @@
 
 
 def attend_back_kernel(
-    start_row, q_ref, k_ref, v_ref, o_ref, g_ref, lse_ref, out_ref, bias, dq_sum
+    start_row, q_ref, k_ref, v_ref, o_ref, g_ref, lse_ref, out_ref, bias, sums
 ):
     count, lanes = q_ref.shape
 
@@ -441,31 +441,50 @@
 
     queries = split_heads(q_ref[...])
     grads = split_heads(g_ref[...])
-    for j in range(count // ROWS):
-        rows = pl.ds(j * ROWS, ROWS)
-        ext = slice(j * ROWS, count)
-        keys, vals = k_ref[rows, :], v_ref[rows, :]
-        dk = dv = dq = None
-        for h, key in enumerate(split_heads(keys)):
-            query, grad = queries[h][ext], grads[h][ext]
-            score = nt(keys, query) * LOG2E + bias[rows, ext]
-            weights = jnp.exp2(score - lse_ref[0, h : h + 1, ext])
-            weights_low = weights.astype(BF16)
-            grad_weights = nt(vals, grad)
-            grad_score = (weights * (grad_weights - deltas[h : h + 1, ext])).astype(BF16)
-            dv_part = nn(weights_low, grad)
-            dk_part = nn(grad_score, query)
-            dq_part = tn(grad_score, key)
-            dv = dv_part if dv is None else dv + dv_part
-            dk = dk_part if dk is None else dk + dk_part
-            dq = dq_part if dq is None else dq + dq_part
-        out_ref[1, rows, :] = dk.astype(BF16)
-        out_ref[2, rows, :] = dv.astype(BF16)
-        if j == 0:
-            dq_sum[...] = dq
-        else:
-            dq_sum[ext, :] += dq
-    out_ref[0] = (dq_sum[...] * 0.125).astype(BF16)
+    wide = 2 * ROWS
+    items = []
+    for s in range(0, count, wide):
+        if s + wide < count:
+            items.append((s, s + wide, s + wide, count))
+        items.append((s, s + ROWS, s, s + wide))
+        items.append((s + ROWS, s + wide, s + ROWS, s + wide))
+    work = [(item, h) for item in items for h in range(2)]
+
+    def products_of(item, h):
+        k_from, k_to, q_from, q_to = item
+        return (
+            nt(k_ref[k_from:k_to, :], queries[h][q_from:q_to]),
+            nt(v_ref[k_from:k_to, :], grads[h][q_from:q_to]),
+        )
+
+    seen_keys, seen_queries = set(), set()
+
+    def add(target, start, part, seen):
+        for r in range(0, part.shape[0], ROWS):
+            rows = pl.ds(start + r, ROWS)
+            if start + r in seen:
+                target[rows, :] += part[r : r + ROWS]
+            else:
+                target[rows, :] = part[r : r + ROWS]
+
+    ahead = products_of(*work[0])
+    for n, (item, h) in enumerate(work):
+        k_from, k_to, q_from, q_to = item
+        score, grad_weights = ahead
+        if n + 1 < len(work):
+            ahead = products_of(*work[n + 1])
+        cols = slice(q_from, q_to)
+        weights = jnp.exp2(score * LOG2E + bias[k_from:k_to, cols] - lse_ref[0, h : h + 1, cols])
+        grad_score = (weights * (grad_weights - deltas[h : h + 1, cols])).astype(BF16)
+        key = split_heads(k_ref[k_from:k_to, :])[h]
+        add(sums.at[2], k_from, nn(weights.astype(BF16), grads[h][cols]), seen_keys)
+        add(sums.at[1], k_from, nn(grad_score, queries[h][cols]), seen_keys)
+        add(sums.at[0], q_from, tn(grad_score, key), seen_queries)
+        seen_keys |= set(range(k_from, k_to, ROWS))
+        seen_queries |= set(range(q_from, q_to, ROWS))
+    out_ref[0] = (sums[0] * 0.125).astype(BF16)
+    out_ref[1] = sums[1].astype(BF16)
+    out_ref[2] = sums[2].astype(BF16)
 
 
 def attend_back(start_row, q, k, v, mixed, grad_mixed, lse):
@@ -481,7 +500,7 @@
         + [pl.BlockSpec((1, 8, count), lambda p: (p, 0, 0))],
         out_specs=pl.BlockSpec((3, count, lanes), lambda p: (0, 0, p)),
         out_shape=jax.ShapeDtypeStruct((3, count, width), BF16),
-        scratch_shapes=[pltpu.VMEM((count, count), F32), pltpu.VMEM((count, lanes), F32)],
+        scratch_shapes=[pltpu.VMEM((count, count), F32), pltpu.VMEM((3, count, lanes), F32)],
         compiler_params=params(),
         cost_estimate=cost(20 * count * count * width, 16 * count * width, HEADS * count * count // 2),
         name="attend_back",
@@ -569,13 +588,14 @@
     return (step % 2) * 2 + step // 2
 
 
-def expert_kernel(device, *refs):
+def expert_kernel(parts, device, source, *refs):
     it = iter(refs)
     take = lambda n: [next(it) for _ in range(n)]
     slots, cots, lives = take(3)
     up, down, up_bias, gain, offset = take(5)
-    grads, mine, theirs, sums, up_sums = take(5)
-    ffn_in, branch, grad_sum = take(3)
+    grads = take(max(len(parts), 1))
+    mine, theirs, sums, up_sums = take(4)
+    ffn_in, branch, grad_sum, low = take(4)
     rows, model = slots.shape
     t = pl.program_id(0)
 
@@ -626,27 +646,38 @@
         normal, root = norm_parts(routed)
         grad = grad_sum[...]
         cot = cots[...].reshape(rows, model).astype(F32)
-        grads[...] = (cot + norm_grad(grad, normal, root, gain[...])).astype(BF16)
+        grad_routed = (cot + norm_grad(grad, normal, root, gain[...])).astype(BF16)
+        if not parts:
+            grads[0][...] = grad_routed
+        else:
+            low[...] = grad_routed
+            short, n = rows // sum(parts), 0
+            for part, blocks in zip(grads, parts):
+                for j in range(blocks):
+                    place = pl.multiple_of(source[n] * short, short)
+                    part[j * short : (j + 1) * short, :] = low[pl.ds(place, short), :]
+                    n += 1
         sums[...] = jnp.zeros_like(sums)
         sums[0:1, :] = jnp.sum(grad * normal, axis=0, keepdims=True)
         sums[1:2, :] = jnp.sum(grad, axis=0, keepdims=True)
         sums[2:3, :] = jnp.sum(branch[...].astype(F32), axis=0, keepdims=True)
 
 
-def expert_chunk(chunk, device, slots, cot, live, ups, downs, up_bias, gain, offset):
+def expert_chunk(chunk, parts, device, source, slots, cot, live, ups, downs, up_bias, gain, offset):
     rows, width = slots.shape
     groups, piece, _ = cot.shape
     short = rows // groups
+    sizes = [short * n for n in parts] or [rows]
     part = ups.shape[2]
     assert part == width and ups.shape[0] == 4
     block = pl.BlockSpec((groups, short, width), lambda t, *_: (0, chunk, 0))
     packet = jax.ShapeDtypeStruct((6, rows, width), BF16)
-    weights = pl.BlockSpec((1, width, part), lambda t, device: (shard_of(t) ^ device[0], 0, 0))
-    bias = pl.BlockSpec((1, 1, part), lambda t, device: (shard_of(t) ^ device[0], 0, 0))
+    weights = pl.BlockSpec((1, width, part), lambda t, device, *_: (shard_of(t) ^ device[0], 0, 0))
+    bias = pl.BlockSpec((1, 1, part), lambda t, device, *_: (shard_of(t) ^ device[0], 0, 0))
     return pl.pallas_call(
-        expert_kernel,
+        functools.partial(expert_kernel, parts),
         grid_spec=pltpu.PrefetchScalarGridSpec(
-            num_scalar_prefetch=1,
+            num_scalar_prefetch=2,
             grid=(4,),
             in_specs=[
                 whole((rows, width)),
@@ -654,8 +685,8 @@
                 pl.BlockSpec((groups, short, 1), lambda t, *_: (0, chunk, 0)),
             ]
             + [weights, weights, bias, whole((1, width)), whole((1, width))],
-            out_specs=[
-                whole((rows, width)),
+            out_specs=[whole((size, width)) for size in sizes]
+            + [
                 pl.BlockSpec((2, rows, width), lambda t, *_: (jnp.minimum(t, 2), 0, 0)),
                 pl.BlockSpec((2, rows, width), lambda t, *_: (jnp.where(t < 2, 2, t - 2), 0, 0)),
                 whole((8, width)),
@@ -665,10 +696,11 @@
                 pltpu.VMEM((rows, width), BF16),
                 pltpu.VMEM((rows, width), BF16),
                 pltpu.VMEM((rows, width), F32),
+                pltpu.VMEM((rows, width), BF16),
             ],
         ),
-        out_shape=[
-            jax.ShapeDtypeStruct((rows, width), BF16),
+        out_shape=[jax.ShapeDtypeStruct((size, width), BF16) for size in sizes]
+        + [
             packet,
             packet,
             jax.ShapeDtypeStruct((8, width), F32),
@@ -677,7 +709,7 @@
         compiler_params=params(),
         cost_estimate=cost(24 * rows * width * part, 16 * width * part, 4 * rows * part),
         name="expert_chunk",
-    )(device, slots, cot, live, ups, downs, up_bias, gain, offset)
+    )(device, source, slots, cot, live, ups, downs, up_bias, gain, offset)
 
 
 def expert_out_kernel(chunks, device, *refs):
@@ -736,65 +768,56 @@
 CUTS = ((224, 800), (304, 400, 320))
 
 
-def expert_grads_kernel(count, *refs):
-    packets, near, fars = refs[:count], refs[count : count + 2], refs[count + 2 : -9]
-    far_act, branch, ffn_in, far_pre, near_act, near_pre, far_low, near_full, sems = refs[-9:]
+def expert_grads_kernel(count, near, *refs):
+    packets, outs = refs[:count], refs[count:-6]
+    act, branch, ffn_in, pre, full, sems = refs[-6:]
     copies = Copies(sems)
     rows = packets[0].shape[1]
 
     def fetch(slot, target):
         return [copies.start(p.at[slot], target.at[pl.ds(n * rows, rows)]) for n, p in enumerate(packets)]
 
-    first = fetch(2, far_act) + fetch(5, branch)
-    second = fetch(4, ffn_in) + fetch(3, far_pre)
-    third = fetch(0, near_act)
-    fourth = fetch(1, near_pre)
+    shard = 0 if near else 2
+    first = fetch(shard, act) + fetch(5, branch)
+    second = fetch(4, ffn_in) + fetch(shard + 1, pre)
     left = []
-
-    def far(m, came, one, two):
+    for m, (came, one, two) in enumerate(((first, act, branch), (second, ffn_in, pre))):
         for copy in came:
             copy.wait()
-        far_low[m] = tn(one[...], two[...]).astype(BF16)
+        full[m] = tn(one[...], two[...]).astype(full.dtype)
+        if near:
+            left.append(copies.start(full.at[m], outs[m].at[0]))
+            continue
         start, skip = 0, sum(len(cuts) for cuts in CUTS[:m])
         for n, cut in enumerate(CUTS[m]):
-            left.append(copies.start(far_low.at[m, pl.ds(start, cut)], fars[skip + n]))
+            left.append(copies.start(full.at[m, pl.ds(start, cut)], outs[skip + n]))
             start += cut
-
-    def close(m, came, one, two):
-        for copy in came:
-            copy.wait()
-        near_full[m] = tn(one[...], two[...])
-        left.append(copies.start(near_full.at[m], near[m].at[0]))
-
-    far(0, first, far_act, branch)
-    far(1, second, ffn_in, far_pre)
-    close(0, third, near_act, branch)
-    close(1, fourth, ffn_in, near_pre)
     for copy in left:
         copy.wait()
 
 
-def expert_grads(packets):
+def expert_grads(near, packets):
     _, rows, width = packets[0].shape
     count = len(packets)
     assert sum(CUTS[0]) == sum(CUTS[1]) == width
-    cuts = [c for cuts in CUTS for c in cuts]
+    if near:
+        shapes = [jax.ShapeDtypeStruct((1, width, width), F32)] * 2
+    else:
+        shapes = [jax.ShapeDtypeStruct((c, width), BF16) for cuts in CUTS for c in cuts]
     return pl.pallas_call(
-        functools.partial(expert_grads_kernel, count),
+        functools.partial(expert_grads_kernel, count, near),
         grid=(1,),
         in_specs=[ANYWHERE] * count,
-        out_specs=[ANYWHERE] * (2 + len(cuts)),
-        out_shape=[jax.ShapeDtypeStruct((1, width, width), F32)] * 2
-        + [jax.ShapeDtypeStruct((c, width), BF16) for c in cuts],
-        scratch_shapes=[pltpu.VMEM((count * rows, width), BF16)] * 6
+        out_specs=[ANYWHERE] * len(shapes),
+        out_shape=shapes,
+        scratch_shapes=[pltpu.VMEM((count * rows, width), BF16)] * 4
         + [
-            pltpu.VMEM((2, width, width), BF16),
-            pltpu.VMEM((2, width, width), F32),
-            pltpu.SemaphoreType.DMA((6 * count + 2 + len(cuts),)),
+            pltpu.VMEM((2, width, width), F32 if near else BF16),
+            pltpu.SemaphoreType.DMA((4 * count + len(shapes),)),
         ],
         compiler_params=params(),
-        cost_estimate=cost(8 * count * rows * width * width, 30 * width * width),
-        name="expert_grads",
+        cost_estimate=cost(4 * count * rows * width * width, 20 * width * width),
+        name="near_grads" if near else "far_grads",
     )(*packets)
 
 
@@ -1078,16 +1101,18 @@
     in_chunks = position.reshape(n_expert, CHUNKS, -1).transpose(1, 0, 2).reshape(count)
     slot_live = (position < total_live).astype(F32).reshape(n_expert, piece)
     start_row, start_col = begin.reshape(1, count), begin.reshape(count, 1)
-    pos_row, pos_col = position.reshape(1, count), position.reshape(count, 1)
-    chunk_row, chunk_col = in_chunks.reshape(1, count), in_chunks.reshape(count, 1)
+    pos_row, chunk_col = position.reshape(1, count), in_chunks.reshape(count, 1)
     shared = SharedSum(n_expert, n_dp, width)
     expert = lax.axis_index("expert")
     codes = jnp.concatenate([jnp.arange(xs, n_expert, 2, dtype=jnp.int32) for xs in range(2)])
     partners = (expert ^ codes).astype(jnp.int32)
     leave_col = jnp.take(position.reshape(n_expert, piece), partners, axis=0).reshape(count, 1)
-    leave_col, partners = tie(leave_col, partners)
-    arrived, start_row, start_col, pos_row, pos_col, chunk_row, chunk_col, live_col, shared.codes = tie(
-        arrived, start_row, start_col, pos_row, pos_col, chunk_row, chunk_col, live_col, shared.codes
+    last_slots = jnp.take(position.reshape(n_expert, CHUNKS, -1)[:, -1], partners, axis=0)
+    came_row = jnp.concatenate([in_chunks[: count - count // CHUNKS], last_slots.reshape(-1)])
+    came_row = came_row.reshape(1, count)
+    leave_col, partners, came_row = tie(leave_col, partners, came_row)
+    arrived, start_row, start_col, pos_row, chunk_col, live_col, shared.codes = tie(
+        arrived, start_row, start_col, pos_row, chunk_col, live_col, shared.codes
     )
     route_live = exchange(slot_live).reshape(n_expert, piece, 1)
 
@@ -1110,38 +1135,47 @@
     up_bias = expert_up_bias[0].reshape(n_dp, 1, part)
     grads, mine, theirs, got, sums, up_sums = ([None] * CHUNKS for _ in range(6))
     returned = []
+    side = n_expert // 2
+    to_partner = lambda v, j: swap(v, ("expert", n_expert, 2 * j))
     for c in range(CHUNKS):
-        grads[c], mine[c], theirs[c], sums[c], up_sums[c] = expert_chunk(
-            c, place, routed[c], blocks(block_cot), route_live, ups, downs, up_bias,
-            row(second_gain), row(second_bias),
+        last = c + 1 == CHUNKS
+        *grads[c], mine[c], theirs[c], sums[c], up_sums[c] = expert_chunk(
+            c, (1,) * side + (side,) if last else (), place, partners, routed[c],
+            blocks(block_cot), route_live, ups, downs, up_bias, row(second_gain), row(second_bias),
         )
         if c > 0:
-            returned.append(exchange(grads[c - 1]))
+            returned.append(exchange(grads[c - 1][0]))
             got[c - 1] = swap(theirs[c - 1], core)
             returned[-1], got[c - 1], grads[c], mine[c], theirs[c] = tie(
                 returned[-1], got[c - 1], grads[c], mine[c], theirs[c]
             )
-        if c + 1 < CHUNKS:
+        if not last:
             routed.append(exchange(sent[c + 1]))
             routed[c + 1], grads[c], mine[c], theirs[c] = tie(
                 routed[c + 1], grads[c], mine[c], theirs[c]
             )
-    returned.append(exchange(grads[-1]))
+    *stay, cross = grads[-1]
     got[-1] = swap(theirs[-1], core)
-
-    *near, down_a, down_b, up_a, up_b, up_c = expert_grads([*mine, *got])
+    cross = swap(cross, ("expert", n_expert, 1))
+    stay = [v if j == 0 else to_partner(v, j) for j, v in enumerate(stay)]
+    cross, got[-1] = tie(cross, got[-1])
+    short = cross.shape[0] // side
+    across = [cross[j * short : (j + 1) * short] for j in range(side)]
+    across = [v if j == 0 else to_partner(v, j) for j, v in enumerate(across)]
+    returned += stay + across
+
+    fars = list(expert_grads(False, [*mine, *got]))
     sums, up_sums = sum(sums), sum(up_sums)
     empty = jnp.zeros((8, width), F32)
     biases = jnp.concatenate([up_sums.reshape(-1, width), sums[2:3], empty[: 7 - n_dp]], axis=0)
 
-    fars = [down_a, down_b, up_a, up_b, up_c]
-
     def over_y(n):
         fars[n] = swap(fars[n], far)
 
-    returned, near, fars, biases = tie(returned, near, fars, biases)
+    returned, fars, biases = tie(returned, fars, biases)
+    packets = [*mine, *got]
     grad_residual, grad_proj, grad_mixed, out_bias_sum = reenter(
-        returned, chunk_row, live_col, out_weight
+        returned, came_row, live_col, out_weight
     )
     over_y(0)
     grad_mixed, fars = tie(grad_mixed, fars)
@@ -1161,7 +1195,6 @@
     total = shared.reduce_first(*halves)
     token_grads, total, others = tie(token_grads, total, others)
 
-    side = n_expert // 2
     *leaving, token_sums = finish(
         [piece] * side + [piece * side // 2] * 2, token_grads, [query_weight, key_weight, value_weight],
         tokens, grad_residual, row(first_gain), leave_col, others,
@@ -1170,7 +1203,6 @@
     leaving, token_sums, total = tie(leaving, token_sums, total)
 
     *stay, cross, cross_rest = leaving
-    to_partner = lambda v, j: swap(v, ("expert", n_expert, 2 * j))
     early = range(1, 1 + (2 * side - 2 + 2) // 3)
     late = range(early.stop, side)
     small_steps = list(shared.steps)
@@ -1188,33 +1220,36 @@
     cross = swap(cross, ("expert", n_expert, 1))
     block_out = expert_out(place, mine, theirs, routed, downs, row(expert_down_bias[0]), route_live)
     total = shared.reduce_rest(total)
-    total, small, block_out, near, fars, cross, cross_rest = tie(
-        total, small, block_out, near, fars, cross, cross_rest
+    total, small, block_out, packets, fars, cross, cross_rest = tie(
+        total, small, block_out, packets, fars, cross, cross_rest
     )
 
     over_y(4)
     total = unstack(shared.gather_rest(total))
-    grad_down = near[0] + jnp.concatenate(fars[:2], axis=0).astype(F32)[None]
+    near = list(expert_grads(True, packets))
     cross_rest = swap(cross_rest, ("expert", n_expert, 1))
-    total, small, grad_down, fars, stay, cross, cross_rest = tie(
-        total, small, grad_down, fars, stay, cross, cross_rest
+    total, small, near, fars, stay, cross, cross_rest = tie(
+        total, small, near, fars, stay, cross, cross_rest
     )
     across = [v[j * piece : (j + 1) * piece] for v in (cross, cross_rest) for j in range(side // 2)]
 
     for j in late:
         stay[j] = to_partner(stay[j], j)
-    across[1] = to_partner(across[1], 1)
     small = small_step(small_step(small))
     total = shared.gather_pair(total, 1)
     grad_up = near[1] + jnp.concatenate(fars[2:], axis=0).astype(F32)[None]
-    total, small, stay, across, grad_up = tie(total, small, stay, across, grad_up)
-
-    for j in range(2, side):
+    total, small, stay, across, grad_up, near[0] = tie(total, small, stay, across, grad_up, near[0])
+
+    middle = (side + 1) // 2 + 1
+    for j in range(1, middle):
         across[j] = to_partner(across[j], j)
     total = shared.gather_pair(total, 0)
     small = small_sum(small, small_steps)
-    total, small, across = tie(total, small, across)
-
+    grad_down = near[0] + jnp.concatenate(fars[:2], axis=0).astype(F32)[None]
+    total, small, across, grad_down = tie(total, small, across, grad_down)
+
+    for j in range(middle, side):
+        across[j] = to_partner(across[j], j)
     nearest, farthest = shared.gather_first(total)
     grads = unmix(shared, *nearest)
     grads, farthest = tie(grads, farthest)

time: 493 us -> 488 us (0.990)
  waiting for transfers between devices: 135 us -> 122 us
    ppermute x36 -> x43, waiting for transfers between devices: 76.9 us -> 65.3 us  [swap(): return lax.ppermute(values, axis, [(i, i ^ bit) for i in range(size)])]
    ppermute x36 -> x43, starting transfers between devices: 36.5 us -> 46.3 us  [swap(): return lax.ppermute(values, axis, [(i, i ^ bit) for i in range(size)])]
    pallas_call x3 -> x4, Pallas kernels: 70.4 us -> 77 us  [the longest x2 48.3 us: expert_chunk(): pl.pallas_call(functools.partial(expert_kernel, parts), grid_spec=pltpu.P...]
    all_to_all x6 -> x5, starting transfers between devices: 35.3 us -> 29.4 us  [exchange(): lax.all_to_all(values, 'expert', split_axis=0, concat_axis=0, tiled=True)]
    all_to_all x6 -> x5, waiting for transfers between devices: 57 us -> 55.5 us  [exchange(): lax.all_to_all(values, 'expert', split_axis=0, concat_axis=0, tiled=True)]
  transfers between devices with their start and end apart: 44 -> 50, of which waited for: 22 -> 19; matrix products, arithmetic and copies ran while one was open for 6% -> 6% of each run, Pallas kernels for 44% -> 45%
where the time goes in v5:
time: 488 us; the launch traced here: 481 us
  Pallas kernels  226 us (46%)
  waiting for transfers between devices  122 us (25%)
  starting transfers between devices  75.7 us (16%)
  other arithmetic  25.5 us (5%)
  local copies, waits for them, and re-layouts  15.6 us (3%)
  between operations  15.4 us (3%)
    ppermute x43, waiting for transfers between devices, swap(): return lax.ppermute(values, axis, [(i, i ^ bit) for i in range(size)])  65.3 us
    all_to_all x5, waiting for transfers between devices, exchange(): lax.all_to_all(values, 'expert', split_axis=0, concat_axis=0, tiled=True)  55.5 us
    pallas_call x2, Pallas kernels, expert_chunk(): pl.pallas_call(functools.partial(expert_kernel, parts), grid_spec=pltpu.P...  48.3 us
    ppermute x43, starting transfers between devices, swap(): return lax.ppermute(values, axis, [(i, i ^ bit) for i in range(size)])  46.3 us
    pallas_call x1, Pallas kernels, attend_back(): pl.pallas_call(attend_back_kernel, grid=(pairs,), in_specs=[whole((1, cou...  34.4 us
    all_to_all x5, starting transfers between devices, exchange(): lax.all_to_all(values, 'expert', split_axis=0, concat_axis=0, tiled=True)  29.4 us
    pallas_call x2, Pallas kernels, expert_grads(): pl.pallas_call(functools.partial(expert_grads_kernel, count, near), grid=...  28.7 us
    pallas_call x1, Pallas kernels, attend(): pl.pallas_call(attend_kernel, grid=(pairs,), in_specs=[whole((count, 1)),...  19.1 us
  transfers between devices with their start and end apart: 50, of which 19 were waited for; matrix products, arithmetic and copies ran while one was open for 6% of the time, Pallas kernels for 45%

profile of v5, /device:TPU:9, one launch (start us, length us, event | category | flops | bytes accessed | tf_op | source)
XLA Modules:
  0.0 480.5 jit_solution(2678236438552302582)
XLA Ops:
  8.7 5.7 %all-to-all-start = ((bf16[8,128,1024]{2,1,0:T(8,128)(2,1)}), bf16[8,128,1024]{2,1,0:T(8,128)(2,1)S(1)}, u32[]{:S(2)}, u32[]{:S(2)}) async-start(bf16[8,128,1024]{2,1,0:T(8,128)(2,1)} %bitcast), calls=%async_computation | async-start | bytes 4194304 | tf_op jit(solution)/shard_map/all_to_all | solution.py:948
  23.1 37.9 %all-to-all-done = bf16[8,128,1024]{2,1,0:T(8,128)(2,1)S(1)} async-done(((bf16[8,128,1024]{2,1,0:T(8,128)(2,1)}), bf16[8,128,1024]{2,1,0:T(8,128)(2,1)S(1)}, u32[]{:S(2)}, u32[]{:S(2)}) %all-to-all-start) | async-done | bytes 2097184 | tf_op jit(solution)/shard_map/all_to_all | solution.py:948
  60.9 5.5 %all-to-all-start.3 = ((f32[8,1,128]{2,1,0:T(1,128)}), f32[8,1,128]{2,1,0:T(1,128)S(1)}, u32[]{:S(2)}, u32[]{:S(2)}) async-start(f32[8,1,128]{2,1,0:T(1,128)} %fusion.4), calls=%async_computation.3 | async-start | bytes 8192 | tf_op jit(solution)/shard_map/all_to_all | solution.py:948
  67.5 13.7 %entry.1 = (bf16[1024,1024]{1,0:T(8,128)(2,1)}, bf16[1024,1024]{1,0:T(8,128)(2,1)}, bf16[1024,1024]{1,0:T(8,128)(2,1)}, bf16[1024,1024]{1,0:T(8,128)(2,1)}, bf16[1024,1024]{1,0:T(8,128)(2,1)}) custom-call(bf16[1024,1024]{1,0:T(8,128)(2,1)} %bitcast.71, s32[1,1024]{1,0:T(1,128)} %pos_row, f32[1,1024]{1,0:T(1,128)} %bitcast.111, f32[1,1024]{1,0:T(1,128)} %bitcast.103, ...), custom_call_target="tpu_custom_call" | custom-call | flops 8589934592 | bytes 18874368 | tf_op jit(solution)/shard_map/entry/pallas_call | solution.py:126
  81.2 19.1 %attend.1 = (bf16[1024,1024]{1,0:T(8,128)(2,1)}, f32[8,8,1024]{2,1,0:T(8,128)}) custom-call(s32[1024,1]{1,0:T(8,128)} %iota_select_fusion.start_col, bf16[1024,1024]{1,0:T(8,128)(2,1)} %get-tuple-element.220.q_ref, bf16[1024,1024]{1,0:T(8,128)(2,1)} %get-tuple-element.221.k_ref, bf16[1024,1024]{1,0:T(8,128)(2,1)} %get-tuple-element.222.v_ref), custom_call_target="tpu_custom_call" | custom-call | flops 8589934592 | bytes 8388608 | tf_op jit(solution)/shard_map/attend/pallas_call | solution.py:261
  100.3 8.0 %leave.1 = (bf16[512,1024]{1,0:T(8,128)(2,1)}, bf16[1024,1024]{1,0:T(8,128)(2,1)}) custom-call(bf16[1024,1024]{1,0:T(8,128)(2,1)} %get-tuple-element.224.mixed.o_ref, bf16[1024,1024]{1,0:T(8,128)(2,1)} %refs_11_.1, f32[1,1024]{1,0:T(1,128)} %bitcast.106, bf16[1024,1024]{1,0:T(8,128)(2,1)} %get-tuple-element.225.tokens, f32[1024,1]{1,0:T(8,128)} %fusion.2.live_col.refs_10_, ...), custom_call_target="tpu_custom_call" | custom-call | flops 3221225472 | bytes 10485760 | tf_op jit(solution)/shard_map/leave/pallas_call | solution.py:311
  108.3 5.5 %all-to-all-start.2 = ((bf16[8,64,1024]{2,1,0:T(8,128)(2,1)}), bf16[8,64,1024]{2,1,0:T(8,128)(2,1)S(1)}, u32[]{:S(2)}, u32[]{:S(2)}) async-start(bf16[8,64,1024]{2,1,0:T(8,128)(2,1)} %bitcast.76), calls=%async_computation.2 | async-start | bytes 2097152 | tf_op jit(solution)/shard_map/all_to_all | solution.py:948
  115.1 4.0 pick.1
  119.0 17.7 %all-to-all-done.2 = bf16[8,64,1024]{2,1,0:T(8,128)(2,1)S(1)} async-done(((bf16[8,64,1024]{2,1,0:T(8,128)(2,1)}), bf16[8,64,1024]{2,1,0:T(8,128)(2,1)S(1)}, u32[]{:S(2)}, u32[]{:S(2)}) %all-to-all-start.2) | async-done | bytes 1048608 | tf_op jit(solution)/shard_map/all_to_all | solution.py:948
  136.7 7.1 %all-to-all-start.1 = ((bf16[8,64,1024]{2,1,0:T(8,128)(2,1)}), bf16[8,64,1024]{2,1,0:T(8,128)(2,1)S(1)}, u32[]{:S(2)}, u32[]{:S(2)}) async-start(bf16[8,64,1024]{2,1,0:T(8,128)(2,1)} %bitcast.75), calls=%async_computation.1 | async-start | bytes 2097152 | tf_op jit(solution)/shard_map/all_to_all | solution.py:948
  146.3 24.0 %expert_chunk.2 = (bf16[512,1024]{1,0:T(8,128)(2,1)}, bf16[6,512,1024]{2,1,0:T(8,128)(2,1)}, bf16[6,512,1024]{2,1,0:T(8,128)(2,1)}, f32[8,1024]{1,0:T(8,128)}, f32[4,1,1024]{2,1,0:T(1,128)}) custom-call(s32[1]{0:T(128)} %bitcast.16.device, s32[8]{0:T(128)} %get-tuple-element.229.source, bf16[512,1024]{1,0:T(8,128)(2,1)} %bitcast.67, ...), custom_call_target="tpu_custom_call" | custom-call | flops 12884901888 | bytes 16777216 | tf_op jit(solution)/shard_map/expert_chunk/pallas_call | solution.py:677
  171.4 5.6 %all-to-all-start.4 = ((bf16[8,64,1024]{2,1,0:T(8,128)(2,1)}), bf16[8,64,1024]{2,1,0:T(8,128)(2,1)S(1)}, u32[]{:S(2)}, u32[]{:S(2)}) async-start(bf16[8,64,1024]{2,1,0:T(8,128)(2,1)} %bitcast.77), calls=%async_computation.4 | async-start | bytes 2097152 | tf_op jit(solution)/shard_map/all_to_all | solution.py:948
  177.1 24.3 %expert_chunk.3 = (bf16[64,1024]{1,0:T(8,128)(2,1)}, bf16[64,1024]{1,0:T(8,128)(2,1)}, bf16[64,1024]{1,0:T(8,128)(2,1)}, bf16[64,1024]{1,0:T(8,128)(2,1)}, bf16[...) custom-call(s32[1]{0:T(128)} %bitcast.16.device, ...), custom_call_target="tpu_custom_call" | custom-call | flops 12884901888 | bytes 16777216 | tf_op jit(solution)/shard_map/expert_chunk/pallas_call | solution.py:677
  205.0 1.6 collective-permute-start.1
  207.8 8.0 %collective-permute-done.4 = bf16[256,1024]{1,0:T(8,128)(2,1)S(1)} collective-permute-done((bf16[256,1024]{1,0:T(8,128)(2,1)}, bf16[256,1024]{1,0:T(8,128)(2,1)S(1)}, u32[]{:S(2)}, u32[]{:S(2)}) %collective-permute-start.4) | collective-permute-done | bytes 524320 | tf_op jit(solution)/shard_map/ppermute | solution.py:944
  216.6 1.6 collective-permute-start.6
  219.7 14.0 %far_grads.1 = (bf16[224,1024]{1,0:T(8,128)(2,1)}, bf16[800,1024]{1,0:T(8,128)(2,1)}, bf16[304,1024]{1,0:T(8,128)(2,1)}, bf16[400,1024]{1,0:T(8,128)(2,1)}, bf16[320,1024]{1,0:T(8,128)(2,1)}) custom-call(bf16[6,512,1024]{2,1,0:T(8,128)(2,1)} %get-tuple-element.348.refs_0_, bf16[6,512,1024]{2,1,0:T(8,128)(2,1)} %get-tuple-element.349.refs_1_, ...), custom_call_target="tpu_custom_call" | custom-call | flops 8589934592 | bytes 20971520 | tf_op jit(solution)/shard_map/far_grads/pallas_call | solution.py:807
  235.1 9.0 %reenter.1 = (bf16[1024,1024]{1,0:T(8,128)(2,1)}, bf16[1024,1024]{1,0:T(8,128)(2,1)}, bf16[1024,1024]{1,0:T(8,128)(2,1)}, f32[1,1024]{1,0:T(1,128)}) custom-call(bf16[512,1024]{1,0:T(8,128)(2,1)} %bitcast.74, bf16[64,1024]{1,0:T(8,128)(2,1)} %get-tuple-element.266.refs_1_, bf16[64,1024]{1,0:T(8,128)(2,1)} %copy-done.29, bf16[64,1024]{1,0:T(8,128)(2,1)} %copy-done.30, ...), custom_call_target="tpu_custom_call" | custom-call | flops 4294967296 | bytes 10485760 | tf_op jit(solution)/shard_map/reenter/pallas_call | solution.py:401
  246.8 34.4 %attend_back.1.token_grads.grads = bf16[3,1024,1024]{2,1,0:T(8,128)(2,1)} custom-call(s32[1,1024]{1,0:T(1,128)} %compare_select_fusion.start_row, bf16[1024,1024]{1,0:T(8,128)(2,1)} %get-tuple-element.220.q_ref, bf16[1024,1024]{1,0:T(8,128)(2,1)} %get-tuple-element.221.k_ref, bf16[1024,1024]{1,0:T(8,128)(2,1)} %get-tuple-element.222.v_ref, ...), custom_call_target="tpu_custom_call" | custom-call | flops 21474836480 | bytes 16777216 | tf_op jit(solution)/shard_map/attend_back/pallas_call | solution.py:495
  282.0 14.2 %shared_grads.1 = (bf16[4,512,1024]{2,1,0:T(8,128)(2,1)}, bf16[4,512,1024]{2,1,0:T(8,128)(2,1)}) custom-call(s32[2]{0:T(128)} %pad_add_fusion.1.codes, bf16[1024,1024]{1,0:T(8,128)(2,1)} %get-tuple-element.290.normed, bf16[1024,1024]{1,0:T(8,128)(2,1)} %get-tuple-element.224.mixed.o_ref, bf16[3,1024,1024]{2,1,0:T(8,128)(2,1)} %attend_back.1.token_grads.grads, ...), custom_call_target="tpu_custom_call" | custom-call | flops 8589934592 | bytes 25165824 | tf_op jit(solution)/shard_map/shared_grads/pallas_call | solution.py:858
  296.3 3.6 collective-permute-start.12
  300.7 6.2 %collective-permute-done.12 = bf16[4,512,1024]{2,1,0:T(8,128)(2,1)S(1)} collective-permute-done((bf16[4,512,1024]{2,1,0:T(8,128)(2,1)}, bf16[4,512,1024]{2,1,0:T(8,128)(2,1)S(1)}, u32[]{:S(2)}, u32[]{:S(2)}) %collective-permute-start.12) | collective-permute-done | bytes 4194336 | tf_op jit(solution)/shard_map/ppermute | solution.py:944
  306.9 4.4 add_convert_fusion.2
  313.8 18.2 %finish.1 = (bf16[128,1024]{1,0:T(8,128)(2,1)}, bf16[128,1024]{1,0:T(8,128)(2,1)}, bf16[128,1024]{1,0:T(8,128)(2,1)}, bf16[128,1024]{1,0:T(8,128)(2,1)}, bf16[25...) custom-call(bf16[3,1024,1024]{2,1,0:T(8,128)(2,1)} %attend_back.1.token_grads.grads, ...), custom_call_target="tpu_custom_call" | custom-call | flops 8589934592 | bytes 20971520 | tf_op jit(solution)/shard_map/finish/pallas_call | solution.py:560
  332.1 4.0 collective-permute-done.14
  336.1 1.6 add_convert_fusion
  337.8 1.9 add_convert_fusion.1
  341.3 1.8 collective-permute-start.17
  343.1 2.0 collective-permute-start.18
  345.7 6.0 %collective-permute-done.15 = bf16[4,64,1024]{2,1,0:T(8,128)(2,1)S(1)} collective-permute-done((bf16[4,64,1024]{2,1,0:T(8,128)(2,1)S(1)}, bf16[4,64,1024]{2,1,0:T(8,128)(2,1)S(1)}, u32[]{:S(2)}, u32[]{:S(2)}) %collective-permute-start.15) | collective-permute-done | bytes 524320 | tf_op jit(solution)/shard_map/ppermute | solution.py:944
  353.3 2.4 collective-permute-done.18.refs_1_
  355.7 2.2 collective-permute-done.19.refs_2_
  358.6 2.2 collective-permute-start.20
  363.6 15.3 %expert_out.1 = bf16[8,128,1024]{2,1,0:T(8,128)(2,1)} custom-call(s32[1]{0:T(128)} %bitcast.16.device, bf16[6,512,1024]{2,1,0:T(8,128)(2,1)} %get-tuple-element.348.refs_0_, bf16[6,512,1024]{2,1,0:T(8,128)(2,1)} %get-tuple-element.349.refs_1_, bf16[6,512,1024]{2,1,0:T(8,128)(2,1)} %get-tuple-element.235.refs_2_, ...), custom_call_target="tpu_custom_call" | custom-call | flops 8589934592 | bytes 16777216 | tf_op jit(solution)/shard_map/expert_out/pallas_call | solution.py:748
  378.9 5.9 %collective-permute-done.22 = bf16[4,2,16,1024]{3,2,0,1:T(8,128)(2,1)S(1)} collective-permute-done((bf16[4,2,16,1024]{3,2,0,1:T(8,128)(2,1)S(1)}, bf16[4,2,16,1024]{3,2,0,1:T(8,128)(2,1)S(1)}, u32[]{:S(2)}, u32[]{:S(2)}) %collective-permute-start.22) | collective-permute-done | bytes 262176 | tf_op jit(solution)/shard_map/ppermute | solution.py:944
  385.1 1.8 collective-permute-start.26
  389.7 14.7 %near_grads.1 = (f32[1,1024,1024]{2,1,0:T(8,128)}, f32[1,1024,1024]{2,1,0:T(8,128)}) custom-call(bf16[6,512,1024]{2,1,0:T(8,128)(2,1)} %get-tuple-element.348.refs_0_, bf16[6,512,1024]{2,1,0:T(8,128)(2,1)} %get-tuple-element.349.refs_1_, bf16[6,512,1024]{2,1,0:T(8,128)(2,1)} %collective-permute-done.refs_2_, bf16[6,512,1024]{2,1,0:T(8,128)(2,1)} %copy-done.25), custom_call_target="tpu_custom_call" | custom-call | flops 8589934592 | bytes 20971520 | tf_op jit(solution)/shard_map/near_grads/pallas_call | solution.py:807
  405.6 3.2 collective-permute-done.27
  412.7 2.8 convert_add_fusion.1
  416.5 6.7 %collective-permute-done.33 = f32[16,1024]{1,0:T(8,128)S(1)} collective-permute-done((f32[16,1024]{1,0:T(8,128)S(1)}, f32[16,1024]{1,0:T(8,128)S(1)}, u32[]{:S(2)}, u32[]{:S(2)}) %collective-permute-start.33) | collective-permute-done | bytes 65568 | tf_op jit(solution)/shard_map/ppermute | solution.py:944
  429.6 2.8 convert_add_fusion
  432.4 5.6 %collective-permute-done.38 = f32[8,1024]{1,0:T(8,128)S(1)} collective-permute-done((f32[8,1024]{1,0:T(8,128)S(1)}, f32[8,1024]{1,0:T(8,128)S(1)}, u32[]{:S(2)}, u32[]{:S(2)}) %collective-permute-start.38) | collective-permute-done | bytes 32800 | tf_op jit(solution)/shard_map/ppermute | solution.py:944
  438.0 8.2 %collective-permute-done.36 = bf16[4,128,1024]{2,1,0:T(8,128)(2,1)S(1)} collective-permute-done((bf16[4,128,1024]{2,1,0:T(8,128)(2,1)S(1)}, bf16[4,128,1024]{2,1,0:T(8,128)(2,1)S(1)}, u32[]{:S(2)}, u32[]{:S(2)}) %collective-permute-start.36) | collective-permute-done | bytes 1048608 | tf_op jit(solution)/shard_map/ppermute | solution.py:944
  446.7 1.5 constant_dynamic-update-slice_fusion.7
  449.8 3.4 collective-permute-start.41
  454.1 5.5 %unmix.2 = (f32[1024,1024]{1,0:T(8,128)}, f32[1024,1024]{1,0:T(8,128)}, f32[1024,1024]{1,0:T(8,128)}, f32[1024,1024]{1,0:T(8,128)}) custom-call(s32[2]{0:T(128)} %pad_add_fusion.1.codes, s32[1]{0:T(128)} %bitcast.39.half_place.source, s32[1]{0:T(128)} %bitcast.39.half_place.source, bf16[4,512,1024]{2,1,0:T(8,128)(2,1)} %constant_dynamic-update-slice_fusion.6.pieces), custom_call_target="tpu_custom_call" | custom-call | flops 2097152 | bytes 12582912 | tf_op jit(solution)/shard_map/unmix/pallas_call | solution.py:919
  460.7 4.1 collective-permute-done.42.refs_7_
  465.6 7.7 %unmix.3 = (f32[1024,1024]{1,0:T(8,128)}, f32[1024,1024]{1,0:T(8,128)}, f32[1024,1024]{1,0:T(8,128)}, f32[1024,1024]{1,0:T(8,128)}, bf16[1024,1024]{1,0:T(8,128)(2,1)}) custom-call(s32[2]{0:T(128)} %pad_add_fusion.1.codes, s32[1]{0:T(128)S(6)} %sub.24.half_place, ...), custom_call_target="tpu_custom_call", output_to_operand_aliasing={{0}: (12, {}), {1}: (13, {}), {2}: (14, {}), {3}: (15, {})} | custom-call | flops 2097152 | bytes 12582912 | tf_op jit(solution)/shard_map/unmix/pallas_call | solution.py:919
  (223 shorter events, 58.5 us)
Async XLA Ops:
  7.2 139.1 %all-gather.5.cloned.1.call-start = ((), (), s32[]{:S(2)}) async-start(), calls=%async_computation.6 | async-start | bytes 10485760 | tf_op jit(solution)/shard_map/all_gather | solution.py:1090
  7.9 138.4 %all-gather.3.cloned.1.call-start = ((), (), s32[]{:S(2)}) async-start(), calls=%async_computation.5 | async-start | bytes 10485760 | tf_op jit(solution)/shard_map/all_gather | solution.py:1089
  8.7 52.2 %all-to-all-start = ((bf16[8,128,1024]{2,1,0:T(8,128)(2,1)}), bf16[8,128,1024]{2,1,0:T(8,128)(2,1)S(1)}, u32[]{:S(2)}, u32[]{:S(2)}) async-start(bf16[8,128,1024]{2,1,0:T(8,128)(2,1)} %bitcast), calls=%async_computation | async-start | bytes 4194304 | tf_op jit(solution)/shard_map/all_to_all | solution.py:948
  60.9 47.4 %all-to-all-start.3 = ((f32[8,1,128]{2,1,0:T(1,128)}), f32[8,1,128]{2,1,0:T(1,128)S(1)}, u32[]{:S(2)}, u32[]{:S(2)}) async-start(f32[8,1,128]{2,1,0:T(1,128)} %fusion.4), calls=%async_computation.3 | async-start | bytes 8192 | tf_op jit(solution)/shard_map/all_to_all | solution.py:948
  108.3 28.4 %all-to-all-start.2 = ((bf16[8,64,1024]{2,1,0:T(8,128)(2,1)}), bf16[8,64,1024]{2,1,0:T(8,128)(2,1)S(1)}, u32[]{:S(2)}, u32[]{:S(2)}) async-start(bf16[8,64,1024]{2,1,0:T(8,128)(2,1)} %bitcast.76), calls=%async_computation.2 | async-start | bytes 2097152 | tf_op jit(solution)/shard_map/all_to_all | solution.py:948
  136.7 33.6 %all-to-all-start.1 = ((bf16[8,64,1024]{2,1,0:T(8,128)(2,1)}), bf16[8,64,1024]{2,1,0:T(8,128)(2,1)S(1)}, u32[]{:S(2)}, u32[]{:S(2)}) async-start(bf16[8,64,1024]{2,1,0:T(8,128)(2,1)} %bitcast.75), calls=%async_computation.1 | async-start | bytes 2097152 | tf_op jit(solution)/shard_map/all_to_all | solution.py:948
  170.3 31.1 %collective-permute-start = (bf16[6,512,1024]{2,1,0:T(8,128)(2,1)}, bf16[6,512,1024]{2,1,0:T(8,128)(2,1)}, u32[]{:S(2)}, u32[]{:S(2)}) collective-permute-start(bf16[6,512,1024]{2,1,0:T(8,128)(2,1)} %get-tuple-element.235.refs_2_), channel_id=1, source_target_pairs={{0,1},{1,0},{2,3},{3,2},{4,5},{5,4},{6,7},{7,6},{8,9},{9,8},{10,11... | collective-permute-start | bytes 18874376 | tf_op jit(solution)/shard_map/ppermute | solution.py:944
  171.4 30.0 %all-to-all-start.4 = ((bf16[8,64,1024]{2,1,0:T(8,128)(2,1)}), bf16[8,64,1024]{2,1,0:T(8,128)(2,1)S(1)}, u32[]{:S(2)}, u32[]{:S(2)}) async-start(bf16[8,64,1024]{2,1,0:T(8,128)(2,1)} %bitcast.77), calls=%async_computation.4 | async-start | bytes 2097152 | tf_op jit(solution)/shard_map/all_to_all | solution.py:948
  201.4 14.4 %collective-permute-start.5 = (bf16[6,512,1024]{2,1,0:T(8,128)(2,1)}, bf16[6,512,1024]{2,1,0:T(8,128)(2,1)S(1)}, u32[]{:S(2)}, u32[]{:S(2)}) collective-permute-start(bf16[6,512,1024]{2,1,0:T(8,128)(2,1)} %get-tuple-element.250.refs_3_), channel_id=1, source_target_pairs={{0,1},{1,0},{2,3},{3,2},{4,5},{5,4},{6,7},{7,6},{8,9},{9,8},{10,11... | collective-permute-start | bytes 18874376 | tf_op jit(solution)/shard_map/ppermute | solution.py:944
  202.1 13.7 %collective-permute-start.4 = (bf16[256,1024]{1,0:T(8,128)(2,1)}, bf16[256,1024]{1,0:T(8,128)(2,1)S(1)}, u32[]{:S(2)}, u32[]{:S(2)}) collective-permute-start(bf16[256,1024]{1,0:T(8,128)(2,1)} %get-tuple-element.249), channel_id=1, source_target_pairs={{0,4},{4,0},{8,12},{12,8},{16,20},{20,16},{24,28},{28,24},{1,5},{5... | collective-permute-start | bytes 1572872 | tf_op jit(solution)/shard_map/ppermute | solution.py:944
  205.0 14.0 %collective-permute-start.1 = (bf16[64,1024]{1,0:T(8,128)(2,1)}, bf16[64,1024]{1,0:T(8,128)(2,1)S(1)}, u32[]{:S(2)}, u32[]{:S(2)}) collective-permute-start(bf16[64,1024]{1,0:T(8,128)(2,1)} %get-tuple-element.246), channel_id=1, source_target_pairs={{0,8},{4,12},{8,0},{12,4},{16,24},{20,28},{24,16},{28,20},{1,9},{5... | collective-permute-start | bytes 393224 | tf_op jit(solution)/shard_map/ppermute | solution.py:944
  206.6 27.1 %collective-permute-start.2 = (bf16[64,1024]{1,0:T(8,128)(2,1)}, bf16[64,1024]{1,0:T(8,128)(2,1)S(1)}, u32[]{:S(2)}, u32[]{:S(2)}) collective-permute-start(bf16[64,1024]{1,0:T(8,128)(2,1)} %get-tuple-element.247), channel_id=1, source_target_pairs={{0,16},{4,20},{8,24},{12,28},{16,0},{20,4},{24,8},{28,12},{1,17},{... | collective-permute-start | bytes 393224 | tf_op jit(solution)/shard_map/ppermute | solution.py:944
  207.3 26.4 %collective-permute-start.3 = (bf16[64,1024]{1,0:T(8,128)(2,1)}, bf16[64,1024]{1,0:T(8,128)(2,1)S(1)}, u32[]{:S(2)}, u32[]{:S(2)}) collective-permute-start(bf16[64,1024]{1,0:T(8,128)(2,1)} %get-tuple-element.248), channel_id=1, source_target_pairs={{0,24},{4,28},{8,16},{12,20},{16,8},{20,12},{24,0},{28,4},{1,25},{... | collective-permute-start | bytes 393224 | tf_op jit(solution)/shard_map/ppermute | solution.py:944
  216.6 17.2 %collective-permute-start.6 = (bf16[64,1024]{1,0:T(8,128)(2,1)S(1)}, bf16[64,1024]{1,0:T(8,128)(2,1)S(1)}, u32[]{:S(2)}, u32[]{:S(2)}) collective-permute-start(bf16[64,1024]{1,0:T(8,128)(2,1)S(1)} %get-tuple-element.434), channel_id=1, source_target_pairs={{0,8},{4,12},{8,0},{12,4},{16,24},{20,28},{24,16},{28,20},{1,9},{5... | collective-permute-start | bytes 393224 | tf_op jit(solution)/shard_map/ppermute | solution.py:944
  218.2 15.6 %collective-permute-start.7 = (bf16[64,1024]{1,0:T(8,128)(2,1)S(1)}, bf16[64,1024]{1,0:T(8,128)(2,1)S(1)}, u32[]{:S(2)}, u32[]{:S(2)}) collective-permute-start(bf16[64,1024]{1,0:T(8,128)(2,1)S(1)} %get-tuple-element.433), channel_id=1, source_target_pairs={{0,16},{4,20},{8,24},{12,28},{16,0},{20,4},{24,8},{28,12},{1,17},{... | collective-permute-start | bytes 393224 | tf_op jit(solution)/shard_map/ppermute | solution.py:944
  218.9 14.8 %collective-permute-start.8 = (bf16[64,1024]{1,0:T(8,128)(2,1)S(1)}, bf16[64,1024]{1,0:T(8,128)(2,1)S(1)}, u32[]{:S(2)}, u32[]{:S(2)}) collective-permute-start(bf16[64,1024]{1,0:T(8,128)(2,1)S(1)} %get-tuple-element.432), channel_id=1, source_target_pairs={{0,24},{4,28},{8,16},{12,20},{16,8},{20,12},{24,0},{28,4},{1,25},{... | collective-permute-start | bytes 393224 | tf_op jit(solution)/shard_map/ppermute | solution.py:944
  233.8 11.0 %collective-permute-start.9 = (bf16[224,1024]{1,0:T(8,128)(2,1)}, bf16[224,1024]{1,0:T(8,128)(2,1)S(1)}, u32[]{:S(2)}, u32[]{:S(2)}) collective-permute-start(bf16[224,1024]{1,0:T(8,128)(2,1)} %get-tuple-element.276), channel_id=1, source_target_pairs={{0,2},{1,3},{2,0},{3,1},{4,6},{5,7},{6,4},{7,5},{8,10},{9,11},{10,... | collective-permute-start | bytes 1376264 | tf_op jit(solution)/shard_map/ppermute | solution.py:944
  245.5 35.7 %collective-permute-start.10 = (bf16[800,1024]{1,0:T(8,128)(2,1)}, bf16[800,1024]{1,0:T(8,128)(2,1)S(1)}, u32[]{:S(2)}, u32[]{:S(2)}) collective-permute-start(bf16[800,1024]{1,0:T(8,128)(2,1)} %get-tuple-element.284), channel_id=1, source_target_pairs={{0,2},{1,3},{2,0},{3,1},{4,6},{5,7},{6,4},{7,5},{8,10},{9,11},{10,... | collective-permute-start | bytes 4915208 | tf_op jit(solution)/shard_map/ppermute | solution.py:944
  281.2 15.1 %collective-permute-start.11 = (bf16[304,1024]{1,0:T(8,128)(2,1)S(1)}, bf16[304,1024]{1,0:T(8,128)(2,1)S(1)}, u32[]{:S(2)}, u32[]{:S(2)}) collective-permute-start(bf16[304,1024]{1,0:T(8,128)(2,1)S(1)} %copy-done.26), channel_id=1, source_target_pairs={{0,2},{1,3},{2,0},{3,1},{4,6},{5,7},{6,4},{7,5},{8,10},{9,11},{10,... | collective-permute-start | bytes 1867784 | tf_op jit(solution)/shard_map/ppermute | solution.py:944
  296.3 10.6 %collective-permute-start.12 = (bf16[4,512,1024]{2,1,0:T(8,128)(2,1)}, bf16[4,512,1024]{2,1,0:T(8,128)(2,1)S(1)}, u32[]{:S(2)}, u32[]{:S(2)}) collective-permute-start(bf16[4,512,1024]{2,1,0:T(8,128)(2,1)} %get-tuple-element.302), channel_id=1, source_target_pairs={{0,1},{1,0},{2,3},{3,2},{4,5},{5,4},{6,7},{7,6},{8,9},{9,8},{10,11... | collective-permute-start | bytes 12582920 | tf_op jit(solution)/shard_map/ppermute | solution.py:944
  311.3 24.8 %collective-permute-start.14 = (bf16[4,128,1024]{2,1,0:T(8,128)(2,1)}, bf16[4,128,1024]{2,1,0:T(8,128)(2,1)}, u32[]{:S(2)}, u32[]{:S(2)}) collective-permute-start(bf16[4,128,1024]{2,1,0:T(8,128)(2,1)} %get-tuple-element.318), channel_id=1, source_target_pairs={{0,4},{4,0},{8,12},{12,8},{16,20},{20,16},{24,28},{28,24},{1,5},{5... | collective-permute-start | bytes 3145736 | tf_op jit(solution)/shard_map/ppermute | solution.py:944
  313.6 24.2 %collective-permute-start.13 = (bf16[4,128,1024]{2,1,0:T(8,128)(2,1)S(1)}, bf16[4,128,1024]{2,1,0:T(8,128)(2,1)}, u32[]{:S(2)}, u32[]{:S(2)}) collective-permute-start(bf16[4,128,1024]{2,1,0:T(8,128)(2,1)S(1)} %get-tuple-element.316), channel_id=1, source_target_pairs={{0,2},{1,3},{2,0},{3,1},{4,6},{5,7},{6,4},{7,5},{8,10},{9,11},{10,... | collective-permute-start | bytes 3145736 | tf_op jit(solution)/shard_map/ppermute | solution.py:944
  339.7 12.0 %collective-permute-start.15 = (bf16[4,64,1024]{2,1,0:T(8,128)(2,1)S(1)}, bf16[4,64,1024]{2,1,0:T(8,128)(2,1)S(1)}, u32[]{:S(2)}, u32[]{:S(2)}) collective-permute-start(bf16[4,64,1024]{2,1,0:T(8,128)(2,1)S(1)} %slice.172), channel_id=1, source_target_pairs={{0,4},{4,0},{8,12},{12,8},{16,20},{20,16},{24,28},{28,24},{1,5},{5... | collective-permute-start | bytes 1572872 | tf_op jit(solution)/shard_map/ppermute | solution.py:944
  341.0 12.0 %collective-permute-start.16 = (bf16[4,64,1024]{2,1,0:T(8,128)(2,1)S(1)}, bf16[4,64,1024]{2,1,0:T(8,128)(2,1)S(1)}, u32[]{:S(2)}, u32[]{:S(2)}) collective-permute-start(bf16[4,64,1024]{2,1,0:T(8,128)(2,1)S(1)} %slice.174), channel_id=1, source_target_pairs={{0,2},{1,3},{2,0},{3,1},{4,6},{5,7},{6,4},{7,5},{8,10},{9,11},{10,... | collective-permute-start | bytes 1572872 | tf_op jit(solution)/shard_map/ppermute | solution.py:944
  343.1 12.5 %collective-permute-start.18 = (bf16[128,1024]{1,0:T(8,128)(2,1)S(1)}, bf16[128,1024]{1,0:T(8,128)(2,1)S(1)}, u32[]{:S(2)}, u32[]{:S(2)}) collective-permute-start(bf16[128,1024]{1,0:T(8,128)(2,1)S(1)} %copy-done.28), channel_id=1, source_target_pairs={{0,8},{4,12},{8,0},{12,4},{16,24},{20,28},{24,16},{28,20},{1,9},{5... | collective-permute-start | bytes 786440 | tf_op jit(solution)/shard_map/ppermute | solution.py:944
  345.1 12.8 %collective-permute-start.19 = (bf16[128,1024]{1,0:T(8,128)(2,1)S(1)}, bf16[128,1024]{1,0:T(8,128)(2,1)S(1)}, u32[]{:S(2)}, u32[]{:S(2)}) collective-permute-start(bf16[128,1024]{1,0:T(8,128)(2,1)S(1)} %copy-done.27), channel_id=1, source_target_pairs={{0,16},{4,20},{8,24},{12,28},{16,0},{20,4},{24,8},{28,12},{1,17},{... | collective-permute-start | bytes 786440 | tf_op jit(solution)/shard_map/ppermute | solution.py:944
  358.6 20.2 %collective-permute-start.20 = (bf16[4,2,16,1024]{3,2,0,1:T(8,128)(2,1)}, bf16[4,2,16,1024]{3,2,0,1:T(8,128)(2,1)S(1)}, u32[]{:S(2)}, u32[]{:S(2)}) collective-permute-start(bf16[4,2,16,1024]{3,2,0,1:T(8,128)(2,1)} %get-tuple-element.425), channel_id=1, source_target_pairs={{0,16},{4,20},{8,24},{12,28},{16,0},{20,4},{24,8},{28,12},{1,17},{... | collective-permute-start | bytes 786440 | tf_op jit(solution)/shard_map/ppermute | solution.py:944
  360.9 18.0 %collective-permute-start.21 = (bf16[4,2,16,1024]{3,2,0,1:T(8,128)(2,1)S(1)}, bf16[4,2,16,1024]{3,2,0,1:T(8,128)(2,1)S(1)}, u32[]{:S(2)}, u32[]{:S(2)}) collective-permute-start(bf16[4,2,16,1024]{3,2,0,1:T(8,128)(2,1)S(1)} %get-tuple-element.427), channel_id=1, source_target_pairs={{0,8},{4,12},{8,0},{12,4},{16,24},{20,28},{24,16},{28,20},{1,9},{5... | collective-permute-start | bytes 786440 | tf_op jit(solution)/shard_map/ppermute | solution.py:944
  360.9 23.9 %collective-permute-start.22 = (bf16[4,2,16,1024]{3,2,0,1:T(8,128)(2,1)S(1)}, bf16[4,2,16,1024]{3,2,0,1:T(8,128)(2,1)S(1)}, u32[]{:S(2)}, u32[]{:S(2)}) collective-permute-start(bf16[4,2,16,1024]{3,2,0,1:T(8,128)(2,1)S(1)} %get-tuple-element.426), channel_id=1, source_target_pairs={{0,24},{4,28},{8,16},{12,20},{16,8},{20,12},{24,0},{28,4},{1,25},{... | collective-permute-start | bytes 786440 | tf_op jit(solution)/shard_map/ppermute | solution.py:944
  361.6 23.5 %collective-permute-start.23 = (bf16[400,1024]{1,0:T(8,128)(2,1)}, bf16[400,1024]{1,0:T(8,128)(2,1)S(1)}, u32[]{:S(2)}, u32[]{:S(2)}) collective-permute-start(bf16[400,1024]{1,0:T(8,128)(2,1)} %get-tuple-element.341), channel_id=1, source_target_pairs={{0,2},{1,3},{2,0},{3,1},{4,6},{5,7},{6,4},{7,5},{8,10},{9,11},{10,... | collective-permute-start | bytes 2457608 | tf_op jit(solution)/shard_map/ppermute | solution.py:944
  362.9 22.1 %collective-permute-start.24 = (bf16[256,1024]{1,0:T(8,128)(2,1)}, bf16[256,1024]{1,0:T(8,128)(2,1)S(1)}, u32[]{:S(2)}, u32[]{:S(2)}) collective-permute-start(bf16[256,1024]{1,0:T(8,128)(2,1)} %get-tuple-element.343), channel_id=1, source_target_pairs={{0,4},{4,0},{8,12},{12,8},{16,20},{20,16},{24,28},{28,24},{1,5},{5... | collective-permute-start | bytes 1572872 | tf_op jit(solution)/shard_map/ppermute | solution.py:944
  385.0 19.4 %collective-permute-start.25 = (bf16[4,2,16,1024]{3,2,0,1:T(8,128)(2,1)S(1)}, bf16[4,2,16,1024]{3,2,0,1:T(8,128)(2,1)}, u32[]{:S(2)}, u32[]{:S(2)}) collective-permute-start(bf16[4,2,16,1024]{3,2,0,1:T(8,128)(2,1)S(1)} %add_convert_fusion.8), channel_id=1, source_target_pairs={{0,16},{4,20},{8,24},{12,28},{16,0},{20,4},{24,8},{28,12},{1,17},{... | collective-permute-start | bytes 786440 | tf_op jit(solution)/shard_map/ppermute | solution.py:944
  385.1 20.5 %collective-permute-start.26 = (bf16[4,2,16,1024]{3,2,0,1:T(8,128)(2,1)S(1)}, bf16[4,2,16,1024]{3,2,0,1:T(8,128)(2,1)S(1)}, u32[]{:S(2)}, u32[]{:S(2)}) collective-permute-start(bf16[4,2,16,1024]{3,2,0,1:T(8,128)(2,1)S(1)} %add_convert_fusion.8), channel_id=1, source_target_pairs={{0,8},{4,12},{8,0},{12,4},{16,24},{20,28},{24,16},{28,20},{1,9},{5... | collective-permute-start | bytes 786440 | tf_op jit(solution)/shard_map/ppermute | solution.py:944
  386.9 21.9 %collective-permute-start.27 = (bf16[4,2,16,1024]{3,2,0,1:T(8,128)(2,1)S(1)}, bf16[4,2,16,1024]{3,2,0,1:T(8,128)(2,1)S(1)}, u32[]{:S(2)}, u32[]{:S(2)}) collective-permute-start(bf16[4,2,16,1024]{3,2,0,1:T(8,128)(2,1)S(1)} %add_convert_fusion.8), channel_id=1, source_target_pairs={{0,24},{4,28},{8,16},{12,20},{16,8},{20,12},{24,0},{28,4},{1,25},{... | collective-permute-start | bytes 786440 | tf_op jit(solution)/shard_map/ppermute | solution.py:944
  387.7 21.2 %collective-permute-start.28 = (bf16[320,1024]{1,0:T(8,128)(2,1)}, bf16[320,1024]{1,0:T(8,128)(2,1)S(1)}, u32[]{:S(2)}, u32[]{:S(2)}) collective-permute-start(bf16[320,1024]{1,0:T(8,128)(2,1)} %get-tuple-element.358), channel_id=1, source_target_pairs={{0,2},{1,3},{2,0},{3,1},{4,6},{5,7},{6,4},{7,5},{8,10},{9,11},{10,... | collective-permute-start | bytes 1966088 | tf_op jit(solution)/shard_map/ppermute | solution.py:944
  389.1 19.8 %collective-permute-start.29 = (bf16[256,1024]{1,0:T(8,128)(2,1)}, bf16[256,1024]{1,0:T(8,128)(2,1)S(1)}, u32[]{:S(2)}, u32[]{:S(2)}) collective-permute-start(bf16[256,1024]{1,0:T(8,128)(2,1)} %get-tuple-element.364), channel_id=1, source_target_pairs={{0,4},{4,0},{8,12},{12,8},{16,20},{20,16},{24,28},{28,24},{1,5},{5... | collective-permute-start | bytes 1572872 | tf_op jit(solution)/shard_map/ppermute | solution.py:944
  409.0 6.6 %collective-permute-start.32 = (f32[8,1024]{1,0:T(8,128)S(1)}, f32[8,1024]{1,0:T(8,128)S(1)}, u32[]{:S(2)}, u32[]{:S(2)}) collective-permute-start(f32[8,1024]{1,0:T(8,128)S(1)} %slice.181), channel_id=1, source_target_pairs={{0,4},{4,0},{8,12},{12,8},{16,20},{20,16},{24,28},{28,24},{1,5},{5... | collective-permute-start | bytes 98312 | tf_op jit(solution)/shard_map/ppermute | solution.py:944
  409.7 13.6 %collective-permute-start.31 = (bf16[4,64,1024]{2,1,0:T(8,128)(2,1)S(1)}, bf16[4,64,1024]{2,1,0:T(8,128)(2,1)S(1)}, u32[]{:S(2)}, u32[]{:S(2)}) collective-permute-start(bf16[4,64,1024]{2,1,0:T(8,128)(2,1)S(1)} %get-tuple-element.366), channel_id=1, source_target_pairs={{0,2},{1,3},{2,0},{3,1},{4,6},{5,7},{6,4},{7,5},{8,10},{9,11},{10,... | collective-permute-start | bytes 1572872 | tf_op jit(solution)/shard_map/ppermute | solution.py:944
  411.1 12.2 %collective-permute-start.30 = (bf16[4,64,1024]{2,1,0:T(8,128)(2,1)S(1)}, bf16[4,64,1024]{2,1,0:T(8,128)(2,1)S(1)}, u32[]{:S(2)}, u32[]{:S(2)}) collective-permute-start(bf16[4,64,1024]{2,1,0:T(8,128)(2,1)S(1)} %get-tuple-element.365), channel_id=1, source_target_pairs={{0,4},{4,0},{8,12},{12,8},{16,20},{20,16},{24,28},{28,24},{1,5},{5... | collective-permute-start | bytes 1572872 | tf_op jit(solution)/shard_map/ppermute | solution.py:944
  411.9 11.7 %collective-permute-start.34 = (bf16[128,1024]{1,0:T(8,128)(2,1)}, bf16[128,1024]{1,0:T(8,128)(2,1)S(1)}, u32[]{:S(2)}, u32[]{:S(2)}) collective-permute-start(bf16[128,1024]{1,0:T(8,128)(2,1)} %get-tuple-element.371), channel_id=1, source_target_pairs={{0,24},{4,28},{8,16},{12,20},{16,8},{20,12},{24,0},{28,4},{1,25},{... | collective-permute-start | bytes 786440 | tf_op jit(solution)/shard_map/ppermute | solution.py:944
  415.6 7.6 %collective-permute-start.33 = (f32[16,1024]{1,0:T(8,128)S(1)}, f32[16,1024]{1,0:T(8,128)S(1)}, u32[]{:S(2)}, u32[]{:S(2)}) collective-permute-start(f32[16,1024]{1,0:T(8,128)S(1)} %pad_maximum_fusion.5), channel_id=1, source_target_pairs={{0,2},{1,3},{2,0},{3,1},{4,6},{5,7},{6,4},{7,5},{8,10},{9,11},{10,... | collective-permute-start | bytes 196616 | tf_op jit(solution)/shard_map/ppermute | solution.py:944
  423.6 22.6 %collective-permute-start.36 = (bf16[4,128,1024]{2,1,0:T(8,128)(2,1)S(1)}, bf16[4,128,1024]{2,1,0:T(8,128)(2,1)S(1)}, u32[]{:S(2)}, u32[]{:S(2)}) collective-permute-start(bf16[4,128,1024]{2,1,0:T(8,128)(2,1)S(1)} %pad_maximum_fusion.4), channel_id=1, source_target_pairs={{0,4},{4,0},{8,12},{12,8},{16,20},{20,16},{24,28},{28,24},{1,5},{5... | collective-permute-start | bytes 3145736 | tf_op jit(solution)/shard_map/ppermute | solution.py:944
  424.3 22.2 %collective-permute-start.35 = (bf16[4,128,1024]{2,1,0:T(8,128)(2,1)S(1)}, bf16[4,128,1024]{2,1,0:T(8,128)(2,1)S(1)}, u32[]{:S(2)}, u32[]{:S(2)}) collective-permute-start(bf16[4,128,1024]{2,1,0:T(8,128)(2,1)S(1)} %pad_maximum_fusion.3), channel_id=1, source_target_pairs={{0,2},{1,3},{2,0},{3,1},{4,6},{5,7},{6,4},{7,5},{8,10},{9,11},{10,... | collective-permute-start | bytes 3145736 | tf_op jit(solution)/shard_map/ppermute | solution.py:944
  425.7 21.0 %collective-permute-start.39 = (bf16[128,1024]{1,0:T(8,128)(2,1)S(1)}, bf16[128,1024]{1,0:T(8,128)(2,1)S(1)}, u32[]{:S(2)}, u32[]{:S(2)}) collective-permute-start(bf16[128,1024]{1,0:T(8,128)(2,1)S(1)} %get-tuple-element.383), channel_id=1, source_target_pairs={{0,8},{4,12},{8,0},{12,4},{16,24},{20,28},{24,16},{28,20},{1,9},{5... | collective-permute-start | bytes 786440 | tf_op jit(solution)/shard_map/ppermute | solution.py:944
  427.2 19.5 %collective-permute-start.40 = (bf16[128,1024]{1,0:T(8,128)(2,1)S(1)}, bf16[128,1024]{1,0:T(8,128)(2,1)S(1)}, u32[]{:S(2)}, u32[]{:S(2)}) collective-permute-start(bf16[128,1024]{1,0:T(8,128)(2,1)S(1)} %get-tuple-element.384), channel_id=1, source_target_pairs={{0,16},{4,20},{8,24},{12,28},{16,0},{20,4},{24,8},{28,12},{1,17},{... | collective-permute-start | bytes 786440 | tf_op jit(solution)/shard_map/ppermute | solution.py:944
  428.5 9.5 %collective-permute-start.38 = (f32[8,1024]{1,0:T(8,128)S(1)}, f32[8,1024]{1,0:T(8,128)S(1)}, u32[]{:S(2)}, u32[]{:S(2)}) collective-permute-start(f32[8,1024]{1,0:T(8,128)S(1)} %get-tuple-element.447), channel_id=1, source_target_pairs={{0,16},{4,20},{8,24},{12,28},{16,0},{20,4},{24,8},{28,12},{1,17},{... | collective-permute-start | bytes 98312 | tf_op jit(solution)/shard_map/ppermute | solution.py:944
  449.8 10.9 %collective-permute-start.41 = (bf16[4,512,1024]{2,1,0:T(8,128)(2,1)}, bf16[4,512,1024]{2,1,0:T(8,128)(2,1)}, u32[]{:S(2)}, u32[]{:S(2)}) collective-permute-start(bf16[4,512,1024]{2,1,0:T(8,128)(2,1)} %constant_dynamic-update-slice_fusion.6.pieces), channel_id=1, source_target_pairs={{0,1},{1,0},{2,3},{3,2},{4,5},{5,4},{6,7},{7,6},{8,9},{9,8},{10,11... | collective-permute-start | bytes 12582920 | tf_op jit(solution)/shard_map/ppermute | solution.py:944
  453.3 11.6 %collective-permute-start.42 = (bf16[128,1024]{1,0:T(8,128)(2,1)S(1)}, bf16[128,1024]{1,0:T(8,128)(2,1)S(1)}, u32[]{:S(2)}, u32[]{:S(2)}) collective-permute-start(bf16[128,1024]{1,0:T(8,128)(2,1)S(1)} %get-tuple-element.404), channel_id=1, source_target_pairs={{0,24},{4,28},{8,16},{12,20},{16,8},{20,12},{24,0},{28,4},{1,25},{... | collective-permute-start | bytes 786440 | tf_op jit(solution)/shard_map/ppermute | solution.py:944
  (37 other events, 379.5 us)
Sparse Core Ops, SparseCore 0:
  9.6 59.8 all-gather.4
  71.0 58.2 all-gather.2

commit v6 on v5

--- a/solution.py
+++ b/solution.py
@@ -768,24 +768,28 @@
 CUTS = ((224, 800), (304, 400, 320))
 
 
-def expert_grads_kernel(count, near, *refs):
-    packets, outs = refs[:count], refs[count:-6]
-    act, branch, ffn_in, pre, full, sems = refs[-6:]
+def expert_grads_kernel(count, shard, added, *refs):
+    packets, parts, outs = refs[:count], refs[count : count + added], refs[count + added : -7]
+    act, branch, ffn_in, pre, earlier, full, sems = refs[-7:]
     copies = Copies(sems)
     rows = packets[0].shape[1]
 
     def fetch(slot, target):
         return [copies.start(p.at[slot], target.at[pl.ds(n * rows, rows)]) for n, p in enumerate(packets)]
 
-    shard = 0 if near else 2
     first = fetch(shard, act) + fetch(5, branch)
+    before = [copies.start(p.at[0], earlier.at[m]) for m, p in enumerate(parts)]
     second = fetch(4, ffn_in) + fetch(shard + 1, pre)
     left = []
     for m, (came, one, two) in enumerate(((first, act, branch), (second, ffn_in, pre))):
         for copy in came:
             copy.wait()
-        full[m] = tn(one[...], two[...]).astype(full.dtype)
-        if near:
+        total = tn(one[...], two[...])
+        if added:
+            before[m].wait()
+            total = total + earlier[m]
+        full[m] = total.astype(full.dtype)
+        if not added:
             left.append(copies.start(full.at[m], outs[m].at[0]))
             continue
         start, skip = 0, sum(len(cuts) for cuts in CUTS[:m])
@@ -796,29 +800,30 @@
         copy.wait()
 
 
-def expert_grads(near, packets):
+def expert_grads(far, packets, parts=()):
     _, rows, width = packets[0].shape
-    count = len(packets)
+    count, added = len(packets), len(parts)
     assert sum(CUTS[0]) == sum(CUTS[1]) == width
-    if near:
+    if added:
+        shapes = [jax.ShapeDtypeStruct((c, width), BF16) for cuts in CUTS for c in cuts]
+    else:
         shapes = [jax.ShapeDtypeStruct((1, width, width), F32)] * 2
-    else:
-        shapes = [jax.ShapeDtypeStruct((c, width), BF16) for cuts in CUTS for c in cuts]
     return pl.pallas_call(
-        functools.partial(expert_grads_kernel, count, near),
+        functools.partial(expert_grads_kernel, count, 2 if far else 0, added),
         grid=(1,),
-        in_specs=[ANYWHERE] * count,
+        in_specs=[ANYWHERE] * (count + added),
         out_specs=[ANYWHERE] * len(shapes),
         out_shape=shapes,
         scratch_shapes=[pltpu.VMEM((count * rows, width), BF16)] * 4
         + [
-            pltpu.VMEM((2, width, width), F32 if near else BF16),
-            pltpu.SemaphoreType.DMA((4 * count + len(shapes),)),
+            pltpu.VMEM((2, width, width) if added else (2, 16, 128), F32),
+            pltpu.VMEM((2, width, width), BF16 if added else F32),
+            pltpu.SemaphoreType.DMA((4 * count + added + len(shapes),)),
         ],
         compiler_params=params(),
         cost_estimate=cost(4 * count * rows * width * width, 20 * width * width),
-        name="near_grads" if near else "far_grads",
-    )(*packets)
+        name="far_rest" if added else ("far_part" if far else "near_grads"),
+    )(*packets, *parts)
 
 
 def shared_grads_kernel(
@@ -1107,10 +1112,13 @@
     codes = jnp.concatenate([jnp.arange(xs, n_expert, 2, dtype=jnp.int32) for xs in range(2)])
     partners = (expert ^ codes).astype(jnp.int32)
     leave_col = jnp.take(position.reshape(n_expert, piece), partners, axis=0).reshape(count, 1)
-    last_slots = jnp.take(position.reshape(n_expert, CHUNKS, -1)[:, -1], partners, axis=0)
+    side = n_expert // 2
+    back_codes = [0] + [2 * j for j in range(2, side)] + [2, 3, 1] + [2 * j + 1 for j in range(2, side)]
+    back = (expert ^ jnp.array(back_codes, jnp.int32)).astype(jnp.int32)
+    last_slots = jnp.take(position.reshape(n_expert, CHUNKS, -1)[:, -1], back, axis=0)
     came_row = jnp.concatenate([in_chunks[: count - count // CHUNKS], last_slots.reshape(-1)])
     came_row = came_row.reshape(1, count)
-    leave_col, partners, came_row = tie(leave_col, partners, came_row)
+    leave_col, partners, back, came_row = tie(leave_col, partners, back, came_row)
     arrived, start_row, start_col, pos_row, chunk_col, live_col, shared.codes = tie(
         arrived, start_row, start_col, pos_row, chunk_col, live_col, shared.codes
     )
@@ -1135,12 +1143,11 @@
     up_bias = expert_up_bias[0].reshape(n_dp, 1, part)
     grads, mine, theirs, got, sums, up_sums = ([None] * CHUNKS for _ in range(6))
     returned = []
-    side = n_expert // 2
     to_partner = lambda v, j: swap(v, ("expert", n_expert, 2 * j))
     for c in range(CHUNKS):
         last = c + 1 == CHUNKS
         *grads[c], mine[c], theirs[c], sums[c], up_sums[c] = expert_chunk(
-            c, (1,) * side + (side,) if last else (), place, partners, routed[c],
+            c, (1,) * (side - 1) + (2, side - 1) if last else (), place, back, routed[c],
             blocks(block_cot), route_live, ups, downs, up_bias, row(second_gain), row(second_bias),
         )
         if c > 0:
@@ -1154,17 +1161,21 @@
             routed[c + 1], grads[c], mine[c], theirs[c] = tie(
                 routed[c + 1], grads[c], mine[c], theirs[c]
             )
-    *stay, cross = grads[-1]
+    across = lambda v: swap(v, ("expert", n_expert, 1))
+    own, *stay, pair, cross = grads[-1]
     got[-1] = swap(theirs[-1], core)
-    cross = swap(cross, ("expert", n_expert, 1))
-    stay = [v if j == 0 else to_partner(v, j) for j, v in enumerate(stay)]
-    cross, got[-1] = tie(cross, got[-1])
-    short = cross.shape[0] // side
-    across = [cross[j * short : (j + 1) * short] for j in range(side)]
-    across = [v if j == 0 else to_partner(v, j) for j, v in enumerate(across)]
-    returned += stay + across
-
-    fars = list(expert_grads(False, [*mine, *got]))
+    pair, cross = to_partner(pair, 1), across(cross)
+    stay = [to_partner(v, j) for j, v in enumerate(stay, 2)]
+    parts = list(expert_grads(True, [*mine, *got[:-1]]))
+    pair, cross, parts = tie(pair, cross, parts)
+    short = own.shape[0]
+    cut = lambda v: [v[n * short : (n + 1) * short] for n in range(v.shape[0] // short)]
+    near_pair, far_pair = cut(pair)
+    crossed, *rest = cut(cross)
+    rest = [to_partner(v, j) for j, v in enumerate(rest, 2)]
+    returned += [own, *stay, near_pair, across(far_pair), crossed, *rest]
+
+    fars = list(expert_grads(True, got[-1:], parts))
     sums, up_sums = sum(sums), sum(up_sums)
     empty = jnp.zeros((8, width), F32)
     biases = jnp.concatenate([up_sums.reshape(-1, width), sums[2:3], empty[: 7 - n_dp]], axis=0)
@@ -1226,7 +1237,7 @@
 
     over_y(4)
     total = unstack(shared.gather_rest(total))
-    near = list(expert_grads(True, packets))
+    near = list(expert_grads(False, packets))
     cross_rest = swap(cross_rest, ("expert", n_expert, 1))
     total, small, near, fars, stay, cross, cross_rest = tie(
         total, small, near, fars, stay, cross, cross_rest

time: 488 us -> 485 us (level)
  waiting for transfers between devices: 122 us -> 113 us
  Pallas kernels: 226 us -> 231 us
    ppermute x43, waiting for transfers between devices: 65.3 us -> 56.4 us  [swap(): return lax.ppermute(values, axis, [(i, i ^ bit) for i in range(size)])]
    pallas_call x2 -> x3, Pallas kernels: 28.7 us -> 34 us  [expert_grads(): pl.pallas_call(functools.partial(expert_grads_kernel, count, 2 if far els...]
  transfers between devices with their start and end apart: 50 -> 50, of which waited for: 19 -> 20; matrix products, arithmetic and copies ran while one was open for 6% -> 6% of each run, Pallas kernels for 45% -> 47%
where the time goes in v6:
time: 485 us; the launch traced here: 478 us
  Pallas kernels  231 us (48%)
  waiting for transfers between devices  113 us (23%)
  starting transfers between devices  75.6 us (16%)
  other arithmetic  26 us (5%)
  local copies, waits for them, and re-layouts  16.2 us (3%)
  between operations  15.4 us (3%)
    ppermute x43, waiting for transfers between devices, swap(): return lax.ppermute(values, axis, [(i, i ^ bit) for i in range(size)])  56.4 us
    all_to_all x5, waiting for transfers between devices, exchange(): lax.all_to_all(values, 'expert', split_axis=0, concat_axis=0, tiled=True)  55.4 us
    pallas_call x2, Pallas kernels, expert_chunk(): pl.pallas_call(functools.partial(expert_kernel, parts), grid_spec=pltpu.P...  48.3 us
    ppermute x43, starting transfers between devices, swap(): return lax.ppermute(values, axis, [(i, i ^ bit) for i in range(size)])  46.1 us
    pallas_call x1, Pallas kernels, attend_back(): pl.pallas_call(attend_back_kernel, grid=(pairs,), in_specs=[whole((1, cou...  34.5 us
    pallas_call x3, Pallas kernels, expert_grads(): pl.pallas_call(functools.partial(expert_grads_kernel, count, 2 if far els...  34 us
    all_to_all x5, starting transfers between devices, exchange(): lax.all_to_all(values, 'expert', split_axis=0, concat_axis=0, tiled=True)  29.4 us
    pallas_call x1, Pallas kernels, attend(): pl.pallas_call(attend_kernel, grid=(pairs,), in_specs=[whole((count, 1)),...  19.1 us
  transfers between devices with their start and end apart: 50, of which 20 were waited for; matrix products, arithmetic and copies ran while one was open for 6% of the time, Pallas kernels for 47%

profile of v6, /device:TPU:9, one launch (start us, length us, event | category | flops | bytes accessed | tf_op | source)
XLA Modules:
  0.0 477.6 jit_solution(3333524512324108081)
XLA Ops:
  8.7 5.7 %all-to-all-start = ((bf16[8,128,1024]{2,1,0:T(8,128)(2,1)}), bf16[8,128,1024]{2,1,0:T(8,128)(2,1)S(1)}, u32[]{:S(2)}, u32[]{:S(2)}) async-start(bf16[8,128,1024]{2,1,0:T(8,128)(2,1)} %bitcast), calls=%async_computation | async-start | bytes 4194304 | tf_op jit(solution)/shard_map/all_to_all | solution.py:953
  23.0 37.9 %all-to-all-done = bf16[8,128,1024]{2,1,0:T(8,128)(2,1)S(1)} async-done(((bf16[8,128,1024]{2,1,0:T(8,128)(2,1)}), bf16[8,128,1024]{2,1,0:T(8,128)(2,1)S(1)}, u32[]{:S(2)}, u32[]{:S(2)}) %all-to-all-start) | async-done | bytes 2097184 | tf_op jit(solution)/shard_map/all_to_all | solution.py:953
  60.9 5.5 %all-to-all-start.3 = ((f32[8,1,128]{2,1,0:T(1,128)}), f32[8,1,128]{2,1,0:T(1,128)S(1)}, u32[]{:S(2)}, u32[]{:S(2)}) async-start(f32[8,1,128]{2,1,0:T(1,128)} %fusion.4), calls=%async_computation.3 | async-start | bytes 8192 | tf_op jit(solution)/shard_map/all_to_all | solution.py:953
  67.5 13.7 %entry.1 = (bf16[1024,1024]{1,0:T(8,128)(2,1)}, bf16[1024,1024]{1,0:T(8,128)(2,1)}, bf16[1024,1024]{1,0:T(8,128)(2,1)}, bf16[1024,1024]{1,0:T(8,128)(2,1)}, bf16[1024,1024]{1,0:T(8,128)(2,1)}) custom-call(bf16[1024,1024]{1,0:T(8,128)(2,1)} %bitcast.71, s32[1,1024]{1,0:T(1,128)} %pos_row, f32[1,1024]{1,0:T(1,128)} %bitcast.111, f32[1,1024]{1,0:T(1,128)} %bitcast.103, ...), custom_call_target="tpu_custom_call" | custom-call | flops 8589934592 | bytes 18874368 | tf_op jit(solution)/shard_map/entry/pallas_call | solution.py:126
  81.2 19.1 %attend.1 = (bf16[1024,1024]{1,0:T(8,128)(2,1)}, f32[8,8,1024]{2,1,0:T(8,128)}) custom-call(s32[1024,1]{1,0:T(8,128)} %iota_select_fusion.start_col, bf16[1024,1024]{1,0:T(8,128)(2,1)} %get-tuple-element.225.q_ref, bf16[1024,1024]{1,0:T(8,128)(2,1)} %get-tuple-element.226.k_ref, bf16[1024,1024]{1,0:T(8,128)(2,1)} %get-tuple-element.227.v_ref), custom_call_target="tpu_custom_call" | custom-call | flops 8589934592 | bytes 8388608 | tf_op jit(solution)/shard_map/attend/pallas_call | solution.py:261
  100.3 8.0 %leave.1 = (bf16[512,1024]{1,0:T(8,128)(2,1)}, bf16[1024,1024]{1,0:T(8,128)(2,1)}) custom-call(bf16[1024,1024]{1,0:T(8,128)(2,1)} %get-tuple-element.229.mixed.o_ref, bf16[1024,1024]{1,0:T(8,128)(2,1)} %refs_11_.1, f32[1,1024]{1,0:T(1,128)} %bitcast.106, bf16[1024,1024]{1,0:T(8,128)(2,1)} %get-tuple-element.230.tokens, f32[1024,1]{1,0:T(8,128)} %fusion.2.live_col.refs_10_, ...), custom_call_target="tpu_custom_call" | custom-call | flops 3221225472 | bytes 10485760 | tf_op jit(solution)/shard_map/leave/pallas_call | solution.py:311
  108.3 5.5 %all-to-all-start.2 = ((bf16[8,64,1024]{2,1,0:T(8,128)(2,1)}), bf16[8,64,1024]{2,1,0:T(8,128)(2,1)S(1)}, u32[]{:S(2)}, u32[]{:S(2)}) async-start(bf16[8,64,1024]{2,1,0:T(8,128)(2,1)} %bitcast.75), calls=%async_computation.2 | async-start | bytes 2097152 | tf_op jit(solution)/shard_map/all_to_all | solution.py:953
  115.3 4.0 pick.1
  119.3 17.4 %all-to-all-done.2 = bf16[8,64,1024]{2,1,0:T(8,128)(2,1)S(1)} async-done(((bf16[8,64,1024]{2,1,0:T(8,128)(2,1)}), bf16[8,64,1024]{2,1,0:T(8,128)(2,1)S(1)}, u32[]{:S(2)}, u32[]{:S(2)}) %all-to-all-start.2) | async-done | bytes 1048608 | tf_op jit(solution)/shard_map/all_to_all | solution.py:953
  136.7 7.1 %all-to-all-start.1 = ((bf16[8,64,1024]{2,1,0:T(8,128)(2,1)}), bf16[8,64,1024]{2,1,0:T(8,128)(2,1)S(1)}, u32[]{:S(2)}, u32[]{:S(2)}) async-start(bf16[8,64,1024]{2,1,0:T(8,128)(2,1)} %bitcast.76), calls=%async_computation.1 | async-start | bytes 2097152 | tf_op jit(solution)/shard_map/all_to_all | solution.py:953
  146.6 24.0 %expert_chunk.2 = (bf16[512,1024]{1,0:T(8,128)(2,1)}, bf16[6,512,1024]{2,1,0:T(8,128)(2,1)}, bf16[6,512,1024]{2,1,0:T(8,128)(2,1)}, f32[8,1024]{1,0:T(8,128)}, f32[4,1,1024]{2,1,0:T(1,128)}) custom-call(s32[1]{0:T(128)} %bitcast.16.device, s32[8]{0:T(128)} %broadcast_xor_fusion.source, bf16[512,1024]{1,0:T(8,128)(2,1)} %bitcast.67, ...), custom_call_target="tpu_custom_call" | custom-call | flops 12884901888 | bytes 16777216 | tf_op jit(solution)/shard_map/expert_chunk/pallas_call | solution.py:677
  171.7 5.6 %all-to-all-start.4 = ((bf16[8,64,1024]{2,1,0:T(8,128)(2,1)}), bf16[8,64,1024]{2,1,0:T(8,128)(2,1)S(1)}, u32[]{:S(2)}, u32[]{:S(2)}) async-start(bf16[8,64,1024]{2,1,0:T(8,128)(2,1)} %bitcast.77), calls=%async_computation.4 | async-start | bytes 2097152 | tf_op jit(solution)/shard_map/all_to_all | solution.py:953
  177.4 24.3 %expert_chunk.3 = (bf16[64,1024]{1,0:T(8,128)(2,1)}, bf16[64,1024]{1,0:T(8,128)(2,1)}, bf16[64,1024]{1,0:T(8,128)(2,1)}, bf16[128,1024]{1,0:T(8,128)(2,1)}, bf16...) custom-call(s32[1]{0:T(128)} %bitcast.16.device, ...), custom_call_target="tpu_custom_call" | custom-call | flops 12884901888 | bytes 16777216 | tf_op jit(solution)/shard_map/expert_chunk/pallas_call | solution.py:677
  205.2 1.6 collective-permute-start.3
  208.1 11.8 %far_part.1 = (f32[1,1024,1024]{2,1,0:T(8,128)}, f32[1,1024,1024]{2,1,0:T(8,128)}) custom-call(bf16[6,512,1024]{2,1,0:T(8,128)(2,1)} %get-tuple-element.357.refs_0_, bf16[6,512,1024]{2,1,0:T(8,128)(2,1)} %get-tuple-element.358.refs_1_, bf16[6,512,1024]{2,1,0:T(8,128)(2,1)} %collective-permute-done.refs_2_), custom_call_target="tpu_custom_call" | custom-call | flops 6442450944 | bytes 20971520 | tf_op jit(solution)/shard_map/far_part/pallas_call | solution.py:811
  220.6 2.8 collective-permute-start.6
  225.2 7.5 %far_rest.1 = (bf16[224,1024]{1,0:T(8,128)(2,1)}, bf16[800,1024]{1,0:T(8,128)(2,1)}, bf16[304,1024]{1,0:T(8,128)(2,1)}, bf16[400,1024]{1,0:T(8,128)(2,1)}, bf16[320,1024]{1,0:T(8,128)(2,1)}) custom-call(bf16[6,512,1024]{2,1,0:T(8,128)(2,1)} %collective-permute-done.8.refs_0_.refs_3_, f32[1,1024,1024]{2,1,0:T(8,128)} %get-tuple-element.263.refs_1_, ...), custom_call_target="tpu_custom_call" | custom-call | flops 2147483648 | bytes 20971520 | tf_op jit(solution)/shard_map/far_rest/pallas_call | solution.py:811
  232.7 3.1 collective-permute-done.7.refs_8_
  237.1 9.0 %reenter.1 = (bf16[1024,1024]{1,0:T(8,128)(2,1)}, bf16[1024,1024]{1,0:T(8,128)(2,1)}, bf16[1024,1024]{1,0:T(8,128)(2,1)}, f32[1,1024]{1,0:T(1,128)}) custom-call(bf16[512,1024]{1,0:T(8,128)(2,1)} %bitcast.74, bf16[64,1024]{1,0:T(8,128)(2,1)} %get-tuple-element.275.refs_1_, bf16[64,1024]{1,0:T(8,128)(2,1)} %copy-done.29, bf16[64,1024]{1,0:T(8,128)(2,1)} %copy-done.30, ...), custom_call_target="tpu_custom_call" | custom-call | flops 4294967296 | bytes 10485760 | tf_op jit(solution)/shard_map/reenter/pallas_call | solution.py:401
  249.7 34.5 %attend_back.1.token_grads.grads = bf16[3,1024,1024]{2,1,0:T(8,128)(2,1)} custom-call(s32[1,1024]{1,0:T(1,128)} %compare_select_fusion.start_row, bf16[1024,1024]{1,0:T(8,128)(2,1)} %get-tuple-element.225.q_ref, bf16[1024,1024]{1,0:T(8,128)(2,1)} %get-tuple-element.226.k_ref, bf16[1024,1024]{1,0:T(8,128)(2,1)} %get-tuple-element.227.v_ref, ...), custom_call_target="tpu_custom_call" | custom-call | flops 21474836480 | bytes 16777216 | tf_op jit(solution)/shard_map/attend_back/pallas_call | solution.py:495
  285.9 14.2 %shared_grads.1 = (bf16[4,512,1024]{2,1,0:T(8,128)(2,1)}, bf16[4,512,1024]{2,1,0:T(8,128)(2,1)}) custom-call(s32[2]{0:T(128)} %pad_add_fusion.1.codes, bf16[1024,1024]{1,0:T(8,128)(2,1)} %get-tuple-element.299.normed, bf16[1024,1024]{1,0:T(8,128)(2,1)} %get-tuple-element.229.mixed.o_ref, bf16[3,1024,1024]{2,1,0:T(8,128)(2,1)} %attend_back.1.token_grads.grads, ...), custom_call_target="tpu_custom_call" | custom-call | flops 8589934592 | bytes 25165824 | tf_op jit(solution)/shard_map/shared_grads/pallas_call | solution.py:863
  300.1 2.7 collective-permute-start.12
  303.7 6.2 %collective-permute-done.12 = bf16[4,512,1024]{2,1,0:T(8,128)(2,1)S(1)} collective-permute-done((bf16[4,512,1024]{2,1,0:T(8,128)(2,1)}, bf16[4,512,1024]{2,1,0:T(8,128)(2,1)S(1)}, u32[]{:S(2)}, u32[]{:S(2)}) %collective-permute-start.12) | collective-permute-done | bytes 4194336 | tf_op jit(solution)/shard_map/ppermute | solution.py:949
  309.9 4.4 add_convert_fusion.2
  316.3 18.2 %finish.1 = (bf16[128,1024]{1,0:T(8,128)(2,1)}, bf16[128,1024]{1,0:T(8,128)(2,1)}, bf16[128,1024]{1,0:T(8,128)(2,1)}, bf16[128,1024]{1,0:T(8,128)(2,1)}, bf16[25...) custom-call(bf16[3,1024,1024]{2,1,0:T(8,128)(2,1)} %attend_back.1.token_grads.grads, ...), custom_call_target="tpu_custom_call" | custom-call | flops 8589934592 | bytes 20971520 | tf_op jit(solution)/shard_map/finish/pallas_call | solution.py:560
  334.5 4.6 collective-permute-done.14
  339.1 1.6 add_convert_fusion
  340.7 1.9 add_convert_fusion.1
  343.7 1.8 collective-permute-start.17
  345.5 1.8 collective-permute-start.19
  347.4 7.5 %collective-permute-done.15 = bf16[4,64,1024]{2,1,0:T(8,128)(2,1)S(1)} collective-permute-done((bf16[4,64,1024]{2,1,0:T(8,128)(2,1)S(1)}, bf16[4,64,1024]{2,1,0:T(8,128)(2,1)S(1)}, u32[]{:S(2)}, u32[]{:S(2)}) %collective-permute-start.15) | collective-permute-done | bytes 524320 | tf_op jit(solution)/shard_map/ppermute | solution.py:949
  356.3 3.2 collective-permute-done.19.refs_2_
  360.2 2.0 collective-permute-start.21
  365.0 15.3 %expert_out.1 = bf16[8,128,1024]{2,1,0:T(8,128)(2,1)} custom-call(s32[1]{0:T(128)} %bitcast.16.device, bf16[6,512,1024]{2,1,0:T(8,128)(2,1)} %get-tuple-element.357.refs_0_, bf16[6,512,1024]{2,1,0:T(8,128)(2,1)} %get-tuple-element.358.refs_1_, bf16[6,512,1024]{2,1,0:T(8,128)(2,1)} %get-tuple-element.240.refs_2_, ...), custom_call_target="tpu_custom_call" | custom-call | flops 8589934592 | bytes 16777216 | tf_op jit(solution)/shard_map/expert_out/pallas_call | solution.py:748
  380.4 2.9 collective-permute-done.22
  383.5 1.7 collective-permute-start.26
  388.1 14.7 %near_grads.1 = (f32[1,1024,1024]{2,1,0:T(8,128)}, f32[1,1024,1024]{2,1,0:T(8,128)}) custom-call(bf16[6,512,1024]{2,1,0:T(8,128)(2,1)} %get-tuple-element.357.refs_0_, bf16[6,512,1024]{2,1,0:T(8,128)(2,1)} %get-tuple-element.358.refs_1_, bf16[6,512,1024]{2,1,0:T(8,128)(2,1)} %collective-permute-done.refs_2_, ...), custom_call_target="tpu_custom_call" | custom-call | flops 8589934592 | bytes 20971520 | tf_op jit(solution)/shard_map/near_grads/pallas_call | solution.py:811
  404.1 1.7 collective-permute-done.27
  410.0 2.8 convert_add_fusion.1
  414.0 5.5 %collective-permute-done.33 = f32[16,1024]{1,0:T(8,128)S(1)} collective-permute-done((f32[16,1024]{1,0:T(8,128)S(1)}, f32[16,1024]{1,0:T(8,128)S(1)}, u32[]{:S(2)}, u32[]{:S(2)}) %collective-permute-start.33) | collective-permute-done | bytes 65568 | tf_op jit(solution)/shard_map/ppermute | solution.py:949
  420.1 2.1 collective-permute-start.35
  426.2 2.8 convert_add_fusion
  428.9 4.6 collective-permute-done.38
  433.5 7.8 %collective-permute-done.36 = bf16[4,128,1024]{2,1,0:T(8,128)(2,1)S(1)} collective-permute-done((bf16[4,128,1024]{2,1,0:T(8,128)(2,1)S(1)}, bf16[4,128,1024]{2,1,0:T(8,128)(2,1)S(1)}, u32[]{:S(2)}, u32[]{:S(2)}) %collective-permute-start.36) | collective-permute-done | bytes 1048608 | tf_op jit(solution)/shard_map/ppermute | solution.py:949
  445.7 4.0 collective-permute-start.41
  450.7 5.5 %unmix.2 = (f32[1024,1024]{1,0:T(8,128)}, f32[1024,1024]{1,0:T(8,128)}, f32[1024,1024]{1,0:T(8,128)}, f32[1024,1024]{1,0:T(8,128)}) custom-call(s32[2]{0:T(128)} %pad_add_fusion.1.codes, s32[1]{0:T(128)} %bitcast.39.half_place.source, s32[1]{0:T(128)} %bitcast.39.half_place.source, bf16[4,512,1024]{2,1,0:T(8,128)(2,1)} %constant_dynamic-update-slice_fusion.6.pieces), custom_call_target="tpu_custom_call" | custom-call | flops 2097152 | bytes 12582912 | tf_op jit(solution)/shard_map/unmix/pallas_call | solution.py:924
  457.4 4.6 collective-permute-done.42.refs_7_
  462.7 7.7 %unmix.3 = (f32[1024,1024]{1,0:T(8,128)}, f32[1024,1024]{1,0:T(8,128)}, f32[1024,1024]{1,0:T(8,128)}, f32[1024,1024]{1,0:T(8,128)}, bf16[1024,1024]{1,0:T(8,128)(2,1)}) custom-call(s32[2]{0:T(128)} %pad_add_fusion.1.codes, s32[1]{0:T(128)S(6)} %sub.24.half_place, ...), custom_call_target="tpu_custom_call", output_to_operand_aliasing={{0}: (12, {}), {1}: (13, {}), {2}: (14, {}), {3}: (15, {})} | custom-call | flops 2097152 | bytes 12582912 | tf_op jit(solution)/shard_map/unmix/pallas_call | solution.py:924
  (226 shorter events, 60.4 us)
Async XLA Ops:
  7.2 139.4 %all-gather.5.cloned.1.call-start = ((), (), s32[]{:S(2)}) async-start(), calls=%async_computation.6 | async-start | bytes 10485760 | tf_op jit(solution)/shard_map/all_gather | solution.py:1095
  7.9 138.7 %all-gather.3.cloned.1.call-start = ((), (), s32[]{:S(2)}) async-start(), calls=%async_computation.5 | async-start | bytes 10485760 | tf_op jit(solution)/shard_map/all_gather | solution.py:1094
  8.7 52.2 %all-to-all-start = ((bf16[8,128,1024]{2,1,0:T(8,128)(2,1)}), bf16[8,128,1024]{2,1,0:T(8,128)(2,1)S(1)}, u32[]{:S(2)}, u32[]{:S(2)}) async-start(bf16[8,128,1024]{2,1,0:T(8,128)(2,1)} %bitcast), calls=%async_computation | async-start | bytes 4194304 | tf_op jit(solution)/shard_map/all_to_all | solution.py:953
  60.9 47.4 %all-to-all-start.3 = ((f32[8,1,128]{2,1,0:T(1,128)}), f32[8,1,128]{2,1,0:T(1,128)S(1)}, u32[]{:S(2)}, u32[]{:S(2)}) async-start(f32[8,1,128]{2,1,0:T(1,128)} %fusion.4), calls=%async_computation.3 | async-start | bytes 8192 | tf_op jit(solution)/shard_map/all_to_all | solution.py:953
  108.3 28.4 %all-to-all-start.2 = ((bf16[8,64,1024]{2,1,0:T(8,128)(2,1)}), bf16[8,64,1024]{2,1,0:T(8,128)(2,1)S(1)}, u32[]{:S(2)}, u32[]{:S(2)}) async-start(bf16[8,64,1024]{2,1,0:T(8,128)(2,1)} %bitcast.75), calls=%async_computation.2 | async-start | bytes 2097152 | tf_op jit(solution)/shard_map/all_to_all | solution.py:953
  136.7 33.9 %all-to-all-start.1 = ((bf16[8,64,1024]{2,1,0:T(8,128)(2,1)}), bf16[8,64,1024]{2,1,0:T(8,128)(2,1)S(1)}, u32[]{:S(2)}, u32[]{:S(2)}) async-start(bf16[8,64,1024]{2,1,0:T(8,128)(2,1)} %bitcast.76), calls=%async_computation.1 | async-start | bytes 2097152 | tf_op jit(solution)/shard_map/all_to_all | solution.py:953
  170.6 31.1 %collective-permute-start = (bf16[6,512,1024]{2,1,0:T(8,128)(2,1)}, bf16[6,512,1024]{2,1,0:T(8,128)(2,1)}, u32[]{:S(2)}, u32[]{:S(2)}) collective-permute-start(bf16[6,512,1024]{2,1,0:T(8,128)(2,1)} %get-tuple-element.240.refs_2_), channel_id=1, source_target_pairs={{0,1},{1,0},{2,3},{3,2},{4,5},{5,4},{6,7},{7,6},{8,9},{9,8},{10,11... | collective-permute-start | bytes 18874376 | tf_op jit(solution)/shard_map/ppermute | solution.py:949
  171.7 30.0 %all-to-all-start.4 = ((bf16[8,64,1024]{2,1,0:T(8,128)(2,1)}), bf16[8,64,1024]{2,1,0:T(8,128)(2,1)S(1)}, u32[]{:S(2)}, u32[]{:S(2)}) async-start(bf16[8,64,1024]{2,1,0:T(8,128)(2,1)} %bitcast.77), calls=%async_computation.4 | async-start | bytes 2097152 | tf_op jit(solution)/shard_map/all_to_all | solution.py:953
  201.7 23.1 %collective-permute-start.8 = (bf16[6,512,1024]{2,1,0:T(8,128)(2,1)}, bf16[6,512,1024]{2,1,0:T(8,128)(2,1)}, u32[]{:S(2)}, u32[]{:S(2)}) collective-permute-start(bf16[6,512,1024]{2,1,0:T(8,128)(2,1)} %get-tuple-element.262.refs_3_), channel_id=1, source_target_pairs={{0,1},{1,0},{2,3},{3,2},{4,5},{5,4},{6,7},{7,6},{8,9},{9,8},{10,11... | collective-permute-start | bytes 18874376 | tf_op jit(solution)/shard_map/ppermute | solution.py:949
  204.0 15.9 %collective-permute-start.4 = (bf16[192,1024]{1,0:T(8,128)(2,1)}, bf16[192,1024]{1,0:T(8,128)(2,1)S(1)}, u32[]{:S(2)}, u32[]{:S(2)}) collective-permute-start(bf16[192,1024]{1,0:T(8,128)(2,1)} %get-tuple-element.254), channel_id=1, source_target_pairs={{0,4},{4,0},{8,12},{12,8},{16,20},{20,16},{24,28},{28,24},{1,5},{5... | collective-permute-start | bytes 1179656 | tf_op jit(solution)/shard_map/ppermute | solution.py:949
  205.2 14.7 %collective-permute-start.3 = (bf16[128,1024]{1,0:T(8,128)(2,1)}, bf16[128,1024]{1,0:T(8,128)(2,1)S(1)}, u32[]{:S(2)}, u32[]{:S(2)}) collective-permute-start(bf16[128,1024]{1,0:T(8,128)(2,1)} %get-tuple-element.253), channel_id=1, source_target_pairs={{0,8},{4,12},{8,0},{12,4},{16,24},{20,28},{24,16},{28,20},{1,9},{5... | collective-permute-start | bytes 786440 | tf_op jit(solution)/shard_map/ppermute | solution.py:949
  206.9 25.7 %collective-permute-start.1 = (bf16[64,1024]{1,0:T(8,128)(2,1)}, bf16[64,1024]{1,0:T(8,128)(2,1)S(1)}, u32[]{:S(2)}, u32[]{:S(2)}) collective-permute-start(bf16[64,1024]{1,0:T(8,128)(2,1)} %get-tuple-element.251), channel_id=1, source_target_pairs={{0,16},{4,20},{8,24},{12,28},{16,0},{20,4},{24,8},{28,12},{1,17},{... | collective-permute-start | bytes 393224 | tf_op jit(solution)/shard_map/ppermute | solution.py:949
  207.6 25.0 %collective-permute-start.2 = (bf16[64,1024]{1,0:T(8,128)(2,1)}, bf16[64,1024]{1,0:T(8,128)(2,1)S(1)}, u32[]{:S(2)}, u32[]{:S(2)}) collective-permute-start(bf16[64,1024]{1,0:T(8,128)(2,1)} %get-tuple-element.252), channel_id=1, source_target_pairs={{0,24},{4,28},{8,16},{12,20},{16,8},{20,12},{24,0},{28,4},{1,25},{... | collective-permute-start | bytes 393224 | tf_op jit(solution)/shard_map/ppermute | solution.py:949
  220.6 12.0 %collective-permute-start.6 = (bf16[64,1024]{1,0:T(8,128)(2,1)S(1)}, bf16[64,1024]{1,0:T(8,128)(2,1)S(1)}, u32[]{:S(2)}, u32[]{:S(2)}) collective-permute-start(bf16[64,1024]{1,0:T(8,128)(2,1)S(1)} %get-tuple-element.447), channel_id=1, source_target_pairs={{0,16},{4,20},{8,24},{12,28},{16,0},{20,4},{24,8},{28,12},{1,17},{... | collective-permute-start | bytes 393224 | tf_op jit(solution)/shard_map/ppermute | solution.py:949
  223.4 12.4 %collective-permute-start.7 = (bf16[64,1024]{1,0:T(8,128)(2,1)S(1)}, bf16[64,1024]{1,0:T(8,128)(2,1)S(1)}, u32[]{:S(2)}, u32[]{:S(2)}) collective-permute-start(bf16[64,1024]{1,0:T(8,128)(2,1)S(1)} %get-tuple-element.446), channel_id=1, source_target_pairs={{0,24},{4,28},{8,16},{12,20},{16,8},{20,12},{24,0},{28,4},{1,25},{... | collective-permute-start | bytes 393224 | tf_op jit(solution)/shard_map/ppermute | solution.py:949
  224.8 11.0 %collective-permute-start.5 = (bf16[64,1024]{1,0:T(8,128)(2,1)S(1)}, bf16[64,1024]{1,0:T(8,128)(2,1)S(1)}, u32[]{:S(2)}, u32[]{:S(2)}) collective-permute-start(bf16[64,1024]{1,0:T(8,128)(2,1)S(1)} %get-tuple-element.449), channel_id=1, source_target_pairs={{0,4},{4,0},{8,12},{12,8},{16,20},{20,16},{24,28},{28,24},{1,5},{5... | collective-permute-start | bytes 393224 | tf_op jit(solution)/shard_map/ppermute | solution.py:949
  235.8 11.9 %collective-permute-start.9 = (bf16[224,1024]{1,0:T(8,128)(2,1)}, bf16[224,1024]{1,0:T(8,128)(2,1)S(1)}, u32[]{:S(2)}, u32[]{:S(2)}) collective-permute-start(bf16[224,1024]{1,0:T(8,128)(2,1)} %get-tuple-element.285), channel_id=1, source_target_pairs={{0,2},{1,3},{2,0},{3,1},{4,6},{5,7},{6,4},{7,5},{8,10},{9,11},{10,... | collective-permute-start | bytes 1376264 | tf_op jit(solution)/shard_map/ppermute | solution.py:949
  248.5 36.2 %collective-permute-start.10 = (bf16[800,1024]{1,0:T(8,128)(2,1)}, bf16[800,1024]{1,0:T(8,128)(2,1)S(1)}, u32[]{:S(2)}, u32[]{:S(2)}) collective-permute-start(bf16[800,1024]{1,0:T(8,128)(2,1)} %get-tuple-element.293), channel_id=1, source_target_pairs={{0,2},{1,3},{2,0},{3,1},{4,6},{5,7},{6,4},{7,5},{8,10},{9,11},{10,... | collective-permute-start | bytes 4915208 | tf_op jit(solution)/shard_map/ppermute | solution.py:949
  284.6 15.5 %collective-permute-start.11 = (bf16[304,1024]{1,0:T(8,128)(2,1)S(1)}, bf16[304,1024]{1,0:T(8,128)(2,1)S(1)}, u32[]{:S(2)}, u32[]{:S(2)}) collective-permute-start(bf16[304,1024]{1,0:T(8,128)(2,1)S(1)} %copy-done.26), channel_id=1, source_target_pairs={{0,2},{1,3},{2,0},{3,1},{4,6},{5,7},{6,4},{7,5},{8,10},{9,11},{10,... | collective-permute-start | bytes 1867784 | tf_op jit(solution)/shard_map/ppermute | solution.py:949
  300.1 9.7 %collective-permute-start.12 = (bf16[4,512,1024]{2,1,0:T(8,128)(2,1)}, bf16[4,512,1024]{2,1,0:T(8,128)(2,1)S(1)}, u32[]{:S(2)}, u32[]{:S(2)}) collective-permute-start(bf16[4,512,1024]{2,1,0:T(8,128)(2,1)} %get-tuple-element.311), channel_id=1, source_target_pairs={{0,1},{1,0},{2,3},{3,2},{4,5},{5,4},{6,7},{7,6},{8,9},{9,8},{10,11... | collective-permute-start | bytes 12582920 | tf_op jit(solution)/shard_map/ppermute | solution.py:949
  314.3 24.8 %collective-permute-start.14 = (bf16[4,128,1024]{2,1,0:T(8,128)(2,1)}, bf16[4,128,1024]{2,1,0:T(8,128)(2,1)}, u32[]{:S(2)}, u32[]{:S(2)}) collective-permute-start(bf16[4,128,1024]{2,1,0:T(8,128)(2,1)} %get-tuple-element.327), channel_id=1, source_target_pairs={{0,4},{4,0},{8,12},{12,8},{16,20},{20,16},{24,28},{28,24},{1,5},{5... | collective-permute-start | bytes 3145736 | tf_op jit(solution)/shard_map/ppermute | solution.py:949
  316.0 24.7 %collective-permute-start.13 = (bf16[4,128,1024]{2,1,0:T(8,128)(2,1)S(1)}, bf16[4,128,1024]{2,1,0:T(8,128)(2,1)}, u32[]{:S(2)}, u32[]{:S(2)}) collective-permute-start(bf16[4,128,1024]{2,1,0:T(8,128)(2,1)S(1)} %get-tuple-element.325), channel_id=1, source_target_pairs={{0,2},{1,3},{2,0},{3,1},{4,6},{5,7},{6,4},{7,5},{8,10},{9,11},{10,... | collective-permute-start | bytes 3145736 | tf_op jit(solution)/shard_map/ppermute | solution.py:949
  342.7 12.3 %collective-permute-start.15 = (bf16[4,64,1024]{2,1,0:T(8,128)(2,1)S(1)}, bf16[4,64,1024]{2,1,0:T(8,128)(2,1)S(1)}, u32[]{:S(2)}, u32[]{:S(2)}) collective-permute-start(bf16[4,64,1024]{2,1,0:T(8,128)(2,1)S(1)} %slice.176), channel_id=1, source_target_pairs={{0,4},{4,0},{8,12},{12,8},{16,20},{20,16},{24,28},{28,24},{1,5},{5... | collective-permute-start | bytes 1572872 | tf_op jit(solution)/shard_map/ppermute | solution.py:949
  343.4 12.0 %collective-permute-start.16 = (bf16[4,64,1024]{2,1,0:T(8,128)(2,1)S(1)}, bf16[4,64,1024]{2,1,0:T(8,128)(2,1)S(1)}, u32[]{:S(2)}, u32[]{:S(2)}) collective-permute-start(bf16[4,64,1024]{2,1,0:T(8,128)(2,1)S(1)} %slice.178), channel_id=1, source_target_pairs={{0,2},{1,3},{2,0},{3,1},{4,6},{5,7},{6,4},{7,5},{8,10},{9,11},{10,... | collective-permute-start | bytes 1572872 | tf_op jit(solution)/shard_map/ppermute | solution.py:949
  345.5 10.7 %collective-permute-start.18 = (bf16[128,1024]{1,0:T(8,128)(2,1)S(1)}, bf16[128,1024]{1,0:T(8,128)(2,1)S(1)}, u32[]{:S(2)}, u32[]{:S(2)}) collective-permute-start(bf16[128,1024]{1,0:T(8,128)(2,1)S(1)} %copy-done.28), channel_id=1, source_target_pairs={{0,8},{4,12},{8,0},{12,4},{16,24},{20,28},{24,16},{28,20},{1,9},{5... | collective-permute-start | bytes 786440 | tf_op jit(solution)/shard_map/ppermute | solution.py:949
  345.5 13.9 %collective-permute-start.19 = (bf16[128,1024]{1,0:T(8,128)(2,1)S(1)}, bf16[128,1024]{1,0:T(8,128)(2,1)S(1)}, u32[]{:S(2)}, u32[]{:S(2)}) collective-permute-start(bf16[128,1024]{1,0:T(8,128)(2,1)S(1)} %copy-done.27), channel_id=1, source_target_pairs={{0,16},{4,20},{8,24},{12,28},{16,0},{20,4},{24,8},{28,12},{1,17},{... | collective-permute-start | bytes 786440 | tf_op jit(solution)/shard_map/ppermute | solution.py:949
  360.2 20.1 %collective-permute-start.20 = (bf16[4,2,16,1024]{3,2,0,1:T(8,128)(2,1)}, bf16[4,2,16,1024]{3,2,0,1:T(8,128)(2,1)S(1)}, u32[]{:S(2)}, u32[]{:S(2)}) collective-permute-start(bf16[4,2,16,1024]{3,2,0,1:T(8,128)(2,1)} %get-tuple-element.437), channel_id=1, source_target_pairs={{0,16},{4,20},{8,24},{12,28},{16,0},{20,4},{24,8},{28,12},{1,17},{... | collective-permute-start | bytes 786440 | tf_op jit(solution)/shard_map/ppermute | solution.py:949
  360.2 20.1 %collective-permute-start.21 = (bf16[4,2,16,1024]{3,2,0,1:T(8,128)(2,1)S(1)}, bf16[4,2,16,1024]{3,2,0,1:T(8,128)(2,1)S(1)}, u32[]{:S(2)}, u32[]{:S(2)}) collective-permute-start(bf16[4,2,16,1024]{3,2,0,1:T(8,128)(2,1)S(1)} %get-tuple-element.439), channel_id=1, source_target_pairs={{0,8},{4,12},{8,0},{12,4},{16,24},{20,28},{24,16},{28,20},{1,9},{5... | collective-permute-start | bytes 786440 | tf_op jit(solution)/shard_map/ppermute | solution.py:949
  362.2 21.0 %collective-permute-start.22 = (bf16[4,2,16,1024]{3,2,0,1:T(8,128)(2,1)S(1)}, bf16[4,2,16,1024]{3,2,0,1:T(8,128)(2,1)S(1)}, u32[]{:S(2)}, u32[]{:S(2)}) collective-permute-start(bf16[4,2,16,1024]{3,2,0,1:T(8,128)(2,1)S(1)} %get-tuple-element.438), channel_id=1, source_target_pairs={{0,24},{4,28},{8,16},{12,20},{16,8},{20,12},{24,0},{28,4},{1,25},{... | collective-permute-start | bytes 786440 | tf_op jit(solution)/shard_map/ppermute | solution.py:949
  362.9 20.6 %collective-permute-start.23 = (bf16[400,1024]{1,0:T(8,128)(2,1)}, bf16[400,1024]{1,0:T(8,128)(2,1)S(1)}, u32[]{:S(2)}, u32[]{:S(2)}) collective-permute-start(bf16[400,1024]{1,0:T(8,128)(2,1)} %get-tuple-element.350), channel_id=1, source_target_pairs={{0,2},{1,3},{2,0},{3,1},{4,6},{5,7},{6,4},{7,5},{8,10},{9,11},{10,... | collective-permute-start | bytes 2457608 | tf_op jit(solution)/shard_map/ppermute | solution.py:949
  364.1 19.3 %collective-permute-start.24 = (bf16[256,1024]{1,0:T(8,128)(2,1)}, bf16[256,1024]{1,0:T(8,128)(2,1)S(1)}, u32[]{:S(2)}, u32[]{:S(2)}) collective-permute-start(bf16[256,1024]{1,0:T(8,128)(2,1)} %get-tuple-element.352), channel_id=1, source_target_pairs={{0,4},{4,0},{8,12},{12,8},{16,20},{20,16},{24,28},{28,24},{1,5},{5... | collective-permute-start | bytes 1572872 | tf_op jit(solution)/shard_map/ppermute | solution.py:949
  383.4 19.4 %collective-permute-start.25 = (bf16[4,2,16,1024]{3,2,0,1:T(8,128)(2,1)S(1)}, bf16[4,2,16,1024]{3,2,0,1:T(8,128)(2,1)}, u32[]{:S(2)}, u32[]{:S(2)}) collective-permute-start(bf16[4,2,16,1024]{3,2,0,1:T(8,128)(2,1)S(1)} %add_convert_fusion.8), channel_id=1, source_target_pairs={{0,16},{4,20},{8,24},{12,28},{16,0},{20,4},{24,8},{28,12},{1,17},{... | collective-permute-start | bytes 786440 | tf_op jit(solution)/shard_map/ppermute | solution.py:949
  383.5 20.5 %collective-permute-start.26 = (bf16[4,2,16,1024]{3,2,0,1:T(8,128)(2,1)S(1)}, bf16[4,2,16,1024]{3,2,0,1:T(8,128)(2,1)S(1)}, u32[]{:S(2)}, u32[]{:S(2)}) collective-permute-start(bf16[4,2,16,1024]{3,2,0,1:T(8,128)(2,1)S(1)} %add_convert_fusion.8), channel_id=1, source_target_pairs={{0,8},{4,12},{8,0},{12,4},{16,24},{20,28},{24,16},{28,20},{1,9},{5... | collective-permute-start | bytes 786440 | tf_op jit(solution)/shard_map/ppermute | solution.py:949
  385.2 20.5 %collective-permute-start.27 = (bf16[4,2,16,1024]{3,2,0,1:T(8,128)(2,1)S(1)}, bf16[4,2,16,1024]{3,2,0,1:T(8,128)(2,1)S(1)}, u32[]{:S(2)}, u32[]{:S(2)}) collective-permute-start(bf16[4,2,16,1024]{3,2,0,1:T(8,128)(2,1)S(1)} %add_convert_fusion.8), channel_id=1, source_target_pairs={{0,24},{4,28},{8,16},{12,20},{16,8},{20,12},{24,0},{28,4},{1,25},{... | collective-permute-start | bytes 786440 | tf_op jit(solution)/shard_map/ppermute | solution.py:949
  386.2 19.7 %collective-permute-start.28 = (bf16[320,1024]{1,0:T(8,128)(2,1)}, bf16[320,1024]{1,0:T(8,128)(2,1)S(1)}, u32[]{:S(2)}, u32[]{:S(2)}) collective-permute-start(bf16[320,1024]{1,0:T(8,128)(2,1)} %get-tuple-element.367), channel_id=1, source_target_pairs={{0,2},{1,3},{2,0},{3,1},{4,6},{5,7},{6,4},{7,5},{8,10},{9,11},{10,... | collective-permute-start | bytes 1966088 | tf_op jit(solution)/shard_map/ppermute | solution.py:949
  387.4 18.4 %collective-permute-start.29 = (bf16[256,1024]{1,0:T(8,128)(2,1)}, bf16[256,1024]{1,0:T(8,128)(2,1)S(1)}, u32[]{:S(2)}, u32[]{:S(2)}) collective-permute-start(bf16[256,1024]{1,0:T(8,128)(2,1)} %get-tuple-element.373), channel_id=1, source_target_pairs={{0,4},{4,0},{8,12},{12,8},{16,20},{20,16},{24,28},{28,24},{1,5},{5... | collective-permute-start | bytes 1572872 | tf_op jit(solution)/shard_map/ppermute | solution.py:949
  405.9 7.0 %collective-permute-start.32 = (f32[8,1024]{1,0:T(8,128)S(1)}, f32[8,1024]{1,0:T(8,128)S(1)}, u32[]{:S(2)}, u32[]{:S(2)}) collective-permute-start(f32[8,1024]{1,0:T(8,128)S(1)} %slice.185), channel_id=1, source_target_pairs={{0,4},{4,0},{8,12},{12,8},{16,20},{20,16},{24,28},{28,24},{1,5},{5... | collective-permute-start | bytes 98312 | tf_op jit(solution)/shard_map/ppermute | solution.py:949
  407.1 12.4 %collective-permute-start.31 = (bf16[4,64,1024]{2,1,0:T(8,128)(2,1)S(1)}, bf16[4,64,1024]{2,1,0:T(8,128)(2,1)S(1)}, u32[]{:S(2)}, u32[]{:S(2)}) collective-permute-start(bf16[4,64,1024]{2,1,0:T(8,128)(2,1)S(1)} %get-tuple-element.375), channel_id=1, source_target_pairs={{0,2},{1,3},{2,0},{3,1},{4,6},{5,7},{6,4},{7,5},{8,10},{9,11},{10,... | collective-permute-start | bytes 1572872 | tf_op jit(solution)/shard_map/ppermute | solution.py:949
  408.4 11.4 %collective-permute-start.30 = (bf16[4,64,1024]{2,1,0:T(8,128)(2,1)S(1)}, bf16[4,64,1024]{2,1,0:T(8,128)(2,1)S(1)}, u32[]{:S(2)}, u32[]{:S(2)}) collective-permute-start(bf16[4,64,1024]{2,1,0:T(8,128)(2,1)S(1)} %get-tuple-element.374), channel_id=1, source_target_pairs={{0,4},{4,0},{8,12},{12,8},{16,20},{20,16},{24,28},{28,24},{1,5},{5... | collective-permute-start | bytes 1572872 | tf_op jit(solution)/shard_map/ppermute | solution.py:949
  408.6 11.2 %collective-permute-start.34 = (bf16[128,1024]{1,0:T(8,128)(2,1)}, bf16[128,1024]{1,0:T(8,128)(2,1)S(1)}, u32[]{:S(2)}, u32[]{:S(2)}) collective-permute-start(bf16[128,1024]{1,0:T(8,128)(2,1)} %get-tuple-element.380), channel_id=1, source_target_pairs={{0,24},{4,28},{8,16},{12,20},{16,8},{20,12},{24,0},{28,4},{1,25},{... | collective-permute-start | bytes 786440 | tf_op jit(solution)/shard_map/ppermute | solution.py:949
  413.0 6.6 %collective-permute-start.33 = (f32[16,1024]{1,0:T(8,128)S(1)}, f32[16,1024]{1,0:T(8,128)S(1)}, u32[]{:S(2)}, u32[]{:S(2)}) collective-permute-start(f32[16,1024]{1,0:T(8,128)S(1)} %pad_maximum_fusion.5), channel_id=1, source_target_pairs={{0,2},{1,3},{2,0},{3,1},{4,6},{5,7},{6,4},{7,5},{8,10},{9,11},{10,... | collective-permute-start | bytes 196616 | tf_op jit(solution)/shard_map/ppermute | solution.py:949
  419.9 21.5 %collective-permute-start.36 = (bf16[4,128,1024]{2,1,0:T(8,128)(2,1)S(1)}, bf16[4,128,1024]{2,1,0:T(8,128)(2,1)S(1)}, u32[]{:S(2)}, u32[]{:S(2)}) collective-permute-start(bf16[4,128,1024]{2,1,0:T(8,128)(2,1)S(1)} %pad_maximum_fusion.4), channel_id=1, source_target_pairs={{0,4},{4,0},{8,12},{12,8},{16,20},{20,16},{24,28},{28,24},{1,5},{5... | collective-permute-start | bytes 3145736 | tf_op jit(solution)/shard_map/ppermute | solution.py:949
  420.1 22.3 %collective-permute-start.35 = (bf16[4,128,1024]{2,1,0:T(8,128)(2,1)S(1)}, bf16[4,128,1024]{2,1,0:T(8,128)(2,1)S(1)}, u32[]{:S(2)}, u32[]{:S(2)}) collective-permute-start(bf16[4,128,1024]{2,1,0:T(8,128)(2,1)S(1)} %pad_maximum_fusion.3), channel_id=1, source_target_pairs={{0,2},{1,3},{2,0},{3,1},{4,6},{5,7},{6,4},{7,5},{8,10},{9,11},{10,... | collective-permute-start | bytes 3145736 | tf_op jit(solution)/shard_map/ppermute | solution.py:949
  422.2 20.4 %collective-permute-start.39 = (bf16[128,1024]{1,0:T(8,128)(2,1)S(1)}, bf16[128,1024]{1,0:T(8,128)(2,1)S(1)}, u32[]{:S(2)}, u32[]{:S(2)}) collective-permute-start(bf16[128,1024]{1,0:T(8,128)(2,1)S(1)} %get-tuple-element.392), channel_id=1, source_target_pairs={{0,8},{4,12},{8,0},{12,4},{16,24},{20,28},{24,16},{28,20},{1,9},{5... | collective-permute-start | bytes 786440 | tf_op jit(solution)/shard_map/ppermute | solution.py:949
  423.7 18.9 %collective-permute-start.40 = (bf16[128,1024]{1,0:T(8,128)(2,1)S(1)}, bf16[128,1024]{1,0:T(8,128)(2,1)S(1)}, u32[]{:S(2)}, u32[]{:S(2)}) collective-permute-start(bf16[128,1024]{1,0:T(8,128)(2,1)S(1)} %get-tuple-element.393), channel_id=1, source_target_pairs={{0,16},{4,20},{8,24},{12,28},{16,0},{20,4},{24,8},{28,12},{1,17},{... | collective-permute-start | bytes 786440 | tf_op jit(solution)/shard_map/ppermute | solution.py:949
  425.0 8.5 %collective-permute-start.38 = (f32[8,1024]{1,0:T(8,128)S(1)}, f32[8,1024]{1,0:T(8,128)S(1)}, u32[]{:S(2)}, u32[]{:S(2)}) collective-permute-start(f32[8,1024]{1,0:T(8,128)S(1)} %get-tuple-element.460), channel_id=1, source_target_pairs={{0,16},{4,20},{8,24},{12,28},{16,0},{20,4},{24,8},{28,12},{1,17},{... | collective-permute-start | bytes 98312 | tf_op jit(solution)/shard_map/ppermute | solution.py:949
  445.7 11.7 %collective-permute-start.41 = (bf16[4,512,1024]{2,1,0:T(8,128)(2,1)}, bf16[4,512,1024]{2,1,0:T(8,128)(2,1)}, u32[]{:S(2)}, u32[]{:S(2)}) collective-permute-start(bf16[4,512,1024]{2,1,0:T(8,128)(2,1)} %constant_dynamic-update-slice_fusion.6.pieces), channel_id=1, source_target_pairs={{0,1},{1,0},{2,3},{3,2},{4,5},{5,4},{6,7},{7,6},{8,9},{9,8},{10,11... | collective-permute-start | bytes 12582920 | tf_op jit(solution)/shard_map/ppermute | solution.py:949
  449.7 12.3 %collective-permute-start.42 = (bf16[128,1024]{1,0:T(8,128)(2,1)S(1)}, bf16[128,1024]{1,0:T(8,128)(2,1)S(1)}, u32[]{:S(2)}, u32[]{:S(2)}) collective-permute-start(bf16[128,1024]{1,0:T(8,128)(2,1)S(1)} %get-tuple-element.414), channel_id=1, source_target_pairs={{0,24},{4,28},{8,16},{12,20},{16,8},{20,12},{24,0},{28,4},{1,25},{... | collective-permute-start | bytes 786440 | tf_op jit(solution)/shard_map/ppermute | solution.py:949
  (36 other events, 351.6 us)
Sparse Core Ops, SparseCore 0:
  9.6 59.8 all-gather.4
  71.0 58.2 all-gather.2

commit v7 on v6

--- a/solution.py
+++ b/solution.py
@@ -765,7 +765,7 @@
     )(device, *mine, *theirs, *slots, downs, bias, live)
 
 
-CUTS = ((224, 800), (304, 400, 320))
+CUTS = ((1024,), (304, 400, 320))
 
 
 def expert_grads_kernel(count, shard, added, *refs):
@@ -1189,16 +1189,15 @@
         returned, came_row, live_col, out_weight
     )
     over_y(0)
-    grad_mixed, fars = tie(grad_mixed, fars)
+    grad_mixed, fars[1:] = tie(grad_mixed, fars[1:])
     unstack = lambda v: [v[:, n] for n in range(shared.streams)]
 
-    over_y(1)
     token_grads = attend_back(
         start_row, query, key, value, mixed, grad_mixed, lse
     )
     token_grads, fars = tie(token_grads, fars)
 
-    over_y(2)
+    over_y(1)
     halves = shared_grads(shared, normed, mixed, token_grads, grad_proj)
     token_grads, halves, fars, out_bias_sum = tie(token_grads, halves, fars, out_bias_sum)
 
@@ -1227,7 +1226,7 @@
         total, small, fars, mine, stay, cross, cross_rest
     )
 
-    over_y(3)
+    over_y(2)
     cross = swap(cross, ("expert", n_expert, 1))
     block_out = expert_out(place, mine, theirs, routed, downs, row(expert_down_bias[0]), route_live)
     total = shared.reduce_rest(total)
@@ -1235,7 +1234,7 @@
         total, small, block_out, packets, fars, cross, cross_rest
     )
 
-    over_y(4)
+    over_y(3)
     total = unstack(shared.gather_rest(total))
     near = list(expert_grads(False, packets))
     cross_rest = swap(cross_rest, ("expert", n_expert, 1))
@@ -1248,7 +1247,7 @@
         stay[j] = to_partner(stay[j], j)
     small = small_step(small_step(small))
     total = shared.gather_pair(total, 1)
-    grad_up = near[1] + jnp.concatenate(fars[2:], axis=0).astype(F32)[None]
+    grad_up = near[1] + jnp.concatenate(fars[1:], axis=0).astype(F32)[None]
     total, small, stay, across, grad_up, near[0] = tie(total, small, stay, across, grad_up, near[0])
 
     middle = (side + 1) // 2 + 1
@@ -1256,7 +1255,7 @@
         across[j] = to_partner(across[j], j)
     total = shared.gather_pair(total, 0)
     small = small_sum(small, small_steps)
-    grad_down = near[0] + jnp.concatenate(fars[:2], axis=0).astype(F32)[None]
+    grad_down = near[0] + jnp.concatenate(fars[:1], axis=0).astype(F32)[None]
     total, small, across, grad_down = tie(total, small, across, grad_down)
 
     for j in range(middle, side):

time: 485 us -> 482 us (level)
    ppermute x43 -> x42, starting transfers between devices: 46.1 us -> 44.4 us  [swap(): return lax.ppermute(values, axis, [(i, i ^ bit) for i in range(size)])]
    ppermute x43 -> x42, waiting for transfers between devices: 56.4 us -> 56.1 us  [swap(): return lax.ppermute(values, axis, [(i, i ^ bit) for i in range(size)])]
  transfers between devices with their start and end apart: 50 -> 49, of which waited for: 20 -> 18; matrix products, arithmetic and copies ran while one was open for 6% -> 6% of each run, Pallas kernels for 47% -> 47%
where the time goes in v7:
time: 482 us; the launch traced here: 475 us
  Pallas kernels  231 us (48%)
  waiting for transfers between devices  113 us (23%)
  starting transfers between devices  73.8 us (15%)
  other arithmetic  26.1 us (5%)
  local copies, waits for them, and re-layouts  15.4 us (3%)
  between operations  15.4 us (3%)
    ppermute x42, waiting for transfers between devices, swap(): return lax.ppermute(values, axis, [(i, i ^ bit) for i in range(size)])  56.1 us
    all_to_all x5, waiting for transfers between devices, exchange(): lax.all_to_all(values, 'expert', split_axis=0, concat_axis=0, tiled=True)  55.3 us
    pallas_call x2, Pallas kernels, expert_chunk(): pl.pallas_call(functools.partial(expert_kernel, parts), grid_spec=pltpu.P...  48.2 us
    ppermute x42, starting transfers between devices, swap(): return lax.ppermute(values, axis, [(i, i ^ bit) for i in range(size)])  44.4 us
    pallas_call x1, Pallas kernels, attend_back(): pl.pallas_call(attend_back_kernel, grid=(pairs,), in_specs=[whole((1, cou...  34.4 us
    pallas_call x3, Pallas kernels, expert_grads(): pl.pallas_call(functools.partial(expert_grads_kernel, count, 2 if far els...  34 us
    all_to_all x5, starting transfers between devices, exchange(): lax.all_to_all(values, 'expert', split_axis=0, concat_axis=0, tiled=True)  29.4 us
    pallas_call x1, Pallas kernels, attend(): pl.pallas_call(attend_kernel, grid=(pairs,), in_specs=[whole((count, 1)),...  19.1 us
  transfers between devices with their start and end apart: 49, of which 18 were waited for; matrix products, arithmetic and copies ran while one was open for 6% of the time, Pallas kernels for 47%

profile of v7, /device:TPU:9, one launch (start us, length us, event | category | flops | bytes accessed | tf_op | source)
XLA Modules:
  0.0 474.8 jit_solution(10717085832064506562)
XLA Ops:
  8.7 5.7 %all-to-all-start = ((bf16[8,128,1024]{2,1,0:T(8,128)(2,1)}), bf16[8,128,1024]{2,1,0:T(8,128)(2,1)S(1)}, u32[]{:S(2)}, u32[]{:S(2)}) async-start(bf16[8,128,1024]{2,1,0:T(8,128)(2,1)} %bitcast), calls=%async_computation | async-start | bytes 4194304 | tf_op jit(solution)/shard_map/all_to_all | solution.py:953
  23.0 38.0 %all-to-all-done = bf16[8,128,1024]{2,1,0:T(8,128)(2,1)S(1)} async-done(((bf16[8,128,1024]{2,1,0:T(8,128)(2,1)}), bf16[8,128,1024]{2,1,0:T(8,128)(2,1)S(1)}, u32[]{:S(2)}, u32[]{:S(2)}) %all-to-all-start) | async-done | bytes 2097184 | tf_op jit(solution)/shard_map/all_to_all | solution.py:953
  60.9 5.5 %all-to-all-start.3 = ((f32[8,1,128]{2,1,0:T(1,128)}), f32[8,1,128]{2,1,0:T(1,128)S(1)}, u32[]{:S(2)}, u32[]{:S(2)}) async-start(f32[8,1,128]{2,1,0:T(1,128)} %fusion.4), calls=%async_computation.3 | async-start | bytes 8192 | tf_op jit(solution)/shard_map/all_to_all | solution.py:953
  67.5 13.7 %entry.1 = (bf16[1024,1024]{1,0:T(8,128)(2,1)}, bf16[1024,1024]{1,0:T(8,128)(2,1)}, bf16[1024,1024]{1,0:T(8,128)(2,1)}, bf16[1024,1024]{1,0:T(8,128)(2,1)}, bf16[1024,1024]{1,0:T(8,128)(2,1)}) custom-call(bf16[1024,1024]{1,0:T(8,128)(2,1)} %bitcast.72, s32[1,1024]{1,0:T(1,128)} %pos_row, f32[1,1024]{1,0:T(1,128)} %bitcast.110, f32[1,1024]{1,0:T(1,128)} %bitcast.102, ...), custom_call_target="tpu_custom_call" | custom-call | flops 8589934592 | bytes 18874368 | tf_op jit(solution)/shard_map/entry/pallas_call | solution.py:126
  81.2 19.1 %attend.1 = (bf16[1024,1024]{1,0:T(8,128)(2,1)}, f32[8,8,1024]{2,1,0:T(8,128)}) custom-call(s32[1024,1]{1,0:T(8,128)} %iota_select_fusion.start_col, bf16[1024,1024]{1,0:T(8,128)(2,1)} %get-tuple-element.216.q_ref, bf16[1024,1024]{1,0:T(8,128)(2,1)} %get-tuple-element.217.k_ref, bf16[1024,1024]{1,0:T(8,128)(2,1)} %get-tuple-element.218.v_ref), custom_call_target="tpu_custom_call" | custom-call | flops 8589934592 | bytes 8388608 | tf_op jit(solution)/shard_map/attend/pallas_call | solution.py:261
  100.3 8.0 %leave.1 = (bf16[512,1024]{1,0:T(8,128)(2,1)}, bf16[1024,1024]{1,0:T(8,128)(2,1)}) custom-call(bf16[1024,1024]{1,0:T(8,128)(2,1)} %get-tuple-element.220.mixed.o_ref, bf16[1024,1024]{1,0:T(8,128)(2,1)} %refs_11_.1, f32[1,1024]{1,0:T(1,128)} %bitcast.105, bf16[1024,1024]{1,0:T(8,128)(2,1)} %get-tuple-element.221.tokens, f32[1024,1]{1,0:T(8,128)} %fusion.2.live_col.refs_10_, ...), custom_call_target="tpu_custom_call" | custom-call | flops 3221225472 | bytes 10485760 | tf_op jit(solution)/shard_map/leave/pallas_call | solution.py:311
  108.4 5.4 %all-to-all-start.2 = ((bf16[8,64,1024]{2,1,0:T(8,128)(2,1)}), bf16[8,64,1024]{2,1,0:T(8,128)(2,1)S(1)}, u32[]{:S(2)}, u32[]{:S(2)}) async-start(bf16[8,64,1024]{2,1,0:T(8,128)(2,1)} %bitcast.75), calls=%async_computation.2 | async-start | bytes 2097152 | tf_op jit(solution)/shard_map/all_to_all | solution.py:953
  115.4 4.0 pick.1
  119.4 17.4 %all-to-all-done.2 = bf16[8,64,1024]{2,1,0:T(8,128)(2,1)S(1)} async-done(((bf16[8,64,1024]{2,1,0:T(8,128)(2,1)}), bf16[8,64,1024]{2,1,0:T(8,128)(2,1)S(1)}, u32[]{:S(2)}, u32[]{:S(2)}) %all-to-all-start.2) | async-done | bytes 1048608 | tf_op jit(solution)/shard_map/all_to_all | solution.py:953
  136.7 7.1 %all-to-all-start.1 = ((bf16[8,64,1024]{2,1,0:T(8,128)(2,1)}), bf16[8,64,1024]{2,1,0:T(8,128)(2,1)S(1)}, u32[]{:S(2)}, u32[]{:S(2)}) async-start(bf16[8,64,1024]{2,1,0:T(8,128)(2,1)} %bitcast.76), calls=%async_computation.1 | async-start | bytes 2097152 | tf_op jit(solution)/shard_map/all_to_all | solution.py:953
  146.6 24.0 %expert_chunk.2 = (bf16[512,1024]{1,0:T(8,128)(2,1)}, bf16[6,512,1024]{2,1,0:T(8,128)(2,1)}, bf16[6,512,1024]{2,1,0:T(8,128)(2,1)}, f32[8,1024]{1,0:T(8,128)}, f32[4,1,1024]{2,1,0:T(1,128)}) custom-call(s32[1]{0:T(128)} %bitcast.16.device, s32[8]{0:T(128)} %broadcast_xor_fusion.source, bf16[512,1024]{1,0:T(8,128)(2,1)} %bitcast.68, ...), custom_call_target="tpu_custom_call" | custom-call | flops 12884901888 | bytes 16777216 | tf_op jit(solution)/shard_map/expert_chunk/pallas_call | solution.py:677
  171.7 5.6 %all-to-all-start.4 = ((bf16[8,64,1024]{2,1,0:T(8,128)(2,1)}), bf16[8,64,1024]{2,1,0:T(8,128)(2,1)S(1)}, u32[]{:S(2)}, u32[]{:S(2)}) async-start(bf16[8,64,1024]{2,1,0:T(8,128)(2,1)} %bitcast.77), calls=%async_computation.4 | async-start | bytes 2097152 | tf_op jit(solution)/shard_map/all_to_all | solution.py:953
  177.4 24.3 %expert_chunk.3 = (bf16[64,1024]{1,0:T(8,128)(2,1)}, bf16[64,1024]{1,0:T(8,128)(2,1)}, bf16[64,1024]{1,0:T(8,128)(2,1)}, bf16[128,1024]{1,0:T(8,128)(2,1)}, bf16...) custom-call(s32[1]{0:T(128)} %bitcast.16.device, ...), custom_call_target="tpu_custom_call" | custom-call | flops 12884901888 | bytes 16777216 | tf_op jit(solution)/shard_map/expert_chunk/pallas_call | solution.py:677
  205.2 1.6 collective-permute-start.3
  208.1 11.8 %far_part.1 = (f32[1,1024,1024]{2,1,0:T(8,128)}, f32[1,1024,1024]{2,1,0:T(8,128)}) custom-call(bf16[6,512,1024]{2,1,0:T(8,128)(2,1)} %get-tuple-element.341.refs_0_, bf16[6,512,1024]{2,1,0:T(8,128)(2,1)} %get-tuple-element.342.refs_1_, bf16[6,512,1024]{2,1,0:T(8,128)(2,1)} %collective-permute-done.refs_2_), custom_call_target="tpu_custom_call" | custom-call | flops 6442450944 | bytes 20971520 | tf_op jit(solution)/shard_map/far_part/pallas_call | solution.py:811
  220.6 2.8 collective-permute-start.6
  225.1 7.5 %far_rest.1 = (bf16[1024,1024]{1,0:T(8,128)(2,1)}, bf16[304,1024]{1,0:T(8,128)(2,1)}, bf16[400,1024]{1,0:T(8,128)(2,1)}, bf16[320,1024]{1,0:T(8,128)(2,1)}) custom-call(bf16[6,512,1024]{2,1,0:T(8,128)(2,1)} %collective-permute-done.8.refs_0_.refs_3_, f32[1,1024,1024]{2,1,0:T(8,128)} %get-tuple-element.254.refs_1_, f32[1,1024,1024]{2,1,0:T(8,128)} %get-tuple-element.255.refs_2_), custom_call_target="tpu_custom_call" | custom-call | flops 2147483648 | bytes 20971520 | tf_op jit(solution)/shard_map/far_rest/pallas_call | solution.py:811
  232.7 3.1 collective-permute-done.7.refs_8_
  237.1 9.0 %reenter.1 = (bf16[1024,1024]{1,0:T(8,128)(2,1)}, bf16[1024,1024]{1,0:T(8,128)(2,1)}, bf16[1024,1024]{1,0:T(8,128)(2,1)}, f32[1,1024]{1,0:T(1,128)}) custom-call(bf16[512,1024]{1,0:T(8,128)(2,1)} %bitcast.74, bf16[64,1024]{1,0:T(8,128)(2,1)} %get-tuple-element.265.refs_1_, bf16[64,1024]{1,0:T(8,128)(2,1)} %copy-done.27, bf16[64,1024]{1,0:T(8,128)(2,1)} %copy-done.28, ...), custom_call_target="tpu_custom_call" | custom-call | flops 4294967296 | bytes 10485760 | tf_op jit(solution)/shard_map/reenter/pallas_call | solution.py:401
  246.1 34.4 %attend_back.1.token_grads.grads = bf16[3,1024,1024]{2,1,0:T(8,128)(2,1)} custom-call(s32[1,1024]{1,0:T(1,128)} %compare_select_fusion.start_row, bf16[1024,1024]{1,0:T(8,128)(2,1)} %get-tuple-element.216.q_ref, bf16[1024,1024]{1,0:T(8,128)(2,1)} %get-tuple-element.217.k_ref, bf16[1024,1024]{1,0:T(8,128)(2,1)} %get-tuple-element.218.v_ref, ...), custom_call_target="tpu_custom_call" | custom-call | flops 21474836480 | bytes 16777216 | tf_op jit(solution)/shard_map/attend_back/pallas_call | solution.py:495
  280.6 2.2 collective-permute-done.9
  284.0 14.2 %shared_grads.1 = (bf16[4,512,1024]{2,1,0:T(8,128)(2,1)}, bf16[4,512,1024]{2,1,0:T(8,128)(2,1)}) custom-call(s32[2]{0:T(128)} %pad_add_fusion.1.codes, bf16[1024,1024]{1,0:T(8,128)(2,1)} %get-tuple-element.286.normed, bf16[1024,1024]{1,0:T(8,128)(2,1)} %get-tuple-element.220.mixed.o_ref, bf16[3,1024,1024]{2,1,0:T(8,128)(2,1)} %attend_back.1.token_grads.grads, ...), custom_call_target="tpu_custom_call" | custom-call | flops 8589934592 | bytes 25165824 | tf_op jit(solution)/shard_map/shared_grads/pallas_call | solution.py:863
  298.3 1.8 collective-permute-start.11
  300.8 6.2 %collective-permute-done.11 = bf16[4,512,1024]{2,1,0:T(8,128)(2,1)S(1)} collective-permute-done((bf16[4,512,1024]{2,1,0:T(8,128)(2,1)}, bf16[4,512,1024]{2,1,0:T(8,128)(2,1)S(1)}, u32[]{:S(2)}, u32[]{:S(2)}) %collective-permute-start.11) | collective-permute-done | bytes 4194336 | tf_op jit(solution)/shard_map/ppermute | solution.py:949
  307.1 4.4 add_convert_fusion.2
  313.6 18.2 %finish.1 = (bf16[128,1024]{1,0:T(8,128)(2,1)}, bf16[128,1024]{1,0:T(8,128)(2,1)}, bf16[128,1024]{1,0:T(8,128)(2,1)}, bf16[128,1024]{1,0:T(8,128)(2,1)}, bf16[25...) custom-call(bf16[3,1024,1024]{2,1,0:T(8,128)(2,1)} %attend_back.1.token_grads.grads, ...), custom_call_target="tpu_custom_call" | custom-call | flops 8589934592 | bytes 20971520 | tf_op jit(solution)/shard_map/finish/pallas_call | solution.py:560
  331.9 4.4 collective-permute-done.13
  336.3 1.6 add_convert_fusion
  337.9 1.9 add_convert_fusion.1
  341.1 1.8 collective-permute-start.16
  342.9 1.8 collective-permute-start.18
  344.8 7.4 %collective-permute-done.14 = bf16[4,64,1024]{2,1,0:T(8,128)(2,1)S(1)} collective-permute-done((bf16[4,64,1024]{2,1,0:T(8,128)(2,1)S(1)}, bf16[4,64,1024]{2,1,0:T(8,128)(2,1)S(1)}, u32[]{:S(2)}, u32[]{:S(2)}) %collective-permute-start.14) | collective-permute-done | bytes 524320 | tf_op jit(solution)/shard_map/ppermute | solution.py:949
  353.6 3.2 collective-permute-done.18.refs_2_
  357.6 2.0 collective-permute-start.20
  362.3 15.3 %expert_out.1 = bf16[8,128,1024]{2,1,0:T(8,128)(2,1)} custom-call(s32[1]{0:T(128)} %bitcast.16.device, bf16[6,512,1024]{2,1,0:T(8,128)(2,1)} %get-tuple-element.341.refs_0_, bf16[6,512,1024]{2,1,0:T(8,128)(2,1)} %get-tuple-element.342.refs_1_, bf16[6,512,1024]{2,1,0:T(8,128)(2,1)} %get-tuple-element.231.refs_2_, ...), custom_call_target="tpu_custom_call" | custom-call | flops 8589934592 | bytes 16777216 | tf_op jit(solution)/shard_map/expert_out/pallas_call | solution.py:748
  377.6 3.1 collective-permute-done.21
  380.9 1.6 collective-permute-start.25
  385.3 14.7 %near_grads.1 = (f32[1,1024,1024]{2,1,0:T(8,128)}, f32[1,1024,1024]{2,1,0:T(8,128)}) custom-call(bf16[6,512,1024]{2,1,0:T(8,128)(2,1)} %get-tuple-element.341.refs_0_, bf16[6,512,1024]{2,1,0:T(8,128)(2,1)} %get-tuple-element.342.refs_1_, bf16[6,512,1024]{2,1,0:T(8,128)(2,1)} %collective-permute-done.refs_2_, ...), custom_call_target="tpu_custom_call" | custom-call | flops 8589934592 | bytes 20971520 | tf_op jit(solution)/shard_map/near_grads/pallas_call | solution.py:811
  401.3 1.8 collective-permute-done.26
  407.3 2.8 convert_add_fusion.1
  411.4 5.6 %collective-permute-done.32 = f32[16,1024]{1,0:T(8,128)S(1)} collective-permute-done((f32[16,1024]{1,0:T(8,128)S(1)}, f32[16,1024]{1,0:T(8,128)S(1)}, u32[]{:S(2)}, u32[]{:S(2)}) %collective-permute-start.32) | collective-permute-done | bytes 65568 | tf_op jit(solution)/shard_map/ppermute | solution.py:949
  423.2 2.8 convert_add_fusion
  426.0 4.8 %collective-permute-done.37 = f32[8,1024]{1,0:T(8,128)S(1)} collective-permute-done((f32[8,1024]{1,0:T(8,128)S(1)}, f32[8,1024]{1,0:T(8,128)S(1)}, u32[]{:S(2)}, u32[]{:S(2)}) %collective-permute-start.37) | collective-permute-done | bytes 32800 | tf_op jit(solution)/shard_map/ppermute | solution.py:949
  430.8 7.8 %collective-permute-done.35 = bf16[4,128,1024]{2,1,0:T(8,128)(2,1)S(1)} collective-permute-done((bf16[4,128,1024]{2,1,0:T(8,128)(2,1)S(1)}, bf16[4,128,1024]{2,1,0:T(8,128)(2,1)S(1)}, u32[]{:S(2)}, u32[]{:S(2)}) %collective-permute-start.35) | collective-permute-done | bytes 1048608 | tf_op jit(solution)/shard_map/ppermute | solution.py:949
  442.6 4.1 collective-permute-start.40
  448.0 5.5 %unmix.2 = (f32[1024,1024]{1,0:T(8,128)}, f32[1024,1024]{1,0:T(8,128)}, f32[1024,1024]{1,0:T(8,128)}, f32[1024,1024]{1,0:T(8,128)}) custom-call(s32[2]{0:T(128)} %pad_add_fusion.1.codes, s32[1]{0:T(128)} %bitcast.39.half_place.source, s32[1]{0:T(128)} %bitcast.39.half_place.source, bf16[4,512,1024]{2,1,0:T(8,128)(2,1)} %constant_dynamic-update-slice_fusion.6.pieces), custom_call_target="tpu_custom_call" | custom-call | flops 2097152 | bytes 12582912 | tf_op jit(solution)/shard_map/unmix/pallas_call | solution.py:924
  454.7 4.5 collective-permute-done.41.refs_7_
  459.9 7.7 %unmix.3 = (f32[1024,1024]{1,0:T(8,128)}, f32[1024,1024]{1,0:T(8,128)}, f32[1024,1024]{1,0:T(8,128)}, f32[1024,1024]{1,0:T(8,128)}, bf16[1024,1024]{1,0:T(8,128)(2,1)}) custom-call(s32[2]{0:T(128)} %pad_add_fusion.1.codes, s32[1]{0:T(128)S(6)} %sub.24.half_place, ...), custom_call_target="tpu_custom_call", output_to_operand_aliasing={{0}: (12, {}), {1}: (13, {}), {2}: (14, {}), {3}: (15, {})} | custom-call | flops 2097152 | bytes 12582912 | tf_op jit(solution)/shard_map/unmix/pallas_call | solution.py:924
  (220 shorter events, 58.2 us)
Async XLA Ops:
  7.2 139.4 %all-gather.5.cloned.1.call-start = ((), (), s32[]{:S(2)}) async-start(), calls=%async_computation.6 | async-start | bytes 10485760 | tf_op jit(solution)/shard_map/all_gather | solution.py:1095
  7.9 138.7 %all-gather.3.cloned.1.call-start = ((), (), s32[]{:S(2)}) async-start(), calls=%async_computation.5 | async-start | bytes 10485760 | tf_op jit(solution)/shard_map/all_gather | solution.py:1094
  8.7 52.2 %all-to-all-start = ((bf16[8,128,1024]{2,1,0:T(8,128)(2,1)}), bf16[8,128,1024]{2,1,0:T(8,128)(2,1)S(1)}, u32[]{:S(2)}, u32[]{:S(2)}) async-start(bf16[8,128,1024]{2,1,0:T(8,128)(2,1)} %bitcast), calls=%async_computation | async-start | bytes 4194304 | tf_op jit(solution)/shard_map/all_to_all | solution.py:953
  60.9 47.4 %all-to-all-start.3 = ((f32[8,1,128]{2,1,0:T(1,128)}), f32[8,1,128]{2,1,0:T(1,128)S(1)}, u32[]{:S(2)}, u32[]{:S(2)}) async-start(f32[8,1,128]{2,1,0:T(1,128)} %fusion.4), calls=%async_computation.3 | async-start | bytes 8192 | tf_op jit(solution)/shard_map/all_to_all | solution.py:953
  108.4 28.4 %all-to-all-start.2 = ((bf16[8,64,1024]{2,1,0:T(8,128)(2,1)}), bf16[8,64,1024]{2,1,0:T(8,128)(2,1)S(1)}, u32[]{:S(2)}, u32[]{:S(2)}) async-start(bf16[8,64,1024]{2,1,0:T(8,128)(2,1)} %bitcast.75), calls=%async_computation.2 | async-start | bytes 2097152 | tf_op jit(solution)/shard_map/all_to_all | solution.py:953
  136.7 33.9 %all-to-all-start.1 = ((bf16[8,64,1024]{2,1,0:T(8,128)(2,1)}), bf16[8,64,1024]{2,1,0:T(8,128)(2,1)S(1)}, u32[]{:S(2)}, u32[]{:S(2)}) async-start(bf16[8,64,1024]{2,1,0:T(8,128)(2,1)} %bitcast.76), calls=%async_computation.1 | async-start | bytes 2097152 | tf_op jit(solution)/shard_map/all_to_all | solution.py:953
  170.6 31.1 %collective-permute-start = (bf16[6,512,1024]{2,1,0:T(8,128)(2,1)}, bf16[6,512,1024]{2,1,0:T(8,128)(2,1)}, u32[]{:S(2)}, u32[]{:S(2)}) collective-permute-start(bf16[6,512,1024]{2,1,0:T(8,128)(2,1)} %get-tuple-element.231.refs_2_), channel_id=1, source_target_pairs={{0,1},{1,0},{2,3},{3,2},{4,5},{5,4},{6,7},{7,6},{8,9},{9,8},{10,11... | collective-permute-start | bytes 18874376 | tf_op jit(solution)/shard_map/ppermute | solution.py:949
  171.7 29.9 %all-to-all-start.4 = ((bf16[8,64,1024]{2,1,0:T(8,128)(2,1)}), bf16[8,64,1024]{2,1,0:T(8,128)(2,1)S(1)}, u32[]{:S(2)}, u32[]{:S(2)}) async-start(bf16[8,64,1024]{2,1,0:T(8,128)(2,1)} %bitcast.77), calls=%async_computation.4 | async-start | bytes 2097152 | tf_op jit(solution)/shard_map/all_to_all | solution.py:953
  201.7 23.1 %collective-permute-start.8 = (bf16[6,512,1024]{2,1,0:T(8,128)(2,1)}, bf16[6,512,1024]{2,1,0:T(8,128)(2,1)}, u32[]{:S(2)}, u32[]{:S(2)}) collective-permute-start(bf16[6,512,1024]{2,1,0:T(8,128)(2,1)} %get-tuple-element.253.refs_3_), channel_id=1, source_target_pairs={{0,1},{1,0},{2,3},{3,2},{4,5},{5,4},{6,7},{7,6},{8,9},{9,8},{10,11... | collective-permute-start | bytes 18874376 | tf_op jit(solution)/shard_map/ppermute | solution.py:949
  204.0 15.9 %collective-permute-start.4 = (bf16[192,1024]{1,0:T(8,128)(2,1)}, bf16[192,1024]{1,0:T(8,128)(2,1)S(1)}, u32[]{:S(2)}, u32[]{:S(2)}) collective-permute-start(bf16[192,1024]{1,0:T(8,128)(2,1)} %get-tuple-element.245), channel_id=1, source_target_pairs={{0,4},{4,0},{8,12},{12,8},{16,20},{20,16},{24,28},{28,24},{1,5},{5... | collective-permute-start | bytes 1179656 | tf_op jit(solution)/shard_map/ppermute | solution.py:949
  205.2 14.7 %collective-permute-start.3 = (bf16[128,1024]{1,0:T(8,128)(2,1)}, bf16[128,1024]{1,0:T(8,128)(2,1)S(1)}, u32[]{:S(2)}, u32[]{:S(2)}) collective-permute-start(bf16[128,1024]{1,0:T(8,128)(2,1)} %get-tuple-element.244), channel_id=1, source_target_pairs={{0,8},{4,12},{8,0},{12,4},{16,24},{20,28},{24,16},{28,20},{1,9},{5... | collective-permute-start | bytes 786440 | tf_op jit(solution)/shard_map/ppermute | solution.py:949
  206.9 25.7 %collective-permute-start.1 = (bf16[64,1024]{1,0:T(8,128)(2,1)}, bf16[64,1024]{1,0:T(8,128)(2,1)S(1)}, u32[]{:S(2)}, u32[]{:S(2)}) collective-permute-start(bf16[64,1024]{1,0:T(8,128)(2,1)} %get-tuple-element.242), channel_id=1, source_target_pairs={{0,16},{4,20},{8,24},{12,28},{16,0},{20,4},{24,8},{28,12},{1,17},{... | collective-permute-start | bytes 393224 | tf_op jit(solution)/shard_map/ppermute | solution.py:949
  207.6 25.1 %collective-permute-start.2 = (bf16[64,1024]{1,0:T(8,128)(2,1)}, bf16[64,1024]{1,0:T(8,128)(2,1)S(1)}, u32[]{:S(2)}, u32[]{:S(2)}) collective-permute-start(bf16[64,1024]{1,0:T(8,128)(2,1)} %get-tuple-element.243), channel_id=1, source_target_pairs={{0,24},{4,28},{8,16},{12,20},{16,8},{20,12},{24,0},{28,4},{1,25},{... | collective-permute-start | bytes 393224 | tf_op jit(solution)/shard_map/ppermute | solution.py:949
  220.6 12.1 %collective-permute-start.6 = (bf16[64,1024]{1,0:T(8,128)(2,1)S(1)}, bf16[64,1024]{1,0:T(8,128)(2,1)S(1)}, u32[]{:S(2)}, u32[]{:S(2)}) collective-permute-start(bf16[64,1024]{1,0:T(8,128)(2,1)S(1)} %get-tuple-element.429), channel_id=1, source_target_pairs={{0,16},{4,20},{8,24},{12,28},{16,0},{20,4},{24,8},{28,12},{1,17},{... | collective-permute-start | bytes 393224 | tf_op jit(solution)/shard_map/ppermute | solution.py:949
  223.4 12.4 %collective-permute-start.7 = (bf16[64,1024]{1,0:T(8,128)(2,1)S(1)}, bf16[64,1024]{1,0:T(8,128)(2,1)S(1)}, u32[]{:S(2)}, u32[]{:S(2)}) collective-permute-start(bf16[64,1024]{1,0:T(8,128)(2,1)S(1)} %get-tuple-element.428), channel_id=1, source_target_pairs={{0,24},{4,28},{8,16},{12,20},{16,8},{20,12},{24,0},{28,4},{1,25},{... | collective-permute-start | bytes 393224 | tf_op jit(solution)/shard_map/ppermute | solution.py:949
  224.8 11.0 %collective-permute-start.5 = (bf16[64,1024]{1,0:T(8,128)(2,1)S(1)}, bf16[64,1024]{1,0:T(8,128)(2,1)S(1)}, u32[]{:S(2)}, u32[]{:S(2)}) collective-permute-start(bf16[64,1024]{1,0:T(8,128)(2,1)S(1)} %get-tuple-element.431), channel_id=1, source_target_pairs={{0,4},{4,0},{8,12},{12,8},{16,20},{20,16},{24,28},{28,24},{1,5},{5... | collective-permute-start | bytes 393224 | tf_op jit(solution)/shard_map/ppermute | solution.py:949
  235.8 47.0 %collective-permute-start.9 = (bf16[1024,1024]{1,0:T(8,128)(2,1)}, bf16[1024,1024]{1,0:T(8,128)(2,1)S(1)}, u32[]{:S(2)}, u32[]{:S(2)}) collective-permute-start(bf16[1024,1024]{1,0:T(8,128)(2,1)} %get-tuple-element.280), channel_id=1, source_target_pairs={{0,2},{1,3},{2,0},{3,1},{4,6},{5,7},{6,4},{7,5},{8,10},{9,11},{10,... | collective-permute-start | bytes 6291464 | tf_op jit(solution)/shard_map/ppermute | solution.py:949
  282.8 15.5 %collective-permute-start.10 = (bf16[304,1024]{1,0:T(8,128)(2,1)S(1)}, bf16[304,1024]{1,0:T(8,128)(2,1)S(1)}, u32[]{:S(2)}, u32[]{:S(2)}) collective-permute-start(bf16[304,1024]{1,0:T(8,128)(2,1)S(1)} %copy-done.24), channel_id=1, source_target_pairs={{0,2},{1,3},{2,0},{3,1},{4,6},{5,7},{6,4},{7,5},{8,10},{9,11},{10,... | collective-permute-start | bytes 1867784 | tf_op jit(solution)/shard_map/ppermute | solution.py:949
  298.3 8.8 %collective-permute-start.11 = (bf16[4,512,1024]{2,1,0:T(8,128)(2,1)}, bf16[4,512,1024]{2,1,0:T(8,128)(2,1)S(1)}, u32[]{:S(2)}, u32[]{:S(2)}) collective-permute-start(bf16[4,512,1024]{2,1,0:T(8,128)(2,1)} %get-tuple-element.297), channel_id=1, source_target_pairs={{0,1},{1,0},{2,3},{3,2},{4,5},{5,4},{6,7},{7,6},{8,9},{9,8},{10,11... | collective-permute-start | bytes 12582920 | tf_op jit(solution)/shard_map/ppermute | solution.py:949
  311.5 24.8 %collective-permute-start.13 = (bf16[4,128,1024]{2,1,0:T(8,128)(2,1)}, bf16[4,128,1024]{2,1,0:T(8,128)(2,1)}, u32[]{:S(2)}, u32[]{:S(2)}) collective-permute-start(bf16[4,128,1024]{2,1,0:T(8,128)(2,1)} %get-tuple-element.313), channel_id=1, source_target_pairs={{0,4},{4,0},{8,12},{12,8},{16,20},{20,16},{24,28},{28,24},{1,5},{5... | collective-permute-start | bytes 3145736 | tf_op jit(solution)/shard_map/ppermute | solution.py:949
  313.3 24.7 %collective-permute-start.12 = (bf16[4,128,1024]{2,1,0:T(8,128)(2,1)S(1)}, bf16[4,128,1024]{2,1,0:T(8,128)(2,1)}, u32[]{:S(2)}, u32[]{:S(2)}) collective-permute-start(bf16[4,128,1024]{2,1,0:T(8,128)(2,1)S(1)} %get-tuple-element.311), channel_id=1, source_target_pairs={{0,2},{1,3},{2,0},{3,1},{4,6},{5,7},{6,4},{7,5},{8,10},{9,11},{10,... | collective-permute-start | bytes 3145736 | tf_op jit(solution)/shard_map/ppermute | solution.py:949
  339.9 12.3 %collective-permute-start.14 = (bf16[4,64,1024]{2,1,0:T(8,128)(2,1)S(1)}, bf16[4,64,1024]{2,1,0:T(8,128)(2,1)S(1)}, u32[]{:S(2)}, u32[]{:S(2)}) collective-permute-start(bf16[4,64,1024]{2,1,0:T(8,128)(2,1)S(1)} %slice.176), channel_id=1, source_target_pairs={{0,4},{4,0},{8,12},{12,8},{16,20},{20,16},{24,28},{28,24},{1,5},{5... | collective-permute-start | bytes 1572872 | tf_op jit(solution)/shard_map/ppermute | solution.py:949
  340.6 12.0 %collective-permute-start.15 = (bf16[4,64,1024]{2,1,0:T(8,128)(2,1)S(1)}, bf16[4,64,1024]{2,1,0:T(8,128)(2,1)S(1)}, u32[]{:S(2)}, u32[]{:S(2)}) collective-permute-start(bf16[4,64,1024]{2,1,0:T(8,128)(2,1)S(1)} %slice.178), channel_id=1, source_target_pairs={{0,2},{1,3},{2,0},{3,1},{4,6},{5,7},{6,4},{7,5},{8,10},{9,11},{10,... | collective-permute-start | bytes 1572872 | tf_op jit(solution)/shard_map/ppermute | solution.py:949
  341.1 3.7 collective-permute-start.16
  342.9 10.7 %collective-permute-start.17 = (bf16[128,1024]{1,0:T(8,128)(2,1)S(1)}, bf16[128,1024]{1,0:T(8,128)(2,1)S(1)}, u32[]{:S(2)}, u32[]{:S(2)}) collective-permute-start(bf16[128,1024]{1,0:T(8,128)(2,1)S(1)} %copy-done.26), channel_id=1, source_target_pairs={{0,8},{4,12},{8,0},{12,4},{16,24},{20,28},{24,16},{28,20},{1,9},{5... | collective-permute-start | bytes 786440 | tf_op jit(solution)/shard_map/ppermute | solution.py:949
  342.9 13.9 %collective-permute-start.18 = (bf16[128,1024]{1,0:T(8,128)(2,1)S(1)}, bf16[128,1024]{1,0:T(8,128)(2,1)S(1)}, u32[]{:S(2)}, u32[]{:S(2)}) collective-permute-start(bf16[128,1024]{1,0:T(8,128)(2,1)S(1)} %copy-done.25), channel_id=1, source_target_pairs={{0,16},{4,20},{8,24},{12,28},{16,0},{20,4},{24,8},{28,12},{1,17},{... | collective-permute-start | bytes 786440 | tf_op jit(solution)/shard_map/ppermute | solution.py:949
  357.6 20.0 %collective-permute-start.19 = (bf16[4,2,16,1024]{3,2,0,1:T(8,128)(2,1)}, bf16[4,2,16,1024]{3,2,0,1:T(8,128)(2,1)S(1)}, u32[]{:S(2)}, u32[]{:S(2)}) collective-permute-start(bf16[4,2,16,1024]{3,2,0,1:T(8,128)(2,1)} %get-tuple-element.419), channel_id=1, source_target_pairs={{0,16},{4,20},{8,24},{12,28},{16,0},{20,4},{24,8},{28,12},{1,17},{... | collective-permute-start | bytes 786440 | tf_op jit(solution)/shard_map/ppermute | solution.py:949
  357.6 20.0 %collective-permute-start.20 = (bf16[4,2,16,1024]{3,2,0,1:T(8,128)(2,1)S(1)}, bf16[4,2,16,1024]{3,2,0,1:T(8,128)(2,1)S(1)}, u32[]{:S(2)}, u32[]{:S(2)}) collective-permute-start(bf16[4,2,16,1024]{3,2,0,1:T(8,128)(2,1)S(1)} %get-tuple-element.421), channel_id=1, source_target_pairs={{0,8},{4,12},{8,0},{12,4},{16,24},{20,28},{24,16},{28,20},{1,9},{5... | collective-permute-start | bytes 786440 | tf_op jit(solution)/shard_map/ppermute | solution.py:949
  359.6 21.0 %collective-permute-start.21 = (bf16[4,2,16,1024]{3,2,0,1:T(8,128)(2,1)S(1)}, bf16[4,2,16,1024]{3,2,0,1:T(8,128)(2,1)S(1)}, u32[]{:S(2)}, u32[]{:S(2)}) collective-permute-start(bf16[4,2,16,1024]{3,2,0,1:T(8,128)(2,1)S(1)} %get-tuple-element.420), channel_id=1, source_target_pairs={{0,24},{4,28},{8,16},{12,20},{16,8},{20,12},{24,0},{28,4},{1,25},{... | collective-permute-start | bytes 786440 | tf_op jit(solution)/shard_map/ppermute | solution.py:949
  360.3 20.6 %collective-permute-start.22 = (bf16[400,1024]{1,0:T(8,128)(2,1)}, bf16[400,1024]{1,0:T(8,128)(2,1)S(1)}, u32[]{:S(2)}, u32[]{:S(2)}) collective-permute-start(bf16[400,1024]{1,0:T(8,128)(2,1)} %get-tuple-element.334), channel_id=1, source_target_pairs={{0,2},{1,3},{2,0},{3,1},{4,6},{5,7},{6,4},{7,5},{8,10},{9,11},{10,... | collective-permute-start | bytes 2457608 | tf_op jit(solution)/shard_map/ppermute | solution.py:949
  361.3 19.5 %collective-permute-start.23 = (bf16[256,1024]{1,0:T(8,128)(2,1)}, bf16[256,1024]{1,0:T(8,128)(2,1)S(1)}, u32[]{:S(2)}, u32[]{:S(2)}) collective-permute-start(bf16[256,1024]{1,0:T(8,128)(2,1)} %get-tuple-element.336), channel_id=1, source_target_pairs={{0,4},{4,0},{8,12},{12,8},{16,20},{20,16},{24,28},{28,24},{1,5},{5... | collective-permute-start | bytes 1572872 | tf_op jit(solution)/shard_map/ppermute | solution.py:949
  380.8 19.2 %collective-permute-start.24 = (bf16[4,2,16,1024]{3,2,0,1:T(8,128)(2,1)S(1)}, bf16[4,2,16,1024]{3,2,0,1:T(8,128)(2,1)}, u32[]{:S(2)}, u32[]{:S(2)}) collective-permute-start(bf16[4,2,16,1024]{3,2,0,1:T(8,128)(2,1)S(1)} %add_convert_fusion.8), channel_id=1, source_target_pairs={{0,16},{4,20},{8,24},{12,28},{16,0},{20,4},{24,8},{28,12},{1,17},{... | collective-permute-start | bytes 786440 | tf_op jit(solution)/shard_map/ppermute | solution.py:949
  380.9 20.3 %collective-permute-start.25 = (bf16[4,2,16,1024]{3,2,0,1:T(8,128)(2,1)S(1)}, bf16[4,2,16,1024]{3,2,0,1:T(8,128)(2,1)S(1)}, u32[]{:S(2)}, u32[]{:S(2)}) collective-permute-start(bf16[4,2,16,1024]{3,2,0,1:T(8,128)(2,1)S(1)} %add_convert_fusion.8), channel_id=1, source_target_pairs={{0,8},{4,12},{8,0},{12,4},{16,24},{20,28},{24,16},{28,20},{1,9},{5... | collective-permute-start | bytes 786440 | tf_op jit(solution)/shard_map/ppermute | solution.py:949
  382.6 20.5 %collective-permute-start.26 = (bf16[4,2,16,1024]{3,2,0,1:T(8,128)(2,1)S(1)}, bf16[4,2,16,1024]{3,2,0,1:T(8,128)(2,1)S(1)}, u32[]{:S(2)}, u32[]{:S(2)}) collective-permute-start(bf16[4,2,16,1024]{3,2,0,1:T(8,128)(2,1)S(1)} %add_convert_fusion.8), channel_id=1, source_target_pairs={{0,24},{4,28},{8,16},{12,20},{16,8},{20,12},{24,0},{28,4},{1,25},{... | collective-permute-start | bytes 786440 | tf_op jit(solution)/shard_map/ppermute | solution.py:949
  383.6 19.6 %collective-permute-start.27 = (bf16[320,1024]{1,0:T(8,128)(2,1)}, bf16[320,1024]{1,0:T(8,128)(2,1)S(1)}, u32[]{:S(2)}, u32[]{:S(2)}) collective-permute-start(bf16[320,1024]{1,0:T(8,128)(2,1)} %get-tuple-element.350), channel_id=1, source_target_pairs={{0,2},{1,3},{2,0},{3,1},{4,6},{5,7},{6,4},{7,5},{8,10},{9,11},{10,... | collective-permute-start | bytes 1966088 | tf_op jit(solution)/shard_map/ppermute | solution.py:949
  384.6 18.5 %collective-permute-start.28 = (bf16[256,1024]{1,0:T(8,128)(2,1)}, bf16[256,1024]{1,0:T(8,128)(2,1)S(1)}, u32[]{:S(2)}, u32[]{:S(2)}) collective-permute-start(bf16[256,1024]{1,0:T(8,128)(2,1)} %get-tuple-element.356), channel_id=1, source_target_pairs={{0,4},{4,0},{8,12},{12,8},{16,20},{20,16},{24,28},{28,24},{1,5},{5... | collective-permute-start | bytes 1572872 | tf_op jit(solution)/shard_map/ppermute | solution.py:949
  403.2 7.0 %collective-permute-start.31 = (f32[8,1024]{1,0:T(8,128)S(1)}, f32[8,1024]{1,0:T(8,128)S(1)}, u32[]{:S(2)}, u32[]{:S(2)}) collective-permute-start(f32[8,1024]{1,0:T(8,128)S(1)} %slice.185), channel_id=1, source_target_pairs={{0,4},{4,0},{8,12},{12,8},{16,20},{20,16},{24,28},{28,24},{1,5},{5... | collective-permute-start | bytes 98312 | tf_op jit(solution)/shard_map/ppermute | solution.py:949
  404.6 12.4 %collective-permute-start.30 = (bf16[4,64,1024]{2,1,0:T(8,128)(2,1)S(1)}, bf16[4,64,1024]{2,1,0:T(8,128)(2,1)S(1)}, u32[]{:S(2)}, u32[]{:S(2)}) collective-permute-start(bf16[4,64,1024]{2,1,0:T(8,128)(2,1)S(1)} %get-tuple-element.358), channel_id=1, source_target_pairs={{0,2},{1,3},{2,0},{3,1},{4,6},{5,7},{6,4},{7,5},{8,10},{9,11},{10,... | collective-permute-start | bytes 1572872 | tf_op jit(solution)/shard_map/ppermute | solution.py:949
  405.7 11.5 %collective-permute-start.29 = (bf16[4,64,1024]{2,1,0:T(8,128)(2,1)S(1)}, bf16[4,64,1024]{2,1,0:T(8,128)(2,1)S(1)}, u32[]{:S(2)}, u32[]{:S(2)}) collective-permute-start(bf16[4,64,1024]{2,1,0:T(8,128)(2,1)S(1)} %get-tuple-element.357), channel_id=1, source_target_pairs={{0,4},{4,0},{8,12},{12,8},{16,20},{20,16},{24,28},{28,24},{1,5},{5... | collective-permute-start | bytes 1572872 | tf_op jit(solution)/shard_map/ppermute | solution.py:949
  405.8 11.4 %collective-permute-start.33 = (bf16[128,1024]{1,0:T(8,128)(2,1)}, bf16[128,1024]{1,0:T(8,128)(2,1)S(1)}, u32[]{:S(2)}, u32[]{:S(2)}) collective-permute-start(bf16[128,1024]{1,0:T(8,128)(2,1)} %get-tuple-element.363), channel_id=1, source_target_pairs={{0,24},{4,28},{8,16},{12,20},{16,8},{20,12},{24,0},{28,4},{1,25},{... | collective-permute-start | bytes 786440 | tf_op jit(solution)/shard_map/ppermute | solution.py:949
  410.2 6.8 %collective-permute-start.32 = (f32[16,1024]{1,0:T(8,128)S(1)}, f32[16,1024]{1,0:T(8,128)S(1)}, u32[]{:S(2)}, u32[]{:S(2)}) collective-permute-start(f32[16,1024]{1,0:T(8,128)S(1)} %pad_maximum_fusion.5), channel_id=1, source_target_pairs={{0,2},{1,3},{2,0},{3,1},{4,6},{5,7},{6,4},{7,5},{8,10},{9,11},{10,... | collective-permute-start | bytes 196616 | tf_op jit(solution)/shard_map/ppermute | solution.py:949
  417.2 21.4 %collective-permute-start.35 = (bf16[4,128,1024]{2,1,0:T(8,128)(2,1)S(1)}, bf16[4,128,1024]{2,1,0:T(8,128)(2,1)S(1)}, u32[]{:S(2)}, u32[]{:S(2)}) collective-permute-start(bf16[4,128,1024]{2,1,0:T(8,128)(2,1)S(1)} %pad_maximum_fusion.4), channel_id=1, source_target_pairs={{0,4},{4,0},{8,12},{12,8},{16,20},{20,16},{24,28},{28,24},{1,5},{5... | collective-permute-start | bytes 3145736 | tf_op jit(solution)/shard_map/ppermute | solution.py:949
  417.7 21.6 %collective-permute-start.34 = (bf16[4,128,1024]{2,1,0:T(8,128)(2,1)S(1)}, bf16[4,128,1024]{2,1,0:T(8,128)(2,1)S(1)}, u32[]{:S(2)}, u32[]{:S(2)}) collective-permute-start(bf16[4,128,1024]{2,1,0:T(8,128)(2,1)S(1)} %pad_maximum_fusion.3), channel_id=1, source_target_pairs={{0,2},{1,3},{2,0},{3,1},{4,6},{5,7},{6,4},{7,5},{8,10},{9,11},{10,... | collective-permute-start | bytes 3145736 | tf_op jit(solution)/shard_map/ppermute | solution.py:949
  419.3 20.2 %collective-permute-start.38 = (bf16[128,1024]{1,0:T(8,128)(2,1)S(1)}, bf16[128,1024]{1,0:T(8,128)(2,1)S(1)}, u32[]{:S(2)}, u32[]{:S(2)}) collective-permute-start(bf16[128,1024]{1,0:T(8,128)(2,1)S(1)} %get-tuple-element.375), channel_id=1, source_target_pairs={{0,8},{4,12},{8,0},{12,4},{16,24},{20,28},{24,16},{28,20},{1,9},{5... | collective-permute-start | bytes 786440 | tf_op jit(solution)/shard_map/ppermute | solution.py:949
  420.8 18.8 %collective-permute-start.39 = (bf16[128,1024]{1,0:T(8,128)(2,1)S(1)}, bf16[128,1024]{1,0:T(8,128)(2,1)S(1)}, u32[]{:S(2)}, u32[]{:S(2)}) collective-permute-start(bf16[128,1024]{1,0:T(8,128)(2,1)S(1)} %get-tuple-element.376), channel_id=1, source_target_pairs={{0,16},{4,20},{8,24},{12,28},{16,0},{20,4},{24,8},{28,12},{1,17},{... | collective-permute-start | bytes 786440 | tf_op jit(solution)/shard_map/ppermute | solution.py:949
  422.1 8.7 %collective-permute-start.37 = (f32[8,1024]{1,0:T(8,128)S(1)}, f32[8,1024]{1,0:T(8,128)S(1)}, u32[]{:S(2)}, u32[]{:S(2)}) collective-permute-start(f32[8,1024]{1,0:T(8,128)S(1)} %get-tuple-element.442), channel_id=1, source_target_pairs={{0,16},{4,20},{8,24},{12,28},{16,0},{20,4},{24,8},{28,12},{1,17},{... | collective-permute-start | bytes 98312 | tf_op jit(solution)/shard_map/ppermute | solution.py:949
  442.6 12.1 %collective-permute-start.40 = (bf16[4,512,1024]{2,1,0:T(8,128)(2,1)}, bf16[4,512,1024]{2,1,0:T(8,128)(2,1)}, u32[]{:S(2)}, u32[]{:S(2)}) collective-permute-start(bf16[4,512,1024]{2,1,0:T(8,128)(2,1)} %constant_dynamic-update-slice_fusion.6.pieces), channel_id=1, source_target_pairs={{0,1},{1,0},{2,3},{3,2},{4,5},{5,4},{6,7},{7,6},{8,9},{9,8},{10,11... | collective-permute-start | bytes 12582920 | tf_op jit(solution)/shard_map/ppermute | solution.py:949
  446.7 12.4 %collective-permute-start.41 = (bf16[128,1024]{1,0:T(8,128)(2,1)S(1)}, bf16[128,1024]{1,0:T(8,128)(2,1)S(1)}, u32[]{:S(2)}, u32[]{:S(2)}) collective-permute-start(bf16[128,1024]{1,0:T(8,128)(2,1)S(1)} %get-tuple-element.396), channel_id=1, source_target_pairs={{0,24},{4,28},{8,16},{12,20},{16,8},{20,12},{24,0},{28,4},{1,25},{... | collective-permute-start | bytes 786440 | tf_op jit(solution)/shard_map/ppermute | solution.py:949
  (33 other events, 330.6 us)
Sparse Core Ops, SparseCore 0:
  9.6 59.8 all-gather.4
  71.0 58.2 all-gather.2
